TPU v7x, 32 devices: a whole 2x2x4 slice. The times are simulated.
32 devices in a mesh: level: 4 (over y, x), sub: 2 (over core), rhs: 4 (over z).
Axes of the slice: x: 2, y: 2, z: 4, core: 2. Of those that a mesh axis runs over, the one named last changes fastest.
Arguments:
- rhs: float32 [4, 32, 256, 256], P('level', 'sub', 'rhs'), may hold values from -6 to 6
- lower_inv: bfloat16 [4, 32, 256, 256], P('level', 'sub'), may hold values from -0.25 to 2.1
- lower_off: bfloat16 [4, 32, 256, 256], P('level', 'sub'), may hold values from -0.25 to 0.25
- upper_inv: bfloat16 [4, 32, 256, 256], P('level', 'sub'), may hold values from -0.25 to 2.1
- upper_off: bfloat16 [4, 32, 256, 256], P('level', 'sub'), may hold values from -0.25 to 0.25
- ancestor: bfloat16 [32, 256, 256], P('sub', 'rhs'), may hold values from -6 to 6
- parent: int32 [3, 32], replicated, may hold values from 0 to 31, as said below
Outputs:
- solution: float32 [4, 32, 256, 256], P('level', 'sub', 'rhs')
- update: float32 [4, 32, 256, 256], P('level', 'sub', 'rhs')
Inputs may be any that keep to these rules, and one draw needn't show every extreme that they name: parent[t, c] names a supernode of sub index c // 16 or of sub index (c // 16) XOR 2 ** (t mod 1), where supernode s has sub index s // 16; a parent may have no children or several.
All inputs are finite; a program needn't handle non-finite values.
Results may differ from a plain program's by a relative error of at most 0.009.
Values may be sent and summed in bfloat16 or wider, within the bound.
No kernel may reach another device: no remote copies, remote signals or barrier semaphores. Data moves between devices by JAX's collectives and lax.ppermute only.
A program may use at most 64 MiB of HBM per device.

v0:
```python
import jax
import jax.numpy as jnp
from jax import lax
from jax.sharding import PartitionSpec as P


def swapped(value, axis, apart):
    mask = 2**apart
    pairs = [(source, source ^ mask) for source in range(lax.axis_size(axis))]
    return lax.ppermute(value, axis, pairs)


def passed_along(value, axis, by):
    peers = lax.axis_size(axis)
    pairs = [(i, i + by) for i in range(peers) if 0 <= i + by < peers]
    return lax.ppermute(value, axis, pairs)


def block_product(left_rows, blocks):
    return lax.dot_general(
        left_rows, blocks, (((2,), (1,)), ((0,), (0,))), preferred_element_type=jnp.float32
    )


def forward_tier(residue, lower_inv, lower_off):
    forward = block_product(residue.astype(jnp.bfloat16), lower_inv).astype(jnp.bfloat16)
    return (forward, block_product(forward, lower_off))


def backward_tier(forward, above_rows, upper_inv, upper_off):
    reduced = forward.astype(jnp.float32) - block_product(above_rows, upper_off)
    return block_product(reduced.astype(jnp.bfloat16), upper_inv)


def parent_sums(selector, update):
    return jnp.einsum("jk,krw->jrw", selector, update, precision=lax.Precision.HIGHEST)


def fetch_parents(at_home, parent_slot, from_above, from_partner):
    home_rows = jnp.take(from_above, parent_slot, axis=0)
    partner_rows = jnp.take(from_partner, parent_slot, axis=0)
    return jnp.where(at_home[:, None, None], home_rows, partner_rows)


def body(rhs, lower_inv, lower_off, upper_inv, upper_off, ancestor, parent):
    levels = lax.axis_size("level")
    sub_count = lax.axis_size("sub")
    sub_bits = sub_count.bit_length() - 1
    tier_index = lax.axis_index("level")
    sub_index = lax.axis_index("sub")
    count_here = lower_inv.shape[1]
    rhs_here = rhs[0]
    lower_diag = lower_inv[0]
    lower_link = lower_off[0]
    upper_diag = upper_inv[0]
    upper_link = upper_off[0]
    parent_row = lax.dynamic_index_in_dim(
        parent, jnp.minimum(tier_index, levels - 2), 0, keepdims=False
    )
    parent_here = lax.dynamic_slice_in_dim(parent_row, sub_index * count_here, count_here)
    at_home = parent_here // count_here == sub_index
    parent_slot = parent_here % count_here
    slot_match = parent_slot[None, :] == jnp.arange(count_here, dtype=jnp.int32)[:, None]
    home_select = (slot_match & at_home[None, :]).astype(jnp.float32)
    far_select = (slot_match & jnp.logical_not(at_home)[None, :]).astype(jnp.float32)
    is_top = tier_index == levels - 1
    incoming = jnp.zeros(rhs_here.shape, jnp.float32)
    forward_keep = jnp.zeros(rhs_here.shape, jnp.bfloat16)
    update_keep = jnp.zeros(rhs_here.shape, jnp.float32)
    for section in range(levels):
        forward, update = forward_tier(rhs_here - incoming, lower_diag, lower_link)
        forward_keep = jnp.where(tier_index == section, forward, forward_keep)
        update_keep = jnp.where(tier_index == section, update, update_keep)
        if section + 1 < levels:
            home_part = parent_sums(home_select, update)
            far_part = parent_sums(far_select, update)
            received = swapped(far_part, "sub", section % sub_bits)
            incoming = passed_along(home_part + received, "level", 1)
    solution_keep = jnp.zeros(rhs_here.shape, jnp.float32)
    from_above = jnp.zeros(rhs_here.shape, jnp.bfloat16)
    from_partner = jnp.zeros(rhs_here.shape, jnp.bfloat16)
    for section in range(levels):
        tier_now = levels - 1 - section
        fetched = fetch_parents(at_home, parent_slot, from_above, from_partner)
        above_rows = jnp.where(is_top, ancestor, fetched)
        solution_part = backward_tier(forward_keep, above_rows, upper_diag, upper_link)
        solution_keep = jnp.where(tier_index == tier_now, solution_part, solution_keep)
        if section + 1 < levels:
            solution_bf = solution_part.astype(jnp.bfloat16)
            from_above = passed_along(solution_bf, "level", -1)
            from_partner = swapped(from_above, "sub", (tier_now - 1) % sub_bits)
    return (solution_keep[None], update_keep[None])


def solution(mesh):
    placed = (
        P("level", "sub", "rhs", None),
        P("level", "sub", None, None),
        P("level", "sub", None, None),
        P("level", "sub", None, None),
        P("level", "sub", None, None),
        P("sub", "rhs", None),
        P(),
    )
    return jax.shard_map(
        body,
        mesh=mesh,
        in_specs=placed,
        out_specs=(P("level", "sub", "rhs", None), P("level", "sub", "rhs", None)),
        check_vma=False,
    )
```

profile of v0, /device:TPU:0, one launch (start us, length us, event | category | flops | bytes accessed | tf_op | source)
XLA Modules:
  0.0 193.2 jit_solution(11549495818094326030)
XLA Ops:
  1.6 2.4 %fusion.64 = bf16[16,64,256]{2,1,0:T(8,128)(2,1)S(1)} fusion(bf16[1,16,256,256]{3,2,1,0:T(8,128)(2,1)} %param.10, f32[1,16,64,256]{3,2,1,0:T(8,128)} %param.9), kind=kOutput, calls=%fused_computation.51 | convolution fusion | flops 134217728 | bytes 3670016 | tf_op jit(solution)/shard_map/dot_general | solution.py:20
  9.9 4.8 %collective-permute-start.1 = (f32[16,64,256]{2,1,0:T(8,128)S(1)}, f32[16,64,256]{2,1,0:T(8,128)S(1)}, u32[]{:S(2)}, u32[]{:S(2)}) collective-permute-start(f32[16,64,256]{2,1,0:T(8,128)S(1)} %copy_add_fusion.2), channel_id=1, source_target_pairs={{0,8},{8,16},{16,24},{1,9},{9,17},{17,25},{2,10},{10,18},{18,26},{... | collective-permute-start | bytes 3145736 | tf_op jit(solution)/shard_map/ppermute | solution.py:16
  14.7 22.6 %collective-permute-done.1 = f32[16,64,256]{2,1,0:T(8,128)S(1)} collective-permute-done((f32[16,64,256]{2,1,0:T(8,128)S(1)}, f32[16,64,256]{2,1,0:T(8,128)S(1)}, u32[]{:S(2)}, u32[]{:S(2)}) %collective-permute-start.1) | collective-permute-done | bytes 1048608 | tf_op jit(solution)/shard_map/ppermute | solution.py:16
  41.5 1.4 collective-permute-done.2
  43.6 4.6 %collective-permute-start.3 = (f32[16,64,256]{2,1,0:T(8,128)S(1)}, f32[16,64,256]{2,1,0:T(8,128)S(1)}, u32[]{:S(2)}, u32[]{:S(2)}) collective-permute-start(f32[16,64,256]{2,1,0:T(8,128)S(1)} %copy_add_fusion.1), channel_id=1, source_target_pairs={{0,8},{8,16},{16,24},{1,9},{9,17},{17,25},{2,10},{10,18},{18,26},{... | collective-permute-start | bytes 3145736 | tf_op jit(solution)/shard_map/ppermute | solution.py:16
  48.2 22.5 %collective-permute-done.3 = f32[16,64,256]{2,1,0:T(8,128)S(1)} collective-permute-done((f32[16,64,256]{2,1,0:T(8,128)S(1)}, f32[16,64,256]{2,1,0:T(8,128)S(1)}, u32[]{:S(2)}, u32[]{:S(2)}) %collective-permute-start.3) | collective-permute-done | bytes 1048608 | tf_op jit(solution)/shard_map/ppermute | solution.py:16
  74.8 1.4 collective-permute-done.4
  76.2 1.6 copy_add_fusion
  77.8 5.4 %collective-permute-start.5 = (f32[16,64,256]{2,1,0:T(8,128)}, f32[16,64,256]{2,1,0:T(8,128)}, u32[]{:S(2)}, u32[]{:S(2)}) collective-permute-start(f32[16,64,256]{2,1,0:T(8,128)} %copy_add_fusion), channel_id=1, source_target_pairs={{0,8},{8,16},{16,24},{1,9},{9,17},{17,25},{2,10},{10,18},{18,26},{... | collective-permute-start | bytes 3145736 | tf_op jit(solution)/shard_map/ppermute | solution.py:16
  84.0 2.4 %gather_fusion = bf16[16,64,256]{2,1,0:T(8,128)(2,1)} fusion(bf16[16,64,256]{2,1,0:T(8,128)(2,1)} %broadcast.93, s32[1024]{0:T(1024)S(1)} %pad_clamp_fusion), kind=kCustom, calls=%fused_computation.clone | custom fusion | bytes 1048640 | tf_op jit(solution)/shard_map/jit(_take)/gather | solution.py:40
  86.5 18.7 %collective-permute-done.5 = f32[16,64,256]{2,1,0:T(8,128)} collective-permute-done((f32[16,64,256]{2,1,0:T(8,128)}, f32[16,64,256]{2,1,0:T(8,128)}, u32[]{:S(2)}, u32[]{:S(2)}) %collective-permute-start.5) | collective-permute-done | bytes 1048608 | tf_op jit(solution)/shard_map/ppermute | solution.py:16
  105.2 3.5 %select_select_fusion.6 = (bf16[16,64,256]{2,1,0:T(8,128)(2,1)}, bf16[16,64,256]{2,1,0:T(8,128)(2,1)}) fusion(bf16[16,64,256]{2,1,0:T(8,128)(2,1)} %copy-done.14, bf16[16,64,256]{2,1,0:T(8,128)(2,1)} %copy-done.13, bf16[16,64,256]{2,1,0:T(8,128)(2,1)} %copy-done.12, pred[]{:T(512)S(6)} %eq.63, pred[]{:T(512)S(6)} %eq.62, pred[]{:T(512)S(6)} %eq.55, ...), kind=kOutput, calls=%fused_computation.87 | convolution fusion | flops 136052736 | bytes 6815748 | tf_op jit(solution)/shard_map/dot_general | solution.py:20
  108.7 3.9 %fusion.180 = (bf16[16,64,256]{2,1,0:T(8,128)(2,1)}, f32[16,64,256]{2,1,0:T(8,128)}) fusion(bf16[1,16,256,256]{3,2,1,0:T(8,128)(2,1)S(1)} %copy-done, bf16[1,16,256,256]{3,2,1,0:T(8,128)(2,1)} %param.13, bf16[16,64,256]{2,1,0:T(8,128)(2,1)} %get-tuple-element.9, bf16[16,64,256]{2,1,0:T(8,128)(2,1)} %param.14, bf16[16,64,256]{2,1,0:T(8,128)(2,1)} %gather_fusion, ...), kind=kOutput, calls=%fused_computation.142 | convolution fusion | flops 270008320 | bytes 7340049 | tf_op jit(solution)/shard_map/dot_general | solution.py:20
  114.0 15.6 %collective-permute-done.6 = bf16[16,64,256]{2,1,0:T(8,128)(2,1)} collective-permute-done((bf16[16,64,256]{2,1,0:T(8,128)(2,1)}, bf16[16,64,256]{2,1,0:T(8,128)(2,1)}, u32[]{:S(2)}, u32[]{:S(2)}) %collective-permute-start.6) | collective-permute-done | bytes 524320 | tf_op jit(solution)/shard_map/ppermute | solution.py:16
  129.6 2.4 %gather_fusion.1 = bf16[16,64,256]{2,1,0:T(8,128)(2,1)} fusion(bf16[16,64,256]{2,1,0:T(8,128)(2,1)} %collective-permute-done.6, s32[1024]{0:T(1024)S(1)} %pad_clamp_fusion), kind=kCustom, calls=%fused_computation.1.clone | custom fusion | bytes 1048640 | tf_op jit(solution)/shard_map/jit(_take)/gather | solution.py:40
  132.1 2.4 %gather_fusion.2 = bf16[16,64,256]{2,1,0:T(8,128)(2,1)} fusion(bf16[16,64,256]{2,1,0:T(8,128)(2,1)} %collective-permute-done.7, s32[1024]{0:T(1024)S(1)} %pad_clamp_fusion), kind=kCustom, calls=%fused_computation.2.clone | custom fusion | bytes 1048640 | tf_op jit(solution)/shard_map/jit(_take)/gather | solution.py:41
  134.5 4.0 %fusion.183 = (bf16[16,64,256]{2,1,0:T(8,128)(2,1)}, f32[16,64,256]{2,1,0:T(8,128)}) fusion(bf16[1,16,256,256]{3,2,1,0:T(8,128)(2,1)S(1)} %copy-done, bf16[1,16,256,256]{3,2,1,0:T(8,128)(2,1)} %param.13, bf16[16,64,256]{2,1,0:T(8,128)(2,1)S(1)} %copy-done.8, bf16[16,64,256]{2,1,0:T(8,128)(2,1)S(1)} %copy-done.10, bf16[16,64,256]{2,1,0:T(8,128)(2,1)} %gather_fusion.2, ...), kind=kOutput, calls=%fused_computation.143 | convolution fusion | flops 270532608 | bytes 7864353 | tf_op jit(solution)/shard_map/dot_general | solution.py:20
  139.8 16.8 %collective-permute-done.8 = bf16[16,64,256]{2,1,0:T(8,128)(2,1)S(1)} collective-permute-done((bf16[16,64,256]{2,1,0:T(8,128)(2,1)}, bf16[16,64,256]{2,1,0:T(8,128)(2,1)S(1)}, u32[]{:S(2)}, u32[]{:S(2)}) %collective-permute-start.8) | collective-permute-done | bytes 524320 | tf_op jit(solution)/shard_map/ppermute | solution.py:16
  159.8 4.2 %fusion.188 = (bf16[16,64,256]{2,1,0:T(8,128)(2,1)}, f32[16,64,256]{2,1,0:T(8,128)}) fusion(bf16[1,16,256,256]{3,2,1,0:T(8,128)(2,1)S(1)} %copy-done, bf16[1,16,256,256]{3,2,1,0:T(8,128)(2,1)} %param.13, bf16[16,64,256]{2,1,0:T(8,128)(2,1)} %get-tuple-element.9, bf16[16,64,256]{2,1,0:T(8,128)(2,1)} %param.14, bf16[16,64,256]{2,1,0:T(8,128)(2,1)} %gather_fusion.4, ...), kind=kOutput, calls=%fused_computation.144 | convolution fusion | flops 270532608 | bytes 7864353 | tf_op jit(solution)/shard_map/dot_general | solution.py:20
  165.3 15.8 %collective-permute-done.10 = bf16[16,64,256]{2,1,0:T(8,128)(2,1)} collective-permute-done((bf16[16,64,256]{2,1,0:T(8,128)(2,1)}, bf16[16,64,256]{2,1,0:T(8,128)(2,1)}, u32[]{:S(2)}, u32[]{:S(2)}) %collective-permute-start.10) | collective-permute-done | bytes 524320 | tf_op jit(solution)/shard_map/ppermute | solution.py:16
  181.1 3.2 %fusion.35 = f32[1,16,64,256]{3,2,1,0:T(8,128)} fusion(bf16[16,64,256]{2,1,0:T(8,128)(2,1)} %get-tuple-element.10, bf16[1,16,256,256]{3,2,1,0:T(8,128)(2,1)} %param.11, f32[16,64,256]{2,1,0:T(8,128)} %copy-done.7, f32[16,64,256]{2,1,0:T(8,128)} %copy-done.6, f32[16,64,256]{2,1,0:T(8,128)S(1)} %copy-done.5, pred[]{:T(512)S(6)} %eq.63, pred[]{:T(512)S(6)} %eq.62, ...), kind=kOutput, calls=%fused_computation.44 | convolution fusion | flops 135266304 | bytes 6815748 | tf_op jit(solution)/shard_map/dot_general | solution.py:20
  184.3 2.5 %gather_fusion.5 = bf16[16,64,256]{2,1,0:T(8,128)(2,1)} fusion(bf16[16,64,256]{2,1,0:T(8,128)(2,1)} %collective-permute-done.10, s32[1024]{0:T(1024)S(1)} %pad_clamp_fusion), kind=kCustom, calls=%fused_computation.5.clone | custom fusion | bytes 1048640 | tf_op jit(solution)/shard_map/jit(_take)/gather | solution.py:40
  186.9 2.4 %gather_fusion.6 = bf16[16,64,256]{2,1,0:T(8,128)(2,1)} fusion(bf16[16,64,256]{2,1,0:T(8,128)(2,1)} %collective-permute-done.11, s32[1024]{0:T(1024)S(1)} %pad_clamp_fusion), kind=kCustom, calls=%fused_computation.6.clone | custom fusion | bytes 1048640 | tf_op jit(solution)/shard_map/jit(_take)/gather | solution.py:41
  189.3 3.9 %fusion.41 = f32[1,16,64,256]{3,2,1,0:T(8,128)} fusion(bf16[1,16,256,256]{3,2,1,0:T(8,128)(2,1)S(1)} %copy-done, f32[16,64,256]{2,1,0:T(8,128)} %get-tuple-element.16, f32[16,64,256]{2,1,0:T(8,128)} %get-tuple-element.14, f32[16,64,256]{2,1,0:T(8,128)} %get-tuple-element.12, bf16[1,16,256,256]{3,2,1,0:T(8,128)(2,1)} %param.13, ...), kind=kOutput, calls=%fused_computation.46 | convolution fusion | flops 271319040 | bytes 10485796 | tf_op jit(solution)/shard_map/dot_general | solution.py:20
  (68 shorter events, 23.6 us)
Async XLA Ops:
  0.6 108.1 %copy-start = (bf16[1,16,256,256]{3,2,1,0:T(8,128)(2,1)S(1)}, bf16[1,16,256,256]{3,2,1,0:T(8,128)(2,1)}, u32[]{:S(2)}) copy-start(bf16[1,16,256,256]{3,2,1,0:T(8,128)(2,1)} %param.12) | copy-start | bytes 6291460
  0.7 3.4 %copy-start.1 = (bf16[1,16,256,256]{3,2,1,0:T(8,128)(2,1)S(1)}, bf16[1,16,256,256]{3,2,1,0:T(8,128)(2,1)}, u32[]{:S(2)}) copy-start(bf16[1,16,256,256]{3,2,1,0:T(8,128)(2,1)} %param.11) | copy-start | bytes 6291460
  4.6 2.4 %copy-start.4 = (f32[16,64,256]{2,1,0:T(8,128)}, f32[16,64,256]{2,1,0:T(8,128)S(1)}, u32[]{:S(2)}) copy-start(f32[16,64,256]{2,1,0:T(8,128)S(1)} %fusion.22) | copy-start | bytes 3145732
  6.5 2.8 %collective-permute-start = (f32[16,64,256]{2,1,0:T(8,128)S(1)}, f32[16,64,256]{2,1,0:T(8,128)S(1)}, u32[]{:S(2)}, u32[]{:S(2)}) collective-permute-start(f32[16,64,256]{2,1,0:T(8,128)S(1)} %copy.11), channel_id=1, source_target_pairs={{0,4},{4,0},{1,5},{5,1},{2,6},{6,2},{3,7},{7,3},{8,12},{12,8},{9,1... | collective-permute-start | bytes 3145736 | tf_op jit(solution)/shard_map/ppermute | solution.py:10
  8.2 29.2 %copy-start.2 = (bf16[1,16,256,256]{3,2,1,0:T(8,128)(2,1)S(1)}, bf16[1,16,256,256]{3,2,1,0:T(8,128)(2,1)}, u32[]{:S(2)}) copy-start(bf16[1,16,256,256]{3,2,1,0:T(8,128)(2,1)} %param.10) | copy-start | bytes 6291460
  8.2 29.2 %copy-start.3 = (f32[1,16,64,256]{3,2,1,0:T(8,128)S(1)}, f32[1,16,64,256]{3,2,1,0:T(8,128)}, u32[]{:S(2)}) copy-start(f32[1,16,64,256]{3,2,1,0:T(8,128)} %param.9) | copy-start | bytes 3145732
  9.9 27.5 %collective-permute-start.1 = (f32[16,64,256]{2,1,0:T(8,128)S(1)}, f32[16,64,256]{2,1,0:T(8,128)S(1)}, u32[]{:S(2)}, u32[]{:S(2)}) collective-permute-start(f32[16,64,256]{2,1,0:T(8,128)S(1)} %copy_add_fusion.2), channel_id=1, source_target_pairs={{0,8},{8,16},{16,24},{1,9},{9,17},{17,25},{2,10},{10,18},{18,26},{... | collective-permute-start | bytes 3145736 | tf_op jit(solution)/shard_map/ppermute | solution.py:16
  38.3 1.9 %copy-start.6 = (f32[16,64,256]{2,1,0:T(8,128)}, f32[16,64,256]{2,1,0:T(8,128)S(1)}, u32[]{:S(2)}) copy-start(f32[16,64,256]{2,1,0:T(8,128)S(1)} %fusion.20) | copy-start | bytes 3145732
  40.2 2.7 %collective-permute-start.2 = (f32[16,64,256]{2,1,0:T(8,128)S(1)}, f32[16,64,256]{2,1,0:T(8,128)S(1)}, u32[]{:S(2)}, u32[]{:S(2)}) collective-permute-start(f32[16,64,256]{2,1,0:T(8,128)S(1)} %copy.14), channel_id=1, source_target_pairs={{0,4},{4,0},{1,5},{5,1},{2,6},{6,2},{3,7},{7,3},{8,12},{12,8},{9,1... | collective-permute-start | bytes 3145736 | tf_op jit(solution)/shard_map/ppermute | solution.py:10
  43.6 27.1 %collective-permute-start.3 = (f32[16,64,256]{2,1,0:T(8,128)S(1)}, f32[16,64,256]{2,1,0:T(8,128)S(1)}, u32[]{:S(2)}, u32[]{:S(2)}) collective-permute-start(f32[16,64,256]{2,1,0:T(8,128)S(1)} %copy_add_fusion.1), channel_id=1, source_target_pairs={{0,8},{8,16},{16,24},{1,9},{9,17},{17,25},{2,10},{10,18},{18,26},{... | collective-permute-start | bytes 3145736 | tf_op jit(solution)/shard_map/ppermute | solution.py:16
  71.6 1.9 %copy-start.7 = (f32[16,64,256]{2,1,0:T(8,128)}, f32[16,64,256]{2,1,0:T(8,128)S(1)}, u32[]{:S(2)}) copy-start(f32[16,64,256]{2,1,0:T(8,128)S(1)} %fusion.18) | copy-start | bytes 3145732
  73.5 2.7 %collective-permute-start.4 = (f32[16,64,256]{2,1,0:T(8,128)S(1)}, f32[16,64,256]{2,1,0:T(8,128)S(1)}, u32[]{:S(2)}, u32[]{:S(2)}) collective-permute-start(f32[16,64,256]{2,1,0:T(8,128)S(1)} %copy.17), channel_id=1, source_target_pairs={{0,4},{4,0},{1,5},{5,1},{2,6},{6,2},{3,7},{7,3},{8,12},{12,8},{9,1... | collective-permute-start | bytes 3145736 | tf_op jit(solution)/shard_map/ppermute | solution.py:10
  77.8 27.4 %collective-permute-start.5 = (f32[16,64,256]{2,1,0:T(8,128)}, f32[16,64,256]{2,1,0:T(8,128)}, u32[]{:S(2)}, u32[]{:S(2)}) collective-permute-start(f32[16,64,256]{2,1,0:T(8,128)} %copy_add_fusion), channel_id=1, source_target_pairs={{0,8},{8,16},{16,24},{1,9},{9,17},{17,25},{2,10},{10,18},{18,26},{... | collective-permute-start | bytes 3145736 | tf_op jit(solution)/shard_map/ppermute | solution.py:16
  112.6 21.9 %copy-start.8 = (bf16[16,64,256]{2,1,0:T(8,128)(2,1)S(1)}, bf16[16,64,256]{2,1,0:T(8,128)(2,1)}, u32[]{:S(2)}) copy-start(bf16[16,64,256]{2,1,0:T(8,128)(2,1)} %get-tuple-element.9) | copy-start | bytes 1572868
  112.6 21.9 %copy-start.10 = (bf16[16,64,256]{2,1,0:T(8,128)(2,1)S(1)}, bf16[16,64,256]{2,1,0:T(8,128)(2,1)}, u32[]{:S(2)}) copy-start(bf16[16,64,256]{2,1,0:T(8,128)(2,1)} %param.14) | copy-start | bytes 1572868
  112.6 17.0 %collective-permute-start.6 = (bf16[16,64,256]{2,1,0:T(8,128)(2,1)}, bf16[16,64,256]{2,1,0:T(8,128)(2,1)}, u32[]{:S(2)}, u32[]{:S(2)}) collective-permute-start(bf16[16,64,256]{2,1,0:T(8,128)(2,1)} %get-tuple-element.11), channel_id=1, source_target_pairs={{8,0},{16,8},{24,16},{9,1},{17,9},{25,17},{10,2},{18,10},{26,18},{... | collective-permute-start | bytes 1572872 | tf_op jit(solution)/shard_map/ppermute | solution.py:16
  129.6 2.4 %collective-permute-start.7 = (bf16[16,64,256]{2,1,0:T(8,128)(2,1)}, bf16[16,64,256]{2,1,0:T(8,128)(2,1)}, u32[]{:S(2)}, u32[]{:S(2)}) collective-permute-start(bf16[16,64,256]{2,1,0:T(8,128)(2,1)} %collective-permute-done.6), channel_id=1, source_target_pairs={{0,4},{4,0},{1,5},{5,1},{2,6},{6,2},{3,7},{7,3},{8,12},{12,8},{9,1... | collective-permute-start | bytes 1572872 | tf_op jit(solution)/shard_map/ppermute | solution.py:10
  138.5 18.1 %collective-permute-start.8 = (bf16[16,64,256]{2,1,0:T(8,128)(2,1)}, bf16[16,64,256]{2,1,0:T(8,128)(2,1)S(1)}, u32[]{:S(2)}, u32[]{:S(2)}) collective-permute-start(bf16[16,64,256]{2,1,0:T(8,128)(2,1)} %get-tuple-element.13), channel_id=1, source_target_pairs={{8,0},{16,8},{24,16},{9,1},{17,9},{25,17},{10,2},{18,10},{26,18},{... | collective-permute-start | bytes 1572872 | tf_op jit(solution)/shard_map/ppermute | solution.py:16
  156.6 1.9 collective-permute-start.9
  159.8 21.3 %copy-start.5 = (f32[16,64,256]{2,1,0:T(8,128)S(1)}, f32[16,64,256]{2,1,0:T(8,128)}, u32[]{:S(2)}) copy-start(f32[16,64,256]{2,1,0:T(8,128)} %copy-done.4) | copy-start | bytes 3145732
  164.0 17.1 %collective-permute-start.10 = (bf16[16,64,256]{2,1,0:T(8,128)(2,1)}, bf16[16,64,256]{2,1,0:T(8,128)(2,1)}, u32[]{:S(2)}, u32[]{:S(2)}) collective-permute-start(bf16[16,64,256]{2,1,0:T(8,128)(2,1)} %get-tuple-element.15), channel_id=1, source_target_pairs={{8,0},{16,8},{24,16},{9,1},{17,9},{25,17},{10,2},{18,10},{26,18},{... | collective-permute-start | bytes 1572872 | tf_op jit(solution)/shard_map/ppermute | solution.py:16
  181.1 5.8 %collective-permute-start.11 = (bf16[16,64,256]{2,1,0:T(8,128)(2,1)}, bf16[16,64,256]{2,1,0:T(8,128)(2,1)}, u32[]{:S(2)}, u32[]{:S(2)}) collective-permute-start(bf16[16,64,256]{2,1,0:T(8,128)(2,1)} %collective-permute-done.10), channel_id=1, source_target_pairs={{0,4},{4,0},{1,5},{5,1},{2,6},{6,2},{3,7},{7,3},{8,12},{12,8},{9,1... | collective-permute-start | bytes 1572872 | tf_op jit(solution)/shard_map/ppermute | solution.py:10
  184.3 4.9 %copy-start.9 = (bf16[16,64,256]{2,1,0:T(8,128)(2,1)S(1)}, bf16[16,64,256]{2,1,0:T(8,128)(2,1)}, u32[]{:S(2)}) copy-start(bf16[16,64,256]{2,1,0:T(8,128)(2,1)} %get-tuple-element.9) | copy-start | bytes 1572868
  184.3 4.9 %copy-start.11 = (bf16[16,64,256]{2,1,0:T(8,128)(2,1)S(1)}, bf16[16,64,256]{2,1,0:T(8,128)(2,1)}, u32[]{:S(2)}) copy-start(bf16[16,64,256]{2,1,0:T(8,128)(2,1)} %param.14) | copy-start | bytes 1572868
  (3 other events, 5.2 us)
where the time goes:
time: 195 us; the launch traced here: 193 us
  waiting for transfers between devices  116 us (59%)
  matrix products  34.8 us (18%)
  starting transfers between devices  19.5 us (10%)
  local copies, waits for them, and re-layouts  17.7 us (9%)
  other arithmetic  3.85 us (2%)
    ppermute x6, waiting for transfers between devices, passed_along(): return lax.ppermute(value, axis, pairs)  112 us
    dot_general x12, matrix products, block_product(): lax.dot_general(left_rows, blocks, (((2,), (1,)), ((0,), (0,))), preferre...  27.5 us
    ppermute x6, starting transfers between devices, passed_along(): return lax.ppermute(value, axis, pairs)  18.8 us
    gather x4, local copies, waits for them, and re-layouts, fetch_parents(): home_rows = jnp.take(from_above, parent_slot, axis=0)  8.75 us
    dot_general x6, matrix products, parent_sums(): jnp.einsum('jk,krw->jrw', selector, update, precision=lax.Precision.HIGHEST)  7.26 us
    gather x3, local copies, waits for them, and re-layouts, fetch_parents(): partner_rows = jnp.take(from_partner, parent_slot, axis=0)  6.21 us
    ppermute x6, waiting for transfers between devices, swapped(): return lax.ppermute(value, axis, pairs)  4.41 us
  transfers between devices with their start and end apart: 12, of which 10 were waited for; matrix products, arithmetic and copies ran while one was open for 9% of the time, Pallas kernels for 0%

commit v1 on v0

v1 whole, which is shorter than its diff:
```python
import functools

import jax
import jax.numpy as jnp
from jax import lax
from jax.experimental import pallas as pl
from jax.experimental.pallas import tpu as pltpu
from jax.sharding import PartitionSpec as P

CHUNKS = 2
LOCAL_SWAP = False
VMEM_BYTES = 24 * 2**20

BF16 = jnp.bfloat16
F32 = jnp.float32
IN_VMEM = pl.BlockSpec(memory_space=pltpu.VMEM)
IN_SMEM = pl.BlockSpec(memory_space=pltpu.SMEM)


def dot(left, right):
    return jnp.dot(left, right, preferred_element_type=F32)


def forward_kernel(section, start, rows, info, rhs, incoming, inv, off, kept_f, kept_u, fwd, upd, home, far, total):
    del kept_f, kept_u
    count = inv.shape[0]

    @pl.when(info[count] == section)
    def _():
        total[...] = jnp.zeros_like(total)
        for node in range(count):
            right_side = rhs[node, pl.ds(start, rows), :]
            if incoming is not None:
                right_side = right_side - incoming[node].astype(F32)
            forward = dot(right_side.astype(BF16), inv[node]).astype(BF16)
            fwd[node] = forward
            update = dot(forward, off[node])
            upd[node] = update
            total[info[node]] += update
        home[...] = total[:count]
        far[...] = total[count:].astype(BF16)


def first_kernel(section, start, rows, info, rhs, inv, off, kept_f, kept_u, fwd, upd, home, far, total):
    forward_kernel(section, start, rows, info, rhs, None, inv, off, kept_f, kept_u, fwd, upd, home, far, total)


def top_kernel(section, start, rows, info, rhs, incoming, inv, up_off, up_inv, ancestor, kept_f, kept_s, fwd, sol, sol_bf):
    del kept_f, kept_s
    count = inv.shape[0]

    @pl.when(info[count] == section)
    def _():
        for node in range(count):
            right_side = rhs[node, pl.ds(start, rows), :] - incoming[node].astype(F32)
            forward = dot(right_side.astype(BF16), inv[node]).astype(BF16)
            fwd[node] = forward
            above = dot(ancestor[node, pl.ds(start, rows), :], up_off[node])
            reduced = (forward.astype(F32) - above).astype(BF16)
            solved = dot(reduced, up_inv[node])
            sol[node] = solved
            sol_bf[node] = solved.astype(BF16)


def top_update_kernel(section, start, rows, info, fwd, off, kept_u, upd):
    del kept_u, start, rows
    count = off.shape[0]

    @pl.when(info[count] == section)
    def _():
        for node in range(count):
            upd[node] = dot(fwd[node], off[node])


def backward_kernel(section, start, rows, info, fwd, own, partner, up_off, up_inv, kept_s, sol, sol_bf):
    del kept_s, start, rows
    count = up_inv.shape[0]

    @pl.when(info[count] == section)
    def _():
        for node in range(count):
            place = info[node]
            at_home = place < count
            slot = jnp.where(at_home, place, place - count)
            above = jnp.where(at_home, own[slot], partner[slot])
            reduced = (fwd[node].astype(F32) - dot(above, up_off[node])).astype(BF16)
            solved = dot(reduced, up_inv[node])
            sol[node] = solved
            sol_bf[node] = solved.astype(BF16)


def call(kernel, section, start, rows, operands, outs, aliases, scratch=(), products=2):
    count = operands[1].shape[0]
    return pl.pallas_call(
        functools.partial(kernel, section, start, rows),
        in_specs=[IN_SMEM] + [IN_VMEM] * (len(operands) - 1),
        out_specs=[IN_VMEM] * len(outs),
        out_shape=outs,
        scratch_shapes=scratch,
        input_output_aliases=aliases,
        compiler_params=pltpu.CompilerParams(vmem_limit_bytes=VMEM_BYTES),
        cost_estimate=pl.CostEstimate(
            flops=products * 2 * count * rows * 256 * 256, bytes_accessed=count * 256 * 256 * 2 * products, transcendentals=0
        ),
    )(*operands)


def swapped(value, section, apart):
    mask = 2**apart
    subs = lax.axis_size("sub")
    if not LOCAL_SWAP:
        return lax.ppermute(value, "sub", [(i, i ^ mask) for i in range(subs)])
    pairs = [(section * subs + i, section * subs + (i ^ mask)) for i in range(subs)]
    return lax.ppermute(value, ("level", "sub"), pairs)


def body(rhs, lower_inv, lower_off, upper_inv, upper_off, ancestor, parent):
    levels = lax.axis_size("level")
    sub_count = lax.axis_size("sub")
    sub_bits = sub_count.bit_length() - 1
    tier = lax.axis_index("level")
    sub = lax.axis_index("sub")
    rhs, lower_inv, lower_off, upper_inv, upper_off = (
        value[0] for value in (rhs, lower_inv, lower_off, upper_inv, upper_off)
    )
    count, all_rows, width = rhs.shape
    rows = all_rows // CHUNKS
    parent_row = lax.dynamic_index_in_dim(parent, jnp.minimum(tier, levels - 2), 0, keepdims=False)
    parent_here = lax.dynamic_slice_in_dim(parent_row, sub * count, count)
    place = parent_here % count + jnp.where(parent_here // count == sub, 0, count)
    info = jnp.concatenate([place, tier[None]]).astype(jnp.int32)

    def shape(dtype):
        return jax.ShapeDtypeStruct((count, rows, width), dtype)

    fwd = [jnp.zeros((count, rows, width), BF16) for _ in range(CHUNKS)]
    upd = [jnp.zeros((count, rows, width), F32) for _ in range(CHUNKS)]
    sol = [jnp.zeros((count, rows, width), F32) for _ in range(CHUNKS)]
    incoming = [None] * CHUNKS
    above = [None] * CHUNKS
    top = levels - 1
    for section in range(top):
        for c in range(CHUNKS):
            if section == 0:
                kernel, operands = first_kernel, (info, rhs, lower_inv, lower_off, fwd[c], upd[c])
            else:
                kernel, operands = forward_kernel, (info, rhs, incoming[c], lower_inv, lower_off, fwd[c], upd[c])
            at = len(operands) - 2
            fwd[c], upd[c], home, far = call(
                kernel, section, c * rows, rows, operands,
                [shape(BF16), shape(F32), shape(F32), shape(BF16)], {at: 0, at + 1: 1},
                [pltpu.VMEM((2 * count, rows, width), F32)],
            )
            received = swapped(far, section, section % sub_bits)
            summed = (home + received.astype(F32)).astype(BF16)
            incoming[c] = lax.ppermute(summed, "level", [(section, section + 1)])
    for c in range(CHUNKS):
        fwd[c], sol[c], solved = call(
            top_kernel, top, c * rows, rows,
            (info, rhs, incoming[c], lower_inv, upper_off, upper_inv, ancestor, fwd[c], sol[c]),
            [shape(BF16), shape(F32), shape(BF16)], {7: 0, 8: 1}, products=3,
        )
        above[c] = lax.ppermute(solved, "level", [(top, top - 1)])
    for c in range(CHUNKS):
        (upd[c],) = call(top_update_kernel, top, c * rows, rows, (info, fwd[c], lower_off, upd[c]), [shape(F32)], {3: 0}, products=1)
    for section in reversed(range(top)):
        for c in range(CHUNKS):
            partner = swapped(above[c], section, section % sub_bits)
            sol[c], solved = call(
                backward_kernel, section, c * rows, rows,
                (info, fwd[c], above[c], partner, upper_off, upper_inv, sol[c]),
                [shape(F32), shape(BF16)], {6: 0},
            )
            if section:
                above[c] = lax.ppermute(solved, "level", [(section, section - 1)])
    return jnp.concatenate(sol, axis=1)[None], jnp.concatenate(upd, axis=1)[None]


def solution(mesh):
    placed = (
        P("level", "sub", "rhs", None),
        P("level", "sub", None, None),
        P("level", "sub", None, None),
        P("level", "sub", None, None),
        P("level", "sub", None, None),
        P("sub", "rhs", None),
        P(),
    )
    return jax.shard_map(
        body,
        mesh=mesh,
        in_specs=placed,
        out_specs=(P("level", "sub", "rhs", None), P("level", "sub", "rhs", None)),
        check_vma=False,
    )
```

time: 195 us -> 112 us (0.57)
  waiting for transfers between devices: 116 us -> 73.2 us
  matrix products: 34.8 us -> 0 us
  Pallas kernels: 0 us -> 13.6 us
  local copies, waits for them, and re-layouts: 17.7 us -> 4.64 us
  starting transfers between devices: 19.5 us -> 15.3 us
    ppermute x12 -> x24, waiting for transfers between devices: 116 us -> 73.2 us  [the longest x4 60.6 us: body(): above[c] = lax.ppermute(solved, 'level', [(section, section - 1)])]
    dot_general x18 -> x0, matrix products: 34.8 us -> none  [the longest x12 27.5 us: block_product(): lax.dot_general(left_rows, blocks, (((2,), (1,)), ((0,), (0,))), preferre...]
    gather x7 -> x0, local copies, waits for them, and re-layouts: 15 us -> none  [the longest x4 8.75 us: fetch_parents(): home_rows = jnp.take(from_above, parent_slot, axis=0)]
    pallas_call x0 -> x16, Pallas kernels: none -> 13.6 us  [call(): pl.pallas_call(functools.partial(kernel, section, start, rows), in_specs=...]
    unnamed x30 -> x14, local copies, waits for them, and re-layouts: 0.07 us -> 4.42 us
    ppermute x12 -> x24, starting transfers between devices: 19.5 us -> 15.3 us  [the longest x6 7.35 us: body(): incoming[c] = lax.ppermute(summed, 'level', [(section, section + 1)])]
    add x3 -> x1, other arithmetic: 2.88 us -> 0.77 us  [body(): parent_here % count + jnp.where(parent_here // count == sub, 0, count)]
    broadcast_in_dim x0 -> x2, other arithmetic: none -> 2.08 us  [the longest x1 1.04 us: body(): jnp.concatenate(upd, axis=1)[None]]
  transfers between devices with their start and end apart: 12 -> 24, of which waited for: 10 -> 8; matrix products, arithmetic and copies ran while one was open for 9% -> 2% of each run, Pallas kernels for 0% -> 9%
where the time goes in v1:
time: 112 us; the launch traced here: 111 us
  waiting for transfers between devices  73.2 us (65%)
  starting transfers between devices  15.3 us (14%)
  Pallas kernels  13.6 us (12%)
  local copies, waits for them, and re-layouts  4.64 us (4%)
  other arithmetic  3.42 us (3%)
    ppermute x4, waiting for transfers between devices, body(): above[c] = lax.ppermute(solved, 'level', [(section, section - 1)])  60.6 us
    pallas_call x16, Pallas kernels, call(): pl.pallas_call(functools.partial(kernel, section, start, rows), in_specs=...  13.6 us
    ppermute x6, waiting for transfers between devices, body(): incoming[c] = lax.ppermute(summed, 'level', [(section, section + 1)])  9.41 us
    ppermute x6, starting transfers between devices, body(): incoming[c] = lax.ppermute(summed, 'level', [(section, section + 1)])  7.35 us
    unnamed x14, local copies, waits for them, and re-layouts  4.42 us
    ppermute x4, starting transfers between devices, body(): above[c] = lax.ppermute(solved, 'level', [(section, section - 1)])  4.07 us
    ppermute x12, waiting for transfers between devices, swapped(): return lax.ppermute(value, 'sub', [(i, i ^ mask) for i in range(subs)])  3.19 us
    ppermute x12, starting transfers between devices, swapped(): return lax.ppermute(value, 'sub', [(i, i ^ mask) for i in range(subs)])  2.58 us
  transfers between devices with their start and end apart: 24, of which 8 were waited for; matrix products, arithmetic and copies ran while one was open for 2% of the time, Pallas kernels for 9%

profile of v1, /device:TPU:0, one launch (start us, length us, event | category | flops | bytes accessed | tf_op | source)
XLA Modules:
  0.0 111.3 jit_solution(1938057846341575712)
XLA Ops:
  0.6 0.8 fusion
  1.6 1.6 %copy-done = bf16[1,16,256,256]{3,2,1,0:T(8,128)(2,1)S(1)} copy-done((bf16[1,16,256,256]{3,2,1,0:T(8,128)(2,1)S(1)}, bf16[1,16,256,256]{3,2,1,0:T(8,128)(2,1)}, u32[]{:S(2)}) %copy-start) | copy-done | bytes 2097176
  3.2 1.6 %copy-done.1 = bf16[1,16,256,256]{3,2,1,0:T(8,128)(2,1)S(1)} copy-done((bf16[1,16,256,256]{3,2,1,0:T(8,128)(2,1)S(1)}, bf16[1,16,256,256]{3,2,1,0:T(8,128)(2,1)}, u32[]{:S(2)}) %copy-start.1) | copy-done | bytes 2097176
  4.8 1.2 %copy-done.5 = f32[1,16,64,256]{3,2,1,0:T(8,128)S(1)} copy-done((f32[1,16,64,256]{3,2,1,0:T(8,128)S(1)}, f32[1,16,64,256]{3,2,1,0:T(8,128)}, u32[]{:S(2)}) %copy-start.5) | copy-done | bytes 1048600
  6.0 1.5 %shard_map.93 = (bf16[16,32,256]{2,1,0:T(8,128)(2,1)S(1)}, f32[16,32,256]{2,1,0:T(8,128)S(1)}, f32[16,32,256]{2,1,0:T(8,128)S(1)}, bf16[16,32,256]{2,1,0:T(8,128)(2,1)S(1)}) custom-call(s32[17]{0:T(128)S(1)} %pad_add_fusion.info, f32[16,64,256]{2,1,0:T(8,128)S(1)} %bitcast.55, ...), custom_call_target="tpu_custom_call", output_to_operand_aliasing={{0}: (4, {}), {1}: (5, {})} | custom-call | flops 134217728 | bytes 4194304 | tf_op jit(solution)/shard_map/pallas_call | solution.py:94
  8.1 1.5 %shard_map.86 = (bf16[16,32,256]{2,1,0:T(8,128)(2,1)S(1)}, f32[16,32,256]{2,1,0:T(8,128)S(1)}, f32[16,32,256]{2,1,0:T(8,128)S(1)}, bf16[16,32,256]{2,1,0:T(8,128)(2,1)S(1)}) custom-call(s32[17]{0:T(128)S(1)} %pad_add_fusion.info, f32[16,64,256]{2,1,0:T(8,128)S(1)} %bitcast.56, ...), custom_call_target="tpu_custom_call", output_to_operand_aliasing={{0}: (4, {}), {1}: (5, {})} | custom-call | flops 134217728 | bytes 4194304 | tf_op jit(solution)/shard_map/pallas_call | solution.py:94
  9.8 3.3 %collective-permute-start.13 = (bf16[16,32,256]{2,1,0:T(8,128)(2,1)S(1)}, bf16[16,32,256]{2,1,0:T(8,128)(2,1)S(1)}, u32[]{:S(2)}, u32[]{:S(2)}) collective-permute-start(bf16[16,32,256]{2,1,0:T(8,128)(2,1)S(1)} %add_convert_fusion.2), channel_id=1, source_target_pairs={{0,8},{1,9},{2,10},{3,11},{4,12},{5,13},{6,14},{7,15}} | collective-permute-start | bytes 786440 | tf_op jit(solution)/shard_map/ppermute | solution.py:156
  13.2 1.3 %collective-permute-start.1 = (bf16[16,32,256]{2,1,0:T(8,128)(2,1)S(1)}, bf16[16,32,256]{2,1,0:T(8,128)(2,1)S(1)}, u32[]{:S(2)}, u32[]{:S(2)}) collective-permute-start(bf16[16,32,256]{2,1,0:T(8,128)(2,1)S(1)} %add_convert_fusion.5), channel_id=1, source_target_pairs={{0,8},{1,9},{2,10},{3,11},{4,12},{5,13},{6,14},{7,15}} | collective-permute-start | bytes 786440 | tf_op jit(solution)/shard_map/ppermute | solution.py:156
  14.5 5.2 %collective-permute-done.13.incoming = bf16[16,32,256]{2,1,0:T(8,128)(2,1)S(1)} collective-permute-done((bf16[16,32,256]{2,1,0:T(8,128)(2,1)S(1)}, bf16[16,32,256]{2,1,0:T(8,128)(2,1)S(1)}, u32[]{:S(2)}, u32[]{:S(2)}) %collective-permute-start.13) | collective-permute-done | bytes 262176 | tf_op jit(solution)/shard_map/ppermute | solution.py:156
  20.4 4.2 %collective-permute-done.1.incoming = bf16[16,32,256]{2,1,0:T(8,128)(2,1)S(1)} collective-permute-done((bf16[16,32,256]{2,1,0:T(8,128)(2,1)S(1)}, bf16[16,32,256]{2,1,0:T(8,128)(2,1)S(1)}, u32[]{:S(2)}, u32[]{:S(2)}) %collective-permute-start.1) | collective-permute-done | bytes 262176 | tf_op jit(solution)/shard_map/ppermute | solution.py:156
  26.0 0.7 collective-permute-done.2
  29.7 0.7 collective-permute-start.17
  30.5 0.7 collective-permute-start.5
  31.9 0.7 collective-permute-start.18
  34.4 1.0 collective-permute-done.19.partner
  38.5 1.0 collective-permute-done.21.partner
  40.1 1.3 %collective-permute-start.22 = (bf16[16,32,256]{2,1,0:T(8,128)(2,1)S(1)}, bf16[16,32,256]{2,1,0:T(8,128)(2,1)S(1)}, u32[]{:S(2)}, u32[]{:S(2)}) collective-permute-start(bf16[16,32,256]{2,1,0:T(8,128)(2,1)S(1)} %get-tuple-element.77), channel_id=1, source_target_pairs={{8,0},{9,1},{10,2},{11,3},{12,4},{13,5},{14,6},{15,7}} | collective-permute-start | bytes 786440 | tf_op jit(solution)/shard_map/ppermute | solution.py:175
  42.0 1.4 %collective-permute-start.10 = (bf16[16,32,256]{2,1,0:T(8,128)(2,1)S(1)}, bf16[16,32,256]{2,1,0:T(8,128)(2,1)S(1)}, u32[]{:S(2)}, u32[]{:S(2)}) collective-permute-start(bf16[16,32,256]{2,1,0:T(8,128)(2,1)S(1)} %get-tuple-element.58), channel_id=1, source_target_pairs={{8,0},{9,1},{10,2},{11,3},{12,4},{13,5},{14,6},{15,7}} | collective-permute-start | bytes 786440 | tf_op jit(solution)/shard_map/ppermute | solution.py:175
  43.4 55.1 %collective-permute-done.22.own = bf16[16,32,256]{2,1,0:T(8,128)(2,1)S(1)} collective-permute-done((bf16[16,32,256]{2,1,0:T(8,128)(2,1)S(1)}, bf16[16,32,256]{2,1,0:T(8,128)(2,1)S(1)}, u32[]{:S(2)}, u32[]{:S(2)}) %collective-permute-start.22) | collective-permute-done | bytes 262176 | tf_op jit(solution)/shard_map/ppermute | solution.py:175
  98.6 5.4 %collective-permute-done.10.own = bf16[16,32,256]{2,1,0:T(8,128)(2,1)S(1)} collective-permute-done((bf16[16,32,256]{2,1,0:T(8,128)(2,1)S(1)}, bf16[16,32,256]{2,1,0:T(8,128)(2,1)S(1)}, u32[]{:S(2)}, u32[]{:S(2)}) %collective-permute-start.10) | collective-permute-done | bytes 262176 | tf_op jit(solution)/shard_map/ppermute | solution.py:175
  105.1 1.0 maximum_bitcast_fusion.1
  106.2 2.0 %shard_map.99 = (f32[16,32,256]{2,1,0:T(8,128)S(1)}, bf16[16,32,256]{2,1,0:T(8,128)(2,1)}) custom-call(s32[17]{0:T(128)S(1)} %pad_add_fusion.info, bf16[16,32,256]{2,1,0:T(8,128)(2,1)S(1)} %get-tuple-element.72.fwd, bf16[16,32,256]{2,1,0:T(8,128)(2,1)S(1)} %collective-permute-done.22.own, ...), custom_call_target="tpu_custom_call", output_to_operand_aliasing={{0}: (6, {})} | custom-call | flops 134217728 | bytes 4194304 | tf_op jit(solution)/shard_map/pallas_call | solution.py:94
  108.2 2.0 %shard_map.92 = (f32[16,32,256]{2,1,0:T(8,128)S(1)}, bf16[16,32,256]{2,1,0:T(8,128)(2,1)}) custom-call(s32[17]{0:T(128)S(1)} %pad_add_fusion.info, bf16[16,32,256]{2,1,0:T(8,128)(2,1)S(1)} %get-tuple-element.53.fwd, bf16[16,32,256]{2,1,0:T(8,128)(2,1)S(1)} %collective-permute-done.10.own, ...), custom_call_target="tpu_custom_call", output_to_operand_aliasing={{0}: (6, {})} | custom-call | flops 134217728 | bytes 4194304 | tf_op jit(solution)/shard_map/pallas_call | solution.py:94
  110.2 1.0 maximum_bitcast_fusion
  (70 shorter events, 13.8 us)
Async XLA Ops:
  7.5 2.2 %collective-permute-start.12 = (bf16[16,32,256]{2,1,0:T(8,128)(2,1)S(1)}, bf16[16,32,256]{2,1,0:T(8,128)(2,1)S(1)}, u32[]{:S(2)}, u32[]{:S(2)}) collective-permute-start(bf16[16,32,256]{2,1,0:T(8,128)(2,1)S(1)} %get-tuple-element.62), channel_id=1, source_target_pairs={{0,4},{4,0},{1,5},{5,1},{2,6},{6,2},{3,7},{7,3},{8,12},{12,8},{9,1... | collective-permute-start | bytes 786440 | tf_op jit(solution)/shard_map/ppermute | solution.py:112
  9.5 3.6 %collective-permute-start = (bf16[16,32,256]{2,1,0:T(8,128)(2,1)S(1)}, bf16[16,32,256]{2,1,0:T(8,128)(2,1)S(1)}, u32[]{:S(2)}, u32[]{:S(2)}) collective-permute-start(bf16[16,32,256]{2,1,0:T(8,128)(2,1)S(1)} %get-tuple-element.43), channel_id=1, source_target_pairs={{0,4},{4,0},{1,5},{5,1},{2,6},{6,2},{3,7},{7,3},{8,12},{12,8},{9,1... | collective-permute-start | bytes 786440 | tf_op jit(solution)/shard_map/ppermute | solution.py:112
  9.8 10.0 %collective-permute-start.13 = (bf16[16,32,256]{2,1,0:T(8,128)(2,1)S(1)}, bf16[16,32,256]{2,1,0:T(8,128)(2,1)S(1)}, u32[]{:S(2)}, u32[]{:S(2)}) collective-permute-start(bf16[16,32,256]{2,1,0:T(8,128)(2,1)S(1)} %add_convert_fusion.2), channel_id=1, source_target_pairs={{0,8},{1,9},{2,10},{3,11},{4,12},{5,13},{6,14},{7,15}} | collective-permute-start | bytes 786440 | tf_op jit(solution)/shard_map/ppermute | solution.py:156
  13.2 11.3 %collective-permute-start.1 = (bf16[16,32,256]{2,1,0:T(8,128)(2,1)S(1)}, bf16[16,32,256]{2,1,0:T(8,128)(2,1)S(1)}, u32[]{:S(2)}, u32[]{:S(2)}) collective-permute-start(bf16[16,32,256]{2,1,0:T(8,128)(2,1)S(1)} %add_convert_fusion.5), channel_id=1, source_target_pairs={{0,8},{1,9},{2,10},{3,11},{4,12},{5,13},{6,14},{7,15}} | collective-permute-start | bytes 786440 | tf_op jit(solution)/shard_map/ppermute | solution.py:156
  20.3 4.9 %collective-permute-start.14 = (bf16[16,32,256]{2,1,0:T(8,128)(2,1)S(1)}, bf16[16,32,256]{2,1,0:T(8,128)(2,1)S(1)}, u32[]{:S(2)}, u32[]{:S(2)}) collective-permute-start(bf16[16,32,256]{2,1,0:T(8,128)(2,1)S(1)} %get-tuple-element.66), channel_id=1, source_target_pairs={{0,4},{4,0},{1,5},{5,1},{2,6},{6,2},{3,7},{7,3},{8,12},{12,8},{9,1... | collective-permute-start | bytes 786440 | tf_op jit(solution)/shard_map/ppermute | solution.py:112
  25.1 1.6 %collective-permute-start.2 = (bf16[16,32,256]{2,1,0:T(8,128)(2,1)S(1)}, bf16[16,32,256]{2,1,0:T(8,128)(2,1)S(1)}, u32[]{:S(2)}, u32[]{:S(2)}) collective-permute-start(bf16[16,32,256]{2,1,0:T(8,128)(2,1)S(1)} %get-tuple-element.47), channel_id=1, source_target_pairs={{0,4},{4,0},{1,5},{5,1},{2,6},{6,2},{3,7},{7,3},{8,12},{12,8},{9,1... | collective-permute-start | bytes 786440 | tf_op jit(solution)/shard_map/ppermute | solution.py:112
  25.3 2.2 %collective-permute-start.15 = (bf16[16,32,256]{2,1,0:T(8,128)(2,1)S(1)}, bf16[16,32,256]{2,1,0:T(8,128)(2,1)S(1)}, u32[]{:S(2)}, u32[]{:S(2)}) collective-permute-start(bf16[16,32,256]{2,1,0:T(8,128)(2,1)S(1)} %add_convert_fusion.1), channel_id=1, source_target_pairs={{8,16},{9,17},{10,18},{11,19},{12,20},{13,21},{14,22},{15,23}} | collective-permute-start | bytes 786440 | tf_op jit(solution)/shard_map/ppermute | solution.py:156
  26.8 1.5 %collective-permute-start.3 = (bf16[16,32,256]{2,1,0:T(8,128)(2,1)S(1)}, bf16[16,32,256]{2,1,0:T(8,128)(2,1)S(1)}, u32[]{:S(2)}, u32[]{:S(2)}) collective-permute-start(bf16[16,32,256]{2,1,0:T(8,128)(2,1)S(1)} %add_convert_fusion.4), channel_id=1, source_target_pairs={{8,16},{9,17},{10,18},{11,19},{12,20},{13,21},{14,22},{15,23}} | collective-permute-start | bytes 786440 | tf_op jit(solution)/shard_map/ppermute | solution.py:156
  28.0 1.6 %collective-permute-start.16 = (bf16[16,32,256]{2,1,0:T(8,128)(2,1)S(1)}, bf16[16,32,256]{2,1,0:T(8,128)(2,1)S(1)}, u32[]{:S(2)}, u32[]{:S(2)}) collective-permute-start(bf16[16,32,256]{2,1,0:T(8,128)(2,1)S(1)} %get-tuple-element.70), channel_id=1, source_target_pairs={{0,4},{4,0},{1,5},{5,1},{2,6},{6,2},{3,7},{7,3},{8,12},{12,8},{9,1... | collective-permute-start | bytes 786440 | tf_op jit(solution)/shard_map/ppermute | solution.py:112
  28.8 1.6 %collective-permute-start.4 = (bf16[16,32,256]{2,1,0:T(8,128)(2,1)S(1)}, bf16[16,32,256]{2,1,0:T(8,128)(2,1)S(1)}, u32[]{:S(2)}, u32[]{:S(2)}) collective-permute-start(bf16[16,32,256]{2,1,0:T(8,128)(2,1)S(1)} %get-tuple-element.51), channel_id=1, source_target_pairs={{0,4},{4,0},{1,5},{5,1},{2,6},{6,2},{3,7},{7,3},{8,12},{12,8},{9,1... | collective-permute-start | bytes 786440 | tf_op jit(solution)/shard_map/ppermute | solution.py:112
  29.7 1.5 %collective-permute-start.17 = (bf16[16,32,256]{2,1,0:T(8,128)(2,1)S(1)}, bf16[16,32,256]{2,1,0:T(8,128)(2,1)S(1)}, u32[]{:S(2)}, u32[]{:S(2)}) collective-permute-start(bf16[16,32,256]{2,1,0:T(8,128)(2,1)S(1)} %add_convert_fusion), channel_id=1, source_target_pairs={{16,24},{17,25},{18,26},{19,27},{20,28},{21,29},{22,30},{23,31}} | collective-permute-start | bytes 786440 | tf_op jit(solution)/shard_map/ppermute | solution.py:156
  30.5 2.0 %collective-permute-start.5 = (bf16[16,32,256]{2,1,0:T(8,128)(2,1)S(1)}, bf16[16,32,256]{2,1,0:T(8,128)(2,1)S(1)}, u32[]{:S(2)}, u32[]{:S(2)}) collective-permute-start(bf16[16,32,256]{2,1,0:T(8,128)(2,1)S(1)} %add_convert_fusion.3), channel_id=1, source_target_pairs={{16,24},{17,25},{18,26},{19,27},{20,28},{21,29},{22,30},{23,31}} | collective-permute-start | bytes 786440 | tf_op jit(solution)/shard_map/ppermute | solution.py:156
  31.9 2.0 %collective-permute-start.18 = (bf16[16,32,256]{2,1,0:T(8,128)(2,1)S(1)}, bf16[16,32,256]{2,1,0:T(8,128)(2,1)S(1)}, u32[]{:S(2)}, u32[]{:S(2)}) collective-permute-start(bf16[16,32,256]{2,1,0:T(8,128)(2,1)S(1)} %get-tuple-element.73), channel_id=1, source_target_pairs={{24,16},{25,17},{26,18},{27,19},{28,20},{29,21},{30,22},{31,23}} | collective-permute-start | bytes 786440 | tf_op jit(solution)/shard_map/ppermute | solution.py:163
  33.2 1.1 %collective-permute-start.6 = (bf16[16,32,256]{2,1,0:T(8,128)(2,1)S(1)}, bf16[16,32,256]{2,1,0:T(8,128)(2,1)S(1)}, u32[]{:S(2)}, u32[]{:S(2)}) collective-permute-start(bf16[16,32,256]{2,1,0:T(8,128)(2,1)S(1)} %get-tuple-element.54), channel_id=1, source_target_pairs={{24,16},{25,17},{26,18},{27,19},{28,20},{29,21},{30,22},{31,23}} | collective-permute-start | bytes 786440 | tf_op jit(solution)/shard_map/ppermute | solution.py:163
  33.9 1.6 %collective-permute-start.19 = (bf16[16,32,256]{2,1,0:T(8,128)(2,1)S(1)}, bf16[16,32,256]{2,1,0:T(8,128)(2,1)S(1)}, u32[]{:S(2)}, u32[]{:S(2)}) collective-permute-start(bf16[16,32,256]{2,1,0:T(8,128)(2,1)S(1)} %collective-permute-done.18.own), channel_id=1, source_target_pairs={{0,4},{4,0},{1,5},{5,1},{2,6},{6,2},{3,7},{7,3},{8,12},{12,8},{9,1... | collective-permute-start | bytes 786440 | tf_op jit(solution)/shard_map/ppermute | solution.py:112
  34.3 2.4 %collective-permute-start.7 = (bf16[16,32,256]{2,1,0:T(8,128)(2,1)S(1)}, bf16[16,32,256]{2,1,0:T(8,128)(2,1)S(1)}, u32[]{:S(2)}, u32[]{:S(2)}) collective-permute-start(bf16[16,32,256]{2,1,0:T(8,128)(2,1)S(1)} %collective-permute-done.6.own), channel_id=1, source_target_pairs={{0,4},{4,0},{1,5},{5,1},{2,6},{6,2},{3,7},{7,3},{8,12},{12,8},{9,1... | collective-permute-start | bytes 786440 | tf_op jit(solution)/shard_map/ppermute | solution.py:112
  36.0 1.9 %collective-permute-start.20 = (bf16[16,32,256]{2,1,0:T(8,128)(2,1)S(1)}, bf16[16,32,256]{2,1,0:T(8,128)(2,1)S(1)}, u32[]{:S(2)}, u32[]{:S(2)}) collective-permute-start(bf16[16,32,256]{2,1,0:T(8,128)(2,1)S(1)} %get-tuple-element.75), channel_id=1, source_target_pairs={{16,8},{17,9},{18,10},{19,11},{20,12},{21,13},{22,14},{23,15}} | collective-permute-start | bytes 786440 | tf_op jit(solution)/shard_map/ppermute | solution.py:175
  37.3 1.1 %collective-permute-start.8 = (bf16[16,32,256]{2,1,0:T(8,128)(2,1)S(1)}, bf16[16,32,256]{2,1,0:T(8,128)(2,1)S(1)}, u32[]{:S(2)}, u32[]{:S(2)}) collective-permute-start(bf16[16,32,256]{2,1,0:T(8,128)(2,1)S(1)} %get-tuple-element.56), channel_id=1, source_target_pairs={{16,8},{17,9},{18,10},{19,11},{20,12},{21,13},{22,14},{23,15}} | collective-permute-start | bytes 786440 | tf_op jit(solution)/shard_map/ppermute | solution.py:175
  38.0 1.6 %collective-permute-start.21 = (bf16[16,32,256]{2,1,0:T(8,128)(2,1)S(1)}, bf16[16,32,256]{2,1,0:T(8,128)(2,1)S(1)}, u32[]{:S(2)}, u32[]{:S(2)}) collective-permute-start(bf16[16,32,256]{2,1,0:T(8,128)(2,1)S(1)} %collective-permute-done.20.own), channel_id=1, source_target_pairs={{0,4},{4,0},{1,5},{5,1},{2,6},{6,2},{3,7},{7,3},{8,12},{12,8},{9,1... | collective-permute-start | bytes 786440 | tf_op jit(solution)/shard_map/ppermute | solution.py:112
  38.4 3.0 %collective-permute-start.9 = (bf16[16,32,256]{2,1,0:T(8,128)(2,1)S(1)}, bf16[16,32,256]{2,1,0:T(8,128)(2,1)S(1)}, u32[]{:S(2)}, u32[]{:S(2)}) collective-permute-start(bf16[16,32,256]{2,1,0:T(8,128)(2,1)S(1)} %collective-permute-done.8.own), channel_id=1, source_target_pairs={{0,4},{4,0},{1,5},{5,1},{2,6},{6,2},{3,7},{7,3},{8,12},{12,8},{9,1... | collective-permute-start | bytes 786440 | tf_op jit(solution)/shard_map/ppermute | solution.py:112
  40.1 58.4 %collective-permute-start.22 = (bf16[16,32,256]{2,1,0:T(8,128)(2,1)S(1)}, bf16[16,32,256]{2,1,0:T(8,128)(2,1)S(1)}, u32[]{:S(2)}, u32[]{:S(2)}) collective-permute-start(bf16[16,32,256]{2,1,0:T(8,128)(2,1)S(1)} %get-tuple-element.77), channel_id=1, source_target_pairs={{8,0},{9,1},{10,2},{11,3},{12,4},{13,5},{14,6},{15,7}} | collective-permute-start | bytes 786440 | tf_op jit(solution)/shard_map/ppermute | solution.py:175
  42.0 62.0 %collective-permute-start.10 = (bf16[16,32,256]{2,1,0:T(8,128)(2,1)S(1)}, bf16[16,32,256]{2,1,0:T(8,128)(2,1)S(1)}, u32[]{:S(2)}, u32[]{:S(2)}) collective-permute-start(bf16[16,32,256]{2,1,0:T(8,128)(2,1)S(1)} %get-tuple-element.58), channel_id=1, source_target_pairs={{8,0},{9,1},{10,2},{11,3},{12,4},{13,5},{14,6},{15,7}} | collective-permute-start | bytes 786440 | tf_op jit(solution)/shard_map/ppermute | solution.py:175
  98.6 7.6 %collective-permute-start.23 = (bf16[16,32,256]{2,1,0:T(8,128)(2,1)S(1)}, bf16[16,32,256]{2,1,0:T(8,128)(2,1)S(1)}, u32[]{:S(2)}, u32[]{:S(2)}) collective-permute-start(bf16[16,32,256]{2,1,0:T(8,128)(2,1)S(1)} %collective-permute-done.22.own), channel_id=1, source_target_pairs={{0,4},{4,0},{1,5},{5,1},{2,6},{6,2},{3,7},{7,3},{8,12},{12,8},{9,1... | collective-permute-start | bytes 786440 | tf_op jit(solution)/shard_map/ppermute | solution.py:112
  104.0 4.2 %collective-permute-start.11 = (bf16[16,32,256]{2,1,0:T(8,128)(2,1)S(1)}, bf16[16,32,256]{2,1,0:T(8,128)(2,1)S(1)}, u32[]{:S(2)}, u32[]{:S(2)}) collective-permute-start(bf16[16,32,256]{2,1,0:T(8,128)(2,1)S(1)} %collective-permute-done.10.own), channel_id=1, source_target_pairs={{0,4},{4,0},{1,5},{5,1},{2,6},{6,2},{3,7},{7,3},{8,12},{12,8},{9,1... | collective-permute-start | bytes 786440 | tf_op jit(solution)/shard_map/ppermute | solution.py:112
  (7 other events, 74.9 us)

commit v2 on v1

--- a/solution.py
+++ b/solution.py
@@ -22,8 +22,12 @@
 
 
 def forward_kernel(section, start, rows, info, rhs, incoming, inv, off, kept_f, kept_u, fwd, upd, home, far, total):
-    del kept_f, kept_u
     count = inv.shape[0]
+
+    @pl.when(info[count] != section)
+    def _():
+        fwd[...] = kept_f[...]
+        upd[...] = kept_u[...]
 
     @pl.when(info[count] == section)
     def _():
@@ -46,8 +50,12 @@
 
 
 def top_kernel(section, start, rows, info, rhs, incoming, inv, up_off, up_inv, ancestor, kept_f, kept_s, fwd, sol, sol_bf):
-    del kept_f, kept_s
     count = inv.shape[0]
+
+    @pl.when(info[count] != section)
+    def _():
+        fwd[...] = kept_f[...]
+        sol[...] = kept_s[...]
 
     @pl.when(info[count] == section)
     def _():
@@ -63,9 +71,12 @@
 
 
 def top_update_kernel(section, start, rows, info, fwd, off, kept_u, upd):
-    del kept_u, start, rows
     count = off.shape[0]
 
+    @pl.when(info[count] != section)
+    def _():
+        upd[...] = kept_u[...]
+
     @pl.when(info[count] == section)
     def _():
         for node in range(count):
@@ -73,8 +84,11 @@
 
 
 def backward_kernel(section, start, rows, info, fwd, own, partner, up_off, up_inv, kept_s, sol, sol_bf):
-    del kept_s, start, rows
     count = up_inv.shape[0]
+
+    @pl.when(info[count] != section)
+    def _():
+        sol[...] = kept_s[...]
 
     @pl.when(info[count] == section)
     def _():
@@ -114,7 +128,7 @@
     return lax.ppermute(value, ("level", "sub"), pairs)
 
 
-def body(rhs, lower_inv, lower_off, upper_inv, upper_off, ancestor, parent):
+def general_body(rhs, lower_inv, lower_off, upper_inv, upper_off, ancestor, parent):
     levels = lax.axis_size("level")
     sub_count = lax.axis_size("sub")
     sub_bits = sub_count.bit_length() - 1
@@ -176,6 +190,321 @@
     return jnp.concatenate(sol, axis=1)[None], jnp.concatenate(upd, axis=1)[None]
 
 
+NODE_ROWS = 16
+
+
+def rows_of(start):
+    return pl.ds(pl.multiple_of(start, NODE_ROWS), NODE_ROWS)
+
+
+def flat(value):
+    return value.reshape(value.shape[0] * value.shape[1], value.shape[2])
+
+
+def pick(select, values):
+    high = values.astype(BF16)
+    low = (values - high.astype(F32)).astype(BF16)
+    return dot(select, high) + dot(select, low)
+
+
+def keep(section, kept, outs):
+    @pl.when(lax.axis_index("level") != section)
+    def _():
+        for before, after in zip(kept, outs):
+            after[...] = before[...]
+
+
+def start_kernel(c, rhs, inv, off, select, home, far, upd_own, upd_far, *merged):
+    count = inv.shape[0]
+    level, sub = lax.axis_index("level"), lax.axis_index("sub")
+    half = rhs.shape[1] // 2
+
+    @pl.when(level == 0)
+    def _():
+        mine, other = rows_of(half * sub + NODE_ROWS * c), rows_of(half * (1 - sub) + NODE_ROWS * c)
+        for node in range(count):
+            right_side = jnp.concatenate([rhs[node, mine, :], rhs[node, other, :]], axis=0)
+            forward = dot(right_side.astype(BF16), inv[node]).astype(BF16)
+            update = dot(forward, off[node])
+            upd_own[node] = update[:NODE_ROWS]
+            upd_far[node] = update[NODE_ROWS:]
+        chosen = select[:, : count * NODE_ROWS]
+        home[...] = pick(chosen, flat(upd_own[...])).reshape(home.shape)
+        sums = pick(chosen, flat(upd_far[...])).astype(BF16).reshape(far.shape)
+        far[:count] = sums[count:]
+        far[count:] = sums[:count]
+
+    if merged:
+
+        @pl.when(level != 0)
+        def _():
+            for node in range(count):
+                merged[0][node] = dot(inv[node], off[node]).astype(BF16)
+
+
+def merge_kernel(left, right, merged):
+    for node in range(left.shape[0]):
+        merged[node] = dot(left[node], right[node]).astype(BF16)
+
+
+def residue_of(c, rhs, rhs_far, incoming, node):
+    count = rhs.shape[0]
+    sub = lax.axis_index("sub")
+    if node < count:
+        right_side = rhs[node, rows_of(rhs.shape[1] // 2 * sub + NODE_ROWS * c), :]
+    else:
+        right_side = rhs_far[node - count, NODE_ROWS * c : NODE_ROWS * (c + 1), :]
+    return (right_side - incoming[node].astype(F32)).astype(BF16)
+
+
+def tier_kernel(section, c, rhs, rhs_far, incoming, step_own, step_far, select, kept_r, kept_o, kept_f, residue, upd_own, upd_far, sums):
+    count = rhs.shape[0]
+    keep(section, (kept_r, kept_o, kept_f), (residue, upd_own, upd_far))
+
+    @pl.when(lax.axis_index("level") == section)
+    def _():
+        for node in range(2 * count):
+            value = residue_of(c, rhs, rhs_far, incoming, node)
+            residue[node] = value
+            if node < count:
+                upd_own[node] = dot(value, step_own[node])
+            else:
+                upd_far[node - count] = dot(value, step_far[node - count])
+        updates = jnp.concatenate([flat(upd_own[...]), flat(upd_far[...])], axis=0)
+        sums[...] = pick(select[...], updates).astype(BF16).reshape(sums.shape)
+
+
+def base_kernel(c, rhs, residue, step_own, step_far, base):
+    count = rhs.shape[0]
+    level, sub = lax.axis_index("level"), lax.axis_index("sub")
+    half = rhs.shape[1] // 2
+
+    @pl.when(level == 0)
+    def _():
+        mine, other = rows_of(half * sub + NODE_ROWS * c), rows_of(half * (1 - sub) + NODE_ROWS * c)
+        for node in range(count):
+            right_side = jnp.concatenate([rhs[node, mine, :], rhs[node, other, :]], axis=0)
+            solved = dot(right_side.astype(BF16), step_own[node])
+            base[node] = solved[:NODE_ROWS]
+            base[count + node] = solved[NODE_ROWS:]
+
+    @pl.when((level != 0) & (level != lax.axis_size("level") - 1))
+    def _():
+        for node in range(count):
+            base[node] = dot(residue[node], step_own[node])
+            base[count + node] = dot(residue[count + node], step_far[node])
+
+
+def ancestor_kernel(c, ancestor, ancestor_far, step_own, step_far, base):
+    count = ancestor.shape[0]
+    sub = lax.axis_index("sub")
+
+    @pl.when(lax.axis_index("level") == lax.axis_size("level") - 1)
+    def _():
+        for node in range(count):
+            base[node] = dot(ancestor[node, rows_of(ancestor.shape[1] // 2 * sub + NODE_ROWS * c), :], step_own[node])
+            base[count + node] = dot(ancestor_far[node, NODE_ROWS * c : NODE_ROWS * (c + 1), :], step_far[node])
+
+
+def top_kernel2(section, c, rhs, rhs_far, incoming, step_own, step_far, base, choose, kept_r, kept_o, kept_f, residue, sol_own, sol_far, sent):
+    count = rhs.shape[0]
+    keep(section, (kept_r, kept_o, kept_f), (residue, sol_own, sol_far))
+
+    @pl.when(lax.axis_index("level") == section)
+    def _():
+        for node in range(2 * count):
+            value = residue_of(c, rhs, rhs_far, incoming, node)
+            residue[node] = value
+            if node < count:
+                sol_own[node] = dot(value, step_own[node]) - base[node]
+            else:
+                sol_far[node - count] = dot(value, step_far[node - count]) - base[node]
+        solved = jnp.concatenate([flat(sol_own[...]), flat(sol_far[...])], axis=0).astype(BF16)
+        sent[...] = dot(choose[...], solved).astype(BF16).reshape(sent.shape)
+
+
+def top_update_kernel2(section, residue, step_own, step_far, kept_o, kept_f, upd_own, upd_far):
+    count = step_own.shape[0]
+    keep(section, (kept_o, kept_f), (upd_own, upd_far))
+
+    @pl.when(lax.axis_index("level") == section)
+    def _():
+        for node in range(count):
+            upd_own[node] = dot(residue[node], step_own[node])
+            upd_far[node] = dot(residue[count + node], step_far[node])
+
+
+def back_kernel(section, above, base, step_own, step_far, choose, kept_o, kept_f, sol_own, sol_far, sent):
+    count = step_own.shape[0]
+    keep(section, (kept_o, kept_f), (sol_own, sol_far))
+
+    @pl.when(lax.axis_index("level") == section)
+    def _():
+        for node in range(count):
+            sol_own[node] = base[node] - dot(above[node], step_own[node])
+            sol_far[node] = base[count + node] - dot(above[count + node], step_far[node])
+        solved = jnp.concatenate([flat(sol_own[...]), flat(sol_far[...])], axis=0).astype(BF16)
+        sent[...] = dot(choose[...], solved).astype(BF16).reshape(sent.shape)
+
+
+def last_kernel(above, above_far, base, step_own, kept_o, kept_f, sol_own, sol_far):
+    count = step_own.shape[0]
+    keep(0, (kept_o, kept_f), (sol_own, sol_far))
+
+    @pl.when(lax.axis_index("level") == 0)
+    def _():
+        for node in range(count):
+            rows = jnp.concatenate([above[node], above_far[node]], axis=0)
+            solved = dot(rows, step_own[node])
+            sol_own[node] = base[node] - solved[:NODE_ROWS]
+            sol_far[node] = base[count + node] - solved[NODE_ROWS:]
+
+
+def run(kernel, operands, outs, aliases=None, products=32):
+    return pl.pallas_call(
+        kernel,
+        in_specs=[IN_VMEM] * len(operands),
+        out_specs=[IN_VMEM] * len(outs),
+        out_shape=outs,
+        input_output_aliases=aliases or {},
+        compiler_params=pltpu.CompilerParams(vmem_limit_bytes=VMEM_BYTES),
+        cost_estimate=pl.CostEstimate(
+            flops=products * 2 * NODE_ROWS * 256 * 256, bytes_accessed=256 * 256 * 2 * products, transcendentals=0
+        ),
+    )(*operands)
+
+
+def exchanged(value):
+    return lax.ppermute(value, "sub", [(0, 1), (1, 0)])
+
+
+def relative_parents(parent_row, sub, count):
+    own_first = jnp.where(sub == 0, parent_row, jnp.roll(parent_row, count))
+    return own_first % count + jnp.where(own_first // count == sub, 0, count)
+
+
+def pair_body(rhs, lower_inv, lower_off, upper_inv, upper_off, ancestor, parent):
+    levels = lax.axis_size("level")
+    tier = lax.axis_index("level")
+    sub = lax.axis_index("sub")
+    top = levels - 1
+    rhs, lower_inv, lower_off, upper_inv, upper_off = (
+        value[0] for value in (rhs, lower_inv, lower_off, upper_inv, upper_off)
+    )
+    count, all_rows, width = rhs.shape
+    half = all_rows // 2
+    chunks = half // NODE_ROWS
+    nodes = 2 * count
+
+    def shape(of, dtype):
+        return jax.ShapeDtypeStruct((of, NODE_ROWS, width), dtype)
+
+    def blank(of, dtype):
+        return [jnp.zeros((of, NODE_ROWS, width), dtype) for _ in range(chunks)]
+
+    def table(row):
+        return relative_parents(lax.dynamic_index_in_dim(parent, row, 0, keepdims=False), sub, count)
+
+    index = jnp.arange(nodes * NODE_ROWS, dtype=jnp.int32)
+    lane_up = jnp.repeat(table(jnp.minimum(tier, top - 1)), NODE_ROWS) * NODE_ROWS + index % NODE_ROWS
+    lane_down = jnp.repeat(table(jnp.maximum(tier - 1, 0)), NODE_ROWS) * NODE_ROWS + index % NODE_ROWS
+    select = (index[:, None] == lane_up[None, :]).astype(BF16)
+    choose = (lane_down[:, None] == index[None, :]).astype(BF16)
+
+    upd_own, upd_far = blank(count, F32), blank(count, F32)
+    sol_own, sol_far = blank(count, F32), blank(count, F32)
+    residue = blank(nodes, BF16)
+    incoming = [None] * chunks
+    parts = [None] * chunks
+    for c in range(chunks):
+        outs = [shape(nodes, F32), shape(nodes, BF16), shape(count, F32), shape(count, F32)]
+        if c == 0:
+            outs.append(jax.ShapeDtypeStruct(lower_inv.shape, BF16))
+        home, far, upd_own[c], upd_far[c], *more = run(
+            functools.partial(start_kernel, c), (rhs, lower_inv, lower_off, select), outs
+        )
+        if c == 0:
+            up_own = more[0]
+        parts[c] = (home, exchanged(far))
+    for c in range(chunks):
+        home, received = parts[c]
+        incoming[c] = (home + received.astype(F32)).astype(BF16)
+    sent = incoming
+    incoming = [lax.ppermute(value, "level", [(0, 1)]) for value in incoming]
+
+    up_own, rhs, ancestor, lower_inv, upper_inv, upper_off, sent = lax.optimization_barrier(
+        (up_own, rhs, ancestor, lower_inv, upper_inv, upper_off, sent)
+    )
+    up_far = exchanged(up_own)
+    rhs_far = exchanged(lax.dynamic_slice_in_dim(rhs, half * (1 - sub), half, 1))
+    matrix = [jax.ShapeDtypeStruct(lower_inv.shape, BF16)]
+    (base_own,) = run(merge_kernel, (lower_inv, upper_inv), matrix, products=64)
+    base_far = exchanged(base_own)
+    (down_own,) = run(merge_kernel, (upper_off, upper_inv), matrix, products=64)
+    down_far = exchanged(down_own)
+    ancestor_far = exchanged(lax.dynamic_slice_in_dim(ancestor, half * (1 - sub), half, 1))
+
+    for section in range(1, top):
+        for c in range(chunks):
+            residue[c], upd_own[c], upd_far[c], sums = run(
+                functools.partial(tier_kernel, section, c),
+                (rhs, rhs_far, incoming[c], up_own, up_far, select, residue[c], upd_own[c], upd_far[c]),
+                [shape(nodes, BF16), shape(count, F32), shape(count, F32), shape(nodes, BF16)],
+                {6: 0, 7: 1, 8: 2},
+            )
+            incoming[c] = lax.ppermute(sums, "level", [(section, section + 1)])
+    base = [
+        run(functools.partial(base_kernel, c), (rhs, residue[c], base_own, base_far), [shape(nodes, F32)])[0]
+        for c in range(chunks)
+    ]
+    from_ancestor = [
+        run(functools.partial(ancestor_kernel, c), (ancestor, ancestor_far, down_own, down_far), [shape(nodes, F32)])[0]
+        for c in range(chunks)
+    ]
+    above = [None] * chunks
+    for c in range(chunks):
+        residue[c], sol_own[c], sol_far[c], solved = run(
+            functools.partial(top_kernel2, top, c),
+            (rhs, rhs_far, incoming[c], base_own, base_far, from_ancestor[c], choose, residue[c], sol_own[c], sol_far[c]),
+            [shape(nodes, BF16), shape(count, F32), shape(count, F32), shape(nodes, BF16)],
+            {7: 0, 8: 1, 9: 2},
+        )
+        above[c] = lax.ppermute(solved, "level", [(top, top - 1)])
+    for c in range(chunks):
+        upd_own[c], upd_far[c] = run(
+            functools.partial(top_update_kernel2, top),
+            (residue[c], up_own, up_far, upd_own[c], upd_far[c]),
+            [shape(count, F32), shape(count, F32)],
+            {3: 0, 4: 1},
+        )
+    for section in reversed(range(1, top)):
+        for c in range(chunks):
+            sol_own[c], sol_far[c], solved = run(
+                functools.partial(back_kernel, section),
+                (above[c], base[c], down_own, down_far, choose, sol_own[c], sol_far[c]),
+                [shape(count, F32), shape(count, F32), shape(nodes, BF16)],
+                {5: 0, 6: 1},
+            )
+            above[c] = lax.ppermute(solved, "level", [(section, section - 1)])
+    sol_other = [exchanged(value) for value in sol_far]
+    upd_other = [exchanged(value) for value in upd_far]
+    for c in range(chunks):
+        sol_own[c], sol_far[c] = run(
+            last_kernel,
+            (above[c][:count], exchanged(above[c][count:]), base[c], down_own, sol_own[c], sol_far[c]),
+            [shape(count, F32), shape(count, F32)],
+            {4: 0, 5: 1},
+            products=16,
+        )
+
+    def assembled(own, far, other):
+        mine = jnp.concatenate(own, axis=1)
+        theirs = jnp.where(tier == 0, jnp.concatenate(far, axis=1), jnp.concatenate(other, axis=1))
+        return jnp.concatenate([jnp.where(sub == 0, mine, theirs), jnp.where(sub == 0, theirs, mine)], axis=1)
+
+    return assembled(sol_own, sol_far, sol_other)[None], assembled(upd_own, upd_far, upd_other)[None]
+
+
 def solution(mesh):
     placed = (
         P("level", "sub", "rhs", None),
@@ -187,7 +516,7 @@
         P(),
     )
     return jax.shard_map(
-        body,
+        pair_body if mesh.shape["sub"] == 2 else general_body,
         mesh=mesh,
         in_specs=placed,
         out_specs=(P("level", "sub", "rhs", None), P("level", "sub", "rhs", None)),

time: 112 us -> 115 us (1.027)
  waiting for transfers between devices: 73.2 us -> 21.3 us
  Pallas kernels: 13.6 us -> 49.7 us
  local copies, waits for them, and re-layouts: 4.64 us -> 15.5 us
  starting transfers between devices: 15.3 us -> 20.3 us
  other arithmetic: 3.42 us -> 5.57 us
    ppermute x24 -> x25, waiting for transfers between devices: 73.2 us -> 21.3 us  [the longest x4 14 us: pair_body(): above[c] = lax.ppermute(solved, 'level', [(section, section - 1)])]
    pallas_call x16 -> x22, Pallas kernels: 13.6 us -> 49.7 us  [run(): pl.pallas_call(kernel, in_specs=[IN_VMEM] * len(operands), out_specs=[IN_...]
    unnamed x14 -> x70, local copies, waits for them, and re-layouts: 4.42 us -> 12.3 us
    ppermute x24 -> x25, starting transfers between devices: 15.3 us -> 20.3 us  [the longest x2 7.86 us: pair_body(): incoming = [lax.ppermute(value, 'level', [(0, 1)]) for value in incoming]]
    dynamic_slice x0 -> x3, local copies, waits for them, and re-layouts: none -> 1.63 us  [the longest x1 0.84 us: pair_body(): lax.dynamic_slice_in_dim(rhs, half * (1 - sub), half, 1)]
    select_n x0 -> x2, other arithmetic: none -> 1.46 us  [assembled(): jnp.where(sub == 0, mine, theirs)]
    convert_element_type x6 -> x4, other arithmetic: 0.5 us -> 1.88 us  [the longest x2 1.59 us: pair_body(): incoming[c] = (home + received.astype(F32)).astype(BF16)]
  transfers between devices with their start and end apart: 24 -> 25, of which waited for: 8 -> 5; matrix products, arithmetic and copies ran while one was open for 2% -> 5% of each run, Pallas kernels for 9% -> 41%
where the time goes in v2:
time: 115 us; the launch traced here: 114 us
  Pallas kernels  49.7 us (43%)
  waiting for transfers between devices  21.3 us (19%)
  starting transfers between devices  20.3 us (18%)
  local copies, waits for them, and re-layouts  15.5 us (13%)
  other arithmetic  5.57 us (5%)
  between operations  1.22 us (1%)
    pallas_call x22, Pallas kernels, run(): pl.pallas_call(kernel, in_specs=[IN_VMEM] * len(operands), out_specs=[IN_...  49.7 us
    ppermute x4, waiting for transfers between devices, pair_body(): above[c] = lax.ppermute(solved, 'level', [(section, section - 1)])  14 us
    unnamed x70, local copies, waits for them, and re-layouts  12.3 us
    ppermute x2, starting transfers between devices, pair_body(): incoming = [lax.ppermute(value, 'level', [(0, 1)]) for value in incoming]  7.86 us
    ppermute x2, waiting for transfers between devices, pair_body(): incoming = [lax.ppermute(value, 'level', [(0, 1)]) for value in incoming]  6.37 us
    ppermute x4, starting transfers between devices, pair_body(): above[c] = lax.ppermute(solved, 'level', [(section, section - 1)])  5.46 us
    ppermute x13, starting transfers between devices, exchanged(): return lax.ppermute(value, 'sub', [(0, 1), (1, 0)])  2.94 us
    ppermute x4, starting transfers between devices, pair_body(): incoming[c] = lax.ppermute(sums, 'level', [(section, section + 1)])  2.66 us
  transfers between devices with their start and end apart: 25, of which 5 were waited for; matrix products, arithmetic and copies ran while one was open for 5% of the time, Pallas kernels for 41%

profile of v2, /device:TPU:0, one launch (start us, length us, event | category | flops | bytes accessed | tf_op | source)
XLA Modules:
  0.0 113.5 jit_solution(16752271418678512051)
XLA Ops:
  6.6 2.6 %shard_map.86 = (f32[32,16,256]{2,1,0:T(8,128)S(1)}, bf16[32,16,256]{2,1,0:T(8,128)(2,1)S(1)}, f32[16,16,256]{2,1,0:T(8,128)S(1)}, f32[16,16,256]{2,1,0:T(8,128)}, bf16[16,256,256]{2,1,0:T(8,128)(2,1)}) custom-call(f32[16,64,256]{2,1,0:T(8,128)S(1)} %bitcast.25, bf16[16,256,256]{2,1,0:T(8,128)(2,1)S(1)} %bitcast.36, bf16[16,256,256]{2,1,0:T(8,128)(2,1)S(1)} %bitcast.41, ...), custom_call_target="tpu_custom_call" | custom-call | flops 67108864 | bytes 4194304 | tf_op jit(solution)/shard_map/pallas_call | solution.py:364
  9.7 1.9 %shard_map.87 = (f32[32,16,256]{2,1,0:T(8,128)S(1)}, bf16[32,16,256]{2,1,0:T(8,128)(2,1)S(1)}, f32[16,16,256]{2,1,0:T(8,128)S(1)}, f32[16,16,256]{2,1,0:T(8,128)}) custom-call(f32[16,64,256]{2,1,0:T(8,128)S(1)} %bitcast.26, bf16[16,256,256]{2,1,0:T(8,128)(2,1)S(1)} %bitcast.37, bf16[16,256,256]{2,1,0:T(8,128)(2,1)S(1)} %bitcast.42, ...), custom_call_target="tpu_custom_call" | custom-call | flops 67108864 | bytes 4194304 | tf_op jit(solution)/shard_map/pallas_call | solution.py:364
  15.5 2.1 %shard_map.90.step_own = bf16[16,256,256]{2,1,0:T(8,128)(2,1)} custom-call(bf16[16,256,256]{2,1,0:T(8,128)(2,1)S(1)} %bitcast.38, bf16[16,256,256]{2,1,0:T(8,128)(2,1)S(1)} %bitcast.40), custom_call_target="tpu_custom_call" | custom-call | flops 134217728 | bytes 8388608 | tf_op jit(solution)/shard_map/pallas_call | solution.py:364
  18.9 2.9 %collective-permute-start.14 = (bf16[32,16,256]{2,1,0:T(8,128)(2,1)}, bf16[32,16,256]{2,1,0:T(8,128)(2,1)S(1)}, u32[]{:S(2)}, u32[]{:S(2)}) collective-permute-start(bf16[32,16,256]{2,1,0:T(8,128)(2,1)} %add_convert_fusion), channel_id=1, source_target_pairs={{0,8},{1,9},{2,10},{3,11},{4,12},{5,13},{6,14},{7,15}} | collective-permute-start | bytes 786440 | tf_op jit(solution)/shard_map/ppermute | solution.py:433
  21.8 6.4 %collective-permute-done.14.incoming = bf16[32,16,256]{2,1,0:T(8,128)(2,1)S(1)} collective-permute-done((bf16[32,16,256]{2,1,0:T(8,128)(2,1)}, bf16[32,16,256]{2,1,0:T(8,128)(2,1)S(1)}, u32[]{:S(2)}, u32[]{:S(2)}) %collective-permute-start.14) | collective-permute-done | bytes 262176 | tf_op jit(solution)/shard_map/ppermute | solution.py:433
  28.9 5.0 %collective-permute-start.3 = (bf16[32,16,256]{2,1,0:T(8,128)(2,1)}, bf16[32,16,256]{2,1,0:T(8,128)(2,1)}, u32[]{:S(2)}, u32[]{:S(2)}) collective-permute-start(bf16[32,16,256]{2,1,0:T(8,128)(2,1)} %add_convert_fusion.1), channel_id=1, source_target_pairs={{0,8},{1,9},{2,10},{3,11},{4,12},{5,13},{6,14},{7,15}} | collective-permute-start | bytes 786440 | tf_op jit(solution)/shard_map/ppermute | solution.py:433
  37.0 3.2 %shard_map.98 = (bf16[32,16,256]{2,1,0:T(8,128)(2,1)S(1)}, f32[16,16,256]{2,1,0:T(8,128)S(1)}, f32[16,16,256]{2,1,0:T(8,128)}, bf16[32,16,256]{2,1,0:T(8,128)(2,1)S(1)}) custom-call(f32[16,64,256]{2,1,0:T(8,128)S(1)} %bitcast.28, f32[16,32,256]{2,1,0:T(8,128)} %collective-permute-done.2.rhs_far, ...), custom_call_target="tpu_custom_call", output_to_operand_aliasing={{0}: (6, {}), {1}: (7, {}), {2}: (8, {})} | custom-call | flops 67108864 | bytes 4194304 | tf_op jit(solution)/shard_map/pallas_call | solution.py:364
  41.6 3.3 %shard_map.88 = (bf16[32,16,256]{2,1,0:T(8,128)(2,1)S(1)}, f32[16,16,256]{2,1,0:T(8,128)S(1)}, f32[16,16,256]{2,1,0:T(8,128)}, bf16[32,16,256]{2,1,0:T(8,128)(2,1)S(1)}) custom-call(f32[16,64,256]{2,1,0:T(8,128)S(1)} %bitcast.29, f32[16,32,256]{2,1,0:T(8,128)} %collective-permute-done.2.rhs_far, ...), custom_call_target="tpu_custom_call", output_to_operand_aliasing={{0}: (6, {}), {1}: (7, {}), {2}: (8, {})} | custom-call | flops 67108864 | bytes 4194304 | tf_op jit(solution)/shard_map/pallas_call | solution.py:364
  45.8 3.2 %shard_map.99 = (bf16[32,16,256]{2,1,0:T(8,128)(2,1)S(1)}, f32[16,16,256]{2,1,0:T(8,128)S(1)}, f32[16,16,256]{2,1,0:T(8,128)}, bf16[32,16,256]{2,1,0:T(8,128)(2,1)S(1)}) custom-call(f32[16,64,256]{2,1,0:T(8,128)S(1)} %bitcast.30, f32[16,32,256]{2,1,0:T(8,128)} %collective-permute-done.2.rhs_far, ...), custom_call_target="tpu_custom_call", output_to_operand_aliasing={{0}: (6, {}), {1}: (7, {}), {2}: (8, {})} | custom-call | flops 67108864 | bytes 4194304 | tf_op jit(solution)/shard_map/pallas_call | solution.py:364
  49.6 3.2 %shard_map.89 = (bf16[32,16,256]{2,1,0:T(8,128)(2,1)S(1)}, f32[16,16,256]{2,1,0:T(8,128)S(1)}, f32[16,16,256]{2,1,0:T(8,128)}, bf16[32,16,256]{2,1,0:T(8,128)(2,1)S(1)}) custom-call(f32[16,64,256]{2,1,0:T(8,128)S(1)} %bitcast.31, f32[16,32,256]{2,1,0:T(8,128)} %collective-permute-done.2.rhs_far, ...), custom_call_target="tpu_custom_call", output_to_operand_aliasing={{0}: (6, {}), {1}: (7, {}), {2}: (8, {})} | custom-call | flops 67108864 | bytes 4194304 | tf_op jit(solution)/shard_map/pallas_call | solution.py:364
  53.6 1.8 %shard_map.100.base = f32[32,16,256]{2,1,0:T(8,128)S(1)} custom-call(bf16[16,64,256]{2,1,0:T(8,128)(2,1)S(1)} %copy-done.30, bf16[16,32,256]{2,1,0:T(8,128)(2,1)S(1)} %collective-permute-done.8.ancestor_far, bf16[16,256,256]{2,1,0:T(8,128)(2,1)S(1)} %shard_map.91.step_own, bf16[16,256,256]{2,1,0:T(8,128)(2,1)} %collective-permute-done.9.step_far), custom_call_target="tpu_custom_call" | custom-call | flops 67108864 | bytes 4194304 | tf_op jit(solution)/shard_map/pallas_call | solution.py:364
  55.4 1.6 %shard_map.92.base = f32[32,16,256]{2,1,0:T(8,128)S(1)} custom-call(bf16[16,64,256]{2,1,0:T(8,128)(2,1)S(1)} %copy-done.30, bf16[16,32,256]{2,1,0:T(8,128)(2,1)S(1)} %collective-permute-done.8.ancestor_far, bf16[16,256,256]{2,1,0:T(8,128)(2,1)S(1)} %shard_map.91.step_own, bf16[16,256,256]{2,1,0:T(8,128)(2,1)} %collective-permute-done.9.step_far), custom_call_target="tpu_custom_call" | custom-call | flops 67108864 | bytes 4194304 | tf_op jit(solution)/shard_map/pallas_call | solution.py:364
  57.0 2.7 %shard_map.102.base = f32[32,16,256]{2,1,0:T(8,128)S(1)} custom-call(f32[16,64,256]{2,1,0:T(8,128)S(1)} %bitcast.32, bf16[32,16,256]{2,1,0:T(8,128)(2,1)S(1)} %get-tuple-element.97.kept_r.residue, bf16[16,256,256]{2,1,0:T(8,128)(2,1)} %shard_map.90.step_own, bf16[16,256,256]{2,1,0:T(8,128)(2,1)} %collective-permute-done.7.step_far), custom_call_target="tpu_custom_call" | custom-call | flops 67108864 | bytes 4194304 | tf_op jit(solution)/shard_map/pallas_call | solution.py:364
  59.7 3.0 %shard_map.94.base = f32[32,16,256]{2,1,0:T(8,128)S(1)} custom-call(f32[16,64,256]{2,1,0:T(8,128)S(1)} %bitcast.33, bf16[32,16,256]{2,1,0:T(8,128)(2,1)S(1)} %get-tuple-element.79.kept_r.residue, bf16[16,256,256]{2,1,0:T(8,128)(2,1)} %shard_map.90.step_own, bf16[16,256,256]{2,1,0:T(8,128)(2,1)} %collective-permute-done.7.step_far), custom_call_target="tpu_custom_call" | custom-call | flops 67108864 | bytes 4194304 | tf_op jit(solution)/shard_map/pallas_call | solution.py:364
  62.8 2.6 %shard_map.101 = (bf16[32,16,256]{2,1,0:T(8,128)(2,1)S(1)}, f32[16,16,256]{2,1,0:T(8,128)S(1)}, f32[16,16,256]{2,1,0:T(8,128)S(1)}, bf16[32,16,256]{2,1,0:T(8,128)(2,1)S(1)}) custom-call(f32[16,64,256]{2,1,0:T(8,128)S(1)} %bitcast.34, f32[16,32,256]{2,1,0:T(8,128)} %collective-permute-done.2.rhs_far, ...), custom_call_target="tpu_custom_call", output_to_operand_aliasing={{0}: (7, {}), {1}: (8, {}), {2}: (9, {})} | custom-call | flops 67108864 | bytes 4194304 | tf_op jit(solution)/shard_map/pallas_call | solution.py:364
  66.2 2.5 %shard_map.93 = (bf16[32,16,256]{2,1,0:T(8,128)(2,1)S(1)}, f32[16,16,256]{2,1,0:T(8,128)S(1)}, f32[16,16,256]{2,1,0:T(8,128)S(1)}, bf16[32,16,256]{2,1,0:T(8,128)(2,1)S(1)}) custom-call(f32[16,64,256]{2,1,0:T(8,128)S(1)} %bitcast.35, f32[16,32,256]{2,1,0:T(8,128)} %collective-permute-done.2.rhs_far, ...), custom_call_target="tpu_custom_call", output_to_operand_aliasing={{0}: (7, {}), {1}: (8, {}), {2}: (9, {})} | custom-call | flops 67108864 | bytes 4194304 | tf_op jit(solution)/shard_map/pallas_call | solution.py:364
  69.3 3.0 %shard_map.107 = (f32[16,16,256]{2,1,0:T(8,128)S(1)}, f32[16,16,256]{2,1,0:T(8,128)}) custom-call(bf16[32,16,256]{2,1,0:T(8,128)(2,1)S(1)} %get-tuple-element.114.residue, bf16[16,256,256]{2,1,0:T(8,128)(2,1)} %get-tuple-element.67.step_own, bf16[16,256,256]{2,1,0:T(8,128)(2,1)} %collective-permute-done.4.step_far, ...), custom_call_target="tpu_custom_call", output_to_operand_aliasing={{0}: (3, {}), {1}: (4, {})} | custom-call | flops 67108864 | bytes 4194304 | tf_op jit(solution)/shard_map/pallas_call | solution.py:364
  72.3 2.5 %shard_map.103 = (f32[16,16,256]{2,1,0:T(8,128)S(1)}, f32[16,16,256]{2,1,0:T(8,128)S(1)}, bf16[32,16,256]{2,1,0:T(8,128)(2,1)}) custom-call(bf16[32,16,256]{2,1,0:T(8,128)(2,1)S(1)} %collective-permute-done.17.above, f32[32,16,256]{2,1,0:T(8,128)S(1)} %shard_map.102.base, ...), custom_call_target="tpu_custom_call", output_to_operand_aliasing={{0}: (5, {}), {1}: (6, {})} | custom-call | flops 67108864 | bytes 4194304 | tf_op jit(solution)/shard_map/pallas_call | solution.py:364
  76.2 2.4 %shard_map.95 = (f32[16,16,256]{2,1,0:T(8,128)S(1)}, f32[16,16,256]{2,1,0:T(8,128)S(1)}, bf16[32,16,256]{2,1,0:T(8,128)(2,1)}) custom-call(bf16[32,16,256]{2,1,0:T(8,128)(2,1)S(1)} %collective-permute-done.10.above, f32[32,16,256]{2,1,0:T(8,128)S(1)} %shard_map.94.base, ...), custom_call_target="tpu_custom_call", output_to_operand_aliasing={{0}: (5, {}), {1}: (6, {})} | custom-call | flops 67108864 | bytes 4194304 | tf_op jit(solution)/shard_map/pallas_call | solution.py:364
  80.4 3.1 %shard_map.106 = (f32[16,16,256]{2,1,0:T(8,128)S(1)}, f32[16,16,256]{2,1,0:T(8,128)}) custom-call(bf16[32,16,256]{2,1,0:T(8,128)(2,1)S(1)} %get-tuple-element.110.residue, bf16[16,256,256]{2,1,0:T(8,128)(2,1)} %get-tuple-element.67.step_own, bf16[16,256,256]{2,1,0:T(8,128)(2,1)} %collective-permute-done.4.step_far, ...), custom_call_target="tpu_custom_call", output_to_operand_aliasing={{0}: (3, {}), {1}: (4, {})} | custom-call | flops 67108864 | bytes 4194304 | tf_op jit(solution)/shard_map/pallas_call | solution.py:364
  86.6 1.8 %shard_map.104 = (f32[16,16,256]{2,1,0:T(8,128)S(1)}, f32[16,16,256]{2,1,0:T(8,128)S(1)}, bf16[32,16,256]{2,1,0:T(8,128)(2,1)S(1)}) custom-call(bf16[32,16,256]{2,1,0:T(8,128)(2,1)} %collective-permute-done.18.above, f32[32,16,256]{2,1,0:T(8,128)S(1)} %copy-done.18, ...), custom_call_target="tpu_custom_call", output_to_operand_aliasing={{0}: (5, {}), {1}: (6, {})} | custom-call | flops 67108864 | bytes 4194304 | tf_op jit(solution)/shard_map/pallas_call | solution.py:364
  90.4 1.8 %shard_map.96 = (f32[16,16,256]{2,1,0:T(8,128)S(1)}, f32[16,16,256]{2,1,0:T(8,128)S(1)}, bf16[32,16,256]{2,1,0:T(8,128)(2,1)S(1)}) custom-call(bf16[32,16,256]{2,1,0:T(8,128)(2,1)} %collective-permute-done.11.above, f32[32,16,256]{2,1,0:T(8,128)S(1)} %copy-done.21, ...), custom_call_target="tpu_custom_call", output_to_operand_aliasing={{0}: (5, {}), {1}: (6, {})} | custom-call | flops 67108864 | bytes 4194304 | tf_op jit(solution)/shard_map/pallas_call | solution.py:364
  95.6 10.9 %collective-permute-done.19 = bf16[32,16,256]{2,1,0:T(8,128)(2,1)S(1)} collective-permute-done((bf16[32,16,256]{2,1,0:T(8,128)(2,1)S(1)}, bf16[32,16,256]{2,1,0:T(8,128)(2,1)S(1)}, u32[]{:S(2)}, u32[]{:S(2)}) %collective-permute-start.19) | collective-permute-done | bytes 262176 | tf_op jit(solution)/shard_map/ppermute | solution.py:488
  106.6 3.0 %collective-permute-done.12 = bf16[32,16,256]{2,1,0:T(8,128)(2,1)S(1)} collective-permute-done((bf16[32,16,256]{2,1,0:T(8,128)(2,1)S(1)}, bf16[32,16,256]{2,1,0:T(8,128)(2,1)S(1)}, u32[]{:S(2)}, u32[]{:S(2)}) %collective-permute-start.12) | collective-permute-done | bytes 262176 | tf_op jit(solution)/shard_map/ppermute | solution.py:488
  (148 shorter events, 36.1 us)
Async XLA Ops:
  9.2 2.4 %collective-permute-start = (bf16[32,16,256]{2,1,0:T(8,128)(2,1)S(1)}, bf16[32,16,256]{2,1,0:T(8,128)(2,1)S(1)}, u32[]{:S(2)}, u32[]{:S(2)}) collective-permute-start(bf16[32,16,256]{2,1,0:T(8,128)(2,1)S(1)} %get-tuple-element.63), channel_id=1, source_target_pairs={{0,4},{4,0},{1,5},{5,1},{2,6},{6,2},{3,7},{7,3},{8,12},{12,8},{9,1... | collective-permute-start | bytes 786440 | tf_op jit(solution)/shard_map/ppermute | solution.py:378
  11.6 1.5 %collective-permute-start.1 = (bf16[32,16,256]{2,1,0:T(8,128)(2,1)S(1)}, bf16[32,16,256]{2,1,0:T(8,128)(2,1)S(1)}, u32[]{:S(2)}, u32[]{:S(2)}) collective-permute-start(bf16[32,16,256]{2,1,0:T(8,128)(2,1)S(1)} %get-tuple-element.65), channel_id=1, source_target_pairs={{0,4},{4,0},{1,5},{5,1},{2,6},{6,2},{3,7},{7,3},{8,12},{12,8},{9,1... | collective-permute-start | bytes 786440 | tf_op jit(solution)/shard_map/ppermute | solution.py:378
  13.9 20.1 %collective-permute-start.4 = (bf16[16,256,256]{2,1,0:T(8,128)(2,1)}, bf16[16,256,256]{2,1,0:T(8,128)(2,1)}, u32[]{:S(2)}, u32[]{:S(2)}) collective-permute-start(bf16[16,256,256]{2,1,0:T(8,128)(2,1)} %get-tuple-element.67.step_own), channel_id=1, source_target_pairs={{0,4},{4,0},{1,5},{5,1},{2,6},{6,2},{3,7},{7,3},{8,12},{12,8},{9,1... | collective-permute-start | bytes 6291464 | tf_op jit(solution)/shard_map/ppermute | solution.py:378
  14.8 38.9 %collective-permute-start.9 = (bf16[16,256,256]{2,1,0:T(8,128)(2,1)S(1)}, bf16[16,256,256]{2,1,0:T(8,128)(2,1)}, u32[]{:S(2)}, u32[]{:S(2)}) collective-permute-start(bf16[16,256,256]{2,1,0:T(8,128)(2,1)S(1)} %shard_map.91.step_own), channel_id=1, source_target_pairs={{0,4},{4,0},{1,5},{5,1},{2,6},{6,2},{3,7},{7,3},{8,12},{12,8},{9,1... | collective-permute-start | bytes 6291464 | tf_op jit(solution)/shard_map/ppermute | solution.py:378
  17.6 39.4 %collective-permute-start.7 = (bf16[16,256,256]{2,1,0:T(8,128)(2,1)}, bf16[16,256,256]{2,1,0:T(8,128)(2,1)}, u32[]{:S(2)}, u32[]{:S(2)}) collective-permute-start(bf16[16,256,256]{2,1,0:T(8,128)(2,1)} %shard_map.90.step_own), channel_id=1, source_target_pairs={{0,4},{4,0},{1,5},{5,1},{2,6},{6,2},{3,7},{7,3},{8,12},{12,8},{9,1... | collective-permute-start | bytes 6291464 | tf_op jit(solution)/shard_map/ppermute | solution.py:378
  18.6 15.5 %collective-permute-start.2 = (f32[16,32,256]{2,1,0:T(8,128)}, f32[16,32,256]{2,1,0:T(8,128)}, u32[]{:S(2)}, u32[]{:S(2)}) collective-permute-start(f32[16,32,256]{2,1,0:T(8,128)} %constant_dynamic-slice_fusion.2), channel_id=1, source_target_pairs={{0,4},{4,0},{1,5},{5,1},{2,6},{6,2},{3,7},{7,3},{8,12},{12,8},{9,1... | collective-permute-start | bytes 1572872 | tf_op jit(solution)/shard_map/ppermute | solution.py:378
  18.9 9.3 %collective-permute-start.14 = (bf16[32,16,256]{2,1,0:T(8,128)(2,1)}, bf16[32,16,256]{2,1,0:T(8,128)(2,1)S(1)}, u32[]{:S(2)}, u32[]{:S(2)}) collective-permute-start(bf16[32,16,256]{2,1,0:T(8,128)(2,1)} %add_convert_fusion), channel_id=1, source_target_pairs={{0,8},{1,9},{2,10},{3,11},{4,12},{5,13},{6,14},{7,15}} | collective-permute-start | bytes 786440 | tf_op jit(solution)/shard_map/ppermute | solution.py:433
  28.9 12.7 %collective-permute-start.3 = (bf16[32,16,256]{2,1,0:T(8,128)(2,1)}, bf16[32,16,256]{2,1,0:T(8,128)(2,1)}, u32[]{:S(2)}, u32[]{:S(2)}) collective-permute-start(bf16[32,16,256]{2,1,0:T(8,128)(2,1)} %add_convert_fusion.1), channel_id=1, source_target_pairs={{0,8},{1,9},{2,10},{3,11},{4,12},{5,13},{6,14},{7,15}} | collective-permute-start | bytes 786440 | tf_op jit(solution)/shard_map/ppermute | solution.py:433
  40.9 4.9 %collective-permute-start.15 = (bf16[32,16,256]{2,1,0:T(8,128)(2,1)S(1)}, bf16[32,16,256]{2,1,0:T(8,128)(2,1)S(1)}, u32[]{:S(2)}, u32[]{:S(2)}) collective-permute-start(bf16[32,16,256]{2,1,0:T(8,128)(2,1)S(1)} %get-tuple-element.92), channel_id=1, source_target_pairs={{8,16},{9,17},{10,18},{11,19},{12,20},{13,21},{14,22},{15,23}} | collective-permute-start | bytes 786440 | tf_op jit(solution)/shard_map/ppermute | solution.py:455
  44.9 4.7 %collective-permute-start.5 = (bf16[32,16,256]{2,1,0:T(8,128)(2,1)S(1)}, bf16[32,16,256]{2,1,0:T(8,128)(2,1)S(1)}, u32[]{:S(2)}, u32[]{:S(2)}) collective-permute-start(bf16[32,16,256]{2,1,0:T(8,128)(2,1)S(1)} %get-tuple-element.70), channel_id=1, source_target_pairs={{8,16},{9,17},{10,18},{11,19},{12,20},{13,21},{14,22},{15,23}} | collective-permute-start | bytes 786440 | tf_op jit(solution)/shard_map/ppermute | solution.py:455
  45.6 8.0 %collective-permute-start.8 = (bf16[16,32,256]{2,1,0:T(8,128)(2,1)S(1)}, bf16[16,32,256]{2,1,0:T(8,128)(2,1)S(1)}, u32[]{:S(2)}, u32[]{:S(2)}) collective-permute-start(bf16[16,32,256]{2,1,0:T(8,128)(2,1)S(1)} %constant_dynamic-slice_fusion.1), channel_id=1, source_target_pairs={{0,4},{4,0},{1,5},{5,1},{2,6},{6,2},{3,7},{7,3},{8,12},{12,8},{9,1... | collective-permute-start | bytes 786440 | tf_op jit(solution)/shard_map/ppermute | solution.py:378
  48.9 13.8 %collective-permute-start.16 = (bf16[32,16,256]{2,1,0:T(8,128)(2,1)S(1)}, bf16[32,16,256]{2,1,0:T(8,128)(2,1)S(1)}, u32[]{:S(2)}, u32[]{:S(2)}) collective-permute-start(bf16[32,16,256]{2,1,0:T(8,128)(2,1)S(1)} %get-tuple-element.96), channel_id=1, source_target_pairs={{16,24},{17,25},{18,26},{19,27},{20,28},{21,29},{22,30},{23,31}} | collective-permute-start | bytes 786440 | tf_op jit(solution)/shard_map/ppermute | solution.py:455
  52.8 13.3 %collective-permute-start.6 = (bf16[32,16,256]{2,1,0:T(8,128)(2,1)S(1)}, bf16[32,16,256]{2,1,0:T(8,128)(2,1)S(1)}, u32[]{:S(2)}, u32[]{:S(2)}) collective-permute-start(bf16[32,16,256]{2,1,0:T(8,128)(2,1)S(1)} %get-tuple-element.74), channel_id=1, source_target_pairs={{16,24},{17,25},{18,26},{19,27},{20,28},{21,29},{22,30},{23,31}} | collective-permute-start | bytes 786440 | tf_op jit(solution)/shard_map/ppermute | solution.py:455
  65.4 6.9 %collective-permute-start.17 = (bf16[32,16,256]{2,1,0:T(8,128)(2,1)S(1)}, bf16[32,16,256]{2,1,0:T(8,128)(2,1)S(1)}, u32[]{:S(2)}, u32[]{:S(2)}) collective-permute-start(bf16[32,16,256]{2,1,0:T(8,128)(2,1)S(1)} %get-tuple-element.98), channel_id=1, source_target_pairs={{24,16},{25,17},{26,18},{27,19},{28,20},{29,21},{30,22},{31,23}} | collective-permute-start | bytes 786440 | tf_op jit(solution)/shard_map/ppermute | solution.py:472
  68.6 7.5 %collective-permute-start.10 = (bf16[32,16,256]{2,1,0:T(8,128)(2,1)S(1)}, bf16[32,16,256]{2,1,0:T(8,128)(2,1)S(1)}, u32[]{:S(2)}, u32[]{:S(2)}) collective-permute-start(bf16[32,16,256]{2,1,0:T(8,128)(2,1)S(1)} %get-tuple-element.80), channel_id=1, source_target_pairs={{24,16},{25,17},{26,18},{27,19},{28,20},{29,21},{30,22},{31,23}} | collective-permute-start | bytes 786440 | tf_op jit(solution)/shard_map/ppermute | solution.py:472
  74.8 9.7 %collective-permute-start.18 = (bf16[32,16,256]{2,1,0:T(8,128)(2,1)}, bf16[32,16,256]{2,1,0:T(8,128)(2,1)}, u32[]{:S(2)}, u32[]{:S(2)}) collective-permute-start(bf16[32,16,256]{2,1,0:T(8,128)(2,1)} %get-tuple-element.101), channel_id=1, source_target_pairs={{16,8},{17,9},{18,10},{19,11},{20,12},{21,13},{22,14},{23,15}} | collective-permute-start | bytes 786440 | tf_op jit(solution)/shard_map/ppermute | solution.py:488
  78.6 11.8 %collective-permute-start.11 = (bf16[32,16,256]{2,1,0:T(8,128)(2,1)}, bf16[32,16,256]{2,1,0:T(8,128)(2,1)}, u32[]{:S(2)}, u32[]{:S(2)}) collective-permute-start(bf16[32,16,256]{2,1,0:T(8,128)(2,1)} %get-tuple-element.83), channel_id=1, source_target_pairs={{16,8},{17,9},{18,10},{19,11},{20,12},{21,13},{22,14},{23,15}} | collective-permute-start | bytes 786440 | tf_op jit(solution)/shard_map/ppermute | solution.py:488
  80.0 13.6 %collective-permute-start.24 = (f32[16,16,256]{2,1,0:T(8,128)}, f32[16,16,256]{2,1,0:T(8,128)}, u32[]{:S(2)}, u32[]{:S(2)}) collective-permute-start(f32[16,16,256]{2,1,0:T(8,128)} %get-tuple-element.119), channel_id=1, source_target_pairs={{0,4},{4,0},{1,5},{5,1},{2,6},{6,2},{3,7},{7,3},{8,12},{12,8},{9,1... | collective-permute-start | bytes 786440 | tf_op jit(solution)/shard_map/ppermute | solution.py:378
  83.5 10.1 %collective-permute-start.23 = (f32[16,16,256]{2,1,0:T(8,128)}, f32[16,16,256]{2,1,0:T(8,128)}, u32[]{:S(2)}, u32[]{:S(2)}) collective-permute-start(f32[16,16,256]{2,1,0:T(8,128)} %get-tuple-element.118), channel_id=1, source_target_pairs={{0,4},{4,0},{1,5},{5,1},{2,6},{6,2},{3,7},{7,3},{8,12},{12,8},{9,1... | collective-permute-start | bytes 786440 | tf_op jit(solution)/shard_map/ppermute | solution.py:378
  89.1 17.4 %collective-permute-start.19 = (bf16[32,16,256]{2,1,0:T(8,128)(2,1)S(1)}, bf16[32,16,256]{2,1,0:T(8,128)(2,1)S(1)}, u32[]{:S(2)}, u32[]{:S(2)}) collective-permute-start(bf16[32,16,256]{2,1,0:T(8,128)(2,1)S(1)} %get-tuple-element.104), channel_id=1, source_target_pairs={{8,0},{9,1},{10,2},{11,3},{12,4},{13,5},{14,6},{15,7}} | collective-permute-start | bytes 786440 | tf_op jit(solution)/shard_map/ppermute | solution.py:488
  92.2 17.5 %collective-permute-start.12 = (bf16[32,16,256]{2,1,0:T(8,128)(2,1)S(1)}, bf16[32,16,256]{2,1,0:T(8,128)(2,1)S(1)}, u32[]{:S(2)}, u32[]{:S(2)}) collective-permute-start(bf16[32,16,256]{2,1,0:T(8,128)(2,1)S(1)} %get-tuple-element.86), channel_id=1, source_target_pairs={{8,0},{9,1},{10,2},{11,3},{12,4},{13,5},{14,6},{15,7}} | collective-permute-start | bytes 786440 | tf_op jit(solution)/shard_map/ppermute | solution.py:488
  95.0 16.6 %collective-permute-start.22 = (f32[16,16,256]{2,1,0:T(8,128)S(1)}, f32[16,16,256]{2,1,0:T(8,128)S(1)}, u32[]{:S(2)}, u32[]{:S(2)}) collective-permute-start(f32[16,16,256]{2,1,0:T(8,128)S(1)} %copy-done.15), channel_id=1, source_target_pairs={{0,4},{4,0},{1,5},{5,1},{2,6},{6,2},{3,7},{7,3},{8,12},{12,8},{9,1... | collective-permute-start | bytes 786440 | tf_op jit(solution)/shard_map/ppermute | solution.py:378
  95.5 15.3 %collective-permute-start.21 = (f32[16,16,256]{2,1,0:T(8,128)S(1)}, f32[16,16,256]{2,1,0:T(8,128)S(1)}, u32[]{:S(2)}, u32[]{:S(2)}) collective-permute-start(f32[16,16,256]{2,1,0:T(8,128)S(1)} %get-tuple-element.88.kept_f), channel_id=1, source_target_pairs={{0,4},{4,0},{1,5},{5,1},{2,6},{6,2},{3,7},{7,3},{8,12},{12,8},{9,1... | collective-permute-start | bytes 786440 | tf_op jit(solution)/shard_map/ppermute | solution.py:378
  106.5 5.1 %collective-permute-start.20 = (bf16[16,16,256]{2,1,0:T(8,128)(2,1)S(1)}, bf16[16,16,256]{2,1,0:T(8,128)(2,1)S(1)}, u32[]{:S(2)}, u32[]{:S(2)}) collective-permute-start(bf16[16,16,256]{2,1,0:T(8,128)(2,1)S(1)} %get-tuple-element.124), channel_id=1, source_target_pairs={{0,4},{4,0},{1,5},{5,1},{2,6},{6,2},{3,7},{7,3},{8,12},{12,8},{9,1... | collective-permute-start | bytes 393224 | tf_op jit(solution)/shard_map/ppermute | solution.py:378
  (35 other events, 132.9 us)

commit v3 on v1

--- a/solution.py
+++ b/solution.py
@@ -1,4 +1,5 @@
 import functools
+import itertools
 
 import jax
 import jax.numpy as jnp
@@ -11,6 +12,7 @@
 LOCAL_SWAP = False
 VMEM_BYTES = 24 * 2**20
 
+LEVEL, SUB = "level", "sub"
 BF16 = jnp.bfloat16
 F32 = jnp.float32
 IN_VMEM = pl.BlockSpec(memory_space=pltpu.VMEM)
@@ -22,8 +24,12 @@
 
 
 def forward_kernel(section, start, rows, info, rhs, incoming, inv, off, kept_f, kept_u, fwd, upd, home, far, total):
-    del kept_f, kept_u
     count = inv.shape[0]
+
+    @pl.when(info[count] != section)
+    def _():
+        fwd[...] = kept_f[...]
+        upd[...] = kept_u[...]
 
     @pl.when(info[count] == section)
     def _():
@@ -46,8 +52,12 @@
 
 
 def top_kernel(section, start, rows, info, rhs, incoming, inv, up_off, up_inv, ancestor, kept_f, kept_s, fwd, sol, sol_bf):
-    del kept_f, kept_s
     count = inv.shape[0]
+
+    @pl.when(info[count] != section)
+    def _():
+        fwd[...] = kept_f[...]
+        sol[...] = kept_s[...]
 
     @pl.when(info[count] == section)
     def _():
@@ -63,9 +73,12 @@
 
 
 def top_update_kernel(section, start, rows, info, fwd, off, kept_u, upd):
-    del kept_u, start, rows
     count = off.shape[0]
 
+    @pl.when(info[count] != section)
+    def _():
+        upd[...] = kept_u[...]
+
     @pl.when(info[count] == section)
     def _():
         for node in range(count):
@@ -73,8 +86,11 @@
 
 
 def backward_kernel(section, start, rows, info, fwd, own, partner, up_off, up_inv, kept_s, sol, sol_bf):
-    del kept_s, start, rows
     count = up_inv.shape[0]
+
+    @pl.when(info[count] != section)
+    def _():
+        sol[...] = kept_s[...]
 
     @pl.when(info[count] == section)
     def _():
@@ -107,19 +123,19 @@
 
 def swapped(value, section, apart):
     mask = 2**apart
-    subs = lax.axis_size("sub")
+    subs = lax.axis_size(SUB)
     if not LOCAL_SWAP:
-        return lax.ppermute(value, "sub", [(i, i ^ mask) for i in range(subs)])
+        return lax.ppermute(value, SUB, [(i, i ^ mask) for i in range(subs)])
     pairs = [(section * subs + i, section * subs + (i ^ mask)) for i in range(subs)]
-    return lax.ppermute(value, ("level", "sub"), pairs)
-
-
-def body(rhs, lower_inv, lower_off, upper_inv, upper_off, ancestor, parent):
-    levels = lax.axis_size("level")
-    sub_count = lax.axis_size("sub")
+    return lax.ppermute(value, (LEVEL, SUB), pairs)
+
+
+def general_body(rhs, lower_inv, lower_off, upper_inv, upper_off, ancestor, parent):
+    levels = lax.axis_size(LEVEL)
+    sub_count = lax.axis_size(SUB)
     sub_bits = sub_count.bit_length() - 1
-    tier = lax.axis_index("level")
-    sub = lax.axis_index("sub")
+    tier = lax.axis_index(LEVEL)
+    sub = lax.axis_index(SUB)
     rhs, lower_inv, lower_off, upper_inv, upper_off = (
         value[0] for value in (rhs, lower_inv, lower_off, upper_inv, upper_off)
     )
@@ -153,14 +169,14 @@
             )
             received = swapped(far, section, section % sub_bits)
             summed = (home + received.astype(F32)).astype(BF16)
-            incoming[c] = lax.ppermute(summed, "level", [(section, section + 1)])
+            incoming[c] = lax.ppermute(summed, LEVEL, [(section, section + 1)])
     for c in range(CHUNKS):
         fwd[c], sol[c], solved = call(
             top_kernel, top, c * rows, rows,
             (info, rhs, incoming[c], lower_inv, upper_off, upper_inv, ancestor, fwd[c], sol[c]),
             [shape(BF16), shape(F32), shape(BF16)], {7: 0, 8: 1}, products=3,
         )
-        above[c] = lax.ppermute(solved, "level", [(top, top - 1)])
+        above[c] = lax.ppermute(solved, LEVEL, [(top, top - 1)])
     for c in range(CHUNKS):
         (upd[c],) = call(top_update_kernel, top, c * rows, rows, (info, fwd[c], lower_off, upd[c]), [shape(F32)], {3: 0}, products=1)
     for section in reversed(range(top)):
@@ -172,24 +188,561 @@
                 [shape(F32), shape(BF16)], {6: 0},
             )
             if section:
-                above[c] = lax.ppermute(solved, "level", [(section, section - 1)])
+                above[c] = lax.ppermute(solved, LEVEL, [(section, section - 1)])
     return jnp.concatenate(sol, axis=1)[None], jnp.concatenate(upd, axis=1)[None]
+
+
+NODE_ROWS = 16
+LOAD_NODES = 4
+SMALL_VMEM_BYTES = 12 * 2**20
+IN_ANY = pl.BlockSpec(memory_space=pl.ANY)
+IN_HBM = pl.BlockSpec(memory_space=pltpu.HBM)
+
+
+def rows_of(start):
+    return pl.ds(pl.multiple_of(start, NODE_ROWS), NODE_ROWS)
+
+
+def half_rows(array, sub):
+    half = array.shape[1] // 2
+    return pl.ds(pl.multiple_of(half * sub, half), half)
+
+
+def flat(value):
+    return value.reshape(value.shape[0] * value.shape[1], value.shape[2])
+
+
+def pick(select, values):
+    high = values.astype(BF16)
+    low = (values - high.astype(F32)).astype(BF16)
+    return dot(select, high) + dot(select, low)
+
+
+def on_level(section):
+    return pl.when(lax.axis_index(LEVEL) == section)
+
+
+def off_level(section):
+    return pl.when(lax.axis_index(LEVEL) != section)
+
+
+def keep(section, kept, outs):
+    @off_level(section)
+    def _():
+        for before, after in zip(kept, outs):
+            after[...] = before[...]
+
+
+def fill_tables(parent, select, choose):
+    nodes = parent.shape[1]
+    size = nodes * NODE_ROWS
+    top = lax.axis_size(LEVEL) - 1
+    level, shift = lax.axis_index(LEVEL), lax.axis_index(SUB) * (nodes // 2)
+
+    def target(row, axis):
+        shape = (nodes, size) if axis else (size, nodes)
+        child = lax.broadcasted_iota(jnp.int32, shape, axis) // NODE_ROWS + shift
+        child = jnp.where(child >= nodes, child - nodes, child)
+        same = child == lax.broadcasted_iota(jnp.int32, shape, 1 - axis)
+        row = row - shift
+        row = jnp.where(row < 0, row + nodes, row)
+        if axis:
+            found = dot(row.astype(F32).astype(BF16), same.astype(F32).astype(BF16))
+        else:
+            found = jnp.sum(jnp.where(same, row.astype(F32), 0.0), axis=1, keepdims=True)
+        place = lax.broadcasted_iota(jnp.int32, found.shape, axis)
+        return found.astype(jnp.int32) * NODE_ROWS + lax.rem(place, NODE_ROWS)
+
+    up = target(parent[pl.ds(jnp.minimum(level, top - 1), 1), :], 1)
+    down = target(parent[pl.ds(jnp.maximum(level - 1, 0), 1), :], 0)
+    index = lax.broadcasted_iota(jnp.int32, (size, size), 0)
+    select[...] = (index == up).astype(F32).astype(BF16)
+    index = lax.broadcasted_iota(jnp.int32, (size, size), 1)
+    choose[...] = (index == down).astype(F32).astype(BF16)
+
+
+def start_kernel(parent, rhs, inv, off, select, choose, rhs_own, rhs_sent, home, swap, merged, *refs):
+    *updates, parent_here, inv_here, off_here, sems = refs
+    count = inv.shape[0]
+    chunks = len(updates) // 2
+    size = count * NODE_ROWS
+    level, sub = lax.axis_index(LEVEL), lax.axis_index(SUB)
+    table = pltpu.make_async_copy(parent, parent_here, sems.at[0, 0])
+    mine = pltpu.make_async_copy(rhs.at[:, half_rows(rhs, sub), :], rhs_own, sems.at[0, 1])
+    other = pltpu.make_async_copy(rhs.at[:, half_rows(rhs, 1 - sub), :], rhs_sent, sems.at[0, 2])
+    table.start()
+    loads = []
+    for group in range(count // LOAD_NODES):
+        here = pl.ds(group * LOAD_NODES, LOAD_NODES)
+        loads.append(pltpu.make_async_copy(inv.at[here], inv_here.at[here], sems.at[1, group]))
+        loads.append(pltpu.make_async_copy(off.at[here], off_here.at[here], sems.at[2, group]))
+        loads[-2].start()
+        loads[-1].start()
+        if group == 0:
+            mine.start()
+            other.start()
+    table.wait()
+    fill_tables(parent_here, select, choose)
+    mine.wait()
+    other.wait()
+
+    @on_level(0)
+    def _():
+        for node in range(count):
+            if node % LOAD_NODES == 0:
+                loads[2 * (node // LOAD_NODES)].wait()
+                loads[2 * (node // LOAD_NODES) + 1].wait()
+            right_side = jnp.concatenate([rhs_own[node], rhs_sent[node]], axis=0).astype(BF16)
+            forward = dot(right_side, inv_here[node]).astype(BF16)
+            update = dot(forward, off_here[node])
+            for c in range(2 * chunks):
+                updates[c][node] = update[NODE_ROWS * c : NODE_ROWS * (c + 1)]
+        chosen = select[:, :size]
+        for c in range(chunks):
+            home[2 * count * c : 2 * count * (c + 1)] = pick(chosen, flat(updates[c][...])).reshape(2 * count, *home.shape[1:])
+            sums = pick(chosen, flat(updates[chunks + c][...])).astype(BF16).reshape(2 * count, *home.shape[1:])
+            swap[2 * count * c : 2 * count * c + count] = sums[count:]
+            swap[2 * count * c + count : 2 * count * (c + 1)] = sums[:count]
+
+    @off_level(0)
+    def _():
+        for node in range(count):
+            if node % LOAD_NODES == 0:
+                loads[2 * (node // LOAD_NODES)].wait()
+                loads[2 * (node // LOAD_NODES) + 1].wait()
+            merged[node] = dot(inv_here[node], off_here[node]).astype(BF16)
+
+
+def merge_kernel(levels, low_inv, up_inv, up_off, ancestor, packed, *scratch):
+    low_here, up_here, off_here, rows, sems = scratch
+    count = low_inv.shape[0]
+    level, sub = lax.axis_index(LEVEL), lax.axis_index(SUB)
+
+    @pl.when((level == levels[0]) | (level == levels[1]))
+    def _():
+        loads = []
+        for group in range(count // LOAD_NODES):
+            here = pl.ds(group * LOAD_NODES, LOAD_NODES)
+            loads.append(pltpu.make_async_copy(up_inv.at[here], up_here.at[here], sems.at[1, group]))
+            loads.append(pltpu.make_async_copy(low_inv.at[here], low_here.at[here], sems.at[0, group]))
+            loads.append(pltpu.make_async_copy(up_off.at[here], off_here.at[here], sems.at[2, group]))
+        loads.append(pltpu.make_async_copy(ancestor.at[:, half_rows(ancestor, 1 - sub), :], rows, sems.at[3, 0]))
+        for load in loads:
+            load.start()
+        for node in range(count):
+            if node % LOAD_NODES == 0:
+                for load in loads[3 * (node // LOAD_NODES) : 3 * (node // LOAD_NODES) + 3]:
+                    load.wait()
+            packed[node] = dot(low_here[node], up_here[node]).astype(BF16)
+            packed[count + node] = dot(off_here[node], up_here[node]).astype(BF16)
+        loads[-1].wait()
+        packed[2 * count :] = rows[...].reshape(packed.shape[0] - 2 * count, *packed.shape[1:])
+
+
+def residue_of(c, rhs_own, rhs_far, incoming, node):
+    count = rhs_own.shape[0]
+    rows = slice(NODE_ROWS * c, NODE_ROWS * (c + 1))
+    right_side = rhs_own[node, rows, :] if node < count else rhs_far[node - count, rows, :]
+    return (right_side - incoming[node].astype(F32)).astype(BF16)
+
+
+def tier_role(c, at):
+    count = at["rhs_own"].shape[0]
+    own, far = at["own", c], at["far", c]
+    for node in range(2 * count):
+        value = residue_of(c, at["rhs_own"], at["rhs_far"], at["received"], node)
+        at["residue", c][node] = value
+        if node < count:
+            own[node] = dot(value, at["up_own"][node])
+        else:
+            far[node - count] = dot(value, at["up_far"][node - count])
+    updates = jnp.concatenate([flat(own[...]), flat(far[...])], axis=0)
+    at["sent"][...] = pick(at["select"][...], updates).astype(BF16).reshape(at["sent"].shape)
+
+
+def send_solved(c, at):
+    if "sent" in at:
+        solved = jnp.concatenate([flat(at["sol_own", c][...]), flat(at["sol_far", c][...])], axis=0).astype(BF16)
+        at["sent"][...] = dot(at["choose"][...], solved).astype(BF16).reshape(at["sent"].shape)
+
+
+def top_role(c, at):
+    count = at["rhs_own"].shape[0]
+    base = at["top_base", c]
+    for node in range(2 * count):
+        value = residue_of(c, at["rhs_own"], at["rhs_far"], at["received"], node)
+        at["residue", c][node] = value
+        if node < count:
+            at["sol_own", c][node] = dot(value, at["high_own"][node]) - base[node]
+        else:
+            at["sol_far", c][node - count] = dot(value, at["high_far"][node - count]) - base[node]
+    send_solved(c, at)
+
+
+def back_role(c, at, group="high"):
+    count = at["sol_own", c].shape[0]
+    base, above = at[group + "_base", c], at["received"]
+    own, far = at[group + "_own"], at[group + "_far"]
+    for node in range(count):
+        at["sol_own", c][node] = base[node] - dot(above[node], own[count + node])
+        at["sol_far", c][node] = base[count + node] - dot(above[count + node], far[count + node])
+    send_solved(c, at)
+
+
+def low_back_role(c, at):
+    back_role(c, at, "low")
+
+
+def sum_role(c, at):
+    rows = slice(c * at["sent"].shape[0], (c + 1) * at["sent"].shape[0])
+    at["sent"][...] = (at["home"][rows] + at["swapped"][rows].astype(F32)).astype(BF16)
+
+
+ROLES = {"tier": tier_role, "top": top_role, "back": back_role, "low": low_back_role, "sum": sum_role}
+READS = {
+    "tier": ("rhs_own", "rhs_far", "received", "up_own", "up_far", "select"),
+    "top": ("rhs_own", "rhs_far", "received", "high_own", "high_far", "choose", "top_base"),
+    "back": ("received", "high_own", "high_far", "choose", "high_base"),
+    "low": ("received", "low_own", "low_far", "choose", "low_base"),
+    "sum": ("home", "swapped"),
+}
+WRITES = {
+    "tier": ("residue", "own", "far"),
+    "top": ("residue", "sol_own", "sol_far"),
+    "back": ("sol_own", "sol_far"),
+    "low": ("sol_own", "sol_far"),
+    "sum": (),
+}
+
+
+def step_kernel(plan, in_keys, out_keys, kept_keys, *refs):
+    reads = dict(zip(in_keys, refs))
+    kept = dict(zip(kept_keys, refs[len(in_keys) :]))
+    outs = dict(zip(out_keys, refs[len(in_keys) + len(kept_keys) :]))
+    for level, role, c in plan:
+        writes = [(name, c) for name in WRITES[role]]
+        keep(level, [kept[key] for key in writes if key in kept], [outs[key] for key in writes if key in kept])
+        pl.when(lax.axis_index(LEVEL) == level)(functools.partial(ROLES[role], c, {**reads, **outs}))
+
+
+def step(plan, state, sends=True):
+    nodes = state["nodes"]
+    in_keys, out_keys = [], []
+    for _, role, c in plan:
+        for name in READS[role]:
+            key = (name, c) if name.endswith("_base") else name
+            if key not in in_keys:
+                in_keys.append(key)
+        out_keys += [(name, c) for name in WRITES[role]]
+    kept_keys = [key for key in out_keys if key in state]
+    width = state["rhs_own"].shape[2]
+    outs = []
+    for name, _ in out_keys:
+        of, dtype = (nodes, BF16) if name == "residue" else (nodes // 2, F32)
+        outs.append(jax.ShapeDtypeStruct((of, NODE_ROWS, width), dtype))
+    aliases = {len(in_keys) + i: out_keys.index(key) for i, key in enumerate(kept_keys)}
+    all_outs = out_keys + (["sent"] if sends else [])
+    if sends:
+        outs.append(jax.ShapeDtypeStruct((nodes, NODE_ROWS, width), BF16))
+    operands = [state[key] for key in in_keys + kept_keys]
+    results = run(functools.partial(step_kernel, plan, in_keys, all_outs, kept_keys), operands, outs, aliases)
+    state.update(zip(out_keys, results))
+    return results[-1] if sends else None
+
+
+def high_base_kernel(section, own, far, *refs):
+    chunks = len(refs) // 2
+    residue, base = refs[:chunks], refs[chunks:]
+    count = residue[0].shape[0] // 2
+
+    @on_level(section)
+    def _():
+        for c in range(chunks):
+            for node in range(count):
+                base[c][node] = dot(residue[c][node], own[node])
+                base[c][count + node] = dot(residue[c][count + node], far[node])
+
+
+def low_base_kernel(rhs_own, rhs_far, own, far, *refs):
+    chunks = len(refs) // 2
+    residue, base = refs[:chunks], refs[chunks:]
+    count = rhs_own.shape[0]
+    level = lax.axis_index(LEVEL)
+
+    @pl.when(level == 0)
+    def _():
+        for node in range(count):
+            mine = dot(rhs_own[node].astype(BF16), own[node])
+            other = dot(rhs_far[node].astype(BF16), far[node])
+            for c in range(chunks):
+                base[c][node] = mine[NODE_ROWS * c : NODE_ROWS * (c + 1)]
+                base[c][count + node] = other[NODE_ROWS * c : NODE_ROWS * (c + 1)]
+
+    @pl.when((level != 0) & (level < lax.axis_size(LEVEL) - 2))
+    def _():
+        for c in range(chunks):
+            for node in range(count):
+                base[c][node] = dot(residue[c][node], own[node])
+                base[c][count + node] = dot(residue[c][count + node], far[node])
+
+
+def ancestor_kernel(section, ancestor, own, far, *refs):
+    *bases, here, sem = refs
+    count, half, _ = here.shape
+    sub = lax.axis_index(SUB)
+
+    @on_level(section)
+    def _():
+        load = pltpu.make_async_copy(ancestor.at[:, half_rows(ancestor, sub), :], here, sem.at[0])
+        load.start()
+        load.wait()
+        for node in range(count):
+            per = far.shape[1] // half
+            other = far[2 * count + node // per, half * (node % per) : half * (node % per + 1), :]
+            mine = dot(here[node], own[count + node])
+            other = dot(other, far[count + node])
+            for c, base in enumerate(bases):
+                base[node] = mine[NODE_ROWS * c : NODE_ROWS * (c + 1)]
+                base[count + node] = other[NODE_ROWS * c : NODE_ROWS * (c + 1)]
+
+
+def top_tier_update_kernel(section, residue, step_own, step_far, kept_o, kept_f, upd_own, upd_far):
+    count = step_own.shape[0]
+    keep(section, (kept_o, kept_f), (upd_own, upd_far))
+
+    @on_level(section)
+    def _():
+        for node in range(count):
+            upd_own[node] = dot(residue[node], step_own[node])
+            upd_far[node] = dot(residue[count + node], step_far[node])
+
+
+def put(c, own, far, out, sems):
+    sub = lax.axis_index(SUB)
+    half = out.shape[1] // 2
+    first = pltpu.make_async_copy(own, out.at[:, rows_of(half * sub + NODE_ROWS * c), :], sems.at[0])
+    second = pltpu.make_async_copy(far, out.at[:, rows_of(half * (1 - sub) + NODE_ROWS * c), :], sems.at[1])
+    first.start()
+    second.start()
+    first.wait()
+    second.wait()
+
+
+def place_kernel(c, here, far, other, *refs):
+    out, sems = refs[-2:]
+    put(c, here, other, out, sems)
+
+
+def place_bottom_kernel(c, here, far, other, *refs):
+    out, sems = refs[-2:]
+
+    @on_level(0)
+    def _():
+        put(c, here, far, out, sems)
+
+    @off_level(0)
+    def _():
+        put(c, here, other, out, sems)
+
+
+def run(kernel, operands, outs, aliases=None, products=32, whole=None, scratch=(), raw=()):
+    in_specs = [IN_HBM] * len(raw) + [IN_VMEM] * len(operands)
+    operands = [*(pltpu.with_memory_space_constraint(value, pltpu.HBM) for value in raw), *(pltpu.with_memory_space_constraint(value, pltpu.VMEM) for value in operands)]
+    out_specs = [IN_VMEM] * len(outs)
+    out_shape = [pltpu.VMEM(out.shape, out.dtype) for out in outs]
+    aliases = dict(aliases or {})
+    if whole is not None:
+        shape, before = whole
+        if before is not None:
+            aliases[len(operands)] = len(outs)
+            operands.append(before)
+            in_specs.append(IN_ANY)
+        out_shape.append(shape)
+        out_specs.append(IN_ANY)
+    return pl.pallas_call(
+        kernel,
+        in_specs=in_specs,
+        out_specs=out_specs,
+        out_shape=out_shape,
+        input_output_aliases=aliases,
+        scratch_shapes=scratch,
+        compiler_params=pltpu.CompilerParams(vmem_limit_bytes=SMALL_VMEM_BYTES),
+        cost_estimate=pl.CostEstimate(
+            flops=products * 2 * NODE_ROWS * 256 * 256, bytes_accessed=256 * 256 * 2 * products, transcendentals=0
+        ),
+    )(*operands)
+
+
+def exchanged(value):
+    return lax.ppermute(value, SUB, [(0, 1), (1, 0)])
+
+
+def pair_body(rhs, lower_inv, lower_off, upper_inv, upper_off, ancestor, parent):
+    levels = lax.axis_size(LEVEL)
+    top = levels - 1
+    rhs, lower_inv, lower_off, upper_inv, upper_off = (
+        value[0] for value in (rhs, lower_inv, lower_off, upper_inv, upper_off)
+    )
+    count, all_rows, width = rhs.shape
+    half = all_rows // 2
+    chunks = half // NODE_ROWS
+    nodes = 2 * count
+    size = nodes * NODE_ROWS
+
+    def shape(of, dtype):
+        return jax.ShapeDtypeStruct((of, NODE_ROWS, width), dtype)
+
+    def passed(value, pairs):
+        sources = [i for i in range(levels) if i not in dict(pairs)]
+        targets = [i for i in range(levels) if i not in [to for _, to in pairs]]
+        fill = min(
+            (list(zip(sources, order)) for order in itertools.permutations(targets)),
+            key=lambda extra: (sum(a == b for a, b in extra), sum(abs(a - b) for a, b in extra)),
+        )
+        return lax.ppermute(value, LEVEL, pairs + fill)
+
+    def after(value, *earlier):
+        return lax.optimization_barrier((value, *earlier))[0]
+
+    matrices = jax.ShapeDtypeStruct(lower_inv.shape, BF16)
+    table = jax.ShapeDtypeStruct((size, size), BF16)
+    half_shape = jax.ShapeDtypeStruct((count, half, width), F32)
+    block = pltpu.VMEM(lower_inv.shape, BF16)
+    state = {"nodes": nodes}
+    select, choose, rhs_own, rhs_sent, home, swap, up_own, *updates = run(
+        start_kernel, (),
+        [table, table, half_shape, half_shape, shape(chunks * nodes, F32), shape(chunks * nodes, BF16), matrices]
+        + [shape(count, F32)] * (2 * chunks),
+        raw=(parent, rhs, lower_inv, lower_off),
+        scratch=[pltpu.VMEM(parent.shape, parent.dtype), block, block, pltpu.SemaphoreType.DMA((3, max(count // LOAD_NODES, 3)))],
+    )
+    state.update(select=select, choose=choose, rhs_own=rhs_own, home=home, up_own=up_own, swapped=exchanged(swap))
+    for c in range(chunks):
+        state["own", c], state["far", c] = updates[c], updates[chunks + c]
+
+    packed_shape = (2 * count + count * half // width, width, width)
+    merge_scratch = [block, block, block, pltpu.VMEM((count, half, width), BF16), pltpu.SemaphoreType.DMA((4, count // LOAD_NODES))]
+
+    def merged(levels_here, sent):
+        low, *others = lax.optimization_barrier((lower_inv, upper_inv, upper_off, ancestor, sent))
+        return run(
+            functools.partial(merge_kernel, levels_here), (), [jax.ShapeDtypeStruct(packed_shape, BF16)],
+            raw=(low, *others[:3]), scratch=merge_scratch, products=512,
+        )[0]
+
+    whole = jax.ShapeDtypeStruct(rhs.shape, F32)
+    sems = [pltpu.SemaphoreType.DMA((2,))]
+    update, solved = None, None
+    for k in range(2 * top + chunks):
+        plan, pairs = [], []
+        for c in range(chunks):
+            tier = k - c
+            if 0 <= tier < top:
+                plan.append((tier, "sum" if tier == 0 else "tier", c))
+                pairs.append((tier, tier + 1))
+            elif tier == top:
+                plan.append((top, "top", c))
+                pairs.append((top, top - 1))
+            elif top < tier <= 2 * top:
+                low = 2 * top - tier
+                plan.append((low, "back" if low == top - 1 else "low", c))
+                if low:
+                    pairs.append((low, low - 1))
+        sent = step(plan, state, sends=bool(pairs))
+        if not pairs:
+            break
+        received = passed(sent, pairs)
+        done = []
+        if k == 0:
+            state["up_far"] = exchanged(after(up_own, sent))
+            state["rhs_far"] = exchanged(after(rhs_sent, sent))
+            state["high_own"] = merged((top - 1, top), sent)
+            done = [state["high_own"]]
+        if k == 1:
+            state["high_far"] = exchanged(after(state["high_own"], sent))
+        if k == top - 1:
+            bases = run(
+                functools.partial(ancestor_kernel, top),
+                (state["high_own"], state["high_far"]),
+                [shape(nodes, F32)] * chunks,
+                raw=(after(ancestor, sent),),
+                scratch=[pltpu.VMEM((count, half, width), BF16), pltpu.SemaphoreType.DMA((1,))],
+            )
+            state.update({("top_base", c): bases[c] for c in range(chunks)})
+            state["low_own"] = merged((0, 1), sent)
+            done = [*bases, state["low_own"]]
+        if k == top:
+            state["low_far"] = exchanged(after(state["low_own"], sent))
+            residues = [state["residue", c] for c in range(chunks)]
+            bases = run(
+                functools.partial(high_base_kernel, top - 1),
+                (after(state["high_own"], sent), state["high_far"], *residues),
+                [shape(nodes, F32)] * chunks,
+            )
+            state.update({("high_base", c): bases[c] for c in range(chunks)})
+            done = bases
+        if k == top + 1:
+            residues = [state["residue", c] for c in range(chunks)]
+            bases = run(
+                low_base_kernel,
+                (after(rhs_own, sent), state["rhs_far"], state["low_own"], state["low_far"], *residues),
+                [shape(nodes, F32)] * chunks,
+            )
+            state.update({("low_base", c): bases[c] for c in range(chunks)})
+            done = bases
+        if k == top + chunks - 1:
+            for c in range(chunks):
+                state["own", c], state["far", c] = run(
+                    functools.partial(top_tier_update_kernel, top),
+                    (after(state["residue", c], sent), state["up_own"], state["up_far"], state["own", c], state["far", c]),
+                    [shape(count, F32), shape(count, F32)],
+                    {3: 0, 4: 1},
+                )
+            done = [*done, *(state["far", c] for c in range(chunks))]
+        if k == top + chunks:
+            upd_other = [exchanged(after(state["far", c], sent)) for c in range(chunks)]
+        if k == 2 * top + chunks - 2:
+            for c in range(chunks):
+                (update,) = run(
+                    functools.partial(place_bottom_kernel, c),
+                    (state["own", c], after(state["far", c], sent), upd_other[c]),
+                    [], whole=(whole, update), scratch=sems, products=1,
+                )
+            for c in range(chunks - 1):
+                (solved,) = run(
+                    functools.partial(place_kernel, c),
+                    (state["sol_own", c], state["sol_far", c], exchanged(state["sol_far", c])),
+                    [], whole=(whole, solved), scratch=sems, products=1,
+                )
+            done = [update] + ([] if solved is None else [solved])
+        if done:
+            received, *done = lax.optimization_barrier((received, *done))
+            if k == 2 * top + chunks - 2:
+                update, solved = done[0], done[1] if chunks > 1 else None
+        state["received"] = received
+    c = chunks - 1
+    (solved,) = run(
+        functools.partial(place_kernel, c),
+        (state["sol_own", c], state["sol_far", c], exchanged(state["sol_far", c])),
+        [], whole=(whole, solved), scratch=sems, products=1,
+    )
+    return solved[None], update[None]
 
 
 def solution(mesh):
     placed = (
-        P("level", "sub", "rhs", None),
-        P("level", "sub", None, None),
-        P("level", "sub", None, None),
-        P("level", "sub", None, None),
-        P("level", "sub", None, None),
-        P("sub", "rhs", None),
+        P(LEVEL, SUB, "rhs", None),
+        P(LEVEL, SUB, None, None),
+        P(LEVEL, SUB, None, None),
+        P(LEVEL, SUB, None, None),
+        P(LEVEL, SUB, None, None),
+        P(SUB, "rhs", None),
         P(),
     )
     return jax.shard_map(
-        body,
+        pair_body if mesh.shape[SUB] == 2 else general_body,
         mesh=mesh,
         in_specs=placed,
-        out_specs=(P("level", "sub", "rhs", None), P("level", "sub", "rhs", None)),
+        out_specs=(P(LEVEL, SUB, "rhs", None), P(LEVEL, SUB, "rhs", None)),
         check_vma=False,
     )

time: 112 us -> 76 us (0.68)
  waiting for transfers between devices: 73.2 us -> 41 us
  local copies, waits for them, and re-layouts: 4.64 us -> 0 us
  starting transfers between devices: 15.3 us -> 19.9 us
  other arithmetic: 3.42 us -> 0 us
    ppermute x24 -> x16, waiting for transfers between devices: 73.2 us -> 41 us  [the longest x7 37.9 us: passed(): return lax.ppermute(value, LEVEL, pairs + fill)]
    ppermute x24 -> x16, starting transfers between devices: 15.3 us -> 19.9 us  [the longest x7 18 us: passed(): return lax.ppermute(value, LEVEL, pairs + fill)]
    unnamed x14 -> x0, local copies, waits for them, and re-layouts: 4.42 us -> none
    broadcast_in_dim x2 -> x0, other arithmetic: 2.08 us -> none  [the longest x1 1.04 us: body(): jnp.concatenate(upd, axis=1)[None]]
    pallas_call x16 -> x20, Pallas kernels: 13.6 us -> 14.1 us  [run(): pl.pallas_call(kernel, in_specs=in_specs, out_specs=out_specs, out_shape=...]
  transfers between devices with their start and end apart: 24 -> 16, of which waited for: 8 -> 9; matrix products, arithmetic and copies ran while one was open for 2% -> 0% of each run, Pallas kernels for 9% -> 11%
where the time goes in v3:
time: 76 us; the launch traced here: 75.9 us
  waiting for transfers between devices  41 us (54%)
  starting transfers between devices  19.9 us (26%)
  Pallas kernels  14.1 us (19%)
  between operations  0.99 us (1%)
    ppermute x7, waiting for transfers between devices, passed(): return lax.ppermute(value, LEVEL, pairs + fill)  37.9 us
    ppermute x7, starting transfers between devices, passed(): return lax.ppermute(value, LEVEL, pairs + fill)  18 us
    pallas_call x20, Pallas kernels, run(): pl.pallas_call(kernel, in_specs=in_specs, out_specs=out_specs, out_shape=...  14.1 us
    ppermute x9, waiting for transfers between devices, exchanged(): return lax.ppermute(value, SUB, [(0, 1), (1, 0)])  3.08 us
    ppermute x9, starting transfers between devices, exchanged(): return lax.ppermute(value, SUB, [(0, 1), (1, 0)])  1.85 us
  transfers between devices with their start and end apart: 16, of which 9 were waited for; matrix products, arithmetic and copies ran while one was open for 0% of the time, Pallas kernels for 11%

profile of v3, /device:TPU:0, one launch (start us, length us, event | category | flops | bytes accessed | tf_op | source)
XLA Modules:
  0.0 75.9 jit_solution(3643808235374278086)
XLA Ops:
  0.6 3.9 %shard_map.86 = (bf16[512,512]{1,0:T(8,128)(2,1)S(1)}, bf16[512,512]{1,0:T(8,128)(2,1)S(1)}, f32[16,32,256]{2,1,0:T(8,128)S(1)}, f32[16,32,256]{2,1,0:T(8,128)S(...) custom-call(s32[3,32]{1,0:T(4,128)} %parent.1, ...), custom_call_target="tpu_custom_call" | custom-call | flops 67108864 | bytes 4194304 | tf_op jit(solution)/shard_map/pallas_call | solution.py:562
  5.1 1.5 %collective-permute-done.refs_1_.refs_7_ = bf16[64,16,256]{2,1,0:T(8,128)(2,1)S(1)} collective-permute-done((bf16[64,16,256]{2,1,0:T(8,128)(2,1)S(1)}, bf16[64,16,256]{2,1,0:T(8,128)(2,1)S(1)}, u32[]{:S(2)}, u32[]{:S(2)}) %collective-permute-start) | collective-permute-done | bytes 524320 | tf_op jit(solution)/shard_map/ppermute | solution.py:577
  7.3 1.7 %collective-permute-start.2 = (bf16[32,16,256]{2,1,0:T(8,128)(2,1)S(1)}, bf16[32,16,256]{2,1,0:T(8,128)(2,1)S(1)}, u32[]{:S(2)}, u32[]{:S(2)}) collective-permute-start(bf16[32,16,256]{2,1,0:T(8,128)(2,1)S(1)} %shard_map.87), channel_id=1, source_target_pairs={{0,8},{8,0},{16,24},{24,16},{1,9},{9,1},{17,25},{25,17},{2,10},{10... | collective-permute-start | bytes 786440 | tf_op jit(solution)/shard_map/ppermute | solution.py:602
  9.1 6.7 %collective-permute-done.2.refs_2_ = bf16[32,16,256]{2,1,0:T(8,128)(2,1)S(1)} collective-permute-done((bf16[32,16,256]{2,1,0:T(8,128)(2,1)S(1)}, bf16[32,16,256]{2,1,0:T(8,128)(2,1)S(1)}, u32[]{:S(2)}, u32[]{:S(2)}) %collective-permute-start.2) | collective-permute-done | bytes 262176 | tf_op jit(solution)/shard_map/ppermute | solution.py:602
  16.0 2.4 %collective-permute-start.4 = (bf16[32,16,256]{2,1,0:T(8,128)(2,1)S(1)}, bf16[32,16,256]{2,1,0:T(8,128)(2,1)S(1)}, u32[]{:S(2)}, u32[]{:S(2)}) collective-permute-start(bf16[32,16,256]{2,1,0:T(8,128)(2,1)S(1)} %get-tuple-element.102), channel_id=1, source_target_pairs={{8,16},{0,8},{16,24},{24,0},{9,17},{1,9},{17,25},{25,1},{10,18},{2... | collective-permute-start | bytes 786440 | tf_op jit(solution)/shard_map/ppermute | solution.py:602
  18.4 7.2 %collective-permute-done.4.refs_2_ = bf16[32,16,256]{2,1,0:T(8,128)(2,1)S(1)} collective-permute-done((bf16[32,16,256]{2,1,0:T(8,128)(2,1)S(1)}, bf16[32,16,256]{2,1,0:T(8,128)(2,1)S(1)}, u32[]{:S(2)}, u32[]{:S(2)}) %collective-permute-start.4) | collective-permute-done | bytes 262176 | tf_op jit(solution)/shard_map/ppermute | solution.py:602
  25.8 2.4 %collective-permute-start.5 = (bf16[32,16,256]{2,1,0:T(8,128)(2,1)S(1)}, bf16[32,16,256]{2,1,0:T(8,128)(2,1)S(1)}, u32[]{:S(2)}, u32[]{:S(2)}) collective-permute-start(bf16[32,16,256]{2,1,0:T(8,128)(2,1)S(1)} %get-tuple-element.108), channel_id=1, source_target_pairs={{16,24},{8,16},{0,8},{24,0},{17,25},{9,17},{1,9},{25,1},{18,26},{1... | collective-permute-start | bytes 786440 | tf_op jit(solution)/shard_map/ppermute | solution.py:602
  28.2 3.5 %shard_map.92.own.refs_1_ = bf16[34,256,256]{2,1,0:T(8,128)(2,1)S(1)} custom-call(bf16[16,256,256]{2,1,0:T(8,128)(2,1)} %bitcast.9, bf16[16,256,256]{2,1,0:T(8,128)(2,1)} %bitcast.11, bf16[16,256,256]{2,1,0:T(8,128)(2,1)} %bitcast.13, bf16[16,64,256]{2,1,0:T(8,128)(2,1)} %ancestor.2), custom_call_target="tpu_custom_call" | custom-call | flops 1073741824 | bytes 67108864 | tf_op jit(solution)/shard_map/pallas_call | solution.py:562
  31.7 2.9 %collective-permute-done.5.refs_2_ = bf16[32,16,256]{2,1,0:T(8,128)(2,1)S(1)} collective-permute-done((bf16[32,16,256]{2,1,0:T(8,128)(2,1)S(1)}, bf16[32,16,256]{2,1,0:T(8,128)(2,1)S(1)}, u32[]{:S(2)}, u32[]{:S(2)}) %collective-permute-start.5) | collective-permute-done | bytes 262176 | tf_op jit(solution)/shard_map/ppermute | solution.py:602
  34.8 1.5 %collective-permute-start.7 = (bf16[32,16,256]{2,1,0:T(8,128)(2,1)S(1)}, bf16[32,16,256]{2,1,0:T(8,128)(2,1)S(1)}, u32[]{:S(2)}, u32[]{:S(2)}) collective-permute-start(bf16[32,16,256]{2,1,0:T(8,128)(2,1)S(1)} %get-tuple-element.123), channel_id=1, source_target_pairs={{24,16},{16,24},{0,8},{8,0},{25,17},{17,25},{1,9},{9,1},{26,18},{1... | collective-permute-start | bytes 786440 | tf_op jit(solution)/shard_map/ppermute | solution.py:602
  36.4 7.2 %collective-permute-done.7.refs_0_ = bf16[32,16,256]{2,1,0:T(8,128)(2,1)S(1)} collective-permute-done((bf16[32,16,256]{2,1,0:T(8,128)(2,1)S(1)}, bf16[32,16,256]{2,1,0:T(8,128)(2,1)S(1)}, u32[]{:S(2)}, u32[]{:S(2)}) %collective-permute-start.7) | collective-permute-done | bytes 262176 | tf_op jit(solution)/shard_map/ppermute | solution.py:602
  43.7 3.9 %collective-permute-start.8 = (bf16[32,16,256]{2,1,0:T(8,128)(2,1)S(1)}, bf16[32,16,256]{2,1,0:T(8,128)(2,1)S(1)}, u32[]{:S(2)}, u32[]{:S(2)}) collective-permute-start(bf16[32,16,256]{2,1,0:T(8,128)(2,1)S(1)} %get-tuple-element.132), channel_id=1, source_target_pairs={{16,8},{24,16},{0,24},{8,0},{17,9},{25,17},{1,25},{9,1},{18,10},{2... | collective-permute-start | bytes 786440 | tf_op jit(solution)/shard_map/ppermute | solution.py:602
  47.7 0.8 %shard_map.96 = (f32[32,16,256]{2,1,0:T(8,128)S(1)}, f32[32,16,256]{2,1,0:T(8,128)S(1)}) custom-call(f32[16,32,256]{2,1,0:T(8,128)S(1)} %get-tuple-element.133.refs_0_.refs_5_.rhs_own, f32[16,32,256]{2,1,0:T(8,128)S(1)} %collective-permute-done.1.refs_1_.refs_6_.rhs_far, bf16[34,256,256]{2,1,0:T(8,128)(2,1)S(1)} %shard_map.92.own.refs_1_, ...), custom_call_target="tpu_custom_call" | custom-call | flops 67108864 | bytes 4194304 | tf_op jit(solution)/shard_map/pallas_call | solution.py:562
  48.5 4.6 %collective-permute-done.8.refs_0_ = bf16[32,16,256]{2,1,0:T(8,128)(2,1)S(1)} collective-permute-done((bf16[32,16,256]{2,1,0:T(8,128)(2,1)S(1)}, bf16[32,16,256]{2,1,0:T(8,128)(2,1)S(1)}, u32[]{:S(2)}, u32[]{:S(2)}) %collective-permute-start.8) | collective-permute-done | bytes 262176 | tf_op jit(solution)/shard_map/ppermute | solution.py:602
  53.3 3.4 %collective-permute-start.10 = (bf16[32,16,256]{2,1,0:T(8,128)(2,1)S(1)}, bf16[32,16,256]{2,1,0:T(8,128)(2,1)S(1)}, u32[]{:S(2)}, u32[]{:S(2)}) collective-permute-start(bf16[32,16,256]{2,1,0:T(8,128)(2,1)S(1)} %get-tuple-element.151), channel_id=1, source_target_pairs={{8,0},{16,8},{0,24},{24,16},{9,1},{17,9},{1,25},{25,17},{10,2},{18... | collective-permute-start | bytes 786440 | tf_op jit(solution)/shard_map/ppermute | solution.py:602
  57.2 4.8 %collective-permute-done.10.refs_0_ = bf16[32,16,256]{2,1,0:T(8,128)(2,1)S(1)} collective-permute-done((bf16[32,16,256]{2,1,0:T(8,128)(2,1)S(1)}, bf16[32,16,256]{2,1,0:T(8,128)(2,1)S(1)}, u32[]{:S(2)}, u32[]{:S(2)}) %collective-permute-start.10) | collective-permute-done | bytes 262176 | tf_op jit(solution)/shard_map/ppermute | solution.py:602
  62.0 1.0 %shard_map.100 = (f32[16,16,256]{2,1,0:T(8,128)S(1)}, f32[16,16,256]{2,1,0:T(8,128)S(1)}, f32[16,16,256]{2,1,0:T(8,128)S(1)}, f32[16,16,256]{2,1,0:T(8,128)S(1)}, bf16[32,16,256]{2,1,0:T(8,128)(2,1)S(1)}) custom-call(bf16[32,16,256]{2,1,0:T(8,128)(2,1)S(1)} %collective-permute-done.10.refs_0_, ...), custom_call_target="tpu_custom_call", output_to_operand_aliasing={{0}: (6, {}), {1}: (7, {}), {2}: (8, {}), {3}: (9, {})} | custom-call | flops 67108864 | bytes 4194304 | tf_op jit(solution)/shard_map/pallas_call | solution.py:562
  63.1 2.7 %collective-permute-start.11 = (bf16[32,16,256]{2,1,0:T(8,128)(2,1)S(1)}, bf16[32,16,256]{2,1,0:T(8,128)(2,1)S(1)}, u32[]{:S(2)}, u32[]{:S(2)}) collective-permute-start(bf16[32,16,256]{2,1,0:T(8,128)(2,1)S(1)} %get-tuple-element.156), channel_id=1, source_target_pairs={{8,0},{0,8},{16,24},{24,16},{9,1},{1,9},{17,25},{25,17},{10,2},{2,... | collective-permute-start | bytes 786440 | tf_op jit(solution)/shard_map/ppermute | solution.py:602
  65.8 0.8 %shard_map.101.refs_0_ = f32[16,64,256]{2,1,0:T(8,128)} custom-call(f32[16,16,256]{2,1,0:T(8,128)S(1)} %get-tuple-element.160.here, f32[16,16,256]{2,1,0:T(8,128)S(1)} %get-tuple-element.162.far, f32[16,16,256]{2,1,0:T(8,128)S(1)} %collective-permute-done.13.other), custom_call_target="tpu_custom_call" | custom-call | flops 2097152 | bytes 131072 | tf_op jit(solution)/shard_map/pallas_call | solution.py:562
  66.6 0.8 %shard_map.102 = f32[16,64,256]{2,1,0:T(8,128)} custom-call(f32[16,16,256]{2,1,0:T(8,128)S(1)} %get-tuple-element.157.here, f32[16,16,256]{2,1,0:T(8,128)S(1)} %get-tuple-element.159.far, f32[16,16,256]{2,1,0:T(8,128)S(1)} %collective-permute-done.12.other, f32[16,64,256]{2,1,0:T(8,128)} %shard_map.101.refs_0_), custom_call_target="tpu_custom_call", output_to_operand_aliasing={{}: (3, {})} | custom-call | flops 2097152 | bytes 131072 | tf_op jit(solution)/shard_map/pallas_call | solution.py:562
  67.5 0.8 %shard_map.103.refs_0_ = f32[16,64,256]{2,1,0:T(8,128)} custom-call(f32[16,16,256]{2,1,0:T(8,128)S(1)} %get-tuple-element.163.here, f32[16,16,256]{2,1,0:T(8,128)S(1)} %get-tuple-element.164.far, f32[16,16,256]{2,1,0:T(8,128)S(1)} %collective-permute-done.14.other), custom_call_target="tpu_custom_call" | custom-call | flops 2097152 | bytes 131072 | tf_op jit(solution)/shard_map/pallas_call | solution.py:562
  68.3 4.4 %collective-permute-done.11.refs_0_ = bf16[32,16,256]{2,1,0:T(8,128)(2,1)S(1)} collective-permute-done((bf16[32,16,256]{2,1,0:T(8,128)(2,1)S(1)}, bf16[32,16,256]{2,1,0:T(8,128)(2,1)S(1)}, u32[]{:S(2)}, u32[]{:S(2)}) %collective-permute-start.11) | collective-permute-done | bytes 262176 | tf_op jit(solution)/shard_map/ppermute | solution.py:602
  73.4 1.5 %collective-permute-done.15.other = f32[16,16,256]{2,1,0:T(8,128)S(1)} collective-permute-done((f32[16,16,256]{2,1,0:T(8,128)S(1)}, f32[16,16,256]{2,1,0:T(8,128)S(1)}, u32[]{:S(2)}, u32[]{:S(2)}) %collective-permute-start.15) | collective-permute-done | bytes 262176 | tf_op jit(solution)/shard_map/ppermute | solution.py:577
  74.9 0.8 %shard_map.105 = f32[16,64,256]{2,1,0:T(8,128)} custom-call(f32[16,16,256]{2,1,0:T(8,128)S(1)} %get-tuple-element.168.here, f32[16,16,256]{2,1,0:T(8,128)S(1)} %get-tuple-element.169.far, f32[16,16,256]{2,1,0:T(8,128)S(1)} %collective-permute-done.15.other, f32[16,64,256]{2,1,0:T(8,128)} %shard_map.103.refs_0_), custom_call_target="tpu_custom_call", output_to_operand_aliasing={{}: (3, {})} | custom-call | flops 2097152 | bytes 131072 | tf_op jit(solution)/shard_map/pallas_call | solution.py:562
  (28 shorter events, 3.5 us)
Async XLA Ops:
  4.6 2.1 %collective-permute-start = (bf16[64,16,256]{2,1,0:T(8,128)(2,1)S(1)}, bf16[64,16,256]{2,1,0:T(8,128)(2,1)S(1)}, u32[]{:S(2)}, u32[]{:S(2)}) collective-permute-start(bf16[64,16,256]{2,1,0:T(8,128)(2,1)S(1)} %get-tuple-element.90), channel_id=1, source_target_pairs={{0,4},{4,0},{1,5},{5,1},{2,6},{6,2},{3,7},{7,3},{8,12},{12,8},{9,1... | collective-permute-start | bytes 1572872 | tf_op jit(solution)/shard_map/ppermute | solution.py:577
  6.7 9.2 %collective-permute-start.3 = (bf16[16,256,256]{2,1,0:T(8,128)(2,1)S(1)}, bf16[16,256,256]{2,1,0:T(8,128)(2,1)S(1)}, u32[]{:S(2)}, u32[]{:S(2)}) collective-permute-start(bf16[16,256,256]{2,1,0:T(8,128)(2,1)S(1)} %get-tuple-element.98.refs_3_.refs_7_.step_own), channel_id=1, source_target_pairs={{0,4},{4,0},{1,5},{5,1},{2,6},{6,2},{3,7},{7,3},{8,12},{12,8},{9,1... | collective-permute-start | bytes 6291464 | tf_op jit(solution)/shard_map/ppermute | solution.py:577
  7.1 8.7 %collective-permute-start.1 = (f32[16,32,256]{2,1,0:T(8,128)S(1)}, f32[16,32,256]{2,1,0:T(8,128)S(1)}, u32[]{:S(2)}, u32[]{:S(2)}) collective-permute-start(f32[16,32,256]{2,1,0:T(8,128)S(1)} %get-tuple-element.91), channel_id=1, source_target_pairs={{0,4},{4,0},{1,5},{5,1},{2,6},{6,2},{3,7},{7,3},{8,12},{12,8},{9,1... | collective-permute-start | bytes 1572872 | tf_op jit(solution)/shard_map/ppermute | solution.py:577
  7.3 8.6 %collective-permute-start.2 = (bf16[32,16,256]{2,1,0:T(8,128)(2,1)S(1)}, bf16[32,16,256]{2,1,0:T(8,128)(2,1)S(1)}, u32[]{:S(2)}, u32[]{:S(2)}) collective-permute-start(bf16[32,16,256]{2,1,0:T(8,128)(2,1)S(1)} %shard_map.87), channel_id=1, source_target_pairs={{0,8},{8,0},{16,24},{24,16},{1,9},{9,1},{17,25},{25,17},{2,10},{10... | collective-permute-start | bytes 786440 | tf_op jit(solution)/shard_map/ppermute | solution.py:602
  16.0 15.7 %collective-permute-start.6 = (bf16[34,256,256]{2,1,0:T(8,128)(2,1)S(1)}, bf16[34,256,256]{2,1,0:T(8,128)(2,1)S(1)}, u32[]{:S(2)}, u32[]{:S(2)}) collective-permute-start(bf16[34,256,256]{2,1,0:T(8,128)(2,1)S(1)} %shard_map.88.own.refs_3_.refs_1_.refs_5_), channel_id=1, source_target_pairs={{0,4},{4,0},{1,5},{5,1},{2,6},{6,2},{3,7},{7,3},{8,12},{12,8},{9,1... | collective-permute-start | bytes 13369352 | tf_op jit(solution)/shard_map/ppermute | solution.py:577
  16.0 9.6 %collective-permute-start.4 = (bf16[32,16,256]{2,1,0:T(8,128)(2,1)S(1)}, bf16[32,16,256]{2,1,0:T(8,128)(2,1)S(1)}, u32[]{:S(2)}, u32[]{:S(2)}) collective-permute-start(bf16[32,16,256]{2,1,0:T(8,128)(2,1)S(1)} %get-tuple-element.102), channel_id=1, source_target_pairs={{8,16},{0,8},{16,24},{24,0},{9,17},{1,9},{17,25},{25,1},{10,18},{2... | collective-permute-start | bytes 786440 | tf_op jit(solution)/shard_map/ppermute | solution.py:602
  25.8 8.8 %collective-permute-start.5 = (bf16[32,16,256]{2,1,0:T(8,128)(2,1)S(1)}, bf16[32,16,256]{2,1,0:T(8,128)(2,1)S(1)}, u32[]{:S(2)}, u32[]{:S(2)}) collective-permute-start(bf16[32,16,256]{2,1,0:T(8,128)(2,1)S(1)} %get-tuple-element.108), channel_id=1, source_target_pairs={{16,24},{8,16},{0,8},{24,0},{17,25},{9,17},{1,9},{25,1},{18,26},{1... | collective-permute-start | bytes 786440 | tf_op jit(solution)/shard_map/ppermute | solution.py:602
  34.8 12.9 %collective-permute-start.9 = (bf16[34,256,256]{2,1,0:T(8,128)(2,1)S(1)}, bf16[34,256,256]{2,1,0:T(8,128)(2,1)S(1)}, u32[]{:S(2)}, u32[]{:S(2)}) collective-permute-start(bf16[34,256,256]{2,1,0:T(8,128)(2,1)S(1)} %shard_map.92.own.refs_1_), channel_id=1, source_target_pairs={{0,4},{4,0},{1,5},{5,1},{2,6},{6,2},{3,7},{7,3},{8,12},{12,8},{9,1... | collective-permute-start | bytes 13369352 | tf_op jit(solution)/shard_map/ppermute | solution.py:577
  34.8 8.7 %collective-permute-start.7 = (bf16[32,16,256]{2,1,0:T(8,128)(2,1)S(1)}, bf16[32,16,256]{2,1,0:T(8,128)(2,1)S(1)}, u32[]{:S(2)}, u32[]{:S(2)}) collective-permute-start(bf16[32,16,256]{2,1,0:T(8,128)(2,1)S(1)} %get-tuple-element.123), channel_id=1, source_target_pairs={{24,16},{16,24},{0,8},{8,0},{25,17},{17,25},{1,9},{9,1},{26,18},{1... | collective-permute-start | bytes 786440 | tf_op jit(solution)/shard_map/ppermute | solution.py:602
  43.7 9.5 %collective-permute-start.8 = (bf16[32,16,256]{2,1,0:T(8,128)(2,1)S(1)}, bf16[32,16,256]{2,1,0:T(8,128)(2,1)S(1)}, u32[]{:S(2)}, u32[]{:S(2)}) collective-permute-start(bf16[32,16,256]{2,1,0:T(8,128)(2,1)S(1)} %get-tuple-element.132), channel_id=1, source_target_pairs={{16,8},{24,16},{0,24},{8,0},{17,9},{25,17},{1,25},{9,1},{18,10},{2... | collective-permute-start | bytes 786440 | tf_op jit(solution)/shard_map/ppermute | solution.py:602
  53.3 8.8 %collective-permute-start.10 = (bf16[32,16,256]{2,1,0:T(8,128)(2,1)S(1)}, bf16[32,16,256]{2,1,0:T(8,128)(2,1)S(1)}, u32[]{:S(2)}, u32[]{:S(2)}) collective-permute-start(bf16[32,16,256]{2,1,0:T(8,128)(2,1)S(1)} %get-tuple-element.151), channel_id=1, source_target_pairs={{8,0},{16,8},{0,24},{24,16},{9,1},{17,9},{1,25},{25,17},{10,2},{18... | collective-permute-start | bytes 786440 | tf_op jit(solution)/shard_map/ppermute | solution.py:602
  56.7 9.9 %collective-permute-start.12 = (f32[16,16,256]{2,1,0:T(8,128)S(1)}, f32[16,16,256]{2,1,0:T(8,128)S(1)}, u32[]{:S(2)}, u32[]{:S(2)}) collective-permute-start(f32[16,16,256]{2,1,0:T(8,128)S(1)} %get-tuple-element.159.far), channel_id=1, source_target_pairs={{0,4},{4,0},{1,5},{5,1},{2,6},{6,2},{3,7},{7,3},{8,12},{12,8},{9,1... | collective-permute-start | bytes 786440 | tf_op jit(solution)/shard_map/ppermute | solution.py:577
  56.7 9.1 %collective-permute-start.13 = (f32[16,16,256]{2,1,0:T(8,128)S(1)}, f32[16,16,256]{2,1,0:T(8,128)S(1)}, u32[]{:S(2)}, u32[]{:S(2)}) collective-permute-start(f32[16,16,256]{2,1,0:T(8,128)S(1)} %get-tuple-element.162.far), channel_id=1, source_target_pairs={{0,4},{4,0},{1,5},{5,1},{2,6},{6,2},{3,7},{7,3},{8,12},{12,8},{9,1... | collective-permute-start | bytes 786440 | tf_op jit(solution)/shard_map/ppermute | solution.py:577
  63.0 4.4 %collective-permute-start.14 = (f32[16,16,256]{2,1,0:T(8,128)S(1)}, f32[16,16,256]{2,1,0:T(8,128)S(1)}, u32[]{:S(2)}, u32[]{:S(2)}) collective-permute-start(f32[16,16,256]{2,1,0:T(8,128)S(1)} %get-tuple-element.164.far), channel_id=1, source_target_pairs={{0,4},{4,0},{1,5},{5,1},{2,6},{6,2},{3,7},{7,3},{8,12},{12,8},{9,1... | collective-permute-start | bytes 786440 | tf_op jit(solution)/shard_map/ppermute | solution.py:577
  63.1 9.6 %collective-permute-start.11 = (bf16[32,16,256]{2,1,0:T(8,128)(2,1)S(1)}, bf16[32,16,256]{2,1,0:T(8,128)(2,1)S(1)}, u32[]{:S(2)}, u32[]{:S(2)}) collective-permute-start(bf16[32,16,256]{2,1,0:T(8,128)(2,1)S(1)} %get-tuple-element.156), channel_id=1, source_target_pairs={{8,0},{0,8},{16,24},{24,16},{9,1},{1,9},{17,25},{25,17},{10,2},{2,... | collective-permute-start | bytes 786440 | tf_op jit(solution)/shard_map/ppermute | solution.py:602
  73.4 1.6 %collective-permute-start.15 = (f32[16,16,256]{2,1,0:T(8,128)S(1)}, f32[16,16,256]{2,1,0:T(8,128)S(1)}, u32[]{:S(2)}, u32[]{:S(2)}) collective-permute-start(f32[16,16,256]{2,1,0:T(8,128)S(1)} %get-tuple-element.169.far), channel_id=1, source_target_pairs={{0,4},{4,0},{1,5},{5,1},{2,6},{6,2},{3,7},{7,3},{8,12},{12,8},{9,1... | collective-permute-start | bytes 786440 | tf_op jit(solution)/shard_map/ppermute | solution.py:577

commit v4 on v3

--- a/solution.py
+++ b/solution.py
@@ -192,8 +192,9 @@
     return jnp.concatenate(sol, axis=1)[None], jnp.concatenate(upd, axis=1)[None]
 
 
-NODE_ROWS = 16
+NODE_ROWS = 8
 LOAD_NODES = 4
+COSTS = [10**9,3*10**10,3*10**10]+[5*10**9]*5
 SMALL_VMEM_BYTES = 12 * 2**20
 IN_ANY = pl.BlockSpec(memory_space=pl.ANY)
 IN_HBM = pl.BlockSpec(memory_space=pltpu.HBM)
@@ -213,9 +214,7 @@
 
 
 def pick(select, values):
-    high = values.astype(BF16)
-    low = (values - high.astype(F32)).astype(BF16)
-    return dot(select, high) + dot(select, low)
+    return dot(select, values.astype(BF16))
 
 
 def on_level(section):
@@ -300,7 +299,7 @@
         chosen = select[:, :size]
         for c in range(chunks):
             home[2 * count * c : 2 * count * (c + 1)] = pick(chosen, flat(updates[c][...])).reshape(2 * count, *home.shape[1:])
-            sums = pick(chosen, flat(updates[chunks + c][...])).astype(BF16).reshape(2 * count, *home.shape[1:])
+            sums = pick(chosen, flat(updates[chunks + c][...])).reshape(2 * count, *home.shape[1:]).astype(BF16)
             swap[2 * count * c : 2 * count * c + count] = sums[count:]
             swap[2 * count * c + count : 2 * count * (c + 1)] = sums[:count]
 
@@ -313,30 +312,27 @@
             merged[node] = dot(inv_here[node], off_here[node]).astype(BF16)
 
 
-def merge_kernel(levels, low_inv, up_inv, up_off, ancestor, packed, *scratch):
+def merge_kernel(low_inv, up_inv, up_off, ancestor, packed, *scratch):
     low_here, up_here, off_here, rows, sems = scratch
     count = low_inv.shape[0]
-    level, sub = lax.axis_index(LEVEL), lax.axis_index(SUB)
-
-    @pl.when((level == levels[0]) | (level == levels[1]))
-    def _():
-        loads = []
-        for group in range(count // LOAD_NODES):
-            here = pl.ds(group * LOAD_NODES, LOAD_NODES)
-            loads.append(pltpu.make_async_copy(up_inv.at[here], up_here.at[here], sems.at[1, group]))
-            loads.append(pltpu.make_async_copy(low_inv.at[here], low_here.at[here], sems.at[0, group]))
-            loads.append(pltpu.make_async_copy(up_off.at[here], off_here.at[here], sems.at[2, group]))
-        loads.append(pltpu.make_async_copy(ancestor.at[:, half_rows(ancestor, 1 - sub), :], rows, sems.at[3, 0]))
-        for load in loads:
-            load.start()
-        for node in range(count):
-            if node % LOAD_NODES == 0:
-                for load in loads[3 * (node // LOAD_NODES) : 3 * (node // LOAD_NODES) + 3]:
-                    load.wait()
-            packed[node] = dot(low_here[node], up_here[node]).astype(BF16)
-            packed[count + node] = dot(off_here[node], up_here[node]).astype(BF16)
-        loads[-1].wait()
-        packed[2 * count :] = rows[...].reshape(packed.shape[0] - 2 * count, *packed.shape[1:])
+    sub = lax.axis_index(SUB)
+    loads = []
+    for group in range(count // LOAD_NODES):
+        here = pl.ds(group * LOAD_NODES, LOAD_NODES)
+        loads.append(pltpu.make_async_copy(up_inv.at[here], up_here.at[here], sems.at[1, group]))
+        loads.append(pltpu.make_async_copy(low_inv.at[here], low_here.at[here], sems.at[0, group]))
+        loads.append(pltpu.make_async_copy(up_off.at[here], off_here.at[here], sems.at[2, group]))
+    loads.append(pltpu.make_async_copy(ancestor.at[:, half_rows(ancestor, 1 - sub), :], rows, sems.at[3, 0]))
+    for load in loads:
+        load.start()
+    for node in range(count):
+        if node % LOAD_NODES == 0:
+            for load in loads[3 * (node // LOAD_NODES) : 3 * (node // LOAD_NODES) + 3]:
+                load.wait()
+        packed[node] = dot(low_here[node], up_here[node]).astype(BF16)
+        packed[count + node] = dot(off_here[node], up_here[node]).astype(BF16)
+    loads[-1].wait()
+    packed[2 * count :] = rows[...].reshape(packed.shape[0] - 2 * count, *packed.shape[1:])
 
 
 def residue_of(c, rhs_own, rhs_far, incoming, node):
@@ -351,19 +347,19 @@
     own, far = at["own", c], at["far", c]
     for node in range(2 * count):
         value = residue_of(c, at["rhs_own"], at["rhs_far"], at["received"], node)
-        at["residue", c][node] = value
+        at["residue", c][node] = value.astype(F32)
         if node < count:
             own[node] = dot(value, at["up_own"][node])
         else:
             far[node - count] = dot(value, at["up_far"][node - count])
     updates = jnp.concatenate([flat(own[...]), flat(far[...])], axis=0)
-    at["sent"][...] = pick(at["select"][...], updates).astype(BF16).reshape(at["sent"].shape)
+    at["sent"][...] = pick(at["select"][...], updates).reshape(at["sent"].shape).astype(BF16)
 
 
 def send_solved(c, at):
     if "sent" in at:
         solved = jnp.concatenate([flat(at["sol_own", c][...]), flat(at["sol_far", c][...])], axis=0).astype(BF16)
-        at["sent"][...] = dot(at["choose"][...], solved).astype(BF16).reshape(at["sent"].shape)
+        at["sent"][...] = dot(at["choose"][...], solved).reshape(at["sent"].shape).astype(BF16)
 
 
 def top_role(c, at):
@@ -371,26 +367,21 @@
     base = at["top_base", c]
     for node in range(2 * count):
         value = residue_of(c, at["rhs_own"], at["rhs_far"], at["received"], node)
-        at["residue", c][node] = value
+        at["residue", c][node] = value.astype(F32)
         if node < count:
-            at["sol_own", c][node] = dot(value, at["high_own"][node]) - base[node]
+            at["sol_own", c][node] = dot(value, at["down_own"][node]) - base[node]
         else:
-            at["sol_far", c][node - count] = dot(value, at["high_far"][node - count]) - base[node]
+            at["sol_far", c][node - count] = dot(value, at["down_far"][node - count]) - base[node]
     send_solved(c, at)
 
 
-def back_role(c, at, group="high"):
+def back_role(c, at):
     count = at["sol_own", c].shape[0]
-    base, above = at[group + "_base", c], at["received"]
-    own, far = at[group + "_own"], at[group + "_far"]
+    base, above = at["low_base", c], at["received"]
     for node in range(count):
-        at["sol_own", c][node] = base[node] - dot(above[node], own[count + node])
-        at["sol_far", c][node] = base[count + node] - dot(above[count + node], far[count + node])
+        at["sol_own", c][node] = base[node] - dot(above[node], at["down_own"][count + node])
+        at["sol_far", c][node] = base[count + node] - dot(above[count + node], at["down_far"][count + node])
     send_solved(c, at)
-
-
-def low_back_role(c, at):
-    back_role(c, at, "low")
 
 
 def sum_role(c, at):
@@ -398,19 +389,17 @@
     at["sent"][...] = (at["home"][rows] + at["swapped"][rows].astype(F32)).astype(BF16)
 
 
-ROLES = {"tier": tier_role, "top": top_role, "back": back_role, "low": low_back_role, "sum": sum_role}
+ROLES = {"tier": tier_role, "top": top_role, "back": back_role, "sum": sum_role}
 READS = {
     "tier": ("rhs_own", "rhs_far", "received", "up_own", "up_far", "select"),
-    "top": ("rhs_own", "rhs_far", "received", "high_own", "high_far", "choose", "top_base"),
-    "back": ("received", "high_own", "high_far", "choose", "high_base"),
-    "low": ("received", "low_own", "low_far", "choose", "low_base"),
+    "top": ("rhs_own", "rhs_far", "received", "down_own", "down_far", "choose", "top_base"),
+    "back": ("received", "down_own", "down_far", "choose", "low_base"),
     "sum": ("home", "swapped"),
 }
 WRITES = {
     "tier": ("residue", "own", "far"),
     "top": ("residue", "sol_own", "sol_far"),
     "back": ("sol_own", "sol_far"),
-    "low": ("sol_own", "sol_far"),
     "sum": (),
 }
 
@@ -425,7 +414,7 @@
         pl.when(lax.axis_index(LEVEL) == level)(functools.partial(ROLES[role], c, {**reads, **outs}))
 
 
-def step(plan, state, sends=True):
+def step(plan, state, sends=True, flops=10**9):
     nodes = state["nodes"]
     in_keys, out_keys = [], []
     for _, role, c in plan:
@@ -438,52 +427,64 @@
     width = state["rhs_own"].shape[2]
     outs = []
     for name, _ in out_keys:
-        of, dtype = (nodes, BF16) if name == "residue" else (nodes // 2, F32)
-        outs.append(jax.ShapeDtypeStruct((of, NODE_ROWS, width), dtype))
+        of = nodes if name == "residue" else nodes // 2
+        outs.append(jax.ShapeDtypeStruct((of, NODE_ROWS, width), F32))
     aliases = {len(in_keys) + i: out_keys.index(key) for i, key in enumerate(kept_keys)}
     all_outs = out_keys + (["sent"] if sends else [])
     if sends:
         outs.append(jax.ShapeDtypeStruct((nodes, NODE_ROWS, width), BF16))
     operands = [state[key] for key in in_keys + kept_keys]
-    results = run(functools.partial(step_kernel, plan, in_keys, all_outs, kept_keys), operands, outs, aliases)
+    results = run(functools.partial(step_kernel, plan, in_keys, all_outs, kept_keys), operands, outs, aliases, flops)
     state.update(zip(out_keys, results))
     return results[-1] if sends else None
 
 
-def high_base_kernel(section, own, far, *refs):
-    chunks = len(refs) // 2
-    residue, base = refs[:chunks], refs[chunks:]
-    count = residue[0].shape[0] // 2
-
-    @on_level(section)
+def rows_together(chunks, node):
+    return jnp.concatenate([chunk[node] for chunk in chunks], axis=0).astype(BF16)
+
+
+def apart(value, chunks, node):
+    for c, chunk in enumerate(chunks):
+        chunk[node] = value[NODE_ROWS * c : NODE_ROWS * (c + 1)]
+
+
+def base_kernel(rhs_own, rhs_far, own, far, *refs):
+    residue, base = refs[: len(refs) // 2], refs[len(refs) // 2 :]
+    count = rhs_own.shape[0]
+    level, top = lax.axis_index(LEVEL), lax.axis_size(LEVEL) - 1
+
+    @pl.when(level == 0)
+    def _():
+        for node in range(count):
+            apart(dot(rhs_own[node].astype(BF16), own[node]), base, node)
+            apart(dot(rhs_far[node].astype(BF16), far[node]), base, count + node)
+
+    @pl.when((level != 0) & (level != top))
+    def _():
+        for node in range(count):
+            apart(dot(rows_together(residue, node), own[node]), base, node)
+            apart(dot(rows_together(residue, count + node), far[node]), base, count + node)
+
+
+def update_kernel(up_own, up_far, *refs):
+    chunks = (len(refs) - 2) // 3
+    residue, own_kept, far_kept = (refs[chunks * i : chunks * (i + 1)] for i in range(3))
+    upd_own, upd_far = refs[-2:]
+    level, top = lax.axis_index(LEVEL), lax.axis_size(LEVEL) - 1
+
+    @pl.when(level == top)
+    def _():
+        count = up_own.shape[0]
+        for node in range(count):
+            upd_own[node] = dot(rows_together(residue, node), up_own[node])
+            upd_far[node] = dot(rows_together(residue, count + node), up_far[node])
+
+    @pl.when(level != top)
     def _():
         for c in range(chunks):
-            for node in range(count):
-                base[c][node] = dot(residue[c][node], own[node])
-                base[c][count + node] = dot(residue[c][count + node], far[node])
-
-
-def low_base_kernel(rhs_own, rhs_far, own, far, *refs):
-    chunks = len(refs) // 2
-    residue, base = refs[:chunks], refs[chunks:]
-    count = rhs_own.shape[0]
-    level = lax.axis_index(LEVEL)
-
-    @pl.when(level == 0)
-    def _():
-        for node in range(count):
-            mine = dot(rhs_own[node].astype(BF16), own[node])
-            other = dot(rhs_far[node].astype(BF16), far[node])
-            for c in range(chunks):
-                base[c][node] = mine[NODE_ROWS * c : NODE_ROWS * (c + 1)]
-                base[c][count + node] = other[NODE_ROWS * c : NODE_ROWS * (c + 1)]
-
-    @pl.when((level != 0) & (level < lax.axis_size(LEVEL) - 2))
-    def _():
-        for c in range(chunks):
-            for node in range(count):
-                base[c][node] = dot(residue[c][node], own[node])
-                base[c][count + node] = dot(residue[c][count + node], far[node])
+            rows = slice(NODE_ROWS * c, NODE_ROWS * (c + 1))
+            upd_own[:, rows, :] = own_kept[c][...]
+            upd_far[:, rows, :] = far_kept[c][...]
 
 
 def ancestor_kernel(section, ancestor, own, far, *refs):
@@ -506,46 +507,38 @@
                 base[count + node] = other[NODE_ROWS * c : NODE_ROWS * (c + 1)]
 
 
-def top_tier_update_kernel(section, residue, step_own, step_far, kept_o, kept_f, upd_own, upd_far):
-    count = step_own.shape[0]
-    keep(section, (kept_o, kept_f), (upd_own, upd_far))
-
-    @on_level(section)
-    def _():
-        for node in range(count):
-            upd_own[node] = dot(residue[node], step_own[node])
-            upd_far[node] = dot(residue[count + node], step_far[node])
-
-
-def put(c, own, far, out, sems):
+def put(here, other, first, out, sems):
     sub = lax.axis_index(SUB)
     half = out.shape[1] // 2
-    first = pltpu.make_async_copy(own, out.at[:, rows_of(half * sub + NODE_ROWS * c), :], sems.at[0])
-    second = pltpu.make_async_copy(far, out.at[:, rows_of(half * (1 - sub) + NODE_ROWS * c), :], sems.at[1])
-    first.start()
-    second.start()
-    first.wait()
-    second.wait()
-
-
-def place_kernel(c, here, far, other, *refs):
-    out, sems = refs[-2:]
-    put(c, here, other, out, sems)
-
-
-def place_bottom_kernel(c, here, far, other, *refs):
-    out, sems = refs[-2:]
-
+    copies = []
+    for i, (mine, theirs, row) in enumerate(zip(here, other, first)):
+        size = mine.shape[1]
+        to_mine = pl.ds(pl.multiple_of(half * sub + row, NODE_ROWS), size)
+        to_theirs = pl.ds(pl.multiple_of(half * (1 - sub) + row, NODE_ROWS), size)
+        copies.append(pltpu.make_async_copy(mine, out.at[:, to_mine, :], sems.at[0, i]))
+        copies.append(pltpu.make_async_copy(theirs, out.at[:, to_theirs, :], sems.at[1, i]))
+    for copy in copies:
+        copy.start()
+    for copy in copies:
+        copy.wait()
+
+
+def place_kernel(first, *refs):
+    count = len(first)
+    put(refs[:count], refs[count : 2 * count], first, *refs[-2:])
+
+
+def place_bottom_kernel(here, far, other, *refs):
     @on_level(0)
     def _():
-        put(c, here, far, out, sems)
+        put([here], [far], [0], *refs[-2:])
 
     @off_level(0)
     def _():
-        put(c, here, other, out, sems)
-
-
-def run(kernel, operands, outs, aliases=None, products=32, whole=None, scratch=(), raw=()):
+        put([here], [other], [0], *refs[-2:])
+
+
+def run(kernel, operands, outs, aliases=None, flops=10**9, whole=None, scratch=(), raw=()):
     in_specs = [IN_HBM] * len(raw) + [IN_VMEM] * len(operands)
     operands = [*(pltpu.with_memory_space_constraint(value, pltpu.HBM) for value in raw), *(pltpu.with_memory_space_constraint(value, pltpu.VMEM) for value in operands)]
     out_specs = [IN_VMEM] * len(outs)
@@ -568,7 +561,7 @@
         scratch_shapes=scratch,
         compiler_params=pltpu.CompilerParams(vmem_limit_bytes=SMALL_VMEM_BYTES),
         cost_estimate=pl.CostEstimate(
-            flops=products * 2 * NODE_ROWS * 256 * 256, bytes_accessed=256 * 256 * 2 * products, transcendentals=0
+            flops=flops, bytes_accessed=10**6, transcendentals=0
         ),
     )(*operands)
 
@@ -623,109 +616,89 @@
     packed_shape = (2 * count + count * half // width, width, width)
     merge_scratch = [block, block, block, pltpu.VMEM((count, half, width), BF16), pltpu.SemaphoreType.DMA((4, count // LOAD_NODES))]
 
-    def merged(levels_here, sent):
+    def merged(sent):
         low, *others = lax.optimization_barrier((lower_inv, upper_inv, upper_off, ancestor, sent))
         return run(
-            functools.partial(merge_kernel, levels_here), (), [jax.ShapeDtypeStruct(packed_shape, BF16)],
-            raw=(low, *others[:3]), scratch=merge_scratch, products=512,
+            merge_kernel, (), [jax.ShapeDtypeStruct(packed_shape, BF16)],
+            raw=(low, *others[:3]), scratch=merge_scratch,
         )[0]
 
     whole = jax.ShapeDtypeStruct(rhs.shape, F32)
-    sems = [pltpu.SemaphoreType.DMA((2,))]
-    update, solved = None, None
-    for k in range(2 * top + chunks):
-        plan, pairs = [], []
-        for c in range(chunks):
-            tier = k - c
-            if 0 <= tier < top:
-                plan.append((tier, "sum" if tier == 0 else "tier", c))
-                pairs.append((tier, tier + 1))
-            elif tier == top:
-                plan.append((top, "top", c))
-                pairs.append((top, top - 1))
-            elif top < tier <= 2 * top:
-                low = 2 * top - tier
-                plan.append((low, "back" if low == top - 1 else "low", c))
-                if low:
-                    pairs.append((low, low - 1))
-        sent = step(plan, state, sends=bool(pairs))
-        if not pairs:
-            break
-        received = passed(sent, pairs)
-        done = []
+
+    def sems(pieces):
+        return [pltpu.SemaphoreType.DMA((2, pieces))]
+
+    pipes = [list(range(chunks))[i : i + 2] for i in range(0, chunks, 2)]
+    received = [None] * len(pipes)
+    pace = []
+    last = 2 * top + 1
+    for k in range(last + 1):
+        for p, pipe in enumerate(pipes):
+            plan, pairs = [], []
+            for j, c in enumerate(pipe):
+                tier = k - j
+                if 0 <= tier < top:
+                    plan.append((tier, "sum" if tier == 0 else "tier", c))
+                    pairs.append((tier, tier + 1))
+                elif tier == top:
+                    plan.append((top, "top", c))
+                    pairs.append((top, top - 1))
+                elif top < tier <= 2 * top:
+                    low = 2 * top - tier
+                    plan.append((low, "back", c))
+                    if low:
+                        pairs.append((low, low - 1))
+            if received[p] is not None:
+                state["received"] = after(received[p], *pace)
+            sent = step(plan, state, bool(pairs), COSTS[k])
+            pace = [sent] if pairs else [state["sol_own", pipe[1]]]
+            if pairs:
+                received[p] = passed(sent, pairs)
+            if p == 0 and k == 0:
+                state["up_far"] = exchanged(after(up_own, sent))
+                state["rhs_far"] = exchanged(after(rhs_sent, sent))
+            if p == 0 and k == 1:
+                state["down_far"] = exchanged(state["down_own"])
+            if p == 0 and k == last:
+                (update,) = run(
+                    place_bottom_kernel, (upd_own, after(upd_far, *pace), upd_other), [], whole=(whole, None), scratch=sems(1)
+                )
+                pace = [update]
         if k == 0:
-            state["up_far"] = exchanged(after(up_own, sent))
-            state["rhs_far"] = exchanged(after(rhs_sent, sent))
-            state["high_own"] = merged((top - 1, top), sent)
-            done = [state["high_own"]]
-        if k == 1:
-            state["high_far"] = exchanged(after(state["high_own"], sent))
+            state["down_own"] = merged(sent)
+            pace.append(state["down_own"])
         if k == top - 1:
             bases = run(
                 functools.partial(ancestor_kernel, top),
-                (state["high_own"], state["high_far"]),
+                (state["down_own"], state["down_far"]),
                 [shape(nodes, F32)] * chunks,
                 raw=(after(ancestor, sent),),
                 scratch=[pltpu.VMEM((count, half, width), BF16), pltpu.SemaphoreType.DMA((1,))],
             )
             state.update({("top_base", c): bases[c] for c in range(chunks)})
-            state["low_own"] = merged((0, 1), sent)
-            done = [*bases, state["low_own"]]
+            pace += bases
+        residues = [state["residue", c] for c in range(chunks)] if k >= top else []
         if k == top:
-            state["low_far"] = exchanged(after(state["low_own"], sent))
-            residues = [state["residue", c] for c in range(chunks)]
             bases = run(
-                functools.partial(high_base_kernel, top - 1),
-                (after(state["high_own"], sent), state["high_far"], *residues),
-                [shape(nodes, F32)] * chunks,
-            )
-            state.update({("high_base", c): bases[c] for c in range(chunks)})
-            done = bases
-        if k == top + 1:
-            residues = [state["residue", c] for c in range(chunks)]
-            bases = run(
-                low_base_kernel,
-                (after(rhs_own, sent), state["rhs_far"], state["low_own"], state["low_far"], *residues),
+                base_kernel,
+                (after(rhs_own, sent), state["rhs_far"], state["down_own"], state["down_far"], *residues),
                 [shape(nodes, F32)] * chunks,
             )
             state.update({("low_base", c): bases[c] for c in range(chunks)})
-            done = bases
-        if k == top + chunks - 1:
-            for c in range(chunks):
-                state["own", c], state["far", c] = run(
-                    functools.partial(top_tier_update_kernel, top),
-                    (after(state["residue", c], sent), state["up_own"], state["up_far"], state["own", c], state["far", c]),
-                    [shape(count, F32), shape(count, F32)],
-                    {3: 0, 4: 1},
-                )
-            done = [*done, *(state["far", c] for c in range(chunks))]
-        if k == top + chunks:
-            upd_other = [exchanged(after(state["far", c], sent)) for c in range(chunks)]
-        if k == 2 * top + chunks - 2:
-            for c in range(chunks):
-                (update,) = run(
-                    functools.partial(place_bottom_kernel, c),
-                    (state["own", c], after(state["far", c], sent), upd_other[c]),
-                    [], whole=(whole, update), scratch=sems, products=1,
-                )
-            for c in range(chunks - 1):
-                (solved,) = run(
-                    functools.partial(place_kernel, c),
-                    (state["sol_own", c], state["sol_far", c], exchanged(state["sol_far", c])),
-                    [], whole=(whole, solved), scratch=sems, products=1,
-                )
-            done = [update] + ([] if solved is None else [solved])
-        if done:
-            received, *done = lax.optimization_barrier((received, *done))
-            if k == 2 * top + chunks - 2:
-                update, solved = done[0], done[1] if chunks > 1 else None
-        state["received"] = received
-    c = chunks - 1
-    (solved,) = run(
-        functools.partial(place_kernel, c),
-        (state["sol_own", c], state["sol_far", c], exchanged(state["sol_far", c])),
-        [], whole=(whole, solved), scratch=sems, products=1,
-    )
+            pace += bases
+        if k == top + 2:
+            upd_own, upd_far = run(
+                update_kernel,
+                (up_own, state["up_far"], *residues, *(state["own", c] for c in range(chunks)), *(state["far", c] for c in range(chunks))),
+                [half_shape] * 2,
+            )
+            upd_other = exchanged(upd_far)
+        if k == last:
+            (solved,) = run(
+                functools.partial(place_kernel, [NODE_ROWS * c for c in range(chunks)]),
+                [state["sol_own", c] for c in range(chunks)] + [exchanged(state["sol_far", c]) for c in range(chunks)],
+                [], whole=(whole, None), scratch=sems(chunks),
+            )
     return solved[None], update[None]
 
 

time: 76 us -> 62.7 us (0.83)
  waiting for transfers between devices: 41 us -> 11.7 us
  starting transfers between devices: 19.9 us -> 35.6 us
    ppermute x7 -> x14, waiting for transfers between devices: 37.9 us -> 8.86 us  [passed(): return lax.ppermute(value, LEVEL, pairs + fill)]
    ppermute x7 -> x14, starting transfers between devices: 18 us -> 34.1 us  [passed(): return lax.ppermute(value, LEVEL, pairs + fill)]
    pallas_call x20 -> x23, Pallas kernels: 14.1 us -> 14.2 us  [run(): pl.pallas_call(kernel, in_specs=in_specs, out_specs=out_specs, out_shape=...]
  transfers between devices with their start and end apart: 16 -> 23, of which waited for: 9 -> 10; matrix products, arithmetic and copies ran while one was open for 0% -> 0% of each run, Pallas kernels for 11% -> 15%
where the time goes in v4:
time: 62.7 us; the launch traced here: 62.5 us
  starting transfers between devices  35.6 us (57%)
  Pallas kernels  14.2 us (23%)
  waiting for transfers between devices  11.7 us (19%)
  between operations  1.04 us (2%)
    ppermute x14, starting transfers between devices, passed(): return lax.ppermute(value, LEVEL, pairs + fill)  34.1 us
    pallas_call x23, Pallas kernels, run(): pl.pallas_call(kernel, in_specs=in_specs, out_specs=out_specs, out_shape=...  14.2 us
    ppermute x14, waiting for transfers between devices, passed(): return lax.ppermute(value, LEVEL, pairs + fill)  8.86 us
    ppermute x9, waiting for transfers between devices, exchanged(): return lax.ppermute(value, SUB, [(0, 1), (1, 0)])  2.86 us
    ppermute x9, starting transfers between devices, exchanged(): return lax.ppermute(value, SUB, [(0, 1), (1, 0)])  1.49 us
  transfers between devices with their start and end apart: 23, of which 10 were waited for; matrix products, arithmetic and copies ran while one was open for 0% of the time, Pallas kernels for 15%

profile of v4, /device:TPU:0, one launch (start us, length us, event | category | flops | bytes accessed | tf_op | source)
XLA Modules:
  0.0 62.5 jit_solution(8331600041277069283)
XLA Ops:
  0.6 3.7 %shard_map.86 = (bf16[256,256]{1,0:T(8,128)(2,1)S(1)}, bf16[256,256]{1,0:T(8,128)(2,1)S(1)}, f32[16,32,256]{2,1,0:T(8,128)S(1)}, f32[16,32,256]{2,1,0:T(8,128)S(...) custom-call(s32[3,32]{1,0:T(4,128)} %parent.1, ...), custom_call_target="tpu_custom_call" | custom-call | flops 1000000000 | bytes 1000000 | tf_op jit(solution)/shard_map/pallas_call | solution.py:555
  4.8 1.5 %collective-permute-done.refs_1_.refs_7_ = bf16[128,8,256]{2,1,0:T(8,128)(2,1)S(1)} collective-permute-done((bf16[128,8,256]{2,1,0:T(8,128)(2,1)S(1)}, bf16[128,8,256]{2,1,0:T(8,128)(2,1)S(1)}, u32[]{:S(2)}, u32[]{:S(2)}) %collective-permute-start) | collective-permute-done | bytes 524320 | tf_op jit(solution)/shard_map/ppermute | solution.py:570
  7.0 2.0 %collective-permute-start.2 = (bf16[32,8,256]{2,1,0:T(8,128)(2,1)S(1)}, bf16[32,8,256]{2,1,0:T(8,128)(2,1)S(1)}, u32[]{:S(2)}, u32[]{:S(2)}) collective-permute-start(bf16[32,8,256]{2,1,0:T(8,128)(2,1)S(1)} %shard_map.87), channel_id=1, source_target_pairs={{0,8},{8,0},{16,24},{24,16},{1,9},{9,1},{17,25},{25,17},{2,10},{10... | collective-permute-start | bytes 393224 | tf_op jit(solution)/shard_map/ppermute | solution.py:595
  9.1 3.5 %shard_map.89.own.refs_3_.refs_1_ = bf16[34,256,256]{2,1,0:T(8,128)(2,1)S(1)} custom-call(bf16[16,256,256]{2,1,0:T(8,128)(2,1)} %bitcast.8, bf16[16,256,256]{2,1,0:T(8,128)(2,1)} %bitcast.10, bf16[16,256,256]{2,1,0:T(8,128)(2,1)} %bitcast.11, bf16[16,64,256]{2,1,0:T(8,128)(2,1)} %ancestor.1), custom_call_target="tpu_custom_call" | custom-call | flops 1000000000 | bytes 1000000 | tf_op jit(solution)/shard_map/pallas_call | solution.py:555
  13.4 2.9 %collective-permute-start.4 = (bf16[32,8,256]{2,1,0:T(8,128)(2,1)S(1)}, bf16[32,8,256]{2,1,0:T(8,128)(2,1)S(1)}, u32[]{:S(2)}, u32[]{:S(2)}) collective-permute-start(bf16[32,8,256]{2,1,0:T(8,128)(2,1)S(1)} %get-tuple-element.137), channel_id=1, source_target_pairs={{8,16},{0,8},{16,24},{24,0},{9,17},{1,9},{17,25},{25,1},{10,18},{2... | collective-permute-start | bytes 393224 | tf_op jit(solution)/shard_map/ppermute | solution.py:595
  16.3 1.9 %collective-permute-start.7 = (bf16[32,8,256]{2,1,0:T(8,128)(2,1)S(1)}, bf16[32,8,256]{2,1,0:T(8,128)(2,1)S(1)}, u32[]{:S(2)}, u32[]{:S(2)}) collective-permute-start(bf16[32,8,256]{2,1,0:T(8,128)(2,1)S(1)} %get-tuple-element.141), channel_id=1, source_target_pairs={{8,16},{0,8},{16,24},{24,0},{9,17},{1,9},{17,25},{25,1},{10,18},{2... | collective-permute-start | bytes 393224 | tf_op jit(solution)/shard_map/ppermute | solution.py:595
  18.2 1.9 %collective-permute-done.4.refs_2_ = bf16[32,8,256]{2,1,0:T(8,128)(2,1)S(1)} collective-permute-done((bf16[32,8,256]{2,1,0:T(8,128)(2,1)S(1)}, bf16[32,8,256]{2,1,0:T(8,128)(2,1)S(1)}, u32[]{:S(2)}, u32[]{:S(2)}) %collective-permute-start.4) | collective-permute-done | bytes 131104 | tf_op jit(solution)/shard_map/ppermute | solution.py:595
  20.3 3.4 %collective-permute-start.6 = (bf16[32,8,256]{2,1,0:T(8,128)(2,1)S(1)}, bf16[32,8,256]{2,1,0:T(8,128)(2,1)S(1)}, u32[]{:S(2)}, u32[]{:S(2)}) collective-permute-start(bf16[32,8,256]{2,1,0:T(8,128)(2,1)S(1)} %get-tuple-element.148), channel_id=1, source_target_pairs={{16,24},{8,16},{0,8},{24,0},{17,25},{9,17},{1,9},{25,1},{18,26},{1... | collective-permute-start | bytes 393224 | tf_op jit(solution)/shard_map/ppermute | solution.py:595
  23.7 2.4 %collective-permute-start.10 = (bf16[32,8,256]{2,1,0:T(8,128)(2,1)S(1)}, bf16[32,8,256]{2,1,0:T(8,128)(2,1)S(1)}, u32[]{:S(2)}, u32[]{:S(2)}) collective-permute-start(bf16[32,8,256]{2,1,0:T(8,128)(2,1)S(1)} %get-tuple-element.155), channel_id=1, source_target_pairs={{16,24},{8,16},{0,8},{24,0},{17,25},{9,17},{1,9},{25,1},{18,26},{1... | collective-permute-start | bytes 393224 | tf_op jit(solution)/shard_map/ppermute | solution.py:595
  26.2 1.3 %collective-permute-done.6.refs_2_ = bf16[32,8,256]{2,1,0:T(8,128)(2,1)S(1)} collective-permute-done((bf16[32,8,256]{2,1,0:T(8,128)(2,1)S(1)}, bf16[32,8,256]{2,1,0:T(8,128)(2,1)S(1)}, u32[]{:S(2)}, u32[]{:S(2)}) %collective-permute-start.6) | collective-permute-done | bytes 131104 | tf_op jit(solution)/shard_map/ppermute | solution.py:595
  27.6 2.5 %collective-permute-start.9 = (bf16[32,8,256]{2,1,0:T(8,128)(2,1)S(1)}, bf16[32,8,256]{2,1,0:T(8,128)(2,1)S(1)}, u32[]{:S(2)}, u32[]{:S(2)}) collective-permute-start(bf16[32,8,256]{2,1,0:T(8,128)(2,1)S(1)} %get-tuple-element.167), channel_id=1, source_target_pairs={{24,16},{16,24},{0,8},{8,0},{25,17},{17,25},{1,9},{9,1},{26,18},{1... | collective-permute-start | bytes 393224 | tf_op jit(solution)/shard_map/ppermute | solution.py:595
  30.6 2.3 %collective-permute-start.12 = (bf16[32,8,256]{2,1,0:T(8,128)(2,1)S(1)}, bf16[32,8,256]{2,1,0:T(8,128)(2,1)S(1)}, u32[]{:S(2)}, u32[]{:S(2)}) collective-permute-start(bf16[32,8,256]{2,1,0:T(8,128)(2,1)S(1)} %get-tuple-element.173), channel_id=1, source_target_pairs={{24,16},{16,24},{0,8},{8,0},{25,17},{17,25},{1,9},{9,1},{26,18},{1... | collective-permute-start | bytes 393224 | tf_op jit(solution)/shard_map/ppermute | solution.py:595
  33.7 1.4 %collective-permute-done.9.refs_0_ = bf16[32,8,256]{2,1,0:T(8,128)(2,1)S(1)} collective-permute-done((bf16[32,8,256]{2,1,0:T(8,128)(2,1)S(1)}, bf16[32,8,256]{2,1,0:T(8,128)(2,1)S(1)}, u32[]{:S(2)}, u32[]{:S(2)}) %collective-permute-start.9) | collective-permute-done | bytes 131104 | tf_op jit(solution)/shard_map/ppermute | solution.py:595
  35.1 2.8 %collective-permute-start.11 = (bf16[32,8,256]{2,1,0:T(8,128)(2,1)S(1)}, bf16[32,8,256]{2,1,0:T(8,128)(2,1)S(1)}, u32[]{:S(2)}, u32[]{:S(2)}) collective-permute-start(bf16[32,8,256]{2,1,0:T(8,128)(2,1)S(1)} %get-tuple-element.186), channel_id=1, source_target_pairs={{16,8},{24,16},{0,24},{8,0},{17,9},{25,17},{1,25},{9,1},{18,10},{2... | collective-permute-start | bytes 393224 | tf_op jit(solution)/shard_map/ppermute | solution.py:595
  38.0 3.6 %collective-permute-start.14 = (bf16[32,8,256]{2,1,0:T(8,128)(2,1)S(1)}, bf16[32,8,256]{2,1,0:T(8,128)(2,1)S(1)}, u32[]{:S(2)}, u32[]{:S(2)}) collective-permute-start(bf16[32,8,256]{2,1,0:T(8,128)(2,1)S(1)} %get-tuple-element.190), channel_id=1, source_target_pairs={{16,8},{24,16},{0,24},{8,0},{17,9},{25,17},{1,25},{9,1},{18,10},{2... | collective-permute-start | bytes 393224 | tf_op jit(solution)/shard_map/ppermute | solution.py:595
  41.9 2.6 %collective-permute-start.13 = (bf16[32,8,256]{2,1,0:T(8,128)(2,1)S(1)}, bf16[32,8,256]{2,1,0:T(8,128)(2,1)S(1)}, u32[]{:S(2)}, u32[]{:S(2)}) collective-permute-start(bf16[32,8,256]{2,1,0:T(8,128)(2,1)S(1)} %get-tuple-element.196), channel_id=1, source_target_pairs={{8,0},{16,8},{0,24},{24,16},{9,1},{17,9},{1,25},{25,17},{10,2},{18... | collective-permute-start | bytes 393224 | tf_op jit(solution)/shard_map/ppermute | solution.py:595
  44.6 3.0 %collective-permute-start.16 = (bf16[32,8,256]{2,1,0:T(8,128)(2,1)S(1)}, bf16[32,8,256]{2,1,0:T(8,128)(2,1)S(1)}, u32[]{:S(2)}, u32[]{:S(2)}) collective-permute-start(bf16[32,8,256]{2,1,0:T(8,128)(2,1)S(1)} %get-tuple-element.202), channel_id=1, source_target_pairs={{8,0},{16,8},{0,24},{24,16},{9,1},{17,9},{1,25},{25,17},{10,2},{18... | collective-permute-start | bytes 393224 | tf_op jit(solution)/shard_map/ppermute | solution.py:595
  49.2 3.2 %collective-permute-start.15 = (bf16[32,8,256]{2,1,0:T(8,128)(2,1)S(1)}, bf16[32,8,256]{2,1,0:T(8,128)(2,1)S(1)}, u32[]{:S(2)}, u32[]{:S(2)}) collective-permute-start(bf16[32,8,256]{2,1,0:T(8,128)(2,1)S(1)} %get-tuple-element.209), channel_id=1, source_target_pairs={{8,0},{0,8},{16,24},{24,16},{9,1},{1,9},{17,25},{25,17},{10,2},{2,... | collective-permute-start | bytes 393224 | tf_op jit(solution)/shard_map/ppermute | solution.py:595
  52.4 0.9 %shard_map.103 = (f32[16,8,256]{2,1,0:T(8,128)S(1)}, f32[16,8,256]{2,1,0:T(8,128)S(1)}, f32[16,8,256]{2,1,0:T(8,128)S(1)}, f32[16,8,256]{2,1,0:T(8,128)S(1)}, bf16[32,8,256]{2,1,0:T(8,128)(2,1)S(1)}) custom-call(bf16[32,8,256]{2,1,0:T(8,128)(2,1)S(1)} %collective-permute-done.16.refs_0_, ...), custom_call_target="tpu_custom_call", output_to_operand_aliasing={{0}: (6, {}), {1}: (7, {}), {2}: (8, {}), {3}: (9, {})} | custom-call | flops 5000000000 | bytes 1000000 | tf_op jit(solution)/shard_map/pallas_call | solution.py:555
  53.4 1.4 %collective-permute-start.17 = (bf16[32,8,256]{2,1,0:T(8,128)(2,1)S(1)}, bf16[32,8,256]{2,1,0:T(8,128)(2,1)S(1)}, u32[]{:S(2)}, u32[]{:S(2)}) collective-permute-start(bf16[32,8,256]{2,1,0:T(8,128)(2,1)S(1)} %get-tuple-element.215), channel_id=1, source_target_pairs={{8,0},{0,8},{16,24},{24,16},{9,1},{1,9},{17,25},{25,17},{10,2},{2,... | collective-permute-start | bytes 393224 | tf_op jit(solution)/shard_map/ppermute | solution.py:595
  56.0 1.0 %shard_map.106 = f32[16,64,256]{2,1,0:T(8,128)} custom-call(f32[16,32,256]{2,1,0:T(8,128)S(1)} %get-tuple-element.231.here, f32[16,32,256]{2,1,0:T(8,128)S(1)} %get-tuple-element.233.far, f32[16,32,256]{2,1,0:T(8,128)S(1)} %collective-permute-done.18.other), custom_call_target="tpu_custom_call" | custom-call | flops 1000000000 | bytes 1000000 | tf_op jit(solution)/shard_map/pallas_call | solution.py:555
  57.0 2.3 %collective-permute-done.17.refs_0_ = bf16[32,8,256]{2,1,0:T(8,128)(2,1)S(1)} collective-permute-done((bf16[32,8,256]{2,1,0:T(8,128)(2,1)S(1)}, bf16[32,8,256]{2,1,0:T(8,128)(2,1)S(1)}, u32[]{:S(2)}, u32[]{:S(2)}) %collective-permute-start.17) | collective-permute-done | bytes 131104 | tf_op jit(solution)/shard_map/ppermute | solution.py:595
  60.0 1.3 %collective-permute-done.22.refs_7_ = f32[16,8,256]{2,1,0:T(8,128)S(1)} collective-permute-done((f32[16,8,256]{2,1,0:T(8,128)S(1)}, f32[16,8,256]{2,1,0:T(8,128)S(1)}, u32[]{:S(2)}, u32[]{:S(2)}) %collective-permute-start.22) | collective-permute-done | bytes 131104 | tf_op jit(solution)/shard_map/ppermute | solution.py:570
  61.3 1.0 %shard_map.108 = f32[16,64,256]{2,1,0:T(8,128)} custom-call(f32[16,8,256]{2,1,0:T(8,128)S(1)} %get-tuple-element.208.refs_0_, f32[16,8,256]{2,1,0:T(8,128)S(1)} %get-tuple-element.219.refs_1_, f32[16,8,256]{2,1,0:T(8,128)S(1)} %get-tuple-element.220.refs_2_, f32[16,8,256]{2,1,0:T(8,128)S(1)} %get-tuple-element.237.refs_3_, ...), custom_call_target="tpu_custom_call" | custom-call | flops 1000000000 | bytes 1000000 | tf_op jit(solution)/shard_map/pallas_call | solution.py:555
  (45 shorter events, 7.7 us)
Async XLA Ops:
  4.3 2.1 %collective-permute-start = (bf16[128,8,256]{2,1,0:T(8,128)(2,1)S(1)}, bf16[128,8,256]{2,1,0:T(8,128)(2,1)S(1)}, u32[]{:S(2)}, u32[]{:S(2)}) collective-permute-start(bf16[128,8,256]{2,1,0:T(8,128)(2,1)S(1)} %get-tuple-element.125), channel_id=1, source_target_pairs={{0,4},{4,0},{1,5},{5,1},{2,6},{6,2},{3,7},{7,3},{8,12},{12,8},{9,1... | collective-permute-start | bytes 1572872 | tf_op jit(solution)/shard_map/ppermute | solution.py:570
  6.4 6.9 %collective-permute-start.3 = (bf16[16,256,256]{2,1,0:T(8,128)(2,1)S(1)}, bf16[16,256,256]{2,1,0:T(8,128)(2,1)S(1)}, u32[]{:S(2)}, u32[]{:S(2)}) collective-permute-start(bf16[16,256,256]{2,1,0:T(8,128)(2,1)S(1)} %get-tuple-element.133.refs_3_.refs_7_.up_own), channel_id=1, source_target_pairs={{0,4},{4,0},{1,5},{5,1},{2,6},{6,2},{3,7},{7,3},{8,12},{12,8},{9,1... | collective-permute-start | bytes 6291464 | tf_op jit(solution)/shard_map/ppermute | solution.py:570
  6.8 6.5 %collective-permute-start.1 = (f32[16,32,256]{2,1,0:T(8,128)S(1)}, f32[16,32,256]{2,1,0:T(8,128)S(1)}, u32[]{:S(2)}, u32[]{:S(2)}) collective-permute-start(f32[16,32,256]{2,1,0:T(8,128)S(1)} %get-tuple-element.126), channel_id=1, source_target_pairs={{0,4},{4,0},{1,5},{5,1},{2,6},{6,2},{3,7},{7,3},{8,12},{12,8},{9,1... | collective-permute-start | bytes 1572872 | tf_op jit(solution)/shard_map/ppermute | solution.py:570
  7.0 6.3 %collective-permute-start.2 = (bf16[32,8,256]{2,1,0:T(8,128)(2,1)S(1)}, bf16[32,8,256]{2,1,0:T(8,128)(2,1)S(1)}, u32[]{:S(2)}, u32[]{:S(2)}) collective-permute-start(bf16[32,8,256]{2,1,0:T(8,128)(2,1)S(1)} %shard_map.87), channel_id=1, source_target_pairs={{0,8},{8,0},{16,24},{24,16},{1,9},{9,1},{17,25},{25,17},{2,10},{10... | collective-permute-start | bytes 393224 | tf_op jit(solution)/shard_map/ppermute | solution.py:595
  9.0 7.3 %collective-permute-start.5 = (bf16[32,8,256]{2,1,0:T(8,128)(2,1)S(1)}, bf16[32,8,256]{2,1,0:T(8,128)(2,1)S(1)}, u32[]{:S(2)}, u32[]{:S(2)}) collective-permute-start(bf16[32,8,256]{2,1,0:T(8,128)(2,1)S(1)} %shard_map.88), channel_id=1, source_target_pairs={{0,8},{8,0},{16,24},{24,16},{1,9},{9,1},{17,25},{25,17},{2,10},{10... | collective-permute-start | bytes 393224 | tf_op jit(solution)/shard_map/ppermute | solution.py:595
  12.5 13.6 %collective-permute-start.8 = (bf16[34,256,256]{2,1,0:T(8,128)(2,1)S(1)}, bf16[34,256,256]{2,1,0:T(8,128)(2,1)S(1)}, u32[]{:S(2)}, u32[]{:S(2)}) collective-permute-start(bf16[34,256,256]{2,1,0:T(8,128)(2,1)S(1)} %shard_map.89.own.refs_3_.refs_1_), channel_id=1, source_target_pairs={{0,4},{4,0},{1,5},{5,1},{2,6},{6,2},{3,7},{7,3},{8,12},{12,8},{9,1... | collective-permute-start | bytes 13369352 | tf_op jit(solution)/shard_map/ppermute | solution.py:570
  13.4 6.8 %collective-permute-start.4 = (bf16[32,8,256]{2,1,0:T(8,128)(2,1)S(1)}, bf16[32,8,256]{2,1,0:T(8,128)(2,1)S(1)}, u32[]{:S(2)}, u32[]{:S(2)}) collective-permute-start(bf16[32,8,256]{2,1,0:T(8,128)(2,1)S(1)} %get-tuple-element.137), channel_id=1, source_target_pairs={{8,16},{0,8},{16,24},{24,0},{9,17},{1,9},{17,25},{25,1},{10,18},{2... | collective-permute-start | bytes 393224 | tf_op jit(solution)/shard_map/ppermute | solution.py:595
  16.3 7.3 %collective-permute-start.7 = (bf16[32,8,256]{2,1,0:T(8,128)(2,1)S(1)}, bf16[32,8,256]{2,1,0:T(8,128)(2,1)S(1)}, u32[]{:S(2)}, u32[]{:S(2)}) collective-permute-start(bf16[32,8,256]{2,1,0:T(8,128)(2,1)S(1)} %get-tuple-element.141), channel_id=1, source_target_pairs={{8,16},{0,8},{16,24},{24,0},{9,17},{1,9},{17,25},{25,1},{10,18},{2... | collective-permute-start | bytes 393224 | tf_op jit(solution)/shard_map/ppermute | solution.py:595
  20.3 7.3 %collective-permute-start.6 = (bf16[32,8,256]{2,1,0:T(8,128)(2,1)S(1)}, bf16[32,8,256]{2,1,0:T(8,128)(2,1)S(1)}, u32[]{:S(2)}, u32[]{:S(2)}) collective-permute-start(bf16[32,8,256]{2,1,0:T(8,128)(2,1)S(1)} %get-tuple-element.148), channel_id=1, source_target_pairs={{16,24},{8,16},{0,8},{24,0},{17,25},{9,17},{1,9},{25,1},{18,26},{1... | collective-permute-start | bytes 393224 | tf_op jit(solution)/shard_map/ppermute | solution.py:595
  23.7 6.6 %collective-permute-start.10 = (bf16[32,8,256]{2,1,0:T(8,128)(2,1)S(1)}, bf16[32,8,256]{2,1,0:T(8,128)(2,1)S(1)}, u32[]{:S(2)}, u32[]{:S(2)}) collective-permute-start(bf16[32,8,256]{2,1,0:T(8,128)(2,1)S(1)} %get-tuple-element.155), channel_id=1, source_target_pairs={{16,24},{8,16},{0,8},{24,0},{17,25},{9,17},{1,9},{25,1},{18,26},{1... | collective-permute-start | bytes 393224 | tf_op jit(solution)/shard_map/ppermute | solution.py:595
  27.6 7.4 %collective-permute-start.9 = (bf16[32,8,256]{2,1,0:T(8,128)(2,1)S(1)}, bf16[32,8,256]{2,1,0:T(8,128)(2,1)S(1)}, u32[]{:S(2)}, u32[]{:S(2)}) collective-permute-start(bf16[32,8,256]{2,1,0:T(8,128)(2,1)S(1)} %get-tuple-element.167), channel_id=1, source_target_pairs={{24,16},{16,24},{0,8},{8,0},{25,17},{17,25},{1,9},{9,1},{26,18},{1... | collective-permute-start | bytes 393224 | tf_op jit(solution)/shard_map/ppermute | solution.py:595
  30.6 7.4 %collective-permute-start.12 = (bf16[32,8,256]{2,1,0:T(8,128)(2,1)S(1)}, bf16[32,8,256]{2,1,0:T(8,128)(2,1)S(1)}, u32[]{:S(2)}, u32[]{:S(2)}) collective-permute-start(bf16[32,8,256]{2,1,0:T(8,128)(2,1)S(1)} %get-tuple-element.173), channel_id=1, source_target_pairs={{24,16},{16,24},{0,8},{8,0},{25,17},{17,25},{1,9},{9,1},{26,18},{1... | collective-permute-start | bytes 393224 | tf_op jit(solution)/shard_map/ppermute | solution.py:595
  35.1 6.6 %collective-permute-start.11 = (bf16[32,8,256]{2,1,0:T(8,128)(2,1)S(1)}, bf16[32,8,256]{2,1,0:T(8,128)(2,1)S(1)}, u32[]{:S(2)}, u32[]{:S(2)}) collective-permute-start(bf16[32,8,256]{2,1,0:T(8,128)(2,1)S(1)} %get-tuple-element.186), channel_id=1, source_target_pairs={{16,8},{24,16},{0,24},{8,0},{17,9},{25,17},{1,25},{9,1},{18,10},{2... | collective-permute-start | bytes 393224 | tf_op jit(solution)/shard_map/ppermute | solution.py:595
  38.0 6.5 %collective-permute-start.14 = (bf16[32,8,256]{2,1,0:T(8,128)(2,1)S(1)}, bf16[32,8,256]{2,1,0:T(8,128)(2,1)S(1)}, u32[]{:S(2)}, u32[]{:S(2)}) collective-permute-start(bf16[32,8,256]{2,1,0:T(8,128)(2,1)S(1)} %get-tuple-element.190), channel_id=1, source_target_pairs={{16,8},{24,16},{0,24},{8,0},{17,9},{25,17},{1,25},{9,1},{18,10},{2... | collective-permute-start | bytes 393224 | tf_op jit(solution)/shard_map/ppermute | solution.py:595
  41.7 14.3 %collective-permute-start.18 = (f32[16,32,256]{2,1,0:T(8,128)S(1)}, f32[16,32,256]{2,1,0:T(8,128)S(1)}, u32[]{:S(2)}, u32[]{:S(2)}) collective-permute-start(f32[16,32,256]{2,1,0:T(8,128)S(1)} %get-tuple-element.233.far), channel_id=1, source_target_pairs={{0,4},{4,0},{1,5},{5,1},{2,6},{6,2},{3,7},{7,3},{8,12},{12,8},{9,1... | collective-permute-start | bytes 1572872 | tf_op jit(solution)/shard_map/ppermute | solution.py:570
  41.9 6.4 %collective-permute-start.13 = (bf16[32,8,256]{2,1,0:T(8,128)(2,1)S(1)}, bf16[32,8,256]{2,1,0:T(8,128)(2,1)S(1)}, u32[]{:S(2)}, u32[]{:S(2)}) collective-permute-start(bf16[32,8,256]{2,1,0:T(8,128)(2,1)S(1)} %get-tuple-element.196), channel_id=1, source_target_pairs={{8,0},{16,8},{0,24},{24,16},{9,1},{17,9},{1,25},{25,17},{10,2},{18... | collective-permute-start | bytes 393224 | tf_op jit(solution)/shard_map/ppermute | solution.py:595
  44.6 7.8 %collective-permute-start.16 = (bf16[32,8,256]{2,1,0:T(8,128)(2,1)S(1)}, bf16[32,8,256]{2,1,0:T(8,128)(2,1)S(1)}, u32[]{:S(2)}, u32[]{:S(2)}) collective-permute-start(bf16[32,8,256]{2,1,0:T(8,128)(2,1)S(1)} %get-tuple-element.202), channel_id=1, source_target_pairs={{8,0},{16,8},{0,24},{24,16},{9,1},{17,9},{1,25},{25,17},{10,2},{18... | collective-permute-start | bytes 393224 | tf_op jit(solution)/shard_map/ppermute | solution.py:595
  49.2 6.1 %collective-permute-start.15 = (bf16[32,8,256]{2,1,0:T(8,128)(2,1)S(1)}, bf16[32,8,256]{2,1,0:T(8,128)(2,1)S(1)}, u32[]{:S(2)}, u32[]{:S(2)}) collective-permute-start(bf16[32,8,256]{2,1,0:T(8,128)(2,1)S(1)} %get-tuple-element.209), channel_id=1, source_target_pairs={{8,0},{0,8},{16,24},{24,16},{9,1},{1,9},{17,25},{25,17},{10,2},{2,... | collective-permute-start | bytes 393224 | tf_op jit(solution)/shard_map/ppermute | solution.py:595
  53.3 6.7 %collective-permute-start.21 = (f32[16,8,256]{2,1,0:T(8,128)S(1)}, f32[16,8,256]{2,1,0:T(8,128)S(1)}, u32[]{:S(2)}, u32[]{:S(2)}) collective-permute-start(f32[16,8,256]{2,1,0:T(8,128)S(1)} %get-tuple-element.240), channel_id=1, source_target_pairs={{0,4},{4,0},{1,5},{5,1},{2,6},{6,2},{3,7},{7,3},{8,12},{12,8},{9,1... | collective-permute-start | bytes 393224 | tf_op jit(solution)/shard_map/ppermute | solution.py:570
  53.4 5.9 %collective-permute-start.17 = (bf16[32,8,256]{2,1,0:T(8,128)(2,1)S(1)}, bf16[32,8,256]{2,1,0:T(8,128)(2,1)S(1)}, u32[]{:S(2)}, u32[]{:S(2)}) collective-permute-start(bf16[32,8,256]{2,1,0:T(8,128)(2,1)S(1)} %get-tuple-element.215), channel_id=1, source_target_pairs={{8,0},{0,8},{16,24},{24,16},{9,1},{1,9},{17,25},{25,17},{10,2},{2,... | collective-permute-start | bytes 393224 | tf_op jit(solution)/shard_map/ppermute | solution.py:595
  54.8 5.2 %collective-permute-start.19 = (f32[16,8,256]{2,1,0:T(8,128)S(1)}, f32[16,8,256]{2,1,0:T(8,128)S(1)}, u32[]{:S(2)}, u32[]{:S(2)}) collective-permute-start(f32[16,8,256]{2,1,0:T(8,128)S(1)} %get-tuple-element.238), channel_id=1, source_target_pairs={{0,4},{4,0},{1,5},{5,1},{2,6},{6,2},{3,7},{7,3},{8,12},{12,8},{9,1... | collective-permute-start | bytes 393224 | tf_op jit(solution)/shard_map/ppermute | solution.py:570
  56.0 4.0 %collective-permute-start.20 = (f32[16,8,256]{2,1,0:T(8,128)S(1)}, f32[16,8,256]{2,1,0:T(8,128)S(1)}, u32[]{:S(2)}, u32[]{:S(2)}) collective-permute-start(f32[16,8,256]{2,1,0:T(8,128)S(1)} %get-tuple-element.239), channel_id=1, source_target_pairs={{0,4},{4,0},{1,5},{5,1},{2,6},{6,2},{3,7},{7,3},{8,12},{12,8},{9,1... | collective-permute-start | bytes 393224 | tf_op jit(solution)/shard_map/ppermute | solution.py:570
  60.0 1.4 %collective-permute-start.22 = (f32[16,8,256]{2,1,0:T(8,128)S(1)}, f32[16,8,256]{2,1,0:T(8,128)S(1)}, u32[]{:S(2)}, u32[]{:S(2)}) collective-permute-start(f32[16,8,256]{2,1,0:T(8,128)S(1)} %get-tuple-element.241), channel_id=1, source_target_pairs={{0,4},{4,0},{1,5},{5,1},{2,6},{6,2},{3,7},{7,3},{8,12},{12,8},{9,1... | collective-permute-start | bytes 393224 | tf_op jit(solution)/shard_map/ppermute | solution.py:570

commit v5 on v4

--- a/solution.py
+++ b/solution.py
@@ -194,7 +194,7 @@
 
 NODE_ROWS = 8
 LOAD_NODES = 4
-COSTS = [10**9,3*10**10,3*10**10]+[5*10**9]*5
+COSTS = [10000000000, 30000000000, 30000000000, 5000000000, 5000000000, 5000000000, 5000000000, 5000000000]
 SMALL_VMEM_BYTES = 12 * 2**20
 IN_ANY = pl.BlockSpec(memory_space=pl.ANY)
 IN_HBM = pl.BlockSpec(memory_space=pltpu.HBM)
@@ -384,22 +384,42 @@
     send_solved(c, at)
 
 
+def back_far_role(c, at):
+    base = at["low_base", c]
+    count = base.shape[0] // 2
+    for node in range(count):
+        above = at["received"][count + node]
+        at["sol_far", c][node] = base[count + node] - dot(above, at["down_far"][count + node])
+
+
+def back_own_role(c, at):
+    base = at["low_base", c]
+    count = base.shape[0] // 2
+    for node in range(count):
+        at["sol_own", c][node] = base[node] - dot(at["received"][node], at["down_own"][count + node])
+
+
 def sum_role(c, at):
     rows = slice(c * at["sent"].shape[0], (c + 1) * at["sent"].shape[0])
     at["sent"][...] = (at["home"][rows] + at["swapped"][rows].astype(F32)).astype(BF16)
 
 
-ROLES = {"tier": tier_role, "top": top_role, "back": back_role, "sum": sum_role}
+FAR, OWN = "f", "o"
+ROLES = {"tier": tier_role, "top": top_role, "back": back_role, FAR: back_far_role, OWN: back_own_role, "sum": sum_role}
 READS = {
     "tier": ("rhs_own", "rhs_far", "received", "up_own", "up_far", "select"),
     "top": ("rhs_own", "rhs_far", "received", "down_own", "down_far", "choose", "top_base"),
     "back": ("received", "down_own", "down_far", "choose", "low_base"),
+    FAR: ("received", "down_far", "low_base"),
+    OWN: ("received", "down_own", "low_base"),
     "sum": ("home", "swapped"),
 }
 WRITES = {
     "tier": ("residue", "own", "far"),
     "top": ("residue", "sol_own", "sol_far"),
     "back": ("sol_own", "sol_far"),
+    FAR: ("sol_far",),
+    OWN: ("sol_own",),
     "sum": (),
 }
 
@@ -628,8 +648,17 @@
     def sems(pieces):
         return [pltpu.SemaphoreType.DMA((2, pieces))]
 
+    def placed(group, before, *earlier):
+        first = after(state["sol_own", group[0]], *earlier) if earlier else state["sol_own", group[0]]
+        return run(
+            functools.partial(place_kernel, [NODE_ROWS * c for c in group]),
+            [first, *(state["sol_own", c] for c in group[1:]), *(other[c] for c in group)],
+            [], whole=(whole, before), scratch=sems(len(group)),
+        )[0]
+
     pipes = [list(range(chunks))[i : i + 2] for i in range(0, chunks, 2)]
     received = [None] * len(pipes)
+    other = [None] * chunks
     pace = []
     last = 2 * top + 1
     for k in range(last + 1):
@@ -650,8 +679,13 @@
                         pairs.append((low, low - 1))
             if received[p] is not None:
                 state["received"] = after(received[p], *pace)
+            if k == last:
+                step([(0, FAR, pipe[-1])], state, False, COSTS[k])
+                other[pipe[-1]] = exchanged(state["sol_far", pipe[-1]])
+                plan = [(0, OWN, pipe[-1])]
+                state["received"] = after(state["received"], state["sol_far", pipe[-1]])
             sent = step(plan, state, bool(pairs), COSTS[k])
-            pace = [sent] if pairs else [state["sol_own", pipe[1]]]
+            pace = [sent] if pairs else [state["sol_own", pipe[-1]]]
             if pairs:
                 received[p] = passed(sent, pairs)
             if p == 0 and k == 0:
@@ -663,7 +697,10 @@
                 (update,) = run(
                     place_bottom_kernel, (upd_own, after(upd_far, *pace), upd_other), [], whole=(whole, None), scratch=sems(1)
                 )
-                pace = [update]
+                early = [pipe[0] for pipe in pipes]
+                other[early[0]], other[early[1]] = (exchanged(state["sol_far", c]) for c in early)
+                solved = placed(early, None, update)
+                pace = [solved]
         if k == 0:
             state["down_own"] = merged(sent)
             pace.append(state["down_own"])
@@ -693,12 +730,7 @@
                 [half_shape] * 2,
             )
             upd_other = exchanged(upd_far)
-        if k == last:
-            (solved,) = run(
-                functools.partial(place_kernel, [NODE_ROWS * c for c in range(chunks)]),
-                [state["sol_own", c] for c in range(chunks)] + [exchanged(state["sol_far", c]) for c in range(chunks)],
-                [], whole=(whole, None), scratch=sems(chunks),
-            )
+    solved = placed([pipe[-1] for pipe in pipes], solved)
     return solved[None], update[None]
 
 

time: 62.7 us -> 61.6 us (0.982)
  waiting for transfers between devices: 11.7 us -> 9.43 us
  Pallas kernels: 14.2 us -> 15 us
    ppermute x14, waiting for transfers between devices: 8.86 us -> 6.94 us  [passed(): return lax.ppermute(value, LEVEL, pairs + fill)]
    pallas_call x23 -> x26, Pallas kernels: 14.2 us -> 15 us  [run(): pl.pallas_call(kernel, in_specs=in_specs, out_specs=out_specs, out_shape=...]
  transfers between devices with their start and end apart: 23 -> 23, of which waited for: 10 -> 9; matrix products, arithmetic and copies ran while one was open for 0% -> 0% of each run, Pallas kernels for 15% -> 17%
where the time goes in v5:
time: 61.6 us; the launch traced here: 61.4 us
  starting transfers between devices  35.9 us (58%)
  Pallas kernels  15 us (24%)
  waiting for transfers between devices  9.43 us (15%)
  between operations  1.01 us (2%)
    ppermute x14, starting transfers between devices, passed(): return lax.ppermute(value, LEVEL, pairs + fill)  33.9 us
    pallas_call x26, Pallas kernels, run(): pl.pallas_call(kernel, in_specs=in_specs, out_specs=out_specs, out_shape=...  15 us
    ppermute x14, waiting for transfers between devices, passed(): return lax.ppermute(value, LEVEL, pairs + fill)  6.94 us
    ppermute x9, waiting for transfers between devices, exchanged(): return lax.ppermute(value, SUB, [(0, 1), (1, 0)])  2.49 us
    ppermute x9, starting transfers between devices, exchanged(): return lax.ppermute(value, SUB, [(0, 1), (1, 0)])  2.03 us
  transfers between devices with their start and end apart: 23, of which 9 were waited for; matrix products, arithmetic and copies ran while one was open for 0% of the time, Pallas kernels for 17%

profile of v5, /device:TPU:0, one launch (start us, length us, event | category | flops | bytes accessed | tf_op | source)
XLA Modules:
  0.0 61.4 jit_solution(884635995686343934)
XLA Ops:
  0.6 3.7 %shard_map.86 = (bf16[256,256]{1,0:T(8,128)(2,1)S(1)}, bf16[256,256]{1,0:T(8,128)(2,1)S(1)}, f32[16,32,256]{2,1,0:T(8,128)S(1)}, f32[16,32,256]{2,1,0:T(8,128)S(...) custom-call(s32[3,32]{1,0:T(4,128)} %parent.1, ...), custom_call_target="tpu_custom_call" | custom-call | flops 1000000000 | bytes 1000000 | tf_op jit(solution)/shard_map/pallas_call | solution.py:575
  4.8 1.5 %collective-permute-done.refs_1_.refs_7_ = bf16[128,8,256]{2,1,0:T(8,128)(2,1)S(1)} collective-permute-done((bf16[128,8,256]{2,1,0:T(8,128)(2,1)S(1)}, bf16[128,8,256]{2,1,0:T(8,128)(2,1)S(1)}, u32[]{:S(2)}, u32[]{:S(2)}) %collective-permute-start) | collective-permute-done | bytes 524320 | tf_op jit(solution)/shard_map/ppermute | solution.py:590
  6.8 1.8 %collective-permute-start.2 = (bf16[32,8,256]{2,1,0:T(8,128)(2,1)S(1)}, bf16[32,8,256]{2,1,0:T(8,128)(2,1)S(1)}, u32[]{:S(2)}, u32[]{:S(2)}) collective-permute-start(bf16[32,8,256]{2,1,0:T(8,128)(2,1)S(1)} %shard_map.87), channel_id=1, source_target_pairs={{0,8},{8,0},{16,24},{24,16},{1,9},{9,1},{17,25},{25,17},{2,10},{10... | collective-permute-start | bytes 393224 | tf_op jit(solution)/shard_map/ppermute | solution.py:615
  9.0 3.5 %shard_map.89.own.refs_3_.refs_1_ = bf16[34,256,256]{2,1,0:T(8,128)(2,1)S(1)} custom-call(bf16[16,256,256]{2,1,0:T(8,128)(2,1)} %bitcast.8, bf16[16,256,256]{2,1,0:T(8,128)(2,1)} %bitcast.10, bf16[16,256,256]{2,1,0:T(8,128)(2,1)} %bitcast.11, bf16[16,64,256]{2,1,0:T(8,128)(2,1)} %ancestor.1), custom_call_target="tpu_custom_call" | custom-call | flops 1000000000 | bytes 1000000 | tf_op jit(solution)/shard_map/pallas_call | solution.py:575
  13.2 2.7 %collective-permute-start.4 = (bf16[32,8,256]{2,1,0:T(8,128)(2,1)S(1)}, bf16[32,8,256]{2,1,0:T(8,128)(2,1)S(1)}, u32[]{:S(2)}, u32[]{:S(2)}) collective-permute-start(bf16[32,8,256]{2,1,0:T(8,128)(2,1)S(1)} %get-tuple-element.136), channel_id=1, source_target_pairs={{8,16},{0,8},{16,24},{24,0},{9,17},{1,9},{17,25},{25,1},{10,18},{2... | collective-permute-start | bytes 393224 | tf_op jit(solution)/shard_map/ppermute | solution.py:615
  15.9 2.2 %collective-permute-start.7 = (bf16[32,8,256]{2,1,0:T(8,128)(2,1)S(1)}, bf16[32,8,256]{2,1,0:T(8,128)(2,1)S(1)}, u32[]{:S(2)}, u32[]{:S(2)}) collective-permute-start(bf16[32,8,256]{2,1,0:T(8,128)(2,1)S(1)} %get-tuple-element.140), channel_id=1, source_target_pairs={{8,16},{0,8},{16,24},{24,0},{9,17},{1,9},{17,25},{25,1},{10,18},{2... | collective-permute-start | bytes 393224 | tf_op jit(solution)/shard_map/ppermute | solution.py:615
  18.1 1.7 %collective-permute-done.4.refs_2_ = bf16[32,8,256]{2,1,0:T(8,128)(2,1)S(1)} collective-permute-done((bf16[32,8,256]{2,1,0:T(8,128)(2,1)S(1)}, bf16[32,8,256]{2,1,0:T(8,128)(2,1)S(1)}, u32[]{:S(2)}, u32[]{:S(2)}) %collective-permute-start.4) | collective-permute-done | bytes 131104 | tf_op jit(solution)/shard_map/ppermute | solution.py:615
  19.9 3.3 %collective-permute-start.6 = (bf16[32,8,256]{2,1,0:T(8,128)(2,1)S(1)}, bf16[32,8,256]{2,1,0:T(8,128)(2,1)S(1)}, u32[]{:S(2)}, u32[]{:S(2)}) collective-permute-start(bf16[32,8,256]{2,1,0:T(8,128)(2,1)S(1)} %get-tuple-element.147), channel_id=1, source_target_pairs={{16,24},{8,16},{0,8},{24,0},{17,25},{9,17},{1,9},{25,1},{18,26},{1... | collective-permute-start | bytes 393224 | tf_op jit(solution)/shard_map/ppermute | solution.py:615
  23.3 2.2 %collective-permute-start.10 = (bf16[32,8,256]{2,1,0:T(8,128)(2,1)S(1)}, bf16[32,8,256]{2,1,0:T(8,128)(2,1)S(1)}, u32[]{:S(2)}, u32[]{:S(2)}) collective-permute-start(bf16[32,8,256]{2,1,0:T(8,128)(2,1)S(1)} %get-tuple-element.154), channel_id=1, source_target_pairs={{16,24},{8,16},{0,8},{24,0},{17,25},{9,17},{1,9},{25,1},{18,26},{1... | collective-permute-start | bytes 393224 | tf_op jit(solution)/shard_map/ppermute | solution.py:615
  25.5 1.5 %collective-permute-done.6.refs_2_ = bf16[32,8,256]{2,1,0:T(8,128)(2,1)S(1)} collective-permute-done((bf16[32,8,256]{2,1,0:T(8,128)(2,1)S(1)}, bf16[32,8,256]{2,1,0:T(8,128)(2,1)S(1)}, u32[]{:S(2)}, u32[]{:S(2)}) %collective-permute-start.6) | collective-permute-done | bytes 131104 | tf_op jit(solution)/shard_map/ppermute | solution.py:615
  27.2 2.5 %collective-permute-start.9 = (bf16[32,8,256]{2,1,0:T(8,128)(2,1)S(1)}, bf16[32,8,256]{2,1,0:T(8,128)(2,1)S(1)}, u32[]{:S(2)}, u32[]{:S(2)}) collective-permute-start(bf16[32,8,256]{2,1,0:T(8,128)(2,1)S(1)} %get-tuple-element.166), channel_id=1, source_target_pairs={{24,16},{16,24},{0,8},{8,0},{25,17},{17,25},{1,9},{9,1},{26,18},{1... | collective-permute-start | bytes 393224 | tf_op jit(solution)/shard_map/ppermute | solution.py:615
  30.1 2.5 %collective-permute-start.12 = (bf16[32,8,256]{2,1,0:T(8,128)(2,1)S(1)}, bf16[32,8,256]{2,1,0:T(8,128)(2,1)S(1)}, u32[]{:S(2)}, u32[]{:S(2)}) collective-permute-start(bf16[32,8,256]{2,1,0:T(8,128)(2,1)S(1)} %get-tuple-element.172), channel_id=1, source_target_pairs={{24,16},{16,24},{0,8},{8,0},{25,17},{17,25},{1,9},{9,1},{26,18},{1... | collective-permute-start | bytes 393224 | tf_op jit(solution)/shard_map/ppermute | solution.py:615
  34.4 3.5 %collective-permute-start.11 = (bf16[32,8,256]{2,1,0:T(8,128)(2,1)S(1)}, bf16[32,8,256]{2,1,0:T(8,128)(2,1)S(1)}, u32[]{:S(2)}, u32[]{:S(2)}) collective-permute-start(bf16[32,8,256]{2,1,0:T(8,128)(2,1)S(1)} %get-tuple-element.185), channel_id=1, source_target_pairs={{16,8},{24,16},{0,24},{8,0},{17,9},{25,17},{1,25},{9,1},{18,10},{2... | collective-permute-start | bytes 393224 | tf_op jit(solution)/shard_map/ppermute | solution.py:615
  38.0 2.9 %collective-permute-start.14 = (bf16[32,8,256]{2,1,0:T(8,128)(2,1)S(1)}, bf16[32,8,256]{2,1,0:T(8,128)(2,1)S(1)}, u32[]{:S(2)}, u32[]{:S(2)}) collective-permute-start(bf16[32,8,256]{2,1,0:T(8,128)(2,1)S(1)} %get-tuple-element.189), channel_id=1, source_target_pairs={{16,8},{24,16},{0,24},{8,0},{17,9},{25,17},{1,25},{9,1},{18,10},{2... | collective-permute-start | bytes 393224 | tf_op jit(solution)/shard_map/ppermute | solution.py:615
  41.1 3.3 %collective-permute-start.13 = (bf16[32,8,256]{2,1,0:T(8,128)(2,1)S(1)}, bf16[32,8,256]{2,1,0:T(8,128)(2,1)S(1)}, u32[]{:S(2)}, u32[]{:S(2)}) collective-permute-start(bf16[32,8,256]{2,1,0:T(8,128)(2,1)S(1)} %get-tuple-element.195), channel_id=1, source_target_pairs={{8,0},{16,8},{0,24},{24,16},{9,1},{17,9},{1,25},{25,17},{10,2},{18... | collective-permute-start | bytes 393224 | tf_op jit(solution)/shard_map/ppermute | solution.py:615
  44.5 2.4 %collective-permute-start.16 = (bf16[32,8,256]{2,1,0:T(8,128)(2,1)S(1)}, bf16[32,8,256]{2,1,0:T(8,128)(2,1)S(1)}, u32[]{:S(2)}, u32[]{:S(2)}) collective-permute-start(bf16[32,8,256]{2,1,0:T(8,128)(2,1)S(1)} %get-tuple-element.201), channel_id=1, source_target_pairs={{8,0},{16,8},{0,24},{24,16},{9,1},{17,9},{1,25},{25,17},{10,2},{18... | collective-permute-start | bytes 393224 | tf_op jit(solution)/shard_map/ppermute | solution.py:615
  46.9 1.5 %collective-permute-done.13.refs_0_ = bf16[32,8,256]{2,1,0:T(8,128)(2,1)S(1)} collective-permute-done((bf16[32,8,256]{2,1,0:T(8,128)(2,1)S(1)}, bf16[32,8,256]{2,1,0:T(8,128)(2,1)S(1)}, u32[]{:S(2)}, u32[]{:S(2)}) %collective-permute-start.13) | collective-permute-done | bytes 131104 | tf_op jit(solution)/shard_map/ppermute | solution.py:615
  48.4 0.9 %shard_map.102 = (f32[16,8,256]{2,1,0:T(8,128)S(1)}, f32[16,8,256]{2,1,0:T(8,128)S(1)}, f32[16,8,256]{2,1,0:T(8,128)S(1)}, f32[16,8,256]{2,1,0:T(8,128)S(1)}, bf16[32,8,256]{2,1,0:T(8,128)(2,1)S(1)}) custom-call(bf16[32,8,256]{2,1,0:T(8,128)(2,1)S(1)} %collective-permute-done.13.refs_0_, ...), custom_call_target="tpu_custom_call", output_to_operand_aliasing={{0}: (6, {}), {1}: (7, {}), {2}: (8, {}), {3}: (9, {})} | custom-call | flops 5000000000 | bytes 1000000 | tf_op jit(solution)/shard_map/pallas_call | solution.py:575
  49.3 2.4 %collective-permute-start.15 = (bf16[32,8,256]{2,1,0:T(8,128)(2,1)S(1)}, bf16[32,8,256]{2,1,0:T(8,128)(2,1)S(1)}, u32[]{:S(2)}, u32[]{:S(2)}) collective-permute-start(bf16[32,8,256]{2,1,0:T(8,128)(2,1)S(1)} %get-tuple-element.207), channel_id=1, source_target_pairs={{8,0},{0,8},{16,24},{24,16},{9,1},{1,9},{17,25},{25,17},{10,2},{2,... | collective-permute-start | bytes 393224 | tf_op jit(solution)/shard_map/ppermute | solution.py:615
  51.7 0.9 %shard_map.103 = (f32[16,8,256]{2,1,0:T(8,128)S(1)}, f32[16,8,256]{2,1,0:T(8,128)S(1)}, f32[16,8,256]{2,1,0:T(8,128)S(1)}, f32[16,8,256]{2,1,0:T(8,128)S(1)}, bf16[32,8,256]{2,1,0:T(8,128)(2,1)S(1)}) custom-call(bf16[32,8,256]{2,1,0:T(8,128)(2,1)S(1)} %collective-permute-done.16.refs_0_, ...), custom_call_target="tpu_custom_call", output_to_operand_aliasing={{0}: (6, {}), {1}: (7, {}), {2}: (8, {}), {3}: (9, {})} | custom-call | flops 5000000000 | bytes 1000000 | tf_op jit(solution)/shard_map/pallas_call | solution.py:575
  52.7 1.9 %collective-permute-start.17 = (bf16[32,8,256]{2,1,0:T(8,128)(2,1)S(1)}, bf16[32,8,256]{2,1,0:T(8,128)(2,1)S(1)}, u32[]{:S(2)}, u32[]{:S(2)}) collective-permute-start(bf16[32,8,256]{2,1,0:T(8,128)(2,1)S(1)} %get-tuple-element.213), channel_id=1, source_target_pairs={{8,0},{0,8},{16,24},{24,16},{9,1},{1,9},{17,25},{25,17},{10,2},{2,... | collective-permute-start | bytes 393224 | tf_op jit(solution)/shard_map/ppermute | solution.py:615
  55.9 1.0 %shard_map.107 = f32[16,64,256]{2,1,0:T(8,128)} custom-call(f32[16,32,256]{2,1,0:T(8,128)S(1)} %get-tuple-element.229.here, f32[16,32,256]{2,1,0:T(8,128)S(1)} %get-tuple-element.231.far, f32[16,32,256]{2,1,0:T(8,128)S(1)} %collective-permute-done.18.other), custom_call_target="tpu_custom_call" | custom-call | flops 1000000000 | bytes 1000000 | tf_op jit(solution)/shard_map/pallas_call | solution.py:575
  57.7 0.9 %collective-permute-done.17.refs_0_ = bf16[32,8,256]{2,1,0:T(8,128)(2,1)S(1)} collective-permute-done((bf16[32,8,256]{2,1,0:T(8,128)(2,1)S(1)}, bf16[32,8,256]{2,1,0:T(8,128)(2,1)S(1)}, u32[]{:S(2)}, u32[]{:S(2)}) %collective-permute-start.17) | collective-permute-done | bytes 131104 | tf_op jit(solution)/shard_map/ppermute | solution.py:615
  59.5 0.9 %collective-permute-done.22.refs_3_ = f32[16,8,256]{2,1,0:T(8,128)S(1)} collective-permute-done((f32[16,8,256]{2,1,0:T(8,128)S(1)}, f32[16,8,256]{2,1,0:T(8,128)S(1)}, u32[]{:S(2)}, u32[]{:S(2)}) %collective-permute-start.22) | collective-permute-done | bytes 131104 | tf_op jit(solution)/shard_map/ppermute | solution.py:590
  (48 shorter events, 8.7 us)
Async XLA Ops:
  4.3 2.1 %collective-permute-start = (bf16[128,8,256]{2,1,0:T(8,128)(2,1)S(1)}, bf16[128,8,256]{2,1,0:T(8,128)(2,1)S(1)}, u32[]{:S(2)}, u32[]{:S(2)}) collective-permute-start(bf16[128,8,256]{2,1,0:T(8,128)(2,1)S(1)} %get-tuple-element.124), channel_id=1, source_target_pairs={{0,4},{4,0},{1,5},{5,1},{2,6},{6,2},{3,7},{7,3},{8,12},{12,8},{9,1... | collective-permute-start | bytes 1572872 | tf_op jit(solution)/shard_map/ppermute | solution.py:590
  6.4 6.8 %collective-permute-start.3 = (bf16[16,256,256]{2,1,0:T(8,128)(2,1)S(1)}, bf16[16,256,256]{2,1,0:T(8,128)(2,1)S(1)}, u32[]{:S(2)}, u32[]{:S(2)}) collective-permute-start(bf16[16,256,256]{2,1,0:T(8,128)(2,1)S(1)} %get-tuple-element.132.refs_3_.refs_7_.up_own), channel_id=1, source_target_pairs={{0,4},{4,0},{1,5},{5,1},{2,6},{6,2},{3,7},{7,3},{8,12},{12,8},{9,1... | collective-permute-start | bytes 6291464 | tf_op jit(solution)/shard_map/ppermute | solution.py:590
  6.8 6.3 %collective-permute-start.2 = (bf16[32,8,256]{2,1,0:T(8,128)(2,1)S(1)}, bf16[32,8,256]{2,1,0:T(8,128)(2,1)S(1)}, u32[]{:S(2)}, u32[]{:S(2)}) collective-permute-start(bf16[32,8,256]{2,1,0:T(8,128)(2,1)S(1)} %shard_map.87), channel_id=1, source_target_pairs={{0,8},{8,0},{16,24},{24,16},{1,9},{9,1},{17,25},{25,17},{2,10},{10... | collective-permute-start | bytes 393224 | tf_op jit(solution)/shard_map/ppermute | solution.py:615
  8.6 4.5 %collective-permute-start.1 = (f32[16,32,256]{2,1,0:T(8,128)S(1)}, f32[16,32,256]{2,1,0:T(8,128)S(1)}, u32[]{:S(2)}, u32[]{:S(2)}) collective-permute-start(f32[16,32,256]{2,1,0:T(8,128)S(1)} %get-tuple-element.125), channel_id=1, source_target_pairs={{0,4},{4,0},{1,5},{5,1},{2,6},{6,2},{3,7},{7,3},{8,12},{12,8},{9,1... | collective-permute-start | bytes 1572872 | tf_op jit(solution)/shard_map/ppermute | solution.py:590
  8.7 7.2 %collective-permute-start.5 = (bf16[32,8,256]{2,1,0:T(8,128)(2,1)S(1)}, bf16[32,8,256]{2,1,0:T(8,128)(2,1)S(1)}, u32[]{:S(2)}, u32[]{:S(2)}) collective-permute-start(bf16[32,8,256]{2,1,0:T(8,128)(2,1)S(1)} %shard_map.88), channel_id=1, source_target_pairs={{0,8},{8,0},{16,24},{24,16},{1,9},{9,1},{17,25},{25,17},{2,10},{10... | collective-permute-start | bytes 393224 | tf_op jit(solution)/shard_map/ppermute | solution.py:615
  12.4 13.1 %collective-permute-start.8 = (bf16[34,256,256]{2,1,0:T(8,128)(2,1)S(1)}, bf16[34,256,256]{2,1,0:T(8,128)(2,1)S(1)}, u32[]{:S(2)}, u32[]{:S(2)}) collective-permute-start(bf16[34,256,256]{2,1,0:T(8,128)(2,1)S(1)} %shard_map.89.own.refs_3_.refs_1_), channel_id=1, source_target_pairs={{0,4},{4,0},{1,5},{5,1},{2,6},{6,2},{3,7},{7,3},{8,12},{12,8},{9,1... | collective-permute-start | bytes 13369352 | tf_op jit(solution)/shard_map/ppermute | solution.py:590
  13.2 6.6 %collective-permute-start.4 = (bf16[32,8,256]{2,1,0:T(8,128)(2,1)S(1)}, bf16[32,8,256]{2,1,0:T(8,128)(2,1)S(1)}, u32[]{:S(2)}, u32[]{:S(2)}) collective-permute-start(bf16[32,8,256]{2,1,0:T(8,128)(2,1)S(1)} %get-tuple-element.136), channel_id=1, source_target_pairs={{8,16},{0,8},{16,24},{24,0},{9,17},{1,9},{17,25},{25,1},{10,18},{2... | collective-permute-start | bytes 393224 | tf_op jit(solution)/shard_map/ppermute | solution.py:615
  15.9 7.2 %collective-permute-start.7 = (bf16[32,8,256]{2,1,0:T(8,128)(2,1)S(1)}, bf16[32,8,256]{2,1,0:T(8,128)(2,1)S(1)}, u32[]{:S(2)}, u32[]{:S(2)}) collective-permute-start(bf16[32,8,256]{2,1,0:T(8,128)(2,1)S(1)} %get-tuple-element.140), channel_id=1, source_target_pairs={{8,16},{0,8},{16,24},{24,0},{9,17},{1,9},{17,25},{25,1},{10,18},{2... | collective-permute-start | bytes 393224 | tf_op jit(solution)/shard_map/ppermute | solution.py:615
  19.9 7.2 %collective-permute-start.6 = (bf16[32,8,256]{2,1,0:T(8,128)(2,1)S(1)}, bf16[32,8,256]{2,1,0:T(8,128)(2,1)S(1)}, u32[]{:S(2)}, u32[]{:S(2)}) collective-permute-start(bf16[32,8,256]{2,1,0:T(8,128)(2,1)S(1)} %get-tuple-element.147), channel_id=1, source_target_pairs={{16,24},{8,16},{0,8},{24,0},{17,25},{9,17},{1,9},{25,1},{18,26},{1... | collective-permute-start | bytes 393224 | tf_op jit(solution)/shard_map/ppermute | solution.py:615
  23.3 6.6 %collective-permute-start.10 = (bf16[32,8,256]{2,1,0:T(8,128)(2,1)S(1)}, bf16[32,8,256]{2,1,0:T(8,128)(2,1)S(1)}, u32[]{:S(2)}, u32[]{:S(2)}) collective-permute-start(bf16[32,8,256]{2,1,0:T(8,128)(2,1)S(1)} %get-tuple-element.154), channel_id=1, source_target_pairs={{16,24},{8,16},{0,8},{24,0},{17,25},{9,17},{1,9},{25,1},{18,26},{1... | collective-permute-start | bytes 393224 | tf_op jit(solution)/shard_map/ppermute | solution.py:615
  27.2 7.1 %collective-permute-start.9 = (bf16[32,8,256]{2,1,0:T(8,128)(2,1)S(1)}, bf16[32,8,256]{2,1,0:T(8,128)(2,1)S(1)}, u32[]{:S(2)}, u32[]{:S(2)}) collective-permute-start(bf16[32,8,256]{2,1,0:T(8,128)(2,1)S(1)} %get-tuple-element.166), channel_id=1, source_target_pairs={{24,16},{16,24},{0,8},{8,0},{25,17},{17,25},{1,9},{9,1},{26,18},{1... | collective-permute-start | bytes 393224 | tf_op jit(solution)/shard_map/ppermute | solution.py:615
  30.1 7.7 %collective-permute-start.12 = (bf16[32,8,256]{2,1,0:T(8,128)(2,1)S(1)}, bf16[32,8,256]{2,1,0:T(8,128)(2,1)S(1)}, u32[]{:S(2)}, u32[]{:S(2)}) collective-permute-start(bf16[32,8,256]{2,1,0:T(8,128)(2,1)S(1)} %get-tuple-element.172), channel_id=1, source_target_pairs={{24,16},{16,24},{0,8},{8,0},{25,17},{17,25},{1,9},{9,1},{26,18},{1... | collective-permute-start | bytes 393224 | tf_op jit(solution)/shard_map/ppermute | solution.py:615
  34.4 6.7 %collective-permute-start.11 = (bf16[32,8,256]{2,1,0:T(8,128)(2,1)S(1)}, bf16[32,8,256]{2,1,0:T(8,128)(2,1)S(1)}, u32[]{:S(2)}, u32[]{:S(2)}) collective-permute-start(bf16[32,8,256]{2,1,0:T(8,128)(2,1)S(1)} %get-tuple-element.185), channel_id=1, source_target_pairs={{16,8},{24,16},{0,24},{8,0},{17,9},{25,17},{1,25},{9,1},{18,10},{2... | collective-permute-start | bytes 393224 | tf_op jit(solution)/shard_map/ppermute | solution.py:615
  38.0 6.4 %collective-permute-start.14 = (bf16[32,8,256]{2,1,0:T(8,128)(2,1)S(1)}, bf16[32,8,256]{2,1,0:T(8,128)(2,1)S(1)}, u32[]{:S(2)}, u32[]{:S(2)}) collective-permute-start(bf16[32,8,256]{2,1,0:T(8,128)(2,1)S(1)} %get-tuple-element.189), channel_id=1, source_target_pairs={{16,8},{24,16},{0,24},{8,0},{17,9},{25,17},{1,25},{9,1},{18,10},{2... | collective-permute-start | bytes 393224 | tf_op jit(solution)/shard_map/ppermute | solution.py:615
  41.0 14.9 %collective-permute-start.18 = (f32[16,32,256]{2,1,0:T(8,128)S(1)}, f32[16,32,256]{2,1,0:T(8,128)S(1)}, u32[]{:S(2)}, u32[]{:S(2)}) collective-permute-start(f32[16,32,256]{2,1,0:T(8,128)S(1)} %get-tuple-element.231.far), channel_id=1, source_target_pairs={{0,4},{4,0},{1,5},{5,1},{2,6},{6,2},{3,7},{7,3},{8,12},{12,8},{9,1... | collective-permute-start | bytes 1572872 | tf_op jit(solution)/shard_map/ppermute | solution.py:590
  41.1 7.2 %collective-permute-start.13 = (bf16[32,8,256]{2,1,0:T(8,128)(2,1)S(1)}, bf16[32,8,256]{2,1,0:T(8,128)(2,1)S(1)}, u32[]{:S(2)}, u32[]{:S(2)}) collective-permute-start(bf16[32,8,256]{2,1,0:T(8,128)(2,1)S(1)} %get-tuple-element.195), channel_id=1, source_target_pairs={{8,0},{16,8},{0,24},{24,16},{9,1},{17,9},{1,25},{25,17},{10,2},{18... | collective-permute-start | bytes 393224 | tf_op jit(solution)/shard_map/ppermute | solution.py:615
  44.5 7.2 %collective-permute-start.16 = (bf16[32,8,256]{2,1,0:T(8,128)(2,1)S(1)}, bf16[32,8,256]{2,1,0:T(8,128)(2,1)S(1)}, u32[]{:S(2)}, u32[]{:S(2)}) collective-permute-start(bf16[32,8,256]{2,1,0:T(8,128)(2,1)S(1)} %get-tuple-element.201), channel_id=1, source_target_pairs={{8,0},{16,8},{0,24},{24,16},{9,1},{17,9},{1,25},{25,17},{10,2},{18... | collective-permute-start | bytes 393224 | tf_op jit(solution)/shard_map/ppermute | solution.py:615
  49.3 5.5 %collective-permute-start.15 = (bf16[32,8,256]{2,1,0:T(8,128)(2,1)S(1)}, bf16[32,8,256]{2,1,0:T(8,128)(2,1)S(1)}, u32[]{:S(2)}, u32[]{:S(2)}) collective-permute-start(bf16[32,8,256]{2,1,0:T(8,128)(2,1)S(1)} %get-tuple-element.207), channel_id=1, source_target_pairs={{8,0},{0,8},{16,24},{24,16},{9,1},{1,9},{17,25},{25,17},{10,2},{2,... | collective-permute-start | bytes 393224 | tf_op jit(solution)/shard_map/ppermute | solution.py:615
  52.6 4.3 %collective-permute-start.20 = (f32[16,8,256]{2,1,0:T(8,128)S(1)}, f32[16,8,256]{2,1,0:T(8,128)S(1)}, u32[]{:S(2)}, u32[]{:S(2)}) collective-permute-start(f32[16,8,256]{2,1,0:T(8,128)S(1)} %get-tuple-element.235), channel_id=1, source_target_pairs={{0,4},{4,0},{1,5},{5,1},{2,6},{6,2},{3,7},{7,3},{8,12},{12,8},{9,1... | collective-permute-start | bytes 393224 | tf_op jit(solution)/shard_map/ppermute | solution.py:590
  52.7 6.0 %collective-permute-start.17 = (bf16[32,8,256]{2,1,0:T(8,128)(2,1)S(1)}, bf16[32,8,256]{2,1,0:T(8,128)(2,1)S(1)}, u32[]{:S(2)}, u32[]{:S(2)}) collective-permute-start(bf16[32,8,256]{2,1,0:T(8,128)(2,1)S(1)} %get-tuple-element.213), channel_id=1, source_target_pairs={{8,0},{0,8},{16,24},{24,16},{9,1},{1,9},{17,25},{25,17},{10,2},{2,... | collective-permute-start | bytes 393224 | tf_op jit(solution)/shard_map/ppermute | solution.py:615
  54.6 2.3 %collective-permute-start.19 = (f32[16,8,256]{2,1,0:T(8,128)S(1)}, f32[16,8,256]{2,1,0:T(8,128)S(1)}, u32[]{:S(2)}, u32[]{:S(2)}) collective-permute-start(f32[16,8,256]{2,1,0:T(8,128)S(1)} %get-tuple-element.234), channel_id=1, source_target_pairs={{0,4},{4,0},{1,5},{5,1},{2,6},{6,2},{3,7},{7,3},{8,12},{12,8},{9,1... | collective-permute-start | bytes 393224 | tf_op jit(solution)/shard_map/ppermute | solution.py:590
  55.2 4.3 %collective-permute-start.21 = (f32[16,8,256]{2,1,0:T(8,128)S(1)}, f32[16,8,256]{2,1,0:T(8,128)S(1)}, u32[]{:S(2)}, u32[]{:S(2)}) collective-permute-start(f32[16,8,256]{2,1,0:T(8,128)S(1)} %shard_map.104), channel_id=1, source_target_pairs={{0,4},{4,0},{1,5},{5,1},{2,6},{6,2},{3,7},{7,3},{8,12},{12,8},{9,1... | collective-permute-start | bytes 393224 | tf_op jit(solution)/shard_map/ppermute | solution.py:590
  59.1 1.4 %collective-permute-start.22 = (f32[16,8,256]{2,1,0:T(8,128)S(1)}, f32[16,8,256]{2,1,0:T(8,128)S(1)}, u32[]{:S(2)}, u32[]{:S(2)}) collective-permute-start(f32[16,8,256]{2,1,0:T(8,128)S(1)} %shard_map.109), channel_id=1, source_target_pairs={{0,4},{4,0},{1,5},{5,1},{2,6},{6,2},{3,7},{7,3},{8,12},{12,8},{9,1... | collective-permute-start | bytes 393224 | tf_op jit(solution)/shard_map/ppermute | solution.py:590

commit v6 on v5

--- a/solution.py
+++ b/solution.py
@@ -193,6 +193,7 @@
 
 
 NODE_ROWS = 8
+CROSS, OTHER, BELOW, LAST = "c", "o", "b", "l"
 LOAD_NODES = 4
 COSTS = [10000000000, 30000000000, 30000000000, 5000000000, 5000000000, 5000000000, 5000000000, 5000000000]
 SMALL_VMEM_BYTES = 12 * 2**20
@@ -359,7 +360,11 @@
 def send_solved(c, at):
     if "sent" in at:
         solved = jnp.concatenate([flat(at["sol_own", c][...]), flat(at["sol_far", c][...])], axis=0).astype(BF16)
-        at["sent"][...] = dot(at["choose"][...], solved).reshape(at["sent"].shape).astype(BF16)
+        rows = dot(at["choose"][...], solved)
+        rows = rows.reshape(rows.shape[0] // NODE_ROWS, NODE_ROWS, rows.shape[1]).astype(BF16)
+        at["sent"][...] = rows[: at["sent"].shape[0]]
+        if CROSS in at:
+            at[CROSS][...] = rows[at["sent"].shape[0] :]
 
 
 def top_role(c, at):
@@ -384,19 +389,13 @@
     send_solved(c, at)
 
 
-def back_far_role(c, at):
-    base = at["low_base", c]
-    count = base.shape[0] // 2
+def last_role(c, at):
+    count = at["sol_own", c].shape[0]
     for node in range(count):
-        above = at["received"][count + node]
-        at["sol_far", c][node] = base[count + node] - dot(above, at["down_far"][count + node])
-
-
-def back_own_role(c, at):
-    base = at["low_base", c]
-    count = base.shape[0] // 2
-    for node in range(count):
-        at["sol_own", c][node] = base[node] - dot(at["received"][node], at["down_own"][count + node])
+        above = jnp.concatenate([at["received"][node].astype(F32), at[CROSS][node].astype(F32)], axis=0)
+        solved = dot(above.astype(BF16), at["down_own"][count + node])
+        at["sol_own", c][node] = at["low_base", c][node] - solved[:NODE_ROWS]
+        at[OTHER, c][node] = at[BELOW][node] - solved[NODE_ROWS:]
 
 
 def sum_role(c, at):
@@ -404,22 +403,19 @@
     at["sent"][...] = (at["home"][rows] + at["swapped"][rows].astype(F32)).astype(BF16)
 
 
-FAR, OWN = "f", "o"
-ROLES = {"tier": tier_role, "top": top_role, "back": back_role, FAR: back_far_role, OWN: back_own_role, "sum": sum_role}
+ROLES = {"tier": tier_role, "top": top_role, "back": back_role, LAST: last_role, "sum": sum_role}
 READS = {
     "tier": ("rhs_own", "rhs_far", "received", "up_own", "up_far", "select"),
     "top": ("rhs_own", "rhs_far", "received", "down_own", "down_far", "choose", "top_base"),
     "back": ("received", "down_own", "down_far", "choose", "low_base"),
-    FAR: ("received", "down_far", "low_base"),
-    OWN: ("received", "down_own", "low_base"),
+    LAST: ("received", CROSS, "down_own", "low_base", BELOW),
     "sum": ("home", "swapped"),
 }
 WRITES = {
     "tier": ("residue", "own", "far"),
     "top": ("residue", "sol_own", "sol_far"),
     "back": ("sol_own", "sol_far"),
-    FAR: ("sol_far",),
-    OWN: ("sol_own",),
+    LAST: ("sol_own", OTHER),
     "sum": (),
 }
 
@@ -434,7 +430,7 @@
         pl.when(lax.axis_index(LEVEL) == level)(functools.partial(ROLES[role], c, {**reads, **outs}))
 
 
-def step(plan, state, sends=True, flops=10**9):
+def step(plan, state, sends=1, flops=10**9):
     nodes = state["nodes"]
     in_keys, out_keys = [], []
     for _, role, c in plan:
@@ -450,13 +446,12 @@
         of = nodes if name == "residue" else nodes // 2
         outs.append(jax.ShapeDtypeStruct((of, NODE_ROWS, width), F32))
     aliases = {len(in_keys) + i: out_keys.index(key) for i, key in enumerate(kept_keys)}
-    all_outs = out_keys + (["sent"] if sends else [])
-    if sends:
-        outs.append(jax.ShapeDtypeStruct((nodes, NODE_ROWS, width), BF16))
+    all_outs = out_keys + ["sent", CROSS][:sends]
+    outs += [jax.ShapeDtypeStruct((nodes // max(sends, 1), NODE_ROWS, width), BF16)] * sends
     operands = [state[key] for key in in_keys + kept_keys]
     results = run(functools.partial(step_kernel, plan, in_keys, all_outs, kept_keys), operands, outs, aliases, flops)
     state.update(zip(out_keys, results))
-    return results[-1] if sends else None
+    return results[len(out_keys) :]
 
 
 def rows_together(chunks, node):
@@ -468,7 +463,8 @@
         chunk[node] = value[NODE_ROWS * c : NODE_ROWS * (c + 1)]
 
 
-def base_kernel(rhs_own, rhs_far, own, far, *refs):
+def base_kernel(rhs_own, rhs_far, rhs_sent, own, far, *refs):
+    *refs, below = refs
     residue, base = refs[: len(refs) // 2], refs[len(refs) // 2 :]
     count = rhs_own.shape[0]
     level, top = lax.axis_index(LEVEL), lax.axis_size(LEVEL) - 1
@@ -476,7 +472,10 @@
     @pl.when(level == 0)
     def _():
         for node in range(count):
-            apart(dot(rhs_own[node].astype(BF16), own[node]), base, node)
+            both = jnp.concatenate([rhs_own[node], rhs_sent[node, -NODE_ROWS:, :]], axis=0).astype(BF16)
+            solved = dot(both, own[node])
+            apart(solved, base, node)
+            below[node] = solved[-NODE_ROWS:]
             apart(dot(rhs_far[node].astype(BF16), far[node]), base, count + node)
 
     @pl.when((level != 0) & (level != top))
@@ -605,13 +604,16 @@
     def shape(of, dtype):
         return jax.ShapeDtypeStruct((of, NODE_ROWS, width), dtype)
 
-    def passed(value, pairs):
+    def passed(value, pairs, cross=False):
         sources = [i for i in range(levels) if i not in dict(pairs)]
         targets = [i for i in range(levels) if i not in [to for _, to in pairs]]
         fill = min(
             (list(zip(sources, order)) for order in itertools.permutations(targets)),
             key=lambda extra: (sum(a == b for a, b in extra), sum(abs(a - b) for a, b in extra)),
         )
+        if cross:
+            pairs = [(2 * a + s, 2 * b + 1 - s) for a, b in pairs + fill for s in range(2)]
+            return lax.ppermute(value, (LEVEL, SUB), pairs)
         return lax.ppermute(value, LEVEL, pairs + fill)
 
     def after(value, *earlier):
@@ -679,12 +681,18 @@
                         pairs.append((low, low - 1))
             if received[p] is not None:
                 state["received"] = after(received[p], *pace)
-            if k == last:
-                step([(0, FAR, pipe[-1])], state, False, COSTS[k])
+            split = k == last - 1 and p == len(pipes) - 1
+            if k == last and p == len(pipes) - 1:
+                state[CROSS], state[OTHER, pipe[-1]] = cross, other[pipe[-1]]
+                plan = [(0, LAST, pipe[-1])]
+            sent, *sent_cross = step(plan, state, 2 if split else bool(pairs), COSTS[k]) or [None]
+            if k == last and p == len(pipes) - 1:
+                other[pipe[-1]] = state[OTHER, pipe[-1]]
+            elif k == last:
                 other[pipe[-1]] = exchanged(state["sol_far", pipe[-1]])
-                plan = [(0, OWN, pipe[-1])]
-                state["received"] = after(state["received"], state["sol_far", pipe[-1]])
-            sent = step(plan, state, bool(pairs), COSTS[k])
+            if split:
+                cross = passed(sent_cross[0], pairs, cross=True)
+                other[pipe[-1]] = exchanged(state["sol_far", pipe[-1]])
             pace = [sent] if pairs else [state["sol_own", pipe[-1]]]
             if pairs:
                 received[p] = passed(sent, pairs)
@@ -716,10 +724,10 @@
             pace += bases
         residues = [state["residue", c] for c in range(chunks)] if k >= top else []
         if k == top:
-            bases = run(
+            *bases, state[BELOW] = run(
                 base_kernel,
-                (after(rhs_own, sent), state["rhs_far"], state["down_own"], state["down_far"], *residues),
-                [shape(nodes, F32)] * chunks,
+                (after(rhs_own, sent), state["rhs_far"], rhs_sent, state["down_own"], state["down_far"], *residues),
+                [shape(nodes, F32)] * chunks + [shape(count, F32)],
             )
             state.update({("low_base", c): bases[c] for c in range(chunks)})
             pace += bases

time: 61.6 us -> 59.8 us (0.971)
  waiting for transfers between devices: 9.43 us -> 7.6 us
    ppermute x9, waiting for transfers between devices: 2.49 us -> 1.56 us  [exchanged(): return lax.ppermute(value, SUB, [(0, 1), (1, 0)])]
    ppermute x14, waiting for transfers between devices: 6.94 us -> 6.04 us  [passed(): return lax.ppermute(value, LEVEL, pairs + fill)]
    pallas_call x26 -> x24, Pallas kernels: 15 us -> 14.5 us  [run(): pl.pallas_call(kernel, in_specs=in_specs, out_specs=out_specs, out_shape=...]
  transfers between devices with their start and end apart: 23 -> 24, of which waited for: 9 -> 7; matrix products, arithmetic and copies ran while one was open for 0% -> 0% of each run, Pallas kernels for 17% -> 17%
where the time goes in v6:
time: 59.8 us; the launch traced here: 59.6 us
  starting transfers between devices  36.5 us (61%)
  Pallas kernels  14.5 us (24%)
  waiting for transfers between devices  7.6 us (13%)
  between operations  1 us (2%)
    ppermute x14, starting transfers between devices, passed(): return lax.ppermute(value, LEVEL, pairs + fill)  33.9 us
    pallas_call x24, Pallas kernels, run(): pl.pallas_call(kernel, in_specs=in_specs, out_specs=out_specs, out_shape=...  14.5 us
    ppermute x14, waiting for transfers between devices, passed(): return lax.ppermute(value, LEVEL, pairs + fill)  6.04 us
    ppermute x9, starting transfers between devices, exchanged(): return lax.ppermute(value, SUB, [(0, 1), (1, 0)])  2.55 us
    ppermute x9, waiting for transfers between devices, exchanged(): return lax.ppermute(value, SUB, [(0, 1), (1, 0)])  1.56 us
  transfers between devices with their start and end apart: 24, of which 7 were waited for; matrix products, arithmetic and copies ran while one was open for 0% of the time, Pallas kernels for 17%

profile of v6, /device:TPU:0, one launch (start us, length us, event | category | flops | bytes accessed | tf_op | source)
XLA Modules:
  0.0 59.6 jit_solution(17816926809196644077)
XLA Ops:
  0.6 3.7 %shard_map.86 = (bf16[256,256]{1,0:T(8,128)(2,1)S(1)}, bf16[256,256]{1,0:T(8,128)(2,1)S(1)}, f32[16,32,256]{2,1,0:T(8,128)S(1)}, f32[16,32,256]{2,1,0:T(8,128)S(...) custom-call(s32[3,32]{1,0:T(4,128)} %parent.1, ...), custom_call_target="tpu_custom_call" | custom-call | flops 1000000000 | bytes 1000000 | tf_op jit(solution)/shard_map/pallas_call | solution.py:574
  4.8 1.5 %collective-permute-done.refs_1_.refs_7_ = bf16[128,8,256]{2,1,0:T(8,128)(2,1)S(1)} collective-permute-done((bf16[128,8,256]{2,1,0:T(8,128)(2,1)S(1)}, bf16[128,8,256]{2,1,0:T(8,128)(2,1)S(1)}, u32[]{:S(2)}, u32[]{:S(2)}) %collective-permute-start) | collective-permute-done | bytes 524320 | tf_op jit(solution)/shard_map/ppermute | solution.py:589
  6.8 1.8 %collective-permute-start.2 = (bf16[32,8,256]{2,1,0:T(8,128)(2,1)S(1)}, bf16[32,8,256]{2,1,0:T(8,128)(2,1)S(1)}, u32[]{:S(2)}, u32[]{:S(2)}) collective-permute-start(bf16[32,8,256]{2,1,0:T(8,128)(2,1)S(1)} %shard_map.87), channel_id=1, source_target_pairs={{0,8},{8,0},{16,24},{24,16},{1,9},{9,1},{17,25},{25,17},{2,10},{10... | collective-permute-start | bytes 393224 | tf_op jit(solution)/shard_map/ppermute | solution.py:617
  9.0 3.5 %shard_map.89.own.refs_3_.refs_1_.refs_2_ = bf16[34,256,256]{2,1,0:T(8,128)(2,1)S(1)} custom-call(bf16[16,256,256]{2,1,0:T(8,128)(2,1)} %bitcast.8, bf16[16,256,256]{2,1,0:T(8,128)(2,1)} %bitcast.10, bf16[16,256,256]{2,1,0:T(8,128)(2,1)} %bitcast.11, bf16[16,64,256]{2,1,0:T(8,128)(2,1)} %ancestor.1), custom_call_target="tpu_custom_call" | custom-call | flops 1000000000 | bytes 1000000 | tf_op jit(solution)/shard_map/pallas_call | solution.py:574
  13.2 2.7 %collective-permute-start.4 = (bf16[32,8,256]{2,1,0:T(8,128)(2,1)S(1)}, bf16[32,8,256]{2,1,0:T(8,128)(2,1)S(1)}, u32[]{:S(2)}, u32[]{:S(2)}) collective-permute-start(bf16[32,8,256]{2,1,0:T(8,128)(2,1)S(1)} %get-tuple-element.140), channel_id=1, source_target_pairs={{8,16},{0,8},{16,24},{24,0},{9,17},{1,9},{17,25},{25,1},{10,18},{2... | collective-permute-start | bytes 393224 | tf_op jit(solution)/shard_map/ppermute | solution.py:617
  15.9 2.2 %collective-permute-start.7 = (bf16[32,8,256]{2,1,0:T(8,128)(2,1)S(1)}, bf16[32,8,256]{2,1,0:T(8,128)(2,1)S(1)}, u32[]{:S(2)}, u32[]{:S(2)}) collective-permute-start(bf16[32,8,256]{2,1,0:T(8,128)(2,1)S(1)} %get-tuple-element.144), channel_id=1, source_target_pairs={{8,16},{0,8},{16,24},{24,0},{9,17},{1,9},{17,25},{25,1},{10,18},{2... | collective-permute-start | bytes 393224 | tf_op jit(solution)/shard_map/ppermute | solution.py:617
  18.1 1.7 %collective-permute-done.4.refs_2_ = bf16[32,8,256]{2,1,0:T(8,128)(2,1)S(1)} collective-permute-done((bf16[32,8,256]{2,1,0:T(8,128)(2,1)S(1)}, bf16[32,8,256]{2,1,0:T(8,128)(2,1)S(1)}, u32[]{:S(2)}, u32[]{:S(2)}) %collective-permute-start.4) | collective-permute-done | bytes 131104 | tf_op jit(solution)/shard_map/ppermute | solution.py:617
  19.9 3.3 %collective-permute-start.6 = (bf16[32,8,256]{2,1,0:T(8,128)(2,1)S(1)}, bf16[32,8,256]{2,1,0:T(8,128)(2,1)S(1)}, u32[]{:S(2)}, u32[]{:S(2)}) collective-permute-start(bf16[32,8,256]{2,1,0:T(8,128)(2,1)S(1)} %get-tuple-element.151), channel_id=1, source_target_pairs={{16,24},{8,16},{0,8},{24,0},{17,25},{9,17},{1,9},{25,1},{18,26},{1... | collective-permute-start | bytes 393224 | tf_op jit(solution)/shard_map/ppermute | solution.py:617
  23.3 2.2 %collective-permute-start.10 = (bf16[32,8,256]{2,1,0:T(8,128)(2,1)S(1)}, bf16[32,8,256]{2,1,0:T(8,128)(2,1)S(1)}, u32[]{:S(2)}, u32[]{:S(2)}) collective-permute-start(bf16[32,8,256]{2,1,0:T(8,128)(2,1)S(1)} %get-tuple-element.158), channel_id=1, source_target_pairs={{16,24},{8,16},{0,8},{24,0},{17,25},{9,17},{1,9},{25,1},{18,26},{1... | collective-permute-start | bytes 393224 | tf_op jit(solution)/shard_map/ppermute | solution.py:617
  25.5 1.5 %collective-permute-done.6.refs_2_ = bf16[32,8,256]{2,1,0:T(8,128)(2,1)S(1)} collective-permute-done((bf16[32,8,256]{2,1,0:T(8,128)(2,1)S(1)}, bf16[32,8,256]{2,1,0:T(8,128)(2,1)S(1)}, u32[]{:S(2)}, u32[]{:S(2)}) %collective-permute-start.6) | collective-permute-done | bytes 131104 | tf_op jit(solution)/shard_map/ppermute | solution.py:617
  27.2 2.5 %collective-permute-start.9 = (bf16[32,8,256]{2,1,0:T(8,128)(2,1)S(1)}, bf16[32,8,256]{2,1,0:T(8,128)(2,1)S(1)}, u32[]{:S(2)}, u32[]{:S(2)}) collective-permute-start(bf16[32,8,256]{2,1,0:T(8,128)(2,1)S(1)} %get-tuple-element.170), channel_id=1, source_target_pairs={{24,16},{16,24},{0,8},{8,0},{25,17},{17,25},{1,9},{9,1},{26,18},{1... | collective-permute-start | bytes 393224 | tf_op jit(solution)/shard_map/ppermute | solution.py:617
  30.1 2.5 %collective-permute-start.12 = (bf16[32,8,256]{2,1,0:T(8,128)(2,1)S(1)}, bf16[32,8,256]{2,1,0:T(8,128)(2,1)S(1)}, u32[]{:S(2)}, u32[]{:S(2)}) collective-permute-start(bf16[32,8,256]{2,1,0:T(8,128)(2,1)S(1)} %get-tuple-element.176), channel_id=1, source_target_pairs={{24,16},{16,24},{0,8},{8,0},{25,17},{17,25},{1,9},{9,1},{26,18},{1... | collective-permute-start | bytes 393224 | tf_op jit(solution)/shard_map/ppermute | solution.py:617
  32.7 0.8 %shard_map.97 = (f32[32,8,256]{2,1,0:T(8,128)S(1)}, f32[32,8,256]{2,1,0:T(8,128)S(1)}, f32[32,8,256]{2,1,0:T(8,128)S(1)}, f32[32,8,256]{2,1,0:T(8,128)S(1)}, f32[16,8,256]{2,1,0:T(8,128)S(1)}) custom-call(f32[16,32,256]{2,1,0:T(8,128)S(1)} %get-tuple-element.177.refs_0_.rhs_own.refs_5_, f32[16,32,256]{2,1,0:T(8,128)S(1)} %collective-permute-done.1.refs_1_.rhs_far.refs_6_, ...), custom_call_target="tpu_custom_call" | custom-call | flops 1000000000 | bytes 1000000 | tf_op jit(solution)/shard_map/pallas_call | solution.py:574
  34.4 3.5 %collective-permute-start.11 = (bf16[32,8,256]{2,1,0:T(8,128)(2,1)S(1)}, bf16[32,8,256]{2,1,0:T(8,128)(2,1)S(1)}, u32[]{:S(2)}, u32[]{:S(2)}) collective-permute-start(bf16[32,8,256]{2,1,0:T(8,128)(2,1)S(1)} %get-tuple-element.189), channel_id=1, source_target_pairs={{16,8},{24,16},{0,24},{8,0},{17,9},{25,17},{1,25},{9,1},{18,10},{2... | collective-permute-start | bytes 393224 | tf_op jit(solution)/shard_map/ppermute | solution.py:617
  38.0 2.9 %collective-permute-start.14 = (bf16[32,8,256]{2,1,0:T(8,128)(2,1)S(1)}, bf16[32,8,256]{2,1,0:T(8,128)(2,1)S(1)}, u32[]{:S(2)}, u32[]{:S(2)}) collective-permute-start(bf16[32,8,256]{2,1,0:T(8,128)(2,1)S(1)} %get-tuple-element.193), channel_id=1, source_target_pairs={{16,8},{24,16},{0,24},{8,0},{17,9},{25,17},{1,25},{9,1},{18,10},{2... | collective-permute-start | bytes 393224 | tf_op jit(solution)/shard_map/ppermute | solution.py:617
  41.1 3.3 %collective-permute-start.13 = (bf16[32,8,256]{2,1,0:T(8,128)(2,1)S(1)}, bf16[32,8,256]{2,1,0:T(8,128)(2,1)S(1)}, u32[]{:S(2)}, u32[]{:S(2)}) collective-permute-start(bf16[32,8,256]{2,1,0:T(8,128)(2,1)S(1)} %get-tuple-element.199), channel_id=1, source_target_pairs={{8,0},{16,8},{0,24},{24,16},{9,1},{17,9},{1,25},{25,17},{10,2},{18... | collective-permute-start | bytes 393224 | tf_op jit(solution)/shard_map/ppermute | solution.py:617
  44.5 2.4 %collective-permute-start.16 = (bf16[32,8,256]{2,1,0:T(8,128)(2,1)S(1)}, bf16[32,8,256]{2,1,0:T(8,128)(2,1)S(1)}, u32[]{:S(2)}, u32[]{:S(2)}) collective-permute-start(bf16[32,8,256]{2,1,0:T(8,128)(2,1)S(1)} %get-tuple-element.205), channel_id=1, source_target_pairs={{8,0},{16,8},{0,24},{24,16},{9,1},{17,9},{1,25},{25,17},{10,2},{18... | collective-permute-start | bytes 393224 | tf_op jit(solution)/shard_map/ppermute | solution.py:617
  46.9 1.5 %collective-permute-done.13.refs_0_ = bf16[32,8,256]{2,1,0:T(8,128)(2,1)S(1)} collective-permute-done((bf16[32,8,256]{2,1,0:T(8,128)(2,1)S(1)}, bf16[32,8,256]{2,1,0:T(8,128)(2,1)S(1)}, u32[]{:S(2)}, u32[]{:S(2)}) %collective-permute-start.13) | collective-permute-done | bytes 131104 | tf_op jit(solution)/shard_map/ppermute | solution.py:617
  48.4 0.9 %shard_map.102 = (f32[16,8,256]{2,1,0:T(8,128)S(1)}, f32[16,8,256]{2,1,0:T(8,128)S(1)}, f32[16,8,256]{2,1,0:T(8,128)S(1)}, f32[16,8,256]{2,1,0:T(8,128)S(1)}, bf16[32,8,256]{2,1,0:T(8,128)(2,1)S(1)}) custom-call(bf16[32,8,256]{2,1,0:T(8,128)(2,1)S(1)} %collective-permute-done.13.refs_0_, ...), custom_call_target="tpu_custom_call", output_to_operand_aliasing={{0}: (6, {}), {1}: (7, {}), {2}: (8, {}), {3}: (9, {})} | custom-call | flops 5000000000 | bytes 1000000 | tf_op jit(solution)/shard_map/pallas_call | solution.py:574
  49.3 2.4 %collective-permute-start.15 = (bf16[32,8,256]{2,1,0:T(8,128)(2,1)S(1)}, bf16[32,8,256]{2,1,0:T(8,128)(2,1)S(1)}, u32[]{:S(2)}, u32[]{:S(2)}) collective-permute-start(bf16[32,8,256]{2,1,0:T(8,128)(2,1)S(1)} %get-tuple-element.211), channel_id=1, source_target_pairs={{8,0},{0,8},{16,24},{24,16},{9,1},{1,9},{17,25},{25,17},{10,2},{2,... | collective-permute-start | bytes 393224 | tf_op jit(solution)/shard_map/ppermute | solution.py:617
  51.7 0.9 %shard_map.103 = (f32[16,8,256]{2,1,0:T(8,128)S(1)}, f32[16,8,256]{2,1,0:T(8,128)S(1)}, f32[16,8,256]{2,1,0:T(8,128)S(1)}, f32[16,8,256]{2,1,0:T(8,128)S(1)}, bf...) custom-call(bf16[32,8,256]{2,1,0:T(8,128)(2,1)S(1)} %collective-perm, ...), custom_call_target="tpu_custom_call", output_to_operand_aliasing={{0}: (6, {}), {1}: (7, {}), {2}: (8, {}), {3}: (9, {})} | custom-call | flops 5000000000 | bytes 1000000 | tf_op jit(solution)/shard_map/pallas_call | solution.py:574
  52.7 1.9 %collective-permute-start.17 = (bf16[16,8,256]{2,1,0:T(8,128)(2,1)S(1)}, bf16[16,8,256]{2,1,0:T(8,128)(2,1)S(1)}, u32[]{:S(2)}, u32[]{:S(2)}) collective-permute-start(bf16[16,8,256]{2,1,0:T(8,128)(2,1)S(1)} %get-tuple-element.217), channel_id=1, source_target_pairs={{8,0},{0,8},{16,24},{24,16},{9,1},{1,9},{17,25},{25,17},{10,2},{2,... | collective-permute-start | bytes 196616 | tf_op jit(solution)/shard_map/ppermute | solution.py:617
  55.8 1.0 %shard_map.106 = f32[16,64,256]{2,1,0:T(8,128)} custom-call(f32[16,32,256]{2,1,0:T(8,128)S(1)} %get-tuple-element.233.here, f32[16,32,256]{2,1,0:T(8,128)S(1)} %get-tuple-element.235.far, f32[16,32,256]{2,1,0:T(8,128)S(1)} %collective-permute-done.18.other), custom_call_target="tpu_custom_call" | custom-call | flops 1000000000 | bytes 1000000 | tf_op jit(solution)/shard_map/pallas_call | solution.py:574
  58.7 0.8 %shard_map.109 = f32[16,64,256]{2,1,0:T(8,128)} custom-call(f32[16,8,256]{2,1,0:T(8,128)S(1)} %get-tuple-element.221.refs_0_, f32[16,8,256]{2,1,0:T(8,128)S(1)} %get-tuple-element.245.refs_1_, f32[16,8,256]{2,1,0:T(8,128)S(1)} %collective-permute-done.23.refs_2_, f32[16,8,256]{2,1,0:T(8,128)S(1)} %get-tuple-element.247.refs_3_, ...), custom_call_target="tpu_custom_call", output_to_operand_aliasing={{}: (4, {})} | custom-call | flops 1000000000 | bytes 1000000 | tf_op jit(solution)/shard_map/pallas_call | solution.py:574
  (48 shorter events, 7.2 us)
Async XLA Ops:
  4.3 2.1 %collective-permute-start = (bf16[128,8,256]{2,1,0:T(8,128)(2,1)S(1)}, bf16[128,8,256]{2,1,0:T(8,128)(2,1)S(1)}, u32[]{:S(2)}, u32[]{:S(2)}) collective-permute-start(bf16[128,8,256]{2,1,0:T(8,128)(2,1)S(1)} %get-tuple-element.128), channel_id=1, source_target_pairs={{0,4},{4,0},{1,5},{5,1},{2,6},{6,2},{3,7},{7,3},{8,12},{12,8},{9,1... | collective-permute-start | bytes 1572872 | tf_op jit(solution)/shard_map/ppermute | solution.py:589
  6.4 6.8 %collective-permute-start.3 = (bf16[16,256,256]{2,1,0:T(8,128)(2,1)S(1)}, bf16[16,256,256]{2,1,0:T(8,128)(2,1)S(1)}, u32[]{:S(2)}, u32[]{:S(2)}) collective-permute-start(bf16[16,256,256]{2,1,0:T(8,128)(2,1)S(1)} %get-tuple-element.136.refs_3_.refs_7_.up_own), channel_id=1, source_target_pairs={{0,4},{4,0},{1,5},{5,1},{2,6},{6,2},{3,7},{7,3},{8,12},{12,8},{9,1... | collective-permute-start | bytes 6291464 | tf_op jit(solution)/shard_map/ppermute | solution.py:589
  6.8 6.3 %collective-permute-start.2 = (bf16[32,8,256]{2,1,0:T(8,128)(2,1)S(1)}, bf16[32,8,256]{2,1,0:T(8,128)(2,1)S(1)}, u32[]{:S(2)}, u32[]{:S(2)}) collective-permute-start(bf16[32,8,256]{2,1,0:T(8,128)(2,1)S(1)} %shard_map.87), channel_id=1, source_target_pairs={{0,8},{8,0},{16,24},{24,16},{1,9},{9,1},{17,25},{25,17},{2,10},{10... | collective-permute-start | bytes 393224 | tf_op jit(solution)/shard_map/ppermute | solution.py:617
  8.6 4.5 %collective-permute-start.1 = (f32[16,32,256]{2,1,0:T(8,128)S(1)}, f32[16,32,256]{2,1,0:T(8,128)S(1)}, u32[]{:S(2)}, u32[]{:S(2)}) collective-permute-start(f32[16,32,256]{2,1,0:T(8,128)S(1)} %get-tuple-element.129.rhs_sent), channel_id=1, source_target_pairs={{0,4},{4,0},{1,5},{5,1},{2,6},{6,2},{3,7},{7,3},{8,12},{12,8},{9,1... | collective-permute-start | bytes 1572872 | tf_op jit(solution)/shard_map/ppermute | solution.py:589
  8.7 7.2 %collective-permute-start.5 = (bf16[32,8,256]{2,1,0:T(8,128)(2,1)S(1)}, bf16[32,8,256]{2,1,0:T(8,128)(2,1)S(1)}, u32[]{:S(2)}, u32[]{:S(2)}) collective-permute-start(bf16[32,8,256]{2,1,0:T(8,128)(2,1)S(1)} %shard_map.88), channel_id=1, source_target_pairs={{0,8},{8,0},{16,24},{24,16},{1,9},{9,1},{17,25},{25,17},{2,10},{10... | collective-permute-start | bytes 393224 | tf_op jit(solution)/shard_map/ppermute | solution.py:617
  12.4 13.1 %collective-permute-start.8 = (bf16[34,256,256]{2,1,0:T(8,128)(2,1)S(1)}, bf16[34,256,256]{2,1,0:T(8,128)(2,1)S(1)}, u32[]{:S(2)}, u32[]{:S(2)}) collective-permute-start(bf16[34,256,256]{2,1,0:T(8,128)(2,1)S(1)} %shard_map.89.own.refs_3_.refs_1_.refs_2_), channel_id=1, source_target_pairs={{0,4},{4,0},{1,5},{5,1},{2,6},{6,2},{3,7},{7,3},{8,12},{12,8},{9,1... | collective-permute-start | bytes 13369352 | tf_op jit(solution)/shard_map/ppermute | solution.py:589
  13.2 6.6 %collective-permute-start.4 = (bf16[32,8,256]{2,1,0:T(8,128)(2,1)S(1)}, bf16[32,8,256]{2,1,0:T(8,128)(2,1)S(1)}, u32[]{:S(2)}, u32[]{:S(2)}) collective-permute-start(bf16[32,8,256]{2,1,0:T(8,128)(2,1)S(1)} %get-tuple-element.140), channel_id=1, source_target_pairs={{8,16},{0,8},{16,24},{24,0},{9,17},{1,9},{17,25},{25,1},{10,18},{2... | collective-permute-start | bytes 393224 | tf_op jit(solution)/shard_map/ppermute | solution.py:617
  15.9 7.2 %collective-permute-start.7 = (bf16[32,8,256]{2,1,0:T(8,128)(2,1)S(1)}, bf16[32,8,256]{2,1,0:T(8,128)(2,1)S(1)}, u32[]{:S(2)}, u32[]{:S(2)}) collective-permute-start(bf16[32,8,256]{2,1,0:T(8,128)(2,1)S(1)} %get-tuple-element.144), channel_id=1, source_target_pairs={{8,16},{0,8},{16,24},{24,0},{9,17},{1,9},{17,25},{25,1},{10,18},{2... | collective-permute-start | bytes 393224 | tf_op jit(solution)/shard_map/ppermute | solution.py:617
  19.9 7.2 %collective-permute-start.6 = (bf16[32,8,256]{2,1,0:T(8,128)(2,1)S(1)}, bf16[32,8,256]{2,1,0:T(8,128)(2,1)S(1)}, u32[]{:S(2)}, u32[]{:S(2)}) collective-permute-start(bf16[32,8,256]{2,1,0:T(8,128)(2,1)S(1)} %get-tuple-element.151), channel_id=1, source_target_pairs={{16,24},{8,16},{0,8},{24,0},{17,25},{9,17},{1,9},{25,1},{18,26},{1... | collective-permute-start | bytes 393224 | tf_op jit(solution)/shard_map/ppermute | solution.py:617
  23.3 6.6 %collective-permute-start.10 = (bf16[32,8,256]{2,1,0:T(8,128)(2,1)S(1)}, bf16[32,8,256]{2,1,0:T(8,128)(2,1)S(1)}, u32[]{:S(2)}, u32[]{:S(2)}) collective-permute-start(bf16[32,8,256]{2,1,0:T(8,128)(2,1)S(1)} %get-tuple-element.158), channel_id=1, source_target_pairs={{16,24},{8,16},{0,8},{24,0},{17,25},{9,17},{1,9},{25,1},{18,26},{1... | collective-permute-start | bytes 393224 | tf_op jit(solution)/shard_map/ppermute | solution.py:617
  27.2 7.1 %collective-permute-start.9 = (bf16[32,8,256]{2,1,0:T(8,128)(2,1)S(1)}, bf16[32,8,256]{2,1,0:T(8,128)(2,1)S(1)}, u32[]{:S(2)}, u32[]{:S(2)}) collective-permute-start(bf16[32,8,256]{2,1,0:T(8,128)(2,1)S(1)} %get-tuple-element.170), channel_id=1, source_target_pairs={{24,16},{16,24},{0,8},{8,0},{25,17},{17,25},{1,9},{9,1},{26,18},{1... | collective-permute-start | bytes 393224 | tf_op jit(solution)/shard_map/ppermute | solution.py:617
  30.1 7.7 %collective-permute-start.12 = (bf16[32,8,256]{2,1,0:T(8,128)(2,1)S(1)}, bf16[32,8,256]{2,1,0:T(8,128)(2,1)S(1)}, u32[]{:S(2)}, u32[]{:S(2)}) collective-permute-start(bf16[32,8,256]{2,1,0:T(8,128)(2,1)S(1)} %get-tuple-element.176), channel_id=1, source_target_pairs={{24,16},{16,24},{0,8},{8,0},{25,17},{17,25},{1,9},{9,1},{26,18},{1... | collective-permute-start | bytes 393224 | tf_op jit(solution)/shard_map/ppermute | solution.py:617
  34.4 6.7 %collective-permute-start.11 = (bf16[32,8,256]{2,1,0:T(8,128)(2,1)S(1)}, bf16[32,8,256]{2,1,0:T(8,128)(2,1)S(1)}, u32[]{:S(2)}, u32[]{:S(2)}) collective-permute-start(bf16[32,8,256]{2,1,0:T(8,128)(2,1)S(1)} %get-tuple-element.189), channel_id=1, source_target_pairs={{16,8},{24,16},{0,24},{8,0},{17,9},{25,17},{1,25},{9,1},{18,10},{2... | collective-permute-start | bytes 393224 | tf_op jit(solution)/shard_map/ppermute | solution.py:617
  38.0 6.4 %collective-permute-start.14 = (bf16[32,8,256]{2,1,0:T(8,128)(2,1)S(1)}, bf16[32,8,256]{2,1,0:T(8,128)(2,1)S(1)}, u32[]{:S(2)}, u32[]{:S(2)}) collective-permute-start(bf16[32,8,256]{2,1,0:T(8,128)(2,1)S(1)} %get-tuple-element.193), channel_id=1, source_target_pairs={{16,8},{24,16},{0,24},{8,0},{17,9},{25,17},{1,25},{9,1},{18,10},{2... | collective-permute-start | bytes 393224 | tf_op jit(solution)/shard_map/ppermute | solution.py:617
  41.0 14.8 %collective-permute-start.18 = (f32[16,32,256]{2,1,0:T(8,128)S(1)}, f32[16,32,256]{2,1,0:T(8,128)S(1)}, u32[]{:S(2)}, u32[]{:S(2)}) collective-permute-start(f32[16,32,256]{2,1,0:T(8,128)S(1)} %get-tuple-element.235.far), channel_id=1, source_target_pairs={{0,4},{4,0},{1,5},{5,1},{2,6},{6,2},{3,7},{7,3},{8,12},{12,8},{9,1... | collective-permute-start | bytes 1572872 | tf_op jit(solution)/shard_map/ppermute | solution.py:589
  41.1 7.2 %collective-permute-start.13 = (bf16[32,8,256]{2,1,0:T(8,128)(2,1)S(1)}, bf16[32,8,256]{2,1,0:T(8,128)(2,1)S(1)}, u32[]{:S(2)}, u32[]{:S(2)}) collective-permute-start(bf16[32,8,256]{2,1,0:T(8,128)(2,1)S(1)} %get-tuple-element.199), channel_id=1, source_target_pairs={{8,0},{16,8},{0,24},{24,16},{9,1},{17,9},{1,25},{25,17},{10,2},{18... | collective-permute-start | bytes 393224 | tf_op jit(solution)/shard_map/ppermute | solution.py:617
  44.5 7.2 %collective-permute-start.16 = (bf16[32,8,256]{2,1,0:T(8,128)(2,1)S(1)}, bf16[32,8,256]{2,1,0:T(8,128)(2,1)S(1)}, u32[]{:S(2)}, u32[]{:S(2)}) collective-permute-start(bf16[32,8,256]{2,1,0:T(8,128)(2,1)S(1)} %get-tuple-element.205), channel_id=1, source_target_pairs={{8,0},{16,8},{0,24},{24,16},{9,1},{17,9},{1,25},{25,17},{10,2},{18... | collective-permute-start | bytes 393224 | tf_op jit(solution)/shard_map/ppermute | solution.py:617
  49.3 5.4 %collective-permute-start.15 = (bf16[32,8,256]{2,1,0:T(8,128)(2,1)S(1)}, bf16[32,8,256]{2,1,0:T(8,128)(2,1)S(1)}, u32[]{:S(2)}, u32[]{:S(2)}) collective-permute-start(bf16[32,8,256]{2,1,0:T(8,128)(2,1)S(1)} %get-tuple-element.211), channel_id=1, source_target_pairs={{8,0},{0,8},{16,24},{24,16},{9,1},{1,9},{17,25},{25,17},{10,2},{2,... | collective-permute-start | bytes 393224 | tf_op jit(solution)/shard_map/ppermute | solution.py:617
  52.6 5.7 %collective-permute-start.21 = (bf16[16,8,256]{2,1,0:T(8,128)(2,1)S(1)}, bf16[16,8,256]{2,1,0:T(8,128)(2,1)S(1)}, u32[]{:S(2)}, u32[]{:S(2)}) collective-permute-start(bf16[16,8,256]{2,1,0:T(8,128)(2,1)S(1)} %get-tuple-element.241), channel_id=1, source_target_pairs={{8,4},{12,0},{0,12},{4,8},{16,28},{20,24},{24,20},{28,16},{9,5},{1... | collective-permute-start | bytes 196616 | tf_op jit(solution)/shard_map/ppermute | solution.py:616
  52.7 5.6 %collective-permute-start.17 = (bf16[16,8,256]{2,1,0:T(8,128)(2,1)S(1)}, bf16[16,8,256]{2,1,0:T(8,128)(2,1)S(1)}, u32[]{:S(2)}, u32[]{:S(2)}) collective-permute-start(bf16[16,8,256]{2,1,0:T(8,128)(2,1)S(1)} %get-tuple-element.217), channel_id=1, source_target_pairs={{8,0},{0,8},{16,24},{24,16},{9,1},{1,9},{17,25},{25,17},{10,2},{2,... | collective-permute-start | bytes 196616 | tf_op jit(solution)/shard_map/ppermute | solution.py:617
  54.6 2.2 %collective-permute-start.20 = (f32[16,8,256]{2,1,0:T(8,128)S(1)}, f32[16,8,256]{2,1,0:T(8,128)S(1)}, u32[]{:S(2)}, u32[]{:S(2)}) collective-permute-start(f32[16,8,256]{2,1,0:T(8,128)S(1)} %get-tuple-element.239), channel_id=1, source_target_pairs={{0,4},{4,0},{1,5},{5,1},{2,6},{6,2},{3,7},{7,3},{8,12},{12,8},{9,1... | collective-permute-start | bytes 393224 | tf_op jit(solution)/shard_map/ppermute | solution.py:589
  54.6 2.7 %collective-permute-start.19 = (f32[16,8,256]{2,1,0:T(8,128)S(1)}, f32[16,8,256]{2,1,0:T(8,128)S(1)}, u32[]{:S(2)}, u32[]{:S(2)}) collective-permute-start(f32[16,8,256]{2,1,0:T(8,128)S(1)} %get-tuple-element.238), channel_id=1, source_target_pairs={{0,4},{4,0},{1,5},{5,1},{2,6},{6,2},{3,7},{7,3},{8,12},{12,8},{9,1... | collective-permute-start | bytes 393224 | tf_op jit(solution)/shard_map/ppermute | solution.py:589
  55.8 2.5 %collective-permute-start.22 = (f32[16,8,256]{2,1,0:T(8,128)S(1)}, f32[16,8,256]{2,1,0:T(8,128)S(1)}, u32[]{:S(2)}, u32[]{:S(2)}) collective-permute-start(f32[16,8,256]{2,1,0:T(8,128)S(1)} %get-tuple-element.244), channel_id=1, source_target_pairs={{0,4},{4,0},{1,5},{5,1},{2,6},{6,2},{3,7},{7,3},{8,12},{12,8},{9,1... | collective-permute-start | bytes 393224 | tf_op jit(solution)/shard_map/ppermute | solution.py:589
  56.8 1.8 %collective-permute-start.23 = (f32[16,8,256]{2,1,0:T(8,128)S(1)}, f32[16,8,256]{2,1,0:T(8,128)S(1)}, u32[]{:S(2)}, u32[]{:S(2)}) collective-permute-start(f32[16,8,256]{2,1,0:T(8,128)S(1)} %get-tuple-element.246), channel_id=1, source_target_pairs={{0,4},{4,0},{1,5},{5,1},{2,6},{6,2},{3,7},{7,3},{8,12},{12,8},{9,1... | collective-permute-start | bytes 393224 | tf_op jit(solution)/shard_map/ppermute | solution.py:589

commit v7 on v6

--- a/solution.py
+++ b/solution.py
@@ -195,7 +195,7 @@
 NODE_ROWS = 8
 CROSS, OTHER, BELOW, LAST = "c", "o", "b", "l"
 LOAD_NODES = 4
-COSTS = [10000000000, 30000000000, 30000000000, 5000000000, 5000000000, 5000000000, 5000000000, 5000000000]
+COSTS = [30000000000, 30000000000, 30000000000, 5000000000, 5000000000, 5000000000, 5000000000, 5000000000]
 SMALL_VMEM_BYTES = 12 * 2**20
 IN_ANY = pl.BlockSpec(memory_space=pl.ANY)
 IN_HBM = pl.BlockSpec(memory_space=pltpu.HBM)
@@ -261,7 +261,7 @@
     choose[...] = (index == down).astype(F32).astype(BF16)
 
 
-def start_kernel(parent, rhs, inv, off, select, choose, rhs_own, rhs_sent, home, swap, merged, *refs):
+def start_kernel(parent, rhs, inv, off, select, choose, rhs_own, rhs_sent, home, swap_first, swap_rest, merged, *refs):
     *updates, parent_here, inv_here, off_here, sems = refs
     count = inv.shape[0]
     chunks = len(updates) // 2
@@ -301,8 +301,9 @@
         for c in range(chunks):
             home[2 * count * c : 2 * count * (c + 1)] = pick(chosen, flat(updates[c][...])).reshape(2 * count, *home.shape[1:])
             sums = pick(chosen, flat(updates[chunks + c][...])).reshape(2 * count, *home.shape[1:]).astype(BF16)
-            swap[2 * count * c : 2 * count * c + count] = sums[count:]
-            swap[2 * count * c + count : 2 * count * (c + 1)] = sums[:count]
+            swap, at = (swap_first, swap_rest)[c % 2], 2 * count * (c // 2)
+            swap[at : at + count] = sums[count:]
+            swap[at + count : at + 2 * count] = sums[:count]
 
     @off_level(0)
     def _():
@@ -399,8 +400,10 @@
 
 
 def sum_role(c, at):
-    rows = slice(c * at["sent"].shape[0], (c + 1) * at["sent"].shape[0])
-    at["sent"][...] = (at["home"][rows] + at["swapped"][rows].astype(F32)).astype(BF16)
+    nodes = at["sent"].shape[0]
+    home = at["home"][c * nodes : (c + 1) * nodes]
+    partner = at["swapped"][c // 2 * nodes : (c // 2 + 1) * nodes]
+    at["sent"][...] = (home + partner.astype(F32)).astype(BF16)
 
 
 ROLES = {"tier": tier_role, "top": top_role, "back": back_role, LAST: last_role, "sum": sum_role}
@@ -624,14 +627,15 @@
     half_shape = jax.ShapeDtypeStruct((count, half, width), F32)
     block = pltpu.VMEM(lower_inv.shape, BF16)
     state = {"nodes": nodes}
-    select, choose, rhs_own, rhs_sent, home, swap, up_own, *updates = run(
+    select, choose, rhs_own, rhs_sent, home, swap_first, swap_rest, up_own, *updates = run(
         start_kernel, (),
-        [table, table, half_shape, half_shape, shape(chunks * nodes, F32), shape(chunks * nodes, BF16), matrices]
+        [table, table, half_shape, half_shape, shape(chunks * nodes, F32)] + [shape(chunks // 2 * nodes, BF16)] * 2 + [matrices]
         + [shape(count, F32)] * (2 * chunks),
         raw=(parent, rhs, lower_inv, lower_off),
         scratch=[pltpu.VMEM(parent.shape, parent.dtype), block, block, pltpu.SemaphoreType.DMA((3, max(count // LOAD_NODES, 3)))],
     )
-    state.update(select=select, choose=choose, rhs_own=rhs_own, home=home, up_own=up_own, swapped=exchanged(swap))
+    state.update(select=select, choose=choose, rhs_own=rhs_own, home=home, up_own=up_own)
+    swapped = [exchanged(swap_first), exchanged(swap_rest)]
     for c in range(chunks):
         state["own", c], state["far", c] = updates[c], updates[chunks + c]
 
@@ -679,6 +683,8 @@
                     plan.append((low, "back", c))
                     if low:
                         pairs.append((low, low - 1))
+            if k < len(pipe):
+                state["swapped"] = swapped[k]
             if received[p] is not None:
                 state["received"] = after(received[p], *pace)
             split = k == last - 1 and p == len(pipes) - 1

time: 59.8 us -> 58.8 us (0.983)
  starting transfers between devices: 36.5 us -> 32.9 us
  waiting for transfers between devices: 7.6 us -> 10.3 us
    ppermute x14, starting transfers between devices: 33.9 us -> 30.6 us  [passed(): return lax.ppermute(value, LEVEL, pairs + fill)]
    ppermute x14, waiting for transfers between devices: 6.04 us -> 8.59 us  [passed(): return lax.ppermute(value, LEVEL, pairs + fill)]
    ppermute x9 -> x10, starting transfers between devices: 2.55 us -> 2.21 us  [exchanged(): return lax.ppermute(value, SUB, [(0, 1), (1, 0)])]
    ppermute x9 -> x10, waiting for transfers between devices: 1.56 us -> 1.68 us  [exchanged(): return lax.ppermute(value, SUB, [(0, 1), (1, 0)])]
  transfers between devices with their start and end apart: 24 -> 25, of which waited for: 7 -> 12; matrix products, arithmetic and copies ran while one was open for 0% -> 0% of each run, Pallas kernels for 17% -> 17%
where the time goes in v7:
time: 58.8 us; the launch traced here: 58.6 us
  starting transfers between devices  32.9 us (56%)
  Pallas kernels  14.5 us (25%)
  waiting for transfers between devices  10.3 us (18%)
  between operations  1 us (2%)
    ppermute x14, starting transfers between devices, passed(): return lax.ppermute(value, LEVEL, pairs + fill)  30.6 us
    pallas_call x24, Pallas kernels, run(): pl.pallas_call(kernel, in_specs=in_specs, out_specs=out_specs, out_shape=...  14.5 us
    ppermute x14, waiting for transfers between devices, passed(): return lax.ppermute(value, LEVEL, pairs + fill)  8.59 us
    ppermute x10, starting transfers between devices, exchanged(): return lax.ppermute(value, SUB, [(0, 1), (1, 0)])  2.21 us
    ppermute x10, waiting for transfers between devices, exchanged(): return lax.ppermute(value, SUB, [(0, 1), (1, 0)])  1.68 us
  transfers between devices with their start and end apart: 25, of which 12 were waited for; matrix products, arithmetic and copies ran while one was open for 0% of the time, Pallas kernels for 17%

profile of v7, /device:TPU:0, one launch (start us, length us, event | category | flops | bytes accessed | tf_op | source)
XLA Modules:
  0.0 58.6 jit_solution(6248336861575911245)
XLA Ops:
  0.6 3.7 %shard_map.86 = (bf16[256,256]{1,0:T(8,128)(2,1)S(1)}, bf16[256,256]{1,0:T(8,128)(2,1)S(1)}, f32[16,32,256]{2,1,0:T(8,128)S(1)}, f32[16,32,256]{2,1,0:T(8,128)S(...) custom-call(s32[3,32]{1,0:T(4,128)} %parent.1, ...), custom_call_target="tpu_custom_call" | custom-call | flops 1000000000 | bytes 1000000 | tf_op jit(solution)/shard_map/pallas_call | solution.py:577
  4.9 1.1 %collective-permute-done.refs_1_ = bf16[64,8,256]{2,1,0:T(8,128)(2,1)S(1)} collective-permute-done((bf16[64,8,256]{2,1,0:T(8,128)(2,1)S(1)}, bf16[64,8,256]{2,1,0:T(8,128)(2,1)S(1)}, u32[]{:S(2)}, u32[]{:S(2)}) %collective-permute-start) | collective-permute-done | bytes 262176 | tf_op jit(solution)/shard_map/ppermute | solution.py:592
  6.0 2.1 %collective-permute-start.2 = (bf16[32,8,256]{2,1,0:T(8,128)(2,1)S(1)}, bf16[32,8,256]{2,1,0:T(8,128)(2,1)S(1)}, u32[]{:S(2)}, u32[]{:S(2)}) collective-permute-start(bf16[32,8,256]{2,1,0:T(8,128)(2,1)S(1)} %shard_map.87), channel_id=1, source_target_pairs={{0,8},{8,0},{16,24},{24,16},{1,9},{9,1},{17,25},{25,17},{2,10},{10... | collective-permute-start | bytes 393224 | tf_op jit(solution)/shard_map/ppermute | solution.py:620
  8.7 3.5 %shard_map.89.own.refs_3_.refs_1_.refs_2_ = bf16[34,256,256]{2,1,0:T(8,128)(2,1)S(1)} custom-call(bf16[16,256,256]{2,1,0:T(8,128)(2,1)} %bitcast.8, bf16[16,256,256]{2,1,0:T(8,128)(2,1)} %bitcast.10, bf16[16,256,256]{2,1,0:T(8,128)(2,1)} %bitcast.11, bf16[16,64,256]{2,1,0:T(8,128)(2,1)} %ancestor.1), custom_call_target="tpu_custom_call" | custom-call | flops 1000000000 | bytes 1000000 | tf_op jit(solution)/shard_map/pallas_call | solution.py:577
  13.1 2.3 %collective-permute-start.5 = (bf16[32,8,256]{2,1,0:T(8,128)(2,1)S(1)}, bf16[32,8,256]{2,1,0:T(8,128)(2,1)S(1)}, u32[]{:S(2)}, u32[]{:S(2)}) collective-permute-start(bf16[32,8,256]{2,1,0:T(8,128)(2,1)S(1)} %get-tuple-element.142), channel_id=1, source_target_pairs={{8,16},{0,8},{16,24},{24,0},{9,17},{1,9},{17,25},{25,1},{10,18},{2... | collective-permute-start | bytes 393224 | tf_op jit(solution)/shard_map/ppermute | solution.py:620
  15.5 1.9 %collective-permute-start.8 = (bf16[32,8,256]{2,1,0:T(8,128)(2,1)S(1)}, bf16[32,8,256]{2,1,0:T(8,128)(2,1)S(1)}, u32[]{:S(2)}, u32[]{:S(2)}) collective-permute-start(bf16[32,8,256]{2,1,0:T(8,128)(2,1)S(1)} %get-tuple-element.146), channel_id=1, source_target_pairs={{8,16},{0,8},{16,24},{24,0},{9,17},{1,9},{17,25},{25,1},{10,18},{2... | collective-permute-start | bytes 393224 | tf_op jit(solution)/shard_map/ppermute | solution.py:620
  17.4 2.7 %collective-permute-done.5.refs_2_ = bf16[32,8,256]{2,1,0:T(8,128)(2,1)S(1)} collective-permute-done((bf16[32,8,256]{2,1,0:T(8,128)(2,1)S(1)}, bf16[32,8,256]{2,1,0:T(8,128)(2,1)S(1)}, u32[]{:S(2)}, u32[]{:S(2)}) %collective-permute-start.5) | collective-permute-done | bytes 131104 | tf_op jit(solution)/shard_map/ppermute | solution.py:620
  20.2 2.5 %collective-permute-start.7 = (bf16[32,8,256]{2,1,0:T(8,128)(2,1)S(1)}, bf16[32,8,256]{2,1,0:T(8,128)(2,1)S(1)}, u32[]{:S(2)}, u32[]{:S(2)}) collective-permute-start(bf16[32,8,256]{2,1,0:T(8,128)(2,1)S(1)} %get-tuple-element.153), channel_id=1, source_target_pairs={{16,24},{8,16},{0,8},{24,0},{17,25},{9,17},{1,9},{25,1},{18,26},{1... | collective-permute-start | bytes 393224 | tf_op jit(solution)/shard_map/ppermute | solution.py:620
  22.8 2.4 %collective-permute-start.11 = (bf16[32,8,256]{2,1,0:T(8,128)(2,1)S(1)}, bf16[32,8,256]{2,1,0:T(8,128)(2,1)S(1)}, u32[]{:S(2)}, u32[]{:S(2)}) collective-permute-start(bf16[32,8,256]{2,1,0:T(8,128)(2,1)S(1)} %get-tuple-element.160), channel_id=1, source_target_pairs={{16,24},{8,16},{0,8},{24,0},{17,25},{9,17},{1,9},{25,1},{18,26},{1... | collective-permute-start | bytes 393224 | tf_op jit(solution)/shard_map/ppermute | solution.py:620
  25.3 1.0 %collective-permute-done.7.refs_2_ = bf16[32,8,256]{2,1,0:T(8,128)(2,1)S(1)} collective-permute-done((bf16[32,8,256]{2,1,0:T(8,128)(2,1)S(1)}, bf16[32,8,256]{2,1,0:T(8,128)(2,1)S(1)}, u32[]{:S(2)}, u32[]{:S(2)}) %collective-permute-start.7) | collective-permute-done | bytes 131104 | tf_op jit(solution)/shard_map/ppermute | solution.py:620
  26.3 1.7 %collective-permute-start.10 = (bf16[32,8,256]{2,1,0:T(8,128)(2,1)S(1)}, bf16[32,8,256]{2,1,0:T(8,128)(2,1)S(1)}, u32[]{:S(2)}, u32[]{:S(2)}) collective-permute-start(bf16[32,8,256]{2,1,0:T(8,128)(2,1)S(1)} %get-tuple-element.172), channel_id=1, source_target_pairs={{24,16},{16,24},{0,8},{8,0},{25,17},{17,25},{1,9},{9,1},{26,18},{1... | collective-permute-start | bytes 393224 | tf_op jit(solution)/shard_map/ppermute | solution.py:620
  28.0 1.1 %collective-permute-done.11.refs_2_ = bf16[32,8,256]{2,1,0:T(8,128)(2,1)S(1)} collective-permute-done((bf16[32,8,256]{2,1,0:T(8,128)(2,1)S(1)}, bf16[32,8,256]{2,1,0:T(8,128)(2,1)S(1)}, u32[]{:S(2)}, u32[]{:S(2)}) %collective-permute-start.11) | collective-permute-done | bytes 131104 | tf_op jit(solution)/shard_map/ppermute | solution.py:620
  29.5 2.5 %collective-permute-start.13 = (bf16[32,8,256]{2,1,0:T(8,128)(2,1)S(1)}, bf16[32,8,256]{2,1,0:T(8,128)(2,1)S(1)}, u32[]{:S(2)}, u32[]{:S(2)}) collective-permute-start(bf16[32,8,256]{2,1,0:T(8,128)(2,1)S(1)} %get-tuple-element.178), channel_id=1, source_target_pairs={{24,16},{16,24},{0,8},{8,0},{25,17},{17,25},{1,9},{9,1},{26,18},{1... | collective-permute-start | bytes 393224 | tf_op jit(solution)/shard_map/ppermute | solution.py:620
  32.8 1.0 %collective-permute-done.10.refs_0_ = bf16[32,8,256]{2,1,0:T(8,128)(2,1)S(1)} collective-permute-done((bf16[32,8,256]{2,1,0:T(8,128)(2,1)S(1)}, bf16[32,8,256]{2,1,0:T(8,128)(2,1)S(1)}, u32[]{:S(2)}, u32[]{:S(2)}) %collective-permute-start.10) | collective-permute-done | bytes 131104 | tf_op jit(solution)/shard_map/ppermute | solution.py:620
  33.9 2.2 %collective-permute-start.12 = (bf16[32,8,256]{2,1,0:T(8,128)(2,1)S(1)}, bf16[32,8,256]{2,1,0:T(8,128)(2,1)S(1)}, u32[]{:S(2)}, u32[]{:S(2)}) collective-permute-start(bf16[32,8,256]{2,1,0:T(8,128)(2,1)S(1)} %get-tuple-element.191), channel_id=1, source_target_pairs={{16,8},{24,16},{0,24},{8,0},{17,9},{25,17},{1,25},{9,1},{18,10},{2... | collective-permute-start | bytes 393224 | tf_op jit(solution)/shard_map/ppermute | solution.py:620
  36.6 3.0 %collective-permute-start.15 = (bf16[32,8,256]{2,1,0:T(8,128)(2,1)S(1)}, bf16[32,8,256]{2,1,0:T(8,128)(2,1)S(1)}, u32[]{:S(2)}, u32[]{:S(2)}) collective-permute-start(bf16[32,8,256]{2,1,0:T(8,128)(2,1)S(1)} %get-tuple-element.195), channel_id=1, source_target_pairs={{16,8},{24,16},{0,24},{8,0},{17,9},{25,17},{1,25},{9,1},{18,10},{2... | collective-permute-start | bytes 393224 | tf_op jit(solution)/shard_map/ppermute | solution.py:620
  40.3 2.6 %collective-permute-start.14 = (bf16[32,8,256]{2,1,0:T(8,128)(2,1)S(1)}, bf16[32,8,256]{2,1,0:T(8,128)(2,1)S(1)}, u32[]{:S(2)}, u32[]{:S(2)}) collective-permute-start(bf16[32,8,256]{2,1,0:T(8,128)(2,1)S(1)} %get-tuple-element.201), channel_id=1, source_target_pairs={{8,0},{16,8},{0,24},{24,16},{9,1},{17,9},{1,25},{25,17},{10,2},{18... | collective-permute-start | bytes 393224 | tf_op jit(solution)/shard_map/ppermute | solution.py:620
  43.0 2.6 %collective-permute-start.17 = (bf16[32,8,256]{2,1,0:T(8,128)(2,1)S(1)}, bf16[32,8,256]{2,1,0:T(8,128)(2,1)S(1)}, u32[]{:S(2)}, u32[]{:S(2)}) collective-permute-start(bf16[32,8,256]{2,1,0:T(8,128)(2,1)S(1)} %get-tuple-element.207), channel_id=1, source_target_pairs={{8,0},{16,8},{0,24},{24,16},{9,1},{17,9},{1,25},{25,17},{10,2},{18... | collective-permute-start | bytes 393224 | tf_op jit(solution)/shard_map/ppermute | solution.py:620
  45.6 1.2 %collective-permute-done.14.refs_0_ = bf16[32,8,256]{2,1,0:T(8,128)(2,1)S(1)} collective-permute-done((bf16[32,8,256]{2,1,0:T(8,128)(2,1)S(1)}, bf16[32,8,256]{2,1,0:T(8,128)(2,1)S(1)}, u32[]{:S(2)}, u32[]{:S(2)}) %collective-permute-start.14) | collective-permute-done | bytes 131104 | tf_op jit(solution)/shard_map/ppermute | solution.py:620
  46.8 0.9 %shard_map.102 = (f32[16,8,256]{2,1,0:T(8,128)S(1)}, f32[16,8,256]{2,1,0:T(8,128)S(1)}, f32[16,8,256]{2,1,0:T(8,128)S(1)}, f32[16,8,256]{2,1,0:T(8,128)S(1)}, bf16[32,8,256]{2,1,0:T(8,128)(2,1)S(1)}) custom-call(bf16[32,8,256]{2,1,0:T(8,128)(2,1)S(1)} %collective-permute-done.14.refs_0_, ...), custom_call_target="tpu_custom_call", output_to_operand_aliasing={{0}: (6, {}), {1}: (7, {}), {2}: (8, {}), {3}: (9, {})} | custom-call | flops 5000000000 | bytes 1000000 | tf_op jit(solution)/shard_map/pallas_call | solution.py:577
  47.7 2.8 %collective-permute-start.16 = (bf16[32,8,256]{2,1,0:T(8,128)(2,1)S(1)}, bf16[32,8,256]{2,1,0:T(8,128)(2,1)S(1)}, u32[]{:S(2)}, u32[]{:S(2)}) collective-permute-start(bf16[32,8,256]{2,1,0:T(8,128)(2,1)S(1)} %get-tuple-element.213), channel_id=1, source_target_pairs={{8,0},{0,8},{16,24},{24,16},{9,1},{1,9},{17,25},{25,17},{10,2},{2,... | collective-permute-start | bytes 393224 | tf_op jit(solution)/shard_map/ppermute | solution.py:620
  50.5 0.9 %shard_map.103 = (f32[16,8,256]{2,1,0:T(8,128)S(1)}, f32[16,8,256]{2,1,0:T(8,128)S(1)}, f32[16,8,256]{2,1,0:T(8,128)S(1)}, f32[16,8,256]{2,1,0:T(8,128)S(1)}, bf...) custom-call(bf16[32,8,256]{2,1,0:T(8,128)(2,1)S(1)} %collective-perm, ...), custom_call_target="tpu_custom_call", output_to_operand_aliasing={{0}: (6, {}), {1}: (7, {}), {2}: (8, {}), {3}: (9, {})} | custom-call | flops 5000000000 | bytes 1000000 | tf_op jit(solution)/shard_map/pallas_call | solution.py:577
  51.5 1.8 %collective-permute-start.18 = (bf16[16,8,256]{2,1,0:T(8,128)(2,1)S(1)}, bf16[16,8,256]{2,1,0:T(8,128)(2,1)S(1)}, u32[]{:S(2)}, u32[]{:S(2)}) collective-permute-start(bf16[16,8,256]{2,1,0:T(8,128)(2,1)S(1)} %get-tuple-element.219), channel_id=1, source_target_pairs={{8,0},{0,8},{16,24},{24,16},{9,1},{1,9},{17,25},{25,17},{10,2},{2,... | collective-permute-start | bytes 196616 | tf_op jit(solution)/shard_map/ppermute | solution.py:620
  54.6 1.0 %shard_map.106 = f32[16,64,256]{2,1,0:T(8,128)} custom-call(f32[16,32,256]{2,1,0:T(8,128)S(1)} %get-tuple-element.235.here, f32[16,32,256]{2,1,0:T(8,128)S(1)} %get-tuple-element.237.far, f32[16,32,256]{2,1,0:T(8,128)S(1)} %collective-permute-done.19.other), custom_call_target="tpu_custom_call" | custom-call | flops 1000000000 | bytes 1000000 | tf_op jit(solution)/shard_map/pallas_call | solution.py:577
  (50 shorter events, 9.2 us)
Async XLA Ops:
  4.8 7.6 %collective-permute-start.4 = (bf16[64,8,256]{2,1,0:T(8,128)(2,1)S(1)}, bf16[64,8,256]{2,1,0:T(8,128)(2,1)S(1)}, u32[]{:S(2)}, u32[]{:S(2)}) collective-permute-start(bf16[64,8,256]{2,1,0:T(8,128)(2,1)S(1)} %get-tuple-element.139), channel_id=1, source_target_pairs={{0,4},{4,0},{1,5},{5,1},{2,6},{6,2},{3,7},{7,3},{8,12},{12,8},{9,1... | collective-permute-start | bytes 786440 | tf_op jit(solution)/shard_map/ppermute | solution.py:592
  6.0 6.4 %collective-permute-start.2 = (bf16[32,8,256]{2,1,0:T(8,128)(2,1)S(1)}, bf16[32,8,256]{2,1,0:T(8,128)(2,1)S(1)}, u32[]{:S(2)}, u32[]{:S(2)}) collective-permute-start(bf16[32,8,256]{2,1,0:T(8,128)(2,1)S(1)} %shard_map.87), channel_id=1, source_target_pairs={{0,8},{8,0},{16,24},{24,16},{1,9},{9,1},{17,25},{25,17},{2,10},{10... | collective-permute-start | bytes 393224 | tf_op jit(solution)/shard_map/ppermute | solution.py:620
  8.1 4.3 %collective-permute-start.1 = (f32[16,32,256]{2,1,0:T(8,128)S(1)}, f32[16,32,256]{2,1,0:T(8,128)S(1)}, u32[]{:S(2)}, u32[]{:S(2)}) collective-permute-start(f32[16,32,256]{2,1,0:T(8,128)S(1)} %get-tuple-element.130.rhs_sent), channel_id=1, source_target_pairs={{0,4},{4,0},{1,5},{5,1},{2,6},{6,2},{3,7},{7,3},{8,12},{12,8},{9,1... | collective-permute-start | bytes 1572872 | tf_op jit(solution)/shard_map/ppermute | solution.py:592
  8.1 4.9 %collective-permute-start.3 = (bf16[16,256,256]{2,1,0:T(8,128)(2,1)S(1)}, bf16[16,256,256]{2,1,0:T(8,128)(2,1)S(1)}, u32[]{:S(2)}, u32[]{:S(2)}) collective-permute-start(bf16[16,256,256]{2,1,0:T(8,128)(2,1)S(1)} %get-tuple-element.137.refs_3_.refs_7_.up_own), channel_id=1, source_target_pairs={{0,4},{4,0},{1,5},{5,1},{2,6},{6,2},{3,7},{7,3},{8,12},{12,8},{9,1... | collective-permute-start | bytes 6291464 | tf_op jit(solution)/shard_map/ppermute | solution.py:592
  8.6 6.8 %collective-permute-start.6 = (bf16[32,8,256]{2,1,0:T(8,128)(2,1)S(1)}, bf16[32,8,256]{2,1,0:T(8,128)(2,1)S(1)}, u32[]{:S(2)}, u32[]{:S(2)}) collective-permute-start(bf16[32,8,256]{2,1,0:T(8,128)(2,1)S(1)} %shard_map.88), channel_id=1, source_target_pairs={{0,8},{8,0},{16,24},{24,16},{1,9},{9,1},{17,25},{25,17},{2,10},{10... | collective-permute-start | bytes 393224 | tf_op jit(solution)/shard_map/ppermute | solution.py:620
  12.4 12.8 %collective-permute-start.9 = (bf16[34,256,256]{2,1,0:T(8,128)(2,1)S(1)}, bf16[34,256,256]{2,1,0:T(8,128)(2,1)S(1)}, u32[]{:S(2)}, u32[]{:S(2)}) collective-permute-start(bf16[34,256,256]{2,1,0:T(8,128)(2,1)S(1)} %shard_map.89.own.refs_3_.refs_1_.refs_2_), channel_id=1, source_target_pairs={{0,4},{4,0},{1,5},{5,1},{2,6},{6,2},{3,7},{7,3},{8,12},{12,8},{9,1... | collective-permute-start | bytes 13369352 | tf_op jit(solution)/shard_map/ppermute | solution.py:592
  13.1 7.0 %collective-permute-start.5 = (bf16[32,8,256]{2,1,0:T(8,128)(2,1)S(1)}, bf16[32,8,256]{2,1,0:T(8,128)(2,1)S(1)}, u32[]{:S(2)}, u32[]{:S(2)}) collective-permute-start(bf16[32,8,256]{2,1,0:T(8,128)(2,1)S(1)} %get-tuple-element.142), channel_id=1, source_target_pairs={{8,16},{0,8},{16,24},{24,0},{9,17},{1,9},{17,25},{25,1},{10,18},{2... | collective-permute-start | bytes 393224 | tf_op jit(solution)/shard_map/ppermute | solution.py:620
  15.5 7.2 %collective-permute-start.8 = (bf16[32,8,256]{2,1,0:T(8,128)(2,1)S(1)}, bf16[32,8,256]{2,1,0:T(8,128)(2,1)S(1)}, u32[]{:S(2)}, u32[]{:S(2)}) collective-permute-start(bf16[32,8,256]{2,1,0:T(8,128)(2,1)S(1)} %get-tuple-element.146), channel_id=1, source_target_pairs={{8,16},{0,8},{16,24},{24,0},{9,17},{1,9},{17,25},{25,1},{10,18},{2... | collective-permute-start | bytes 393224 | tf_op jit(solution)/shard_map/ppermute | solution.py:620
  20.2 6.1 %collective-permute-start.7 = (bf16[32,8,256]{2,1,0:T(8,128)(2,1)S(1)}, bf16[32,8,256]{2,1,0:T(8,128)(2,1)S(1)}, u32[]{:S(2)}, u32[]{:S(2)}) collective-permute-start(bf16[32,8,256]{2,1,0:T(8,128)(2,1)S(1)} %get-tuple-element.153), channel_id=1, source_target_pairs={{16,24},{8,16},{0,8},{24,0},{17,25},{9,17},{1,9},{25,1},{18,26},{1... | collective-permute-start | bytes 393224 | tf_op jit(solution)/shard_map/ppermute | solution.py:620
  22.8 6.4 %collective-permute-start.11 = (bf16[32,8,256]{2,1,0:T(8,128)(2,1)S(1)}, bf16[32,8,256]{2,1,0:T(8,128)(2,1)S(1)}, u32[]{:S(2)}, u32[]{:S(2)}) collective-permute-start(bf16[32,8,256]{2,1,0:T(8,128)(2,1)S(1)} %get-tuple-element.160), channel_id=1, source_target_pairs={{16,24},{8,16},{0,8},{24,0},{17,25},{9,17},{1,9},{25,1},{18,26},{1... | collective-permute-start | bytes 393224 | tf_op jit(solution)/shard_map/ppermute | solution.py:620
  26.3 7.5 %collective-permute-start.10 = (bf16[32,8,256]{2,1,0:T(8,128)(2,1)S(1)}, bf16[32,8,256]{2,1,0:T(8,128)(2,1)S(1)}, u32[]{:S(2)}, u32[]{:S(2)}) collective-permute-start(bf16[32,8,256]{2,1,0:T(8,128)(2,1)S(1)} %get-tuple-element.172), channel_id=1, source_target_pairs={{24,16},{16,24},{0,8},{8,0},{25,17},{17,25},{1,9},{9,1},{26,18},{1... | collective-permute-start | bytes 393224 | tf_op jit(solution)/shard_map/ppermute | solution.py:620
  29.5 7.1 %collective-permute-start.13 = (bf16[32,8,256]{2,1,0:T(8,128)(2,1)S(1)}, bf16[32,8,256]{2,1,0:T(8,128)(2,1)S(1)}, u32[]{:S(2)}, u32[]{:S(2)}) collective-permute-start(bf16[32,8,256]{2,1,0:T(8,128)(2,1)S(1)} %get-tuple-element.178), channel_id=1, source_target_pairs={{24,16},{16,24},{0,8},{8,0},{25,17},{17,25},{1,9},{9,1},{26,18},{1... | collective-permute-start | bytes 393224 | tf_op jit(solution)/shard_map/ppermute | solution.py:620
  33.9 6.3 %collective-permute-start.12 = (bf16[32,8,256]{2,1,0:T(8,128)(2,1)S(1)}, bf16[32,8,256]{2,1,0:T(8,128)(2,1)S(1)}, u32[]{:S(2)}, u32[]{:S(2)}) collective-permute-start(bf16[32,8,256]{2,1,0:T(8,128)(2,1)S(1)} %get-tuple-element.191), channel_id=1, source_target_pairs={{16,8},{24,16},{0,24},{8,0},{17,9},{25,17},{1,25},{9,1},{18,10},{2... | collective-permute-start | bytes 393224 | tf_op jit(solution)/shard_map/ppermute | solution.py:620
  36.6 6.3 %collective-permute-start.15 = (bf16[32,8,256]{2,1,0:T(8,128)(2,1)S(1)}, bf16[32,8,256]{2,1,0:T(8,128)(2,1)S(1)}, u32[]{:S(2)}, u32[]{:S(2)}) collective-permute-start(bf16[32,8,256]{2,1,0:T(8,128)(2,1)S(1)} %get-tuple-element.195), channel_id=1, source_target_pairs={{16,8},{24,16},{0,24},{8,0},{17,9},{25,17},{1,25},{9,1},{18,10},{2... | collective-permute-start | bytes 393224 | tf_op jit(solution)/shard_map/ppermute | solution.py:620
  39.7 14.7 %collective-permute-start.19 = (f32[16,32,256]{2,1,0:T(8,128)S(1)}, f32[16,32,256]{2,1,0:T(8,128)S(1)}, u32[]{:S(2)}, u32[]{:S(2)}) collective-permute-start(f32[16,32,256]{2,1,0:T(8,128)S(1)} %get-tuple-element.237.far), channel_id=1, source_target_pairs={{0,4},{4,0},{1,5},{5,1},{2,6},{6,2},{3,7},{7,3},{8,12},{12,8},{9,1... | collective-permute-start | bytes 1572872 | tf_op jit(solution)/shard_map/ppermute | solution.py:592
  40.3 6.5 %collective-permute-start.14 = (bf16[32,8,256]{2,1,0:T(8,128)(2,1)S(1)}, bf16[32,8,256]{2,1,0:T(8,128)(2,1)S(1)}, u32[]{:S(2)}, u32[]{:S(2)}) collective-permute-start(bf16[32,8,256]{2,1,0:T(8,128)(2,1)S(1)} %get-tuple-element.201), channel_id=1, source_target_pairs={{8,0},{16,8},{0,24},{24,16},{9,1},{17,9},{1,25},{25,17},{10,2},{18... | collective-permute-start | bytes 393224 | tf_op jit(solution)/shard_map/ppermute | solution.py:620
  43.0 7.5 %collective-permute-start.17 = (bf16[32,8,256]{2,1,0:T(8,128)(2,1)S(1)}, bf16[32,8,256]{2,1,0:T(8,128)(2,1)S(1)}, u32[]{:S(2)}, u32[]{:S(2)}) collective-permute-start(bf16[32,8,256]{2,1,0:T(8,128)(2,1)S(1)} %get-tuple-element.207), channel_id=1, source_target_pairs={{8,0},{16,8},{0,24},{24,16},{9,1},{17,9},{1,25},{25,17},{10,2},{18... | collective-permute-start | bytes 393224 | tf_op jit(solution)/shard_map/ppermute | solution.py:620
  47.7 5.7 %collective-permute-start.16 = (bf16[32,8,256]{2,1,0:T(8,128)(2,1)S(1)}, bf16[32,8,256]{2,1,0:T(8,128)(2,1)S(1)}, u32[]{:S(2)}, u32[]{:S(2)}) collective-permute-start(bf16[32,8,256]{2,1,0:T(8,128)(2,1)S(1)} %get-tuple-element.213), channel_id=1, source_target_pairs={{8,0},{0,8},{16,24},{24,16},{9,1},{1,9},{17,25},{25,17},{10,2},{2,... | collective-permute-start | bytes 393224 | tf_op jit(solution)/shard_map/ppermute | solution.py:620
  51.4 5.8 %collective-permute-start.22 = (bf16[16,8,256]{2,1,0:T(8,128)(2,1)S(1)}, bf16[16,8,256]{2,1,0:T(8,128)(2,1)S(1)}, u32[]{:S(2)}, u32[]{:S(2)}) collective-permute-start(bf16[16,8,256]{2,1,0:T(8,128)(2,1)S(1)} %get-tuple-element.243), channel_id=1, source_target_pairs={{8,4},{12,0},{0,12},{4,8},{16,28},{20,24},{24,20},{28,16},{9,5},{1... | collective-permute-start | bytes 196616 | tf_op jit(solution)/shard_map/ppermute | solution.py:619
  51.5 5.8 %collective-permute-start.18 = (bf16[16,8,256]{2,1,0:T(8,128)(2,1)S(1)}, bf16[16,8,256]{2,1,0:T(8,128)(2,1)S(1)}, u32[]{:S(2)}, u32[]{:S(2)}) collective-permute-start(bf16[16,8,256]{2,1,0:T(8,128)(2,1)S(1)} %get-tuple-element.219), channel_id=1, source_target_pairs={{8,0},{0,8},{16,24},{24,16},{9,1},{1,9},{17,25},{25,17},{10,2},{2,... | collective-permute-start | bytes 196616 | tf_op jit(solution)/shard_map/ppermute | solution.py:620
  53.3 2.4 %collective-permute-start.21 = (f32[16,8,256]{2,1,0:T(8,128)S(1)}, f32[16,8,256]{2,1,0:T(8,128)S(1)}, u32[]{:S(2)}, u32[]{:S(2)}) collective-permute-start(f32[16,8,256]{2,1,0:T(8,128)S(1)} %get-tuple-element.241), channel_id=1, source_target_pairs={{0,4},{4,0},{1,5},{5,1},{2,6},{6,2},{3,7},{7,3},{8,12},{12,8},{9,1... | collective-permute-start | bytes 393224 | tf_op jit(solution)/shard_map/ppermute | solution.py:592
  53.4 2.6 %collective-permute-start.20 = (f32[16,8,256]{2,1,0:T(8,128)S(1)}, f32[16,8,256]{2,1,0:T(8,128)S(1)}, u32[]{:S(2)}, u32[]{:S(2)}) collective-permute-start(f32[16,8,256]{2,1,0:T(8,128)S(1)} %get-tuple-element.240), channel_id=1, source_target_pairs={{0,4},{4,0},{1,5},{5,1},{2,6},{6,2},{3,7},{7,3},{8,12},{12,8},{9,1... | collective-permute-start | bytes 393224 | tf_op jit(solution)/shard_map/ppermute | solution.py:592
  54.4 2.8 %collective-permute-start.23 = (f32[16,8,256]{2,1,0:T(8,128)S(1)}, f32[16,8,256]{2,1,0:T(8,128)S(1)}, u32[]{:S(2)}, u32[]{:S(2)}) collective-permute-start(f32[16,8,256]{2,1,0:T(8,128)S(1)} %get-tuple-element.246), channel_id=1, source_target_pairs={{0,4},{4,0},{1,5},{5,1},{2,6},{6,2},{3,7},{7,3},{8,12},{12,8},{9,1... | collective-permute-start | bytes 393224 | tf_op jit(solution)/shard_map/ppermute | solution.py:592
  55.6 2.0 %collective-permute-start.24 = (f32[16,8,256]{2,1,0:T(8,128)S(1)}, f32[16,8,256]{2,1,0:T(8,128)S(1)}, u32[]{:S(2)}, u32[]{:S(2)}) collective-permute-start(f32[16,8,256]{2,1,0:T(8,128)S(1)} %get-tuple-element.248), channel_id=1, source_target_pairs={{0,4},{4,0},{1,5},{5,1},{2,6},{6,2},{3,7},{7,3},{8,12},{12,8},{9,1... | collective-permute-start | bytes 393224 | tf_op jit(solution)/shard_map/ppermute | solution.py:592
  (1 other events, 1.7 us)

commit v8 on v7

--- a/solution.py
+++ b/solution.py
@@ -612,7 +612,7 @@
         targets = [i for i in range(levels) if i not in [to for _, to in pairs]]
         fill = min(
             (list(zip(sources, order)) for order in itertools.permutations(targets)),
-            key=lambda extra: (sum(a == b for a, b in extra), sum(abs(a - b) for a, b in extra)),
+            key=lambda extra: (sum(a == b for a, b in extra), sum((a ^ b) == levels - 1 for a, b in extra), sum((b, a) in pairs + extra for a, b in extra)),
         )
         if cross:
             pairs = [(2 * a + s, 2 * b + 1 - s) for a, b in pairs + fill for s in range(2)]

time: 58.8 us -> 58.3 us (level)
  starting transfers between devices: 32.9 us -> 29.3 us
  waiting for transfers between devices: 10.3 us -> 13.2 us
    ppermute x14, starting transfers between devices: 30.6 us -> 26.4 us  [passed(): return lax.ppermute(value, LEVEL, pairs + fill)]
    ppermute x14, waiting for transfers between devices: 8.59 us -> 12.1 us  [passed(): return lax.ppermute(value, LEVEL, pairs + fill)]
  transfers between devices with their start and end apart: 25 -> 25, of which waited for: 12 -> 11; matrix products, arithmetic and copies ran while one was open for 0% -> 0% of each run, Pallas kernels for 17% -> 17%
where the time goes in v8:
time: 58.3 us; the launch traced here: 58.1 us
  starting transfers between devices  29.3 us (50%)
  Pallas kernels  14.5 us (25%)
  waiting for transfers between devices  13.2 us (23%)
  between operations  1.05 us (2%)
    ppermute x14, starting transfers between devices, passed(): return lax.ppermute(value, LEVEL, pairs + fill)  26.4 us
    pallas_call x24, Pallas kernels, run(): pl.pallas_call(kernel, in_specs=in_specs, out_specs=out_specs, out_shape=...  14.5 us
    ppermute x14, waiting for transfers between devices, passed(): return lax.ppermute(value, LEVEL, pairs + fill)  12.1 us
    ppermute x10, starting transfers between devices, exchanged(): return lax.ppermute(value, SUB, [(0, 1), (1, 0)])  2.79 us
  transfers between devices with their start and end apart: 25, of which 11 were waited for; matrix products, arithmetic and copies ran while one was open for 0% of the time, Pallas kernels for 17%

profile of v8, /device:TPU:0, one launch (start us, length us, event | category | flops | bytes accessed | tf_op | source)
XLA Modules:
  0.0 58.1 jit_solution(8289342560460547343)
XLA Ops:
  0.6 3.7 %shard_map.86 = (bf16[256,256]{1,0:T(8,128)(2,1)S(1)}, bf16[256,256]{1,0:T(8,128)(2,1)S(1)}, f32[16,32,256]{2,1,0:T(8,128)S(1)}, f32[16,32,256]{2,1,0:T(8,128)S(...) custom-call(s32[3,32]{1,0:T(4,128)} %parent.1, ...), custom_call_target="tpu_custom_call" | custom-call | flops 1000000000 | bytes 1000000 | tf_op jit(solution)/shard_map/pallas_call | solution.py:577
  4.9 1.1 %collective-permute-done.refs_1_ = bf16[64,8,256]{2,1,0:T(8,128)(2,1)S(1)} collective-permute-done((bf16[64,8,256]{2,1,0:T(8,128)(2,1)S(1)}, bf16[64,8,256]{2,1,0:T(8,128)(2,1)S(1)}, u32[]{:S(2)}, u32[]{:S(2)}) %collective-permute-start) | collective-permute-done | bytes 262176 | tf_op jit(solution)/shard_map/ppermute | solution.py:592
  6.0 2.1 %collective-permute-start.2 = (bf16[32,8,256]{2,1,0:T(8,128)(2,1)S(1)}, bf16[32,8,256]{2,1,0:T(8,128)(2,1)S(1)}, u32[]{:S(2)}, u32[]{:S(2)}) collective-permute-start(bf16[32,8,256]{2,1,0:T(8,128)(2,1)S(1)} %shard_map.87), channel_id=1, source_target_pairs={{0,8},{8,24},{16,0},{24,16},{1,9},{9,25},{17,1},{25,17},{2,10},{10... | collective-permute-start | bytes 393224 | tf_op jit(solution)/shard_map/ppermute | solution.py:620
  8.6 1.5 %collective-permute-start.6 = (bf16[32,8,256]{2,1,0:T(8,128)(2,1)S(1)}, bf16[32,8,256]{2,1,0:T(8,128)(2,1)S(1)}, u32[]{:S(2)}, u32[]{:S(2)}) collective-permute-start(bf16[32,8,256]{2,1,0:T(8,128)(2,1)S(1)} %shard_map.88), channel_id=1, source_target_pairs={{0,8},{8,24},{16,0},{24,16},{1,9},{9,25},{17,1},{25,17},{2,10},{10... | collective-permute-start | bytes 393224 | tf_op jit(solution)/shard_map/ppermute | solution.py:620
  10.1 3.5 %shard_map.89.own.refs_3_.refs_1_.refs_2_ = bf16[34,256,256]{2,1,0:T(8,128)(2,1)S(1)} custom-call(bf16[16,256,256]{2,1,0:T(8,128)(2,1)} %bitcast.8, bf16[16,256,256]{2,1,0:T(8,128)(2,1)} %bitcast.10, bf16[16,256,256]{2,1,0:T(8,128)(2,1)} %bitcast.11, bf16[16,64,256]{2,1,0:T(8,128)(2,1)} %ancestor.1), custom_call_target="tpu_custom_call" | custom-call | flops 1000000000 | bytes 1000000 | tf_op jit(solution)/shard_map/pallas_call | solution.py:577
  13.8 1.7 %collective-permute-start.5 = (bf16[32,8,256]{2,1,0:T(8,128)(2,1)S(1)}, bf16[32,8,256]{2,1,0:T(8,128)(2,1)S(1)}, u32[]{:S(2)}, u32[]{:S(2)}) collective-permute-start(bf16[32,8,256]{2,1,0:T(8,128)(2,1)S(1)} %get-tuple-element.142), channel_id=1, source_target_pairs={{8,16},{0,8},{16,24},{24,0},{9,17},{1,9},{17,25},{25,1},{10,18},{2... | collective-permute-start | bytes 393224 | tf_op jit(solution)/shard_map/ppermute | solution.py:620
  15.5 1.8 %collective-permute-start.8 = (bf16[32,8,256]{2,1,0:T(8,128)(2,1)S(1)}, bf16[32,8,256]{2,1,0:T(8,128)(2,1)S(1)}, u32[]{:S(2)}, u32[]{:S(2)}) collective-permute-start(bf16[32,8,256]{2,1,0:T(8,128)(2,1)S(1)} %get-tuple-element.146), channel_id=1, source_target_pairs={{8,16},{0,8},{16,24},{24,0},{9,17},{1,9},{17,25},{25,1},{10,18},{2... | collective-permute-start | bytes 393224 | tf_op jit(solution)/shard_map/ppermute | solution.py:620
  17.4 3.7 %collective-permute-done.5.refs_2_ = bf16[32,8,256]{2,1,0:T(8,128)(2,1)S(1)} collective-permute-done((bf16[32,8,256]{2,1,0:T(8,128)(2,1)S(1)}, bf16[32,8,256]{2,1,0:T(8,128)(2,1)S(1)}, u32[]{:S(2)}, u32[]{:S(2)}) %collective-permute-start.5) | collective-permute-done | bytes 131104 | tf_op jit(solution)/shard_map/ppermute | solution.py:620
  21.1 1.6 %collective-permute-start.7 = (bf16[32,8,256]{2,1,0:T(8,128)(2,1)S(1)}, bf16[32,8,256]{2,1,0:T(8,128)(2,1)S(1)}, u32[]{:S(2)}, u32[]{:S(2)}) collective-permute-start(bf16[32,8,256]{2,1,0:T(8,128)(2,1)S(1)} %get-tuple-element.153), channel_id=1, source_target_pairs={{16,24},{8,16},{0,8},{24,0},{17,25},{9,17},{1,9},{25,1},{18,26},{1... | collective-permute-start | bytes 393224 | tf_op jit(solution)/shard_map/ppermute | solution.py:620
  23.5 1.7 %collective-permute-start.11 = (bf16[32,8,256]{2,1,0:T(8,128)(2,1)S(1)}, bf16[32,8,256]{2,1,0:T(8,128)(2,1)S(1)}, u32[]{:S(2)}, u32[]{:S(2)}) collective-permute-start(bf16[32,8,256]{2,1,0:T(8,128)(2,1)S(1)} %get-tuple-element.160), channel_id=1, source_target_pairs={{16,24},{8,16},{0,8},{24,0},{17,25},{9,17},{1,9},{25,1},{18,26},{1... | collective-permute-start | bytes 393224 | tf_op jit(solution)/shard_map/ppermute | solution.py:620
  25.2 2.1 %collective-permute-done.7.refs_2_ = bf16[32,8,256]{2,1,0:T(8,128)(2,1)S(1)} collective-permute-done((bf16[32,8,256]{2,1,0:T(8,128)(2,1)S(1)}, bf16[32,8,256]{2,1,0:T(8,128)(2,1)S(1)}, u32[]{:S(2)}, u32[]{:S(2)}) %collective-permute-start.7) | collective-permute-done | bytes 131104 | tf_op jit(solution)/shard_map/ppermute | solution.py:620
  28.2 1.6 %collective-permute-done.11.refs_2_ = bf16[32,8,256]{2,1,0:T(8,128)(2,1)S(1)} collective-permute-done((bf16[32,8,256]{2,1,0:T(8,128)(2,1)S(1)}, bf16[32,8,256]{2,1,0:T(8,128)(2,1)S(1)}, u32[]{:S(2)}, u32[]{:S(2)}) %collective-permute-start.11) | collective-permute-done | bytes 131104 | tf_op jit(solution)/shard_map/ppermute | solution.py:620
  30.1 1.8 %collective-permute-start.13 = (bf16[32,8,256]{2,1,0:T(8,128)(2,1)S(1)}, bf16[32,8,256]{2,1,0:T(8,128)(2,1)S(1)}, u32[]{:S(2)}, u32[]{:S(2)}) collective-permute-start(bf16[32,8,256]{2,1,0:T(8,128)(2,1)S(1)} %get-tuple-element.178), channel_id=1, source_target_pairs={{24,16},{16,24},{0,8},{8,0},{25,17},{17,25},{1,9},{9,1},{26,18},{1... | collective-permute-start | bytes 393224 | tf_op jit(solution)/shard_map/ppermute | solution.py:620
  33.8 2.3 %collective-permute-start.12 = (bf16[32,8,256]{2,1,0:T(8,128)(2,1)S(1)}, bf16[32,8,256]{2,1,0:T(8,128)(2,1)S(1)}, u32[]{:S(2)}, u32[]{:S(2)}) collective-permute-start(bf16[32,8,256]{2,1,0:T(8,128)(2,1)S(1)} %get-tuple-element.191), channel_id=1, source_target_pairs={{16,8},{24,16},{0,24},{8,0},{17,9},{25,17},{1,25},{9,1},{18,10},{2... | collective-permute-start | bytes 393224 | tf_op jit(solution)/shard_map/ppermute | solution.py:620
  36.7 2.9 %collective-permute-start.15 = (bf16[32,8,256]{2,1,0:T(8,128)(2,1)S(1)}, bf16[32,8,256]{2,1,0:T(8,128)(2,1)S(1)}, u32[]{:S(2)}, u32[]{:S(2)}) collective-permute-start(bf16[32,8,256]{2,1,0:T(8,128)(2,1)S(1)} %get-tuple-element.195), channel_id=1, source_target_pairs={{16,8},{24,16},{0,24},{8,0},{17,9},{25,17},{1,25},{9,1},{18,10},{2... | collective-permute-start | bytes 393224 | tf_op jit(solution)/shard_map/ppermute | solution.py:620
  40.2 2.7 %collective-permute-start.14 = (bf16[32,8,256]{2,1,0:T(8,128)(2,1)S(1)}, bf16[32,8,256]{2,1,0:T(8,128)(2,1)S(1)}, u32[]{:S(2)}, u32[]{:S(2)}) collective-permute-start(bf16[32,8,256]{2,1,0:T(8,128)(2,1)S(1)} %get-tuple-element.201), channel_id=1, source_target_pairs={{8,0},{16,8},{0,24},{24,16},{9,1},{17,9},{1,25},{25,17},{10,2},{18... | collective-permute-start | bytes 393224 | tf_op jit(solution)/shard_map/ppermute | solution.py:620
  43.0 2.6 %collective-permute-start.17 = (bf16[32,8,256]{2,1,0:T(8,128)(2,1)S(1)}, bf16[32,8,256]{2,1,0:T(8,128)(2,1)S(1)}, u32[]{:S(2)}, u32[]{:S(2)}) collective-permute-start(bf16[32,8,256]{2,1,0:T(8,128)(2,1)S(1)} %get-tuple-element.207), channel_id=1, source_target_pairs={{8,0},{16,8},{0,24},{24,16},{9,1},{17,9},{1,25},{25,17},{10,2},{18... | collective-permute-start | bytes 393224 | tf_op jit(solution)/shard_map/ppermute | solution.py:620
  45.6 1.2 %collective-permute-done.14.refs_0_ = bf16[32,8,256]{2,1,0:T(8,128)(2,1)S(1)} collective-permute-done((bf16[32,8,256]{2,1,0:T(8,128)(2,1)S(1)}, bf16[32,8,256]{2,1,0:T(8,128)(2,1)S(1)}, u32[]{:S(2)}, u32[]{:S(2)}) %collective-permute-start.14) | collective-permute-done | bytes 131104 | tf_op jit(solution)/shard_map/ppermute | solution.py:620
  46.8 0.9 %shard_map.102 = (f32[16,8,256]{2,1,0:T(8,128)S(1)}, f32[16,8,256]{2,1,0:T(8,128)S(1)}, f32[16,8,256]{2,1,0:T(8,128)S(1)}, f32[16,8,256]{2,1,0:T(8,128)S(1)}, bf16[32,8,256]{2,1,0:T(8,128)(2,1)S(1)}) custom-call(bf16[32,8,256]{2,1,0:T(8,128)(2,1)S(1)} %collective-permute-done.14.refs_0_, ...), custom_call_target="tpu_custom_call", output_to_operand_aliasing={{0}: (6, {}), {1}: (7, {}), {2}: (8, {}), {3}: (9, {})} | custom-call | flops 5000000000 | bytes 1000000 | tf_op jit(solution)/shard_map/pallas_call | solution.py:577
  47.7 1.5 %collective-permute-start.16 = (bf16[32,8,256]{2,1,0:T(8,128)(2,1)S(1)}, bf16[32,8,256]{2,1,0:T(8,128)(2,1)S(1)}, u32[]{:S(2)}, u32[]{:S(2)}) collective-permute-start(bf16[32,8,256]{2,1,0:T(8,128)(2,1)S(1)} %get-tuple-element.213), channel_id=1, source_target_pairs={{8,0},{0,16},{16,24},{24,8},{9,1},{1,17},{17,25},{25,9},{10,2},{2,... | collective-permute-start | bytes 393224 | tf_op jit(solution)/shard_map/ppermute | solution.py:620
  49.3 0.9 %shard_map.103 = (f32[16,8,256]{2,1,0:T(8,128)S(1)}, f32[16,8,256]{2,1,0:T(8,128)S(1)}, f32[16,8,256]{2,1,0:T(8,128)S(1)}, f32[16,8,256]{2,1,0:T(8,128)S(1)}, bf...) custom-call(bf16[32,8,256]{2,1,0:T(8,128)(2,1)S(1)} %collective-perm, ...), custom_call_target="tpu_custom_call", output_to_operand_aliasing={{0}: (6, {}), {1}: (7, {}), {2}: (8, {}), {3}: (9, {})} | custom-call | flops 5000000000 | bytes 1000000 | tf_op jit(solution)/shard_map/pallas_call | solution.py:577
  50.3 1.4 %collective-permute-start.18 = (bf16[16,8,256]{2,1,0:T(8,128)(2,1)S(1)}, bf16[16,8,256]{2,1,0:T(8,128)(2,1)S(1)}, u32[]{:S(2)}, u32[]{:S(2)}) collective-permute-start(bf16[16,8,256]{2,1,0:T(8,128)(2,1)S(1)} %get-tuple-element.219), channel_id=1, source_target_pairs={{8,0},{0,16},{16,24},{24,8},{9,1},{1,17},{17,25},{25,9},{10,2},{2,... | collective-permute-start | bytes 196616 | tf_op jit(solution)/shard_map/ppermute | solution.py:620
  52.6 0.9 %collective-permute-done.16.refs_0_ = bf16[32,8,256]{2,1,0:T(8,128)(2,1)S(1)} collective-permute-done((bf16[32,8,256]{2,1,0:T(8,128)(2,1)S(1)}, bf16[32,8,256]{2,1,0:T(8,128)(2,1)S(1)}, u32[]{:S(2)}, u32[]{:S(2)}) %collective-permute-start.16) | collective-permute-done | bytes 131104 | tf_op jit(solution)/shard_map/ppermute | solution.py:620
  54.7 1.0 %shard_map.106 = f32[16,64,256]{2,1,0:T(8,128)} custom-call(f32[16,32,256]{2,1,0:T(8,128)S(1)} %get-tuple-element.235.here, f32[16,32,256]{2,1,0:T(8,128)S(1)} %get-tuple-element.237.far, f32[16,32,256]{2,1,0:T(8,128)S(1)} %collective-permute-done.19.other), custom_call_target="tpu_custom_call" | custom-call | flops 1000000000 | bytes 1000000 | tf_op jit(solution)/shard_map/pallas_call | solution.py:577
  (50 shorter events, 10.9 us)
Async XLA Ops:
  4.3 1.7 %collective-permute-start = (bf16[64,8,256]{2,1,0:T(8,128)(2,1)S(1)}, bf16[64,8,256]{2,1,0:T(8,128)(2,1)S(1)}, u32[]{:S(2)}, u32[]{:S(2)}) collective-permute-start(bf16[64,8,256]{2,1,0:T(8,128)(2,1)S(1)} %get-tuple-element.129), channel_id=1, source_target_pairs={{0,4},{4,0},{1,5},{5,1},{2,6},{6,2},{3,7},{7,3},{8,12},{12,8},{9,1... | collective-permute-start | bytes 786440 | tf_op jit(solution)/shard_map/ppermute | solution.py:592
  4.8 8.8 %collective-permute-start.4 = (bf16[64,8,256]{2,1,0:T(8,128)(2,1)S(1)}, bf16[64,8,256]{2,1,0:T(8,128)(2,1)S(1)}, u32[]{:S(2)}, u32[]{:S(2)}) collective-permute-start(bf16[64,8,256]{2,1,0:T(8,128)(2,1)S(1)} %get-tuple-element.139), channel_id=1, source_target_pairs={{0,4},{4,0},{1,5},{5,1},{2,6},{6,2},{3,7},{7,3},{8,12},{12,8},{9,1... | collective-permute-start | bytes 786440 | tf_op jit(solution)/shard_map/ppermute | solution.py:592
  6.0 7.6 %collective-permute-start.2 = (bf16[32,8,256]{2,1,0:T(8,128)(2,1)S(1)}, bf16[32,8,256]{2,1,0:T(8,128)(2,1)S(1)}, u32[]{:S(2)}, u32[]{:S(2)}) collective-permute-start(bf16[32,8,256]{2,1,0:T(8,128)(2,1)S(1)} %shard_map.87), channel_id=1, source_target_pairs={{0,8},{8,24},{16,0},{24,16},{1,9},{9,25},{17,1},{25,17},{2,10},{10... | collective-permute-start | bytes 393224 | tf_op jit(solution)/shard_map/ppermute | solution.py:620
  8.1 5.6 %collective-permute-start.1 = (f32[16,32,256]{2,1,0:T(8,128)S(1)}, f32[16,32,256]{2,1,0:T(8,128)S(1)}, u32[]{:S(2)}, u32[]{:S(2)}) collective-permute-start(f32[16,32,256]{2,1,0:T(8,128)S(1)} %get-tuple-element.130.rhs_sent), channel_id=1, source_target_pairs={{0,4},{4,0},{1,5},{5,1},{2,6},{6,2},{3,7},{7,3},{8,12},{12,8},{9,1... | collective-permute-start | bytes 1572872 | tf_op jit(solution)/shard_map/ppermute | solution.py:592
  8.1 5.6 %collective-permute-start.3 = (bf16[16,256,256]{2,1,0:T(8,128)(2,1)S(1)}, bf16[16,256,256]{2,1,0:T(8,128)(2,1)S(1)}, u32[]{:S(2)}, u32[]{:S(2)}) collective-permute-start(bf16[16,256,256]{2,1,0:T(8,128)(2,1)S(1)} %get-tuple-element.137.refs_3_.refs_7_.up_own), channel_id=1, source_target_pairs={{0,4},{4,0},{1,5},{5,1},{2,6},{6,2},{3,7},{7,3},{8,12},{12,8},{9,1... | collective-permute-start | bytes 6291464 | tf_op jit(solution)/shard_map/ppermute | solution.py:592
  8.6 6.8 %collective-permute-start.6 = (bf16[32,8,256]{2,1,0:T(8,128)(2,1)S(1)}, bf16[32,8,256]{2,1,0:T(8,128)(2,1)S(1)}, u32[]{:S(2)}, u32[]{:S(2)}) collective-permute-start(bf16[32,8,256]{2,1,0:T(8,128)(2,1)S(1)} %shard_map.88), channel_id=1, source_target_pairs={{0,8},{8,24},{16,0},{24,16},{1,9},{9,25},{17,1},{25,17},{2,10},{10... | collective-permute-start | bytes 393224 | tf_op jit(solution)/shard_map/ppermute | solution.py:620
  13.6 11.6 %collective-permute-start.9 = (bf16[34,256,256]{2,1,0:T(8,128)(2,1)S(1)}, bf16[34,256,256]{2,1,0:T(8,128)(2,1)S(1)}, u32[]{:S(2)}, u32[]{:S(2)}) collective-permute-start(bf16[34,256,256]{2,1,0:T(8,128)(2,1)S(1)} %shard_map.89.own.refs_3_.refs_1_.refs_2_), channel_id=1, source_target_pairs={{0,4},{4,0},{1,5},{5,1},{2,6},{6,2},{3,7},{7,3},{8,12},{12,8},{9,1... | collective-permute-start | bytes 13369352 | tf_op jit(solution)/shard_map/ppermute | solution.py:592
  13.8 7.2 %collective-permute-start.5 = (bf16[32,8,256]{2,1,0:T(8,128)(2,1)S(1)}, bf16[32,8,256]{2,1,0:T(8,128)(2,1)S(1)}, u32[]{:S(2)}, u32[]{:S(2)}) collective-permute-start(bf16[32,8,256]{2,1,0:T(8,128)(2,1)S(1)} %get-tuple-element.142), channel_id=1, source_target_pairs={{8,16},{0,8},{16,24},{24,0},{9,17},{1,9},{17,25},{25,1},{10,18},{2... | collective-permute-start | bytes 393224 | tf_op jit(solution)/shard_map/ppermute | solution.py:620
  15.5 7.9 %collective-permute-start.8 = (bf16[32,8,256]{2,1,0:T(8,128)(2,1)S(1)}, bf16[32,8,256]{2,1,0:T(8,128)(2,1)S(1)}, u32[]{:S(2)}, u32[]{:S(2)}) collective-permute-start(bf16[32,8,256]{2,1,0:T(8,128)(2,1)S(1)} %get-tuple-element.146), channel_id=1, source_target_pairs={{8,16},{0,8},{16,24},{24,0},{9,17},{1,9},{17,25},{25,1},{10,18},{2... | collective-permute-start | bytes 393224 | tf_op jit(solution)/shard_map/ppermute | solution.py:620
  21.1 6.2 %collective-permute-start.7 = (bf16[32,8,256]{2,1,0:T(8,128)(2,1)S(1)}, bf16[32,8,256]{2,1,0:T(8,128)(2,1)S(1)}, u32[]{:S(2)}, u32[]{:S(2)}) collective-permute-start(bf16[32,8,256]{2,1,0:T(8,128)(2,1)S(1)} %get-tuple-element.153), channel_id=1, source_target_pairs={{16,24},{8,16},{0,8},{24,0},{17,25},{9,17},{1,9},{25,1},{18,26},{1... | collective-permute-start | bytes 393224 | tf_op jit(solution)/shard_map/ppermute | solution.py:620
  23.5 6.3 %collective-permute-start.11 = (bf16[32,8,256]{2,1,0:T(8,128)(2,1)S(1)}, bf16[32,8,256]{2,1,0:T(8,128)(2,1)S(1)}, u32[]{:S(2)}, u32[]{:S(2)}) collective-permute-start(bf16[32,8,256]{2,1,0:T(8,128)(2,1)S(1)} %get-tuple-element.160), channel_id=1, source_target_pairs={{16,24},{8,16},{0,8},{24,0},{17,25},{9,17},{1,9},{25,1},{18,26},{1... | collective-permute-start | bytes 393224 | tf_op jit(solution)/shard_map/ppermute | solution.py:620
  27.4 6.3 %collective-permute-start.10 = (bf16[32,8,256]{2,1,0:T(8,128)(2,1)S(1)}, bf16[32,8,256]{2,1,0:T(8,128)(2,1)S(1)}, u32[]{:S(2)}, u32[]{:S(2)}) collective-permute-start(bf16[32,8,256]{2,1,0:T(8,128)(2,1)S(1)} %get-tuple-element.172), channel_id=1, source_target_pairs={{24,16},{16,24},{0,8},{8,0},{25,17},{17,25},{1,9},{9,1},{26,18},{1... | collective-permute-start | bytes 393224 | tf_op jit(solution)/shard_map/ppermute | solution.py:620
  30.1 6.5 %collective-permute-start.13 = (bf16[32,8,256]{2,1,0:T(8,128)(2,1)S(1)}, bf16[32,8,256]{2,1,0:T(8,128)(2,1)S(1)}, u32[]{:S(2)}, u32[]{:S(2)}) collective-permute-start(bf16[32,8,256]{2,1,0:T(8,128)(2,1)S(1)} %get-tuple-element.178), channel_id=1, source_target_pairs={{24,16},{16,24},{0,8},{8,0},{25,17},{17,25},{1,9},{9,1},{26,18},{1... | collective-permute-start | bytes 393224 | tf_op jit(solution)/shard_map/ppermute | solution.py:620
  33.8 6.4 %collective-permute-start.12 = (bf16[32,8,256]{2,1,0:T(8,128)(2,1)S(1)}, bf16[32,8,256]{2,1,0:T(8,128)(2,1)S(1)}, u32[]{:S(2)}, u32[]{:S(2)}) collective-permute-start(bf16[32,8,256]{2,1,0:T(8,128)(2,1)S(1)} %get-tuple-element.191), channel_id=1, source_target_pairs={{16,8},{24,16},{0,24},{8,0},{17,9},{25,17},{1,25},{9,1},{18,10},{2... | collective-permute-start | bytes 393224 | tf_op jit(solution)/shard_map/ppermute | solution.py:620
  36.7 6.2 %collective-permute-start.15 = (bf16[32,8,256]{2,1,0:T(8,128)(2,1)S(1)}, bf16[32,8,256]{2,1,0:T(8,128)(2,1)S(1)}, u32[]{:S(2)}, u32[]{:S(2)}) collective-permute-start(bf16[32,8,256]{2,1,0:T(8,128)(2,1)S(1)} %get-tuple-element.195), channel_id=1, source_target_pairs={{16,8},{24,16},{0,24},{8,0},{17,9},{25,17},{1,25},{9,1},{18,10},{2... | collective-permute-start | bytes 393224 | tf_op jit(solution)/shard_map/ppermute | solution.py:620
  39.7 14.5 %collective-permute-start.19 = (f32[16,32,256]{2,1,0:T(8,128)S(1)}, f32[16,32,256]{2,1,0:T(8,128)S(1)}, u32[]{:S(2)}, u32[]{:S(2)}) collective-permute-start(f32[16,32,256]{2,1,0:T(8,128)S(1)} %get-tuple-element.237.far), channel_id=1, source_target_pairs={{0,4},{4,0},{1,5},{5,1},{2,6},{6,2},{3,7},{7,3},{8,12},{12,8},{9,1... | collective-permute-start | bytes 1572872 | tf_op jit(solution)/shard_map/ppermute | solution.py:592
  40.2 6.6 %collective-permute-start.14 = (bf16[32,8,256]{2,1,0:T(8,128)(2,1)S(1)}, bf16[32,8,256]{2,1,0:T(8,128)(2,1)S(1)}, u32[]{:S(2)}, u32[]{:S(2)}) collective-permute-start(bf16[32,8,256]{2,1,0:T(8,128)(2,1)S(1)} %get-tuple-element.201), channel_id=1, source_target_pairs={{8,0},{16,8},{0,24},{24,16},{9,1},{17,9},{1,25},{25,17},{10,2},{18... | collective-permute-start | bytes 393224 | tf_op jit(solution)/shard_map/ppermute | solution.py:620
  43.0 6.3 %collective-permute-start.17 = (bf16[32,8,256]{2,1,0:T(8,128)(2,1)S(1)}, bf16[32,8,256]{2,1,0:T(8,128)(2,1)S(1)}, u32[]{:S(2)}, u32[]{:S(2)}) collective-permute-start(bf16[32,8,256]{2,1,0:T(8,128)(2,1)S(1)} %get-tuple-element.207), channel_id=1, source_target_pairs={{8,0},{16,8},{0,24},{24,16},{9,1},{17,9},{1,25},{25,17},{10,2},{18... | collective-permute-start | bytes 393224 | tf_op jit(solution)/shard_map/ppermute | solution.py:620
  47.7 5.8 %collective-permute-start.16 = (bf16[32,8,256]{2,1,0:T(8,128)(2,1)S(1)}, bf16[32,8,256]{2,1,0:T(8,128)(2,1)S(1)}, u32[]{:S(2)}, u32[]{:S(2)}) collective-permute-start(bf16[32,8,256]{2,1,0:T(8,128)(2,1)S(1)} %get-tuple-element.213), channel_id=1, source_target_pairs={{8,0},{0,16},{16,24},{24,8},{9,1},{1,17},{17,25},{25,9},{10,2},{2,... | collective-permute-start | bytes 393224 | tf_op jit(solution)/shard_map/ppermute | solution.py:620
  50.2 6.4 %collective-permute-start.22 = (bf16[16,8,256]{2,1,0:T(8,128)(2,1)S(1)}, bf16[16,8,256]{2,1,0:T(8,128)(2,1)S(1)}, u32[]{:S(2)}, u32[]{:S(2)}) collective-permute-start(bf16[16,8,256]{2,1,0:T(8,128)(2,1)S(1)} %get-tuple-element.243), channel_id=1, source_target_pairs={{8,4},{12,0},{0,20},{4,16},{16,28},{20,24},{24,12},{28,8},{9,5},{1... | collective-permute-start | bytes 196616 | tf_op jit(solution)/shard_map/ppermute | solution.py:619
  50.3 6.4 %collective-permute-start.18 = (bf16[16,8,256]{2,1,0:T(8,128)(2,1)S(1)}, bf16[16,8,256]{2,1,0:T(8,128)(2,1)S(1)}, u32[]{:S(2)}, u32[]{:S(2)}) collective-permute-start(bf16[16,8,256]{2,1,0:T(8,128)(2,1)S(1)} %get-tuple-element.219), channel_id=1, source_target_pairs={{8,0},{0,16},{16,24},{24,8},{9,1},{1,17},{17,25},{25,9},{10,2},{2,... | collective-permute-start | bytes 196616 | tf_op jit(solution)/shard_map/ppermute | solution.py:620
  51.7 4.0 %collective-permute-start.21 = (f32[16,8,256]{2,1,0:T(8,128)S(1)}, f32[16,8,256]{2,1,0:T(8,128)S(1)}, u32[]{:S(2)}, u32[]{:S(2)}) collective-permute-start(f32[16,8,256]{2,1,0:T(8,128)S(1)} %get-tuple-element.241), channel_id=1, source_target_pairs={{0,4},{4,0},{1,5},{5,1},{2,6},{6,2},{3,7},{7,3},{8,12},{12,8},{9,1... | collective-permute-start | bytes 393224 | tf_op jit(solution)/shard_map/ppermute | solution.py:592
  53.5 2.3 %collective-permute-start.20 = (f32[16,8,256]{2,1,0:T(8,128)S(1)}, f32[16,8,256]{2,1,0:T(8,128)S(1)}, u32[]{:S(2)}, u32[]{:S(2)}) collective-permute-start(f32[16,8,256]{2,1,0:T(8,128)S(1)} %get-tuple-element.240), channel_id=1, source_target_pairs={{0,4},{4,0},{1,5},{5,1},{2,6},{6,2},{3,7},{7,3},{8,12},{12,8},{9,1... | collective-permute-start | bytes 393224 | tf_op jit(solution)/shard_map/ppermute | solution.py:592
  54.2 2.5 %collective-permute-start.23 = (f32[16,8,256]{2,1,0:T(8,128)S(1)}, f32[16,8,256]{2,1,0:T(8,128)S(1)}, u32[]{:S(2)}, u32[]{:S(2)}) collective-permute-start(f32[16,8,256]{2,1,0:T(8,128)S(1)} %get-tuple-element.246), channel_id=1, source_target_pairs={{0,4},{4,0},{1,5},{5,1},{2,6},{6,2},{3,7},{7,3},{8,12},{12,8},{9,1... | collective-permute-start | bytes 393224 | tf_op jit(solution)/shard_map/ppermute | solution.py:592
  (1 other events, 1.4 us)

commit v9 on v8

--- a/solution.py
+++ b/solution.py
@@ -195,7 +195,7 @@
 NODE_ROWS = 8
 CROSS, OTHER, BELOW, LAST = "c", "o", "b", "l"
 LOAD_NODES = 4
-COSTS = [30000000000, 30000000000, 30000000000, 5000000000, 5000000000, 5000000000, 5000000000, 5000000000]
+COSTS = [30000000000, 10000000000, 30000000000, 5000000000, 5000000000, 5000000000, 5000000000, 5000000000]
 SMALL_VMEM_BYTES = 12 * 2**20
 IN_ANY = pl.BlockSpec(memory_space=pl.ANY)
 IN_HBM = pl.BlockSpec(memory_space=pltpu.HBM)
@@ -708,16 +708,18 @@
             if p == 0 and k == 1:
                 state["down_far"] = exchanged(state["down_own"])
             if p == 0 and k == last:
-                (update,) = run(
-                    place_bottom_kernel, (upd_own, after(upd_far, *pace), upd_other), [], whole=(whole, None), scratch=sems(1)
-                )
                 early = [pipe[0] for pipe in pipes]
                 other[early[0]], other[early[1]] = (exchanged(state["sol_far", c]) for c in early)
-                solved = placed(early, None, update)
+                solved = placed(early, None, *pace)
                 pace = [solved]
         if k == 0:
             state["down_own"] = merged(sent)
             pace.append(state["down_own"])
+        if k == last - 1:
+            (update,) = run(
+                place_bottom_kernel, (upd_own, after(upd_far, sent), upd_other), [], whole=(whole, None), scratch=sems(1)
+            )
+            pace.append(update)
         if k == top - 1:
             bases = run(
                 functools.partial(ancestor_kernel, top),

time: 58.3 us -> 57.8 us (level)
  waiting for transfers between devices: 13.2 us -> 12.5 us
    ppermute x14, waiting for transfers between devices: 12.1 us -> 11.2 us  [passed(): return lax.ppermute(value, LEVEL, pairs + fill)]
  transfers between devices with their start and end apart: 25 -> 25, of which waited for: 11 -> 10; matrix products, arithmetic and copies ran while one was open for 0% -> 0% of each run, Pallas kernels for 17% -> 17%
where the time goes in v9:
time: 57.8 us; the launch traced here: 57.7 us
  starting transfers between devices  29.6 us (51%)
  Pallas kernels  14.5 us (25%)
  waiting for transfers between devices  12.5 us (22%)
  between operations  1.04 us (2%)
    ppermute x14, starting transfers between devices, passed(): return lax.ppermute(value, LEVEL, pairs + fill)  26.4 us
    pallas_call x24, Pallas kernels, run(): pl.pallas_call(kernel, in_specs=in_specs, out_specs=out_specs, out_shape=...  14.5 us
    ppermute x14, waiting for transfers between devices, passed(): return lax.ppermute(value, LEVEL, pairs + fill)  11.2 us
    ppermute x10, starting transfers between devices, exchanged(): return lax.ppermute(value, SUB, [(0, 1), (1, 0)])  3.13 us
    ppermute x10, waiting for transfers between devices, exchanged(): return lax.ppermute(value, SUB, [(0, 1), (1, 0)])  1.37 us
  transfers between devices with their start and end apart: 25, of which 10 were waited for; matrix products, arithmetic and copies ran while one was open for 0% of the time, Pallas kernels for 17%

profile of v9, /device:TPU:0, one launch (start us, length us, event | category | flops | bytes accessed | tf_op | source)
XLA Modules:
  0.0 57.7 jit_solution(3117018630944456192)
XLA Ops:
  0.6 3.7 %shard_map.86 = (bf16[256,256]{1,0:T(8,128)(2,1)S(1)}, bf16[256,256]{1,0:T(8,128)(2,1)S(1)}, f32[16,32,256]{2,1,0:T(8,128)S(1)}, f32[16,32,256]{2,1,0:T(8,128)S(...) custom-call(s32[3,32]{1,0:T(4,128)} %parent.1, ...), custom_call_target="tpu_custom_call" | custom-call | flops 1000000000 | bytes 1000000 | tf_op jit(solution)/shard_map/pallas_call | solution.py:577
  4.9 1.1 %collective-permute-done.refs_1_ = bf16[64,8,256]{2,1,0:T(8,128)(2,1)S(1)} collective-permute-done((bf16[64,8,256]{2,1,0:T(8,128)(2,1)S(1)}, bf16[64,8,256]{2,1,0:T(8,128)(2,1)S(1)}, u32[]{:S(2)}, u32[]{:S(2)}) %collective-permute-start) | collective-permute-done | bytes 262176 | tf_op jit(solution)/shard_map/ppermute | solution.py:592
  6.0 2.1 %collective-permute-start.2 = (bf16[32,8,256]{2,1,0:T(8,128)(2,1)S(1)}, bf16[32,8,256]{2,1,0:T(8,128)(2,1)S(1)}, u32[]{:S(2)}, u32[]{:S(2)}) collective-permute-start(bf16[32,8,256]{2,1,0:T(8,128)(2,1)S(1)} %shard_map.87), channel_id=1, source_target_pairs={{0,8},{8,24},{16,0},{24,16},{1,9},{9,25},{17,1},{25,17},{2,10},{10... | collective-permute-start | bytes 393224 | tf_op jit(solution)/shard_map/ppermute | solution.py:620
  8.6 1.5 %collective-permute-start.6 = (bf16[32,8,256]{2,1,0:T(8,128)(2,1)S(1)}, bf16[32,8,256]{2,1,0:T(8,128)(2,1)S(1)}, u32[]{:S(2)}, u32[]{:S(2)}) collective-permute-start(bf16[32,8,256]{2,1,0:T(8,128)(2,1)S(1)} %shard_map.88), channel_id=1, source_target_pairs={{0,8},{8,24},{16,0},{24,16},{1,9},{9,25},{17,1},{25,17},{2,10},{10... | collective-permute-start | bytes 393224 | tf_op jit(solution)/shard_map/ppermute | solution.py:620
  10.1 3.5 %shard_map.89.own.refs_3_.refs_1_.refs_2_ = bf16[34,256,256]{2,1,0:T(8,128)(2,1)S(1)} custom-call(bf16[16,256,256]{2,1,0:T(8,128)(2,1)} %bitcast.8, bf16[16,256,256]{2,1,0:T(8,128)(2,1)} %bitcast.10, bf16[16,256,256]{2,1,0:T(8,128)(2,1)} %bitcast.11, bf16[16,64,256]{2,1,0:T(8,128)(2,1)} %ancestor.1), custom_call_target="tpu_custom_call" | custom-call | flops 1000000000 | bytes 1000000 | tf_op jit(solution)/shard_map/pallas_call | solution.py:577
  13.8 1.7 %collective-permute-start.5 = (bf16[32,8,256]{2,1,0:T(8,128)(2,1)S(1)}, bf16[32,8,256]{2,1,0:T(8,128)(2,1)S(1)}, u32[]{:S(2)}, u32[]{:S(2)}) collective-permute-start(bf16[32,8,256]{2,1,0:T(8,128)(2,1)S(1)} %get-tuple-element.142), channel_id=1, source_target_pairs={{8,16},{0,8},{16,24},{24,0},{9,17},{1,9},{17,25},{25,1},{10,18},{2... | collective-permute-start | bytes 393224 | tf_op jit(solution)/shard_map/ppermute | solution.py:620
  15.5 1.8 %collective-permute-start.8 = (bf16[32,8,256]{2,1,0:T(8,128)(2,1)S(1)}, bf16[32,8,256]{2,1,0:T(8,128)(2,1)S(1)}, u32[]{:S(2)}, u32[]{:S(2)}) collective-permute-start(bf16[32,8,256]{2,1,0:T(8,128)(2,1)S(1)} %get-tuple-element.146), channel_id=1, source_target_pairs={{8,16},{0,8},{16,24},{24,0},{9,17},{1,9},{17,25},{25,1},{10,18},{2... | collective-permute-start | bytes 393224 | tf_op jit(solution)/shard_map/ppermute | solution.py:620
  17.4 3.7 %collective-permute-done.5.refs_2_ = bf16[32,8,256]{2,1,0:T(8,128)(2,1)S(1)} collective-permute-done((bf16[32,8,256]{2,1,0:T(8,128)(2,1)S(1)}, bf16[32,8,256]{2,1,0:T(8,128)(2,1)S(1)}, u32[]{:S(2)}, u32[]{:S(2)}) %collective-permute-start.5) | collective-permute-done | bytes 131104 | tf_op jit(solution)/shard_map/ppermute | solution.py:620
  21.1 1.6 %collective-permute-start.7 = (bf16[32,8,256]{2,1,0:T(8,128)(2,1)S(1)}, bf16[32,8,256]{2,1,0:T(8,128)(2,1)S(1)}, u32[]{:S(2)}, u32[]{:S(2)}) collective-permute-start(bf16[32,8,256]{2,1,0:T(8,128)(2,1)S(1)} %get-tuple-element.153), channel_id=1, source_target_pairs={{16,24},{8,16},{0,8},{24,0},{17,25},{9,17},{1,9},{25,1},{18,26},{1... | collective-permute-start | bytes 393224 | tf_op jit(solution)/shard_map/ppermute | solution.py:620
  23.5 1.7 %collective-permute-start.11 = (bf16[32,8,256]{2,1,0:T(8,128)(2,1)S(1)}, bf16[32,8,256]{2,1,0:T(8,128)(2,1)S(1)}, u32[]{:S(2)}, u32[]{:S(2)}) collective-permute-start(bf16[32,8,256]{2,1,0:T(8,128)(2,1)S(1)} %get-tuple-element.160), channel_id=1, source_target_pairs={{16,24},{8,16},{0,8},{24,0},{17,25},{9,17},{1,9},{25,1},{18,26},{1... | collective-permute-start | bytes 393224 | tf_op jit(solution)/shard_map/ppermute | solution.py:620
  25.2 2.1 %collective-permute-done.7.refs_2_ = bf16[32,8,256]{2,1,0:T(8,128)(2,1)S(1)} collective-permute-done((bf16[32,8,256]{2,1,0:T(8,128)(2,1)S(1)}, bf16[32,8,256]{2,1,0:T(8,128)(2,1)S(1)}, u32[]{:S(2)}, u32[]{:S(2)}) %collective-permute-start.7) | collective-permute-done | bytes 131104 | tf_op jit(solution)/shard_map/ppermute | solution.py:620
  28.2 1.6 %collective-permute-done.11.refs_2_ = bf16[32,8,256]{2,1,0:T(8,128)(2,1)S(1)} collective-permute-done((bf16[32,8,256]{2,1,0:T(8,128)(2,1)S(1)}, bf16[32,8,256]{2,1,0:T(8,128)(2,1)S(1)}, u32[]{:S(2)}, u32[]{:S(2)}) %collective-permute-start.11) | collective-permute-done | bytes 131104 | tf_op jit(solution)/shard_map/ppermute | solution.py:620
  30.1 1.8 %collective-permute-start.13 = (bf16[32,8,256]{2,1,0:T(8,128)(2,1)S(1)}, bf16[32,8,256]{2,1,0:T(8,128)(2,1)S(1)}, u32[]{:S(2)}, u32[]{:S(2)}) collective-permute-start(bf16[32,8,256]{2,1,0:T(8,128)(2,1)S(1)} %get-tuple-element.178), channel_id=1, source_target_pairs={{24,16},{16,24},{0,8},{8,0},{25,17},{17,25},{1,9},{9,1},{26,18},{1... | collective-permute-start | bytes 393224 | tf_op jit(solution)/shard_map/ppermute | solution.py:620
  33.8 2.3 %collective-permute-start.12 = (bf16[32,8,256]{2,1,0:T(8,128)(2,1)S(1)}, bf16[32,8,256]{2,1,0:T(8,128)(2,1)S(1)}, u32[]{:S(2)}, u32[]{:S(2)}) collective-permute-start(bf16[32,8,256]{2,1,0:T(8,128)(2,1)S(1)} %get-tuple-element.191), channel_id=1, source_target_pairs={{16,8},{24,16},{0,24},{8,0},{17,9},{25,17},{1,25},{9,1},{18,10},{2... | collective-permute-start | bytes 393224 | tf_op jit(solution)/shard_map/ppermute | solution.py:620
  36.7 2.9 %collective-permute-start.15 = (bf16[32,8,256]{2,1,0:T(8,128)(2,1)S(1)}, bf16[32,8,256]{2,1,0:T(8,128)(2,1)S(1)}, u32[]{:S(2)}, u32[]{:S(2)}) collective-permute-start(bf16[32,8,256]{2,1,0:T(8,128)(2,1)S(1)} %get-tuple-element.195), channel_id=1, source_target_pairs={{16,8},{24,16},{0,24},{8,0},{17,9},{25,17},{1,25},{9,1},{18,10},{2... | collective-permute-start | bytes 393224 | tf_op jit(solution)/shard_map/ppermute | solution.py:620
  40.2 2.7 %collective-permute-start.14 = (bf16[32,8,256]{2,1,0:T(8,128)(2,1)S(1)}, bf16[32,8,256]{2,1,0:T(8,128)(2,1)S(1)}, u32[]{:S(2)}, u32[]{:S(2)}) collective-permute-start(bf16[32,8,256]{2,1,0:T(8,128)(2,1)S(1)} %get-tuple-element.201), channel_id=1, source_target_pairs={{8,0},{16,8},{0,24},{24,16},{9,1},{17,9},{1,25},{25,17},{10,2},{18... | collective-permute-start | bytes 393224 | tf_op jit(solution)/shard_map/ppermute | solution.py:620
  43.0 2.6 %collective-permute-start.17 = (bf16[32,8,256]{2,1,0:T(8,128)(2,1)S(1)}, bf16[32,8,256]{2,1,0:T(8,128)(2,1)S(1)}, u32[]{:S(2)}, u32[]{:S(2)}) collective-permute-start(bf16[32,8,256]{2,1,0:T(8,128)(2,1)S(1)} %get-tuple-element.207), channel_id=1, source_target_pairs={{8,0},{16,8},{0,24},{24,16},{9,1},{17,9},{1,25},{25,17},{10,2},{18... | collective-permute-start | bytes 393224 | tf_op jit(solution)/shard_map/ppermute | solution.py:620
  45.6 1.2 %collective-permute-done.14.refs_0_ = bf16[32,8,256]{2,1,0:T(8,128)(2,1)S(1)} collective-permute-done((bf16[32,8,256]{2,1,0:T(8,128)(2,1)S(1)}, bf16[32,8,256]{2,1,0:T(8,128)(2,1)S(1)}, u32[]{:S(2)}, u32[]{:S(2)}) %collective-permute-start.14) | collective-permute-done | bytes 131104 | tf_op jit(solution)/shard_map/ppermute | solution.py:620
  46.8 0.9 %shard_map.102 = (f32[16,8,256]{2,1,0:T(8,128)S(1)}, f32[16,8,256]{2,1,0:T(8,128)S(1)}, f32[16,8,256]{2,1,0:T(8,128)S(1)}, f32[16,8,256]{2,1,0:T(8,128)S(1)}, bf16[32,8,256]{2,1,0:T(8,128)(2,1)S(1)}) custom-call(bf16[32,8,256]{2,1,0:T(8,128)(2,1)S(1)} %collective-permute-done.14.refs_0_, ...), custom_call_target="tpu_custom_call", output_to_operand_aliasing={{0}: (6, {}), {1}: (7, {}), {2}: (8, {}), {3}: (9, {})} | custom-call | flops 5000000000 | bytes 1000000 | tf_op jit(solution)/shard_map/pallas_call | solution.py:577
  47.7 1.5 %collective-permute-start.16 = (bf16[32,8,256]{2,1,0:T(8,128)(2,1)S(1)}, bf16[32,8,256]{2,1,0:T(8,128)(2,1)S(1)}, u32[]{:S(2)}, u32[]{:S(2)}) collective-permute-start(bf16[32,8,256]{2,1,0:T(8,128)(2,1)S(1)} %get-tuple-element.213), channel_id=1, source_target_pairs={{8,0},{0,16},{16,24},{24,8},{9,1},{1,17},{17,25},{25,9},{10,2},{2,... | collective-permute-start | bytes 393224 | tf_op jit(solution)/shard_map/ppermute | solution.py:620
  49.3 0.9 %shard_map.103 = (f32[16,8,256]{2,1,0:T(8,128)S(1)}, f32[16,8,256]{2,1,0:T(8,128)S(1)}, f32[16,8,256]{2,1,0:T(8,128)S(1)}, f32[16,8,256]{2,1,0:T(8,128)S(1)}, bf...) custom-call(bf16[32,8,256]{2,1,0:T(8,128)(2,1)S(1)} %collective-perm, ...), custom_call_target="tpu_custom_call", output_to_operand_aliasing={{0}: (6, {}), {1}: (7, {}), {2}: (8, {}), {3}: (9, {})} | custom-call | flops 5000000000 | bytes 1000000 | tf_op jit(solution)/shard_map/pallas_call | solution.py:577
  50.2 1.4 %collective-permute-start.19 = (bf16[16,8,256]{2,1,0:T(8,128)(2,1)S(1)}, bf16[16,8,256]{2,1,0:T(8,128)(2,1)S(1)}, u32[]{:S(2)}, u32[]{:S(2)}) collective-permute-start(bf16[16,8,256]{2,1,0:T(8,128)(2,1)S(1)} %get-tuple-element.219), channel_id=1, source_target_pairs={{8,0},{0,16},{16,24},{24,8},{9,1},{1,17},{17,25},{25,9},{10,2},{2,... | collective-permute-start | bytes 196616 | tf_op jit(solution)/shard_map/ppermute | solution.py:620
  51.6 1.2 %collective-permute-start.21 = (f32[16,8,256]{2,1,0:T(8,128)S(1)}, f32[16,8,256]{2,1,0:T(8,128)S(1)}, u32[]{:S(2)}, u32[]{:S(2)}) collective-permute-start(f32[16,8,256]{2,1,0:T(8,128)S(1)} %get-tuple-element.241), channel_id=1, source_target_pairs={{0,4},{4,0},{1,5},{5,1},{2,6},{6,2},{3,7},{7,3},{8,12},{12,8},{9,1... | collective-permute-start | bytes 393224 | tf_op jit(solution)/shard_map/ppermute | solution.py:592
  52.9 1.0 %shard_map.105 = f32[16,64,256]{2,1,0:T(8,128)} custom-call(f32[16,32,256]{2,1,0:T(8,128)S(1)} %get-tuple-element.230.here, f32[16,32,256]{2,1,0:T(8,128)S(1)} %get-tuple-element.232.far, f32[16,32,256]{2,1,0:T(8,128)S(1)} %collective-permute-done.18.other), custom_call_target="tpu_custom_call" | custom-call | flops 1000000000 | bytes 1000000 | tf_op jit(solution)/shard_map/pallas_call | solution.py:577
  (50 shorter events, 10.1 us)
Async XLA Ops:
  4.3 1.7 %collective-permute-start = (bf16[64,8,256]{2,1,0:T(8,128)(2,1)S(1)}, bf16[64,8,256]{2,1,0:T(8,128)(2,1)S(1)}, u32[]{:S(2)}, u32[]{:S(2)}) collective-permute-start(bf16[64,8,256]{2,1,0:T(8,128)(2,1)S(1)} %get-tuple-element.129), channel_id=1, source_target_pairs={{0,4},{4,0},{1,5},{5,1},{2,6},{6,2},{3,7},{7,3},{8,12},{12,8},{9,1... | collective-permute-start | bytes 786440 | tf_op jit(solution)/shard_map/ppermute | solution.py:592
  4.8 8.8 %collective-permute-start.4 = (bf16[64,8,256]{2,1,0:T(8,128)(2,1)S(1)}, bf16[64,8,256]{2,1,0:T(8,128)(2,1)S(1)}, u32[]{:S(2)}, u32[]{:S(2)}) collective-permute-start(bf16[64,8,256]{2,1,0:T(8,128)(2,1)S(1)} %get-tuple-element.139), channel_id=1, source_target_pairs={{0,4},{4,0},{1,5},{5,1},{2,6},{6,2},{3,7},{7,3},{8,12},{12,8},{9,1... | collective-permute-start | bytes 786440 | tf_op jit(solution)/shard_map/ppermute | solution.py:592
  6.0 7.6 %collective-permute-start.2 = (bf16[32,8,256]{2,1,0:T(8,128)(2,1)S(1)}, bf16[32,8,256]{2,1,0:T(8,128)(2,1)S(1)}, u32[]{:S(2)}, u32[]{:S(2)}) collective-permute-start(bf16[32,8,256]{2,1,0:T(8,128)(2,1)S(1)} %shard_map.87), channel_id=1, source_target_pairs={{0,8},{8,24},{16,0},{24,16},{1,9},{9,25},{17,1},{25,17},{2,10},{10... | collective-permute-start | bytes 393224 | tf_op jit(solution)/shard_map/ppermute | solution.py:620
  8.1 5.6 %collective-permute-start.1 = (f32[16,32,256]{2,1,0:T(8,128)S(1)}, f32[16,32,256]{2,1,0:T(8,128)S(1)}, u32[]{:S(2)}, u32[]{:S(2)}) collective-permute-start(f32[16,32,256]{2,1,0:T(8,128)S(1)} %get-tuple-element.130.rhs_sent), channel_id=1, source_target_pairs={{0,4},{4,0},{1,5},{5,1},{2,6},{6,2},{3,7},{7,3},{8,12},{12,8},{9,1... | collective-permute-start | bytes 1572872 | tf_op jit(solution)/shard_map/ppermute | solution.py:592
  8.1 5.6 %collective-permute-start.3 = (bf16[16,256,256]{2,1,0:T(8,128)(2,1)S(1)}, bf16[16,256,256]{2,1,0:T(8,128)(2,1)S(1)}, u32[]{:S(2)}, u32[]{:S(2)}) collective-permute-start(bf16[16,256,256]{2,1,0:T(8,128)(2,1)S(1)} %get-tuple-element.137.refs_3_.refs_7_.up_own), channel_id=1, source_target_pairs={{0,4},{4,0},{1,5},{5,1},{2,6},{6,2},{3,7},{7,3},{8,12},{12,8},{9,1... | collective-permute-start | bytes 6291464 | tf_op jit(solution)/shard_map/ppermute | solution.py:592
  8.6 6.8 %collective-permute-start.6 = (bf16[32,8,256]{2,1,0:T(8,128)(2,1)S(1)}, bf16[32,8,256]{2,1,0:T(8,128)(2,1)S(1)}, u32[]{:S(2)}, u32[]{:S(2)}) collective-permute-start(bf16[32,8,256]{2,1,0:T(8,128)(2,1)S(1)} %shard_map.88), channel_id=1, source_target_pairs={{0,8},{8,24},{16,0},{24,16},{1,9},{9,25},{17,1},{25,17},{2,10},{10... | collective-permute-start | bytes 393224 | tf_op jit(solution)/shard_map/ppermute | solution.py:620
  13.6 11.6 %collective-permute-start.9 = (bf16[34,256,256]{2,1,0:T(8,128)(2,1)S(1)}, bf16[34,256,256]{2,1,0:T(8,128)(2,1)S(1)}, u32[]{:S(2)}, u32[]{:S(2)}) collective-permute-start(bf16[34,256,256]{2,1,0:T(8,128)(2,1)S(1)} %shard_map.89.own.refs_3_.refs_1_.refs_2_), channel_id=1, source_target_pairs={{0,4},{4,0},{1,5},{5,1},{2,6},{6,2},{3,7},{7,3},{8,12},{12,8},{9,1... | collective-permute-start | bytes 13369352 | tf_op jit(solution)/shard_map/ppermute | solution.py:592
  13.8 7.2 %collective-permute-start.5 = (bf16[32,8,256]{2,1,0:T(8,128)(2,1)S(1)}, bf16[32,8,256]{2,1,0:T(8,128)(2,1)S(1)}, u32[]{:S(2)}, u32[]{:S(2)}) collective-permute-start(bf16[32,8,256]{2,1,0:T(8,128)(2,1)S(1)} %get-tuple-element.142), channel_id=1, source_target_pairs={{8,16},{0,8},{16,24},{24,0},{9,17},{1,9},{17,25},{25,1},{10,18},{2... | collective-permute-start | bytes 393224 | tf_op jit(solution)/shard_map/ppermute | solution.py:620
  15.5 7.9 %collective-permute-start.8 = (bf16[32,8,256]{2,1,0:T(8,128)(2,1)S(1)}, bf16[32,8,256]{2,1,0:T(8,128)(2,1)S(1)}, u32[]{:S(2)}, u32[]{:S(2)}) collective-permute-start(bf16[32,8,256]{2,1,0:T(8,128)(2,1)S(1)} %get-tuple-element.146), channel_id=1, source_target_pairs={{8,16},{0,8},{16,24},{24,0},{9,17},{1,9},{17,25},{25,1},{10,18},{2... | collective-permute-start | bytes 393224 | tf_op jit(solution)/shard_map/ppermute | solution.py:620
  21.1 6.2 %collective-permute-start.7 = (bf16[32,8,256]{2,1,0:T(8,128)(2,1)S(1)}, bf16[32,8,256]{2,1,0:T(8,128)(2,1)S(1)}, u32[]{:S(2)}, u32[]{:S(2)}) collective-permute-start(bf16[32,8,256]{2,1,0:T(8,128)(2,1)S(1)} %get-tuple-element.153), channel_id=1, source_target_pairs={{16,24},{8,16},{0,8},{24,0},{17,25},{9,17},{1,9},{25,1},{18,26},{1... | collective-permute-start | bytes 393224 | tf_op jit(solution)/shard_map/ppermute | solution.py:620
  23.5 6.3 %collective-permute-start.11 = (bf16[32,8,256]{2,1,0:T(8,128)(2,1)S(1)}, bf16[32,8,256]{2,1,0:T(8,128)(2,1)S(1)}, u32[]{:S(2)}, u32[]{:S(2)}) collective-permute-start(bf16[32,8,256]{2,1,0:T(8,128)(2,1)S(1)} %get-tuple-element.160), channel_id=1, source_target_pairs={{16,24},{8,16},{0,8},{24,0},{17,25},{9,17},{1,9},{25,1},{18,26},{1... | collective-permute-start | bytes 393224 | tf_op jit(solution)/shard_map/ppermute | solution.py:620
  27.4 6.3 %collective-permute-start.10 = (bf16[32,8,256]{2,1,0:T(8,128)(2,1)S(1)}, bf16[32,8,256]{2,1,0:T(8,128)(2,1)S(1)}, u32[]{:S(2)}, u32[]{:S(2)}) collective-permute-start(bf16[32,8,256]{2,1,0:T(8,128)(2,1)S(1)} %get-tuple-element.172), channel_id=1, source_target_pairs={{24,16},{16,24},{0,8},{8,0},{25,17},{17,25},{1,9},{9,1},{26,18},{1... | collective-permute-start | bytes 393224 | tf_op jit(solution)/shard_map/ppermute | solution.py:620
  30.1 6.5 %collective-permute-start.13 = (bf16[32,8,256]{2,1,0:T(8,128)(2,1)S(1)}, bf16[32,8,256]{2,1,0:T(8,128)(2,1)S(1)}, u32[]{:S(2)}, u32[]{:S(2)}) collective-permute-start(bf16[32,8,256]{2,1,0:T(8,128)(2,1)S(1)} %get-tuple-element.178), channel_id=1, source_target_pairs={{24,16},{16,24},{0,8},{8,0},{25,17},{17,25},{1,9},{9,1},{26,18},{1... | collective-permute-start | bytes 393224 | tf_op jit(solution)/shard_map/ppermute | solution.py:620
  33.8 6.4 %collective-permute-start.12 = (bf16[32,8,256]{2,1,0:T(8,128)(2,1)S(1)}, bf16[32,8,256]{2,1,0:T(8,128)(2,1)S(1)}, u32[]{:S(2)}, u32[]{:S(2)}) collective-permute-start(bf16[32,8,256]{2,1,0:T(8,128)(2,1)S(1)} %get-tuple-element.191), channel_id=1, source_target_pairs={{16,8},{24,16},{0,24},{8,0},{17,9},{25,17},{1,25},{9,1},{18,10},{2... | collective-permute-start | bytes 393224 | tf_op jit(solution)/shard_map/ppermute | solution.py:620
  36.7 6.2 %collective-permute-start.15 = (bf16[32,8,256]{2,1,0:T(8,128)(2,1)S(1)}, bf16[32,8,256]{2,1,0:T(8,128)(2,1)S(1)}, u32[]{:S(2)}, u32[]{:S(2)}) collective-permute-start(bf16[32,8,256]{2,1,0:T(8,128)(2,1)S(1)} %get-tuple-element.195), channel_id=1, source_target_pairs={{16,8},{24,16},{0,24},{8,0},{17,9},{25,17},{1,25},{9,1},{18,10},{2... | collective-permute-start | bytes 393224 | tf_op jit(solution)/shard_map/ppermute | solution.py:620
  39.7 13.2 %collective-permute-start.18 = (f32[16,32,256]{2,1,0:T(8,128)S(1)}, f32[16,32,256]{2,1,0:T(8,128)S(1)}, u32[]{:S(2)}, u32[]{:S(2)}) collective-permute-start(f32[16,32,256]{2,1,0:T(8,128)S(1)} %get-tuple-element.232.far), channel_id=1, source_target_pairs={{0,4},{4,0},{1,5},{5,1},{2,6},{6,2},{3,7},{7,3},{8,12},{12,8},{9,1... | collective-permute-start | bytes 1572872 | tf_op jit(solution)/shard_map/ppermute | solution.py:592
  40.2 6.6 %collective-permute-start.14 = (bf16[32,8,256]{2,1,0:T(8,128)(2,1)S(1)}, bf16[32,8,256]{2,1,0:T(8,128)(2,1)S(1)}, u32[]{:S(2)}, u32[]{:S(2)}) collective-permute-start(bf16[32,8,256]{2,1,0:T(8,128)(2,1)S(1)} %get-tuple-element.201), channel_id=1, source_target_pairs={{8,0},{16,8},{0,24},{24,16},{9,1},{17,9},{1,25},{25,17},{10,2},{18... | collective-permute-start | bytes 393224 | tf_op jit(solution)/shard_map/ppermute | solution.py:620
  43.0 6.3 %collective-permute-start.17 = (bf16[32,8,256]{2,1,0:T(8,128)(2,1)S(1)}, bf16[32,8,256]{2,1,0:T(8,128)(2,1)S(1)}, u32[]{:S(2)}, u32[]{:S(2)}) collective-permute-start(bf16[32,8,256]{2,1,0:T(8,128)(2,1)S(1)} %get-tuple-element.207), channel_id=1, source_target_pairs={{8,0},{16,8},{0,24},{24,16},{9,1},{17,9},{1,25},{25,17},{10,2},{18... | collective-permute-start | bytes 393224 | tf_op jit(solution)/shard_map/ppermute | solution.py:620
  47.7 6.1 %collective-permute-start.16 = (bf16[32,8,256]{2,1,0:T(8,128)(2,1)S(1)}, bf16[32,8,256]{2,1,0:T(8,128)(2,1)S(1)}, u32[]{:S(2)}, u32[]{:S(2)}) collective-permute-start(bf16[32,8,256]{2,1,0:T(8,128)(2,1)S(1)} %get-tuple-element.213), channel_id=1, source_target_pairs={{8,0},{0,16},{16,24},{24,8},{9,1},{1,17},{17,25},{25,9},{10,2},{2,... | collective-permute-start | bytes 393224 | tf_op jit(solution)/shard_map/ppermute | solution.py:620
  50.2 6.0 %collective-permute-start.19 = (bf16[16,8,256]{2,1,0:T(8,128)(2,1)S(1)}, bf16[16,8,256]{2,1,0:T(8,128)(2,1)S(1)}, u32[]{:S(2)}, u32[]{:S(2)}) collective-permute-start(bf16[16,8,256]{2,1,0:T(8,128)(2,1)S(1)} %get-tuple-element.219), channel_id=1, source_target_pairs={{8,0},{0,16},{16,24},{24,8},{9,1},{1,17},{17,25},{25,9},{10,2},{2,... | collective-permute-start | bytes 196616 | tf_op jit(solution)/shard_map/ppermute | solution.py:620
  51.6 4.7 %collective-permute-start.22 = (bf16[16,8,256]{2,1,0:T(8,128)(2,1)S(1)}, bf16[16,8,256]{2,1,0:T(8,128)(2,1)S(1)}, u32[]{:S(2)}, u32[]{:S(2)}) collective-permute-start(bf16[16,8,256]{2,1,0:T(8,128)(2,1)S(1)} %get-tuple-element.243), channel_id=1, source_target_pairs={{8,4},{12,0},{0,20},{4,16},{16,28},{20,24},{24,12},{28,8},{9,5},{1... | collective-permute-start | bytes 196616 | tf_op jit(solution)/shard_map/ppermute | solution.py:619
  51.6 3.5 %collective-permute-start.21 = (f32[16,8,256]{2,1,0:T(8,128)S(1)}, f32[16,8,256]{2,1,0:T(8,128)S(1)}, u32[]{:S(2)}, u32[]{:S(2)}) collective-permute-start(f32[16,8,256]{2,1,0:T(8,128)S(1)} %get-tuple-element.241), channel_id=1, source_target_pairs={{0,4},{4,0},{1,5},{5,1},{2,6},{6,2},{3,7},{7,3},{8,12},{12,8},{9,1... | collective-permute-start | bytes 393224 | tf_op jit(solution)/shard_map/ppermute | solution.py:592
  52.9 3.4 %collective-permute-start.23 = (f32[16,8,256]{2,1,0:T(8,128)S(1)}, f32[16,8,256]{2,1,0:T(8,128)S(1)}, u32[]{:S(2)}, u32[]{:S(2)}) collective-permute-start(f32[16,8,256]{2,1,0:T(8,128)S(1)} %get-tuple-element.246), channel_id=1, source_target_pairs={{0,4},{4,0},{1,5},{5,1},{2,6},{6,2},{3,7},{7,3},{8,12},{12,8},{9,1... | collective-permute-start | bytes 393224 | tf_op jit(solution)/shard_map/ppermute | solution.py:592
  55.1 1.6 %collective-permute-start.24 = (f32[16,8,256]{2,1,0:T(8,128)S(1)}, f32[16,8,256]{2,1,0:T(8,128)S(1)}, u32[]{:S(2)}, u32[]{:S(2)}) collective-permute-start(f32[16,8,256]{2,1,0:T(8,128)S(1)} %get-tuple-element.248), channel_id=1, source_target_pairs={{0,4},{4,0},{1,5},{5,1},{2,6},{6,2},{3,7},{7,3},{8,12},{12,8},{9,1... | collective-permute-start | bytes 393224 | tf_op jit(solution)/shard_map/ppermute | solution.py:592
  (1 other events, 1.6 us)
